TPU v7x, 32 devices: a whole 2x2x4 slice. The times are simulated.
32 devices in a mesh: ctx: 8 (over y, x, core), head: 4 (over z).
Axes of the slice: x: 2, y: 2, z: 4, core: 2. Of those that a mesh axis runs over, the one named last changes fastest.
Arguments:
- query: bfloat16 [512, 64, 128], P('ctx', 'head'), may hold values from -6 to 6
- weights: bfloat16 [512, 64], P('ctx', 'head'), as said below
- keys: bfloat16 [16384, 128], P('ctx'), may hold values from -6 to 6
- main_logits: bfloat16 [512, 16384], P(None, 'ctx'), as said below
- row_weight: float32 [512], replicated, may hold values from 4 to 40
- offset: int32 [1], replicated, may hold values from 15360 to 15872
Outputs:
- query_grad: float32 [512, 64, 128], P('ctx', 'head')
- key_grad: float32 [16384, 128], P(('ctx', 'head'))
- weight_grad: float32 [512, 64], P('ctx', 'head')
Inputs may be any that keep to these rules, and one draw needn't show every extreme that they name: query row t of the block sits at position offset + t. Finite weights. `main_logits`: finite logits.
All inputs are finite; a program needn't handle non-finite values.
Results may differ from a plain program's by a relative error of at most 0.0065.
Values may be sent and summed in bfloat16 or wider, within the bound.
No kernel may reach another device: no remote copies, remote signals or barrier semaphores. Data moves between devices by JAX's collectives and lax.ppermute only.
A program may use at most 64 MiB of HBM per device.

v0:
```python
import jax
import jax.numpy as jnp
from jax import lax
from jax.sharding import PartitionSpec as P

masked_value = -1e30


def exp_total(masked, peak, allowed):
    return jnp.sum(jnp.where(allowed, jnp.exp(masked - peak[:, None]), 0.0), axis=1)


def global_stats(masked, tmasked, allowed):
    peak = jnp.max(masked, axis=1)
    tpeak = jnp.max(tmasked, axis=1)
    peak, tpeak = lax.pmax((peak, tpeak), ("ctx", "head"))
    total, ttotal = lax.psum(
        (exp_total(masked, peak, allowed), exp_total(tmasked, tpeak, allowed)), ("ctx", "head")
    )
    return (peak, total, tpeak, ttotal)


def finish_grad(masked, tmasked, allowed, stats, row_weight, loss_scale):
    peak, total, tpeak, ttotal = stats
    index_prob = jnp.where(allowed, jnp.exp(masked - peak[:, None]), 0.0) / total[:, None]
    target = jnp.where(allowed, jnp.exp(tmasked - tpeak[:, None]), 0.0) / ttotal[:, None]
    return jnp.where(allowed, row_weight[:, None] * loss_scale * (index_prob - target), 0.0).astype(
        jnp.bfloat16
    )


def per_device(query, weights, keys, main_logits, row_weight, offset):
    gathered_q, gathered_w = (
        lax.all_gather(query, "ctx", axis=0, tiled=True),
        lax.all_gather(weights, "ctx", axis=0, tiled=True),
    )
    rows_total = gathered_q.shape[0]
    heads_here = gathered_q.shape[1]
    depth = gathered_q.shape[2]
    key_count = keys.shape[0]
    block_len = min(512, key_count)
    nblocks = key_count // block_len
    total_keys = key_count * lax.axis_size("ctx")
    head_scale = depth ** (-0.5)
    loss_scale = float(total_keys) ** 0.5
    high = lax.Precision.HIGHEST
    weight_f = gathered_w.astype(jnp.float32)
    key_blocks = keys.reshape(nblocks, block_len, depth)

    def forward_block(key_block):
        dotted = jnp.einsum(
            "thd,sd->ths", gathered_q, key_block, preferred_element_type=jnp.float32
        )
        active = jnp.maximum(dotted, 0.0) * head_scale
        return jnp.einsum("th,ths->ts", weight_f, active, precision=high)

    partial_scores = jnp.moveaxis(lax.map(forward_block, key_blocks), 0, 1).reshape(
        rows_total, key_count
    )
    limit = offset[0] + jnp.arange(rows_total, dtype=jnp.int32)[:, None]
    ctx_first = lax.axis_index("ctx") * key_count
    share_width = key_count // lax.axis_size("head")
    share_first = lax.axis_index("head") * share_width
    scores = lax.psum(partial_scores, "head")
    positions = ctx_first + jnp.arange(key_count, dtype=jnp.int32)
    allowed = positions[None, :] <= limit
    masked = jnp.where(allowed, scores, masked_value)
    tmasked = jnp.where(allowed, main_logits.astype(jnp.float32), masked_value)
    share_masked = lax.dynamic_slice_in_dim(masked, share_first, share_width, 1)
    share_tmasked = lax.dynamic_slice_in_dim(tmasked, share_first, share_width, 1)
    share_allowed = lax.dynamic_slice_in_dim(allowed, share_first, share_width, 1)
    stats = global_stats(share_masked, share_tmasked, share_allowed)
    score_grad = finish_grad(masked, tmasked, allowed, stats, row_weight, loss_scale)
    grad_blocks = jnp.moveaxis(score_grad.reshape(rows_total, nblocks, block_len), 1, 0)

    def backward_block(carry, inputs):
        query_acc, weight_acc = carry
        key_block, grad_block = inputs
        dotted = jnp.einsum(
            "thd,sd->ths", gathered_q, key_block, preferred_element_type=jnp.float32
        )
        active = jnp.maximum(dotted, 0.0) * head_scale
        grad_f = grad_block.astype(jnp.float32)
        pre_grad = jnp.where(
            dotted > 0, grad_f[:, None, :] * weight_f[:, :, None] * head_scale, 0.0
        ).astype(jnp.bfloat16)
        query_acc = query_acc + jnp.einsum(
            "ths,sd->thd", pre_grad, key_block, preferred_element_type=jnp.float32
        )
        weight_acc = weight_acc + jnp.einsum("ts,ths->th", grad_f, active, precision=high)
        key_part = jnp.einsum(
            "ths,thd->sd", pre_grad, gathered_q, preferred_element_type=jnp.float32
        )
        return ((query_acc, weight_acc), key_part)

    start_carry = (
        jnp.zeros((rows_total, heads_here, depth), jnp.float32),
        jnp.zeros((rows_total, heads_here), jnp.float32),
    )
    (query_acc, weight_acc), key_parts = lax.scan(
        backward_block, start_carry, (key_blocks, grad_blocks)
    )
    key_grad = lax.psum_scatter(
        key_parts.reshape(key_count, depth), "head", scatter_dimension=0, tiled=True
    )
    query_grad, weight_grad = (
        lax.psum_scatter(query_acc, "ctx", scatter_dimension=0, tiled=True),
        lax.psum_scatter(weight_acc, "ctx", scatter_dimension=0, tiled=True),
    )
    return (query_grad, key_grad, weight_grad)


def solution(mesh):
    in_specs = (P("ctx", "head", None), P("ctx", "head"), P("ctx", None), P(None, "ctx"), P(), P())
    out_specs = (P("ctx", "head", None), P(("ctx", "head"), None), P("ctx", "head"))
    return jax.shard_map(
        per_device, mesh=mesh, in_specs=in_specs, out_specs=out_specs, check_vma=False
    )
```

profile of v0, /device:TPU:0, one launch (start us, length us, event | category | flops | bytes accessed | tf_op | source)
XLA Modules:
  0.0 497.5 jit_solution(10502718043094056174)
XLA Ops:
  9.0 10.7 %all-gather = bf16[8,64,16]{1,2,0:T(8,128)(2,1)S(1)} all-gather(bf16[1,64,16]{1,2,0:T(8,128)(2,1)} %bitcast.81), channel_id=1, replica_groups=mesh['ctx'=8,'head'=4] {'ctx'}, dimensions={0}, use_global_device_ids=true | all-gather | bytes 18432 | tf_op jit(solution)/shard_map/all_gather | solution.py:35
  19.8 21.3 %all-gather.3.cloned.1.call-done = bf16[512,16,128]{2,0,1:T(8,128)(2,1)} async-done(((bf16[64,16,128]{2,0,1:T(8,128)(2,1)}), bf16[512,16,128]{2,0,1:T(8,128)(2,1)}) %all-gather.3.cloned.1.call-update) | async-done | bytes 2097168 | tf_op jit(solution)/shard_map/all_gather | solution.py:34
  41.1 24.1 %while.25 = (s32[]{:T(128)}, f32[4,512,512]{1,2,0:T(8,128)}, bf16[4,512,128]{2,1,0:T(8,128)(2,1)}, bf16[512,16,128]{2,0,1:T(8,128)(2,1)}, f32[512,16]{0,1:T(8,128)S(1)}, /*index=5*/s32[]{:T(128)}) while((s32[]{:T(128)}, f32[4,512,512]{1,2,0:T(8,128)}, bf16[4,512,128]{2,1,0:T(8,128)(2,1)}, bf16[512,16,128]{2,0,1:T(8,128)(2,1)}, ...), condition=%wide.region_1.2_spmd, body=%wide.region_0.1_spmd.sunk | while | flops 1090256896 | bytes 9601109 | solution.py:57
  41.1 4.3 fusion.31
  47.2 4.3 fusion.31
  53.2 4.3 fusion.31
  59.2 4.3 fusion.31
  69.7 150.7 %all-reduce.4.cloned.1.call-done = f32[512,2048]{0,1:T(8,128)} async-done(((f32[512,2048]{0,1:T(8,128)}), f32[512,2048]{0,1:T(8,128)}) %all-reduce.4.cloned.1.call-update) | async-done | bytes 4194320 | tf_op jit(solution)/shard_map/psum | solution.py:64
  220.4 4.0 compare_select_fusion.2
  227.8 39.3 %all-reduce.1 = (f32[512]{0:T(512)S(1)}, f32[512]{0:T(512)S(1)}) all-reduce(f32[512]{0:T(512)S(1)} %get-tuple-element.152, f32[512]{0:T(512)S(1)} %get-tuple-element.151), channel_id=1, replica_groups=mesh['ctx'=8,'head'=4] {'ctx','head'}, use_global_device_ids=true, to_apply=%region_4.5 | all-reduce | flops 1024 | bytes 8192 | tf_op jit(solution)/shard_map/pmax | solution.py:16
  269.0 40.2 %all-reduce = (f32[512]{0:T(512)S(1)}, f32[512]{0:T(512)S(1)}) all-reduce(f32[512]{0:T(512)S(1)} %get-tuple-element.116, f32[512]{0:T(512)S(1)} %get-tuple-element.115), channel_id=1, replica_groups=mesh['ctx'=8,'head'=4] {'ctx','head'}, use_global_device_ids=true, to_apply=%region_10.11 | all-reduce | flops 1024 | bytes 8192 | tf_op jit(solution)/shard_map/psum | solution.py:17
  309.2 5.6 %fusion.17 = bf16[512,2048]{0,1:T(8,128)(2,1)} fusion(f32[512]{0:T(512)S(1)} %get-tuple-element.143, f32[512]{0:T(512)S(1)} %get-tuple-element.146, f32[512]{0:T(512)S(1)} %get-tuple-element.144, f32[512]{0:T(512)S(1)} %get-tuple-element.145, f32[512]{0:T(512)S(1)} %broadcast_multiply_fusion, s32[512]{0:T(512)S(1)} %iota_add_fusion.1, ...), kind=kLoop, calls=%fused_computation.30 | loop fusion | flops 14680064 | bytes 8409088 | tf_op jit(solution)/shard_map/convert_element_type | solution.py:27
  314.8 57.5 %while.26 = (s32[]{:T(128)}, f32[512,16,128]{2,0,1:T(8,128)}, f32[512,16]{0,1:T(8,128)S(1)}, f32[4,512,128]{2,1,0:T(8,128)}, bf16[4,512,128]{2,1,0:T(8,128)(2,1)...) while((s32[]{:T(128)}, f32[512,16,128]{2,0,1:T(8,128)}, ...), condition=%wide.region_12.13_spmd.clone, body=%wide.region_11.12_spmd.clone.sunk | while | flops 3282313216 | bytes 68354184 | solution.py:100
  321.7 6.3 %select_add_fusion.4 = f32[512,16,128]{2,0,1:T(8,128)} fusion(f32[512,16,128]{2,0,1:T(8,128)} %get-tuple-element.266, pred[]{:T(512)S(6)} %compare.3, bf16[4,512,128]{2,1,0:T(8,128)(2,1)S(1)} %get-tuple-element.279, s32[]{:T(128)S(6)} %copy.70, f32[512,512,16]{1,0,2:T(8,128)S(1)} %get-tuple-element.235, f32[512,16]{0,1:T(8,128)S(1)} %get-tuple-element.282, ...), kind=kOutput, calls=%fused_computation.9.clone.1 | convolution fusion | flops 1096810496 | bytes 26378244 | tf_op jit(solution)/shard_map/while/body/eval_jaxpr/ths,sd->thd/dot_general | solution.py:87
  331.8 3.0 fusion.36
  334.9 7.9 %select_add_fusion.4 = f32[512,16,128]{2,0,1:T(8,128)} fusion(f32[512,16,128]{2,0,1:T(8,128)} %get-tuple-element.266, pred[]{:T(512)S(6)} %compare.3, bf16[4,512,128]{2,1,0:T(8,128)(2,1)S(1)} %get-tuple-element.279, s32[]{:T(128)S(6)} %copy.70, f32[512,512,16]{1,0,2:T(8,128)S(1)} %get-tuple-element.235, f32[512,16]{0,1:T(8,128)S(1)} %get-tuple-element.282, ...), kind=kOutput, calls=%fused_computation.9.clone.1 | convolution fusion | flops 1096810496 | bytes 26378244 | tf_op jit(solution)/shard_map/while/body/eval_jaxpr/ths,sd->thd/dot_general | solution.py:87
  346.6 3.1 fusion.36
  349.6 7.9 %select_add_fusion.4 = f32[512,16,128]{2,0,1:T(8,128)} fusion(f32[512,16,128]{2,0,1:T(8,128)} %get-tuple-element.266, pred[]{:T(512)S(6)} %compare.3, bf16[4,512,128]{2,1,0:T(8,128)(2,1)S(1)} %get-tuple-element.279, s32[]{:T(128)S(6)} %copy.70, f32[512,512,16]{1,0,2:T(8,128)S(1)} %get-tuple-element.235, f32[512,16]{0,1:T(8,128)S(1)} %get-tuple-element.282, ...), kind=kOutput, calls=%fused_computation.9.clone.1 | convolution fusion | flops 1096810496 | bytes 26378244 | tf_op jit(solution)/shard_map/while/body/eval_jaxpr/ths,sd->thd/dot_general | solution.py:87
  361.4 3.1 fusion.36
  364.4 7.9 %select_add_fusion.4 = f32[512,16,128]{2,0,1:T(8,128)} fusion(f32[512,16,128]{2,0,1:T(8,128)} %get-tuple-element.266, pred[]{:T(512)S(6)} %compare.3, bf16[4,512,128]{2,1,0:T(8,128)(2,1)S(1)} %get-tuple-element.279, s32[]{:T(128)S(6)} %copy.70, f32[512,512,16]{1,0,2:T(8,128)S(1)} %get-tuple-element.235, f32[512,16]{0,1:T(8,128)S(1)} %get-tuple-element.282, ...), kind=kOutput, calls=%fused_computation.9.clone.1 | convolution fusion | flops 1096810496 | bytes 26378244 | tf_op jit(solution)/shard_map/while/body/eval_jaxpr/ths,sd->thd/dot_general | solution.py:87
  374.0 6.6 %copy.32 = f32[512,16,128]{2,1,0:T(8,128)} copy(f32[512,16,128]{2,0,1:T(8,128)} %get-tuple-element.75) | data formatting | bytes 8388608 | tf_op jit(solution)/shard_map/while | solution.py:100
  380.6 26.2 %reduce-scatter.10.cloned.1.call-done = f32[64,16]{1,0:T(8,128)} async-done(((f32[512,16]{1,0:T(8,128)}), f32[64,16]{1,0:T(8,128)}) %reduce-scatter.10.cloned.1.call-update) | async-done | bytes 4112
  408.3 28.5 %reduce-scatter.8.cloned.1.call-done = f32[512,128]{1,0:T(8,128)} async-done(((f32[2048,128]{1,0:T(8,128)}), f32[512,128]{1,0:T(8,128)}) %reduce-scatter.8.cloned.1.call-update) | async-done | bytes 262160 | tf_op jit(solution)/shard_map/reduce_scatter | solution.py:103
  436.8 54.2 %reduce-scatter.6.cloned.1.call-done = f32[64,16,128]{2,1,0:T(8,128)} async-done(((f32[512,16,128]{2,1,0:T(8,128)}), f32[64,16,128]{2,1,0:T(8,128)}) %reduce-scatter.6.cloned.1.call-update) | async-done | bytes 524304 | tf_op jit(solution)/shard_map/reduce_scatter | solution.py:107
  (61 shorter events, 39.4 us)
Async XLA Ops:
  7.2 33.9 %all-gather.3.cloned.1.call-start = ((), (), s32[]{:S(2)}) async-start(), calls=%async_computation.3 | async-start | bytes 2359296 | tf_op jit(solution)/shard_map/all_gather | solution.py:34
  9.0 211.4 %all-reduce.4.cloned.1.call-start = ((), (), s32[]{:S(2)}) async-start(), calls=%async_computation.4 | async-start | bytes 8388608 | tf_op jit(solution)/shard_map/psum | solution.py:64
  65.2 3.7 copy-start.4
  65.3 341.6 %reduce-scatter.10.cloned.1.call-start = ((), (), s32[]{:S(2)}) async-start(), calls=%async_computation.7 | async-start | bytes 294912
  68.9 240.3 %copy-start.1 = (bf16[512,2048]{0,1:T(8,128)(2,1)}, bf16[512,2048]{0,1:T(8,128)(2,1)S(1)}, u32[]{:S(2)}) copy-start(bf16[512,2048]{0,1:T(8,128)(2,1)S(1)} %copy.31) | copy-start | bytes 6291460
  224.4 2.0 copy-start.2
  309.2 5.6 %copy-start = (bf16[512,16,128]{2,0,1:T(8,128)(2,1)S(1)}, bf16[512,16,128]{2,0,1:T(8,128)(2,1)}, u32[]{:S(2)}) copy-start(bf16[512,16,128]{2,0,1:T(8,128)(2,1)} %get-tuple-element.291) | copy-start | bytes 6291460
  309.2 5.6 %copy-start.3 = (bf16[4,512,128]{2,1,0:T(8,128)(2,1)S(1)}, bf16[4,512,128]{2,1,0:T(8,128)(2,1)}, u32[]{:S(2)}) copy-start(bf16[4,512,128]{2,1,0:T(8,128)(2,1)} %get-tuple-element.301) | copy-start | bytes 1572868
  373.2 63.6 %reduce-scatter.8.cloned.1.call-start = ((), (), s32[]{:S(2)}) async-start(), calls=%async_computation.6 | async-start | bytes 1310720 | tf_op jit(solution)/shard_map/reduce_scatter | solution.py:103
  373.8 117.2 %reduce-scatter.6.cloned.1.call-start = ((), (), s32[]{:S(2)}) async-start(), calls=%async_computation.5 | async-start | bytes 4718592 | tf_op jit(solution)/shard_map/reduce_scatter | solution.py:107
Sparse Core Ops, SparseCore 0:
  10.5 30.5 all-gather.2
  65.4 154.9 all-reduce.3
  373.3 33.5 reduce-scatter.9
  409.6 27.1 reduce-scatter.7
  440.9 49.9 reduce-scatter.5
where the time goes:
time: 498 us
  waiting for transfers between devices  282 us (57%)
  blocking collectives  90.1 us (18%)
  matrix products  69.9 us (14%)
  local copies, waits for them, and re-layouts  22.4 us (4%)
  other arithmetic  18.4 us (4%)
  between operations  14.5 us (3%)
    psum x1, waiting for transfers between devices, per_device(): scores = lax.psum(partial_scores, 'head')  151 us
    reduce_scatter x1, waiting for transfers between devices, per_device(): lax.psum_scatter(query_acc, 'ctx', scatter_dimension=0, tiled=True)  54.2 us
    psum x1, blocking collectives, global_stats(): lax.psum((exp_total(masked, peak, allowed), exp_total(tmasked, tpeak, all...  40.2 us
    pmax x1, blocking collectives, global_stats(): peak, tpeak = lax.pmax((peak, tpeak), ('ctx', 'head'))  39.3 us
    dot_general x4, matrix products, backward_block(): jnp.einsum('ths,sd->thd', pre_grad, key_block, preferred_element_type=jnp...  29.9 us
    reduce_scatter x1, waiting for transfers between devices, per_device(): lax.psum_scatter(key_parts.reshape(key_count, depth), 'head', scatter_dim...  28.5 us
    unnamed x6, waiting for transfers between devices  26.8 us
    all_gather x1, waiting for transfers between devices, per_device(): lax.all_gather(query, 'ctx', axis=0, tiled=True)  21.3 us
  transfers between devices with their start and end apart: 5, of which 5 were waited for; matrix products, arithmetic and copies ran while one was open for 2% of the time, Pallas kernels for 0%

commit v1 on v0

v1 whole, which is shorter than its diff:
```python
import functools

import jax
import jax.numpy as jnp
from jax import lax
from jax.experimental import pallas as pl
from jax.experimental.pallas import tpu as pltpu
from jax.sharding import PartitionSpec as P

masked_value = -1e30
lanes = 128
stat_rows = 8
vmem_bytes = 26 * 1024 * 1024
contract_last = (((1,), (1,)), ((), ()))


def swap(value, axis, distance):
    size = lax.axis_size(axis)
    return lax.ppermute(value, axis, [(i, i ^ distance) for i in range(size)])


def in_pairs(count, first, step):
    first(0, 0)

    def body(i, _):
        step(0, 2 * i, 2 * i + 1)
        step(1, 2 * i + 1, 2 * i + 2)
        return 0

    lax.fori_loop(0, count // 2 - 1, body, 0)
    step(0, count - 2, count - 1)
    step(1, count - 1, None)


def row_limits(meta_ref, rows_here):
    row = lax.broadcasted_iota(jnp.int32, (rows_here, 1), 0)
    return meta_ref[0] + meta_ref[1] * rows_here + row


def piece_allowed(meta_ref, limit, k, kc, chunk):
    first = (meta_ref[1] ^ k) * kc + meta_ref[2] * chunk
    position = first + lax.broadcasted_iota(jnp.int32, (limit.shape[0], chunk), 1)
    return position <= limit


def forward_kernel(cfg, meta_ref, *refs):
    n, nh, rows_here, hh, depth, kc, chunk, scale = cfg
    q_refs, k_refs = refs[:nh], refs[nh : nh + n]
    logits_ref, score_ref, keys_ref, qw_ref, stats_ref = refs[nh + n : nh + n + 5]
    q_all, wb, dots, cols = refs[nh + n + 5 :]
    groups, rows = q_all.shape[0], q_all.shape[1]
    bt = rows_here // groups
    part = bt * hh
    tile = dots.shape[3]
    for k in range(n):
        keys_ref[k * chunk : (k + 1) * chunk, :] = k_refs[k][...]
    eye = (
        lax.broadcasted_iota(jnp.int32, (hh, lanes), 0)
        == lax.broadcasted_iota(jnp.int32, (hh, lanes), 1)
    ).astype(jnp.float32)
    for j in range(nh):
        slab = q_refs[j][rows_here:].reshape(rows_here, lanes).astype(jnp.float32)
        for g in range(groups):
            w = slab[g * bt : (g + 1) * bt]
            picked = jnp.sum(w[:, None, :] * eye[None], axis=-1, keepdims=True)
            wide = jnp.broadcast_to(picked, (bt, hh, lanes)).reshape(part, lanes)
            q = q_refs[j][g * bt : (g + 1) * bt].reshape(part, depth)
            q_all[g, j * part : (j + 1) * part, :] = q
            wb[g, j * part : (j + 1) * part, :] = wide
            scaled = (q.astype(jnp.float32) * (wide * scale)).T.astype(jnp.bfloat16)
            qw_ref[j, :, g * part : (g + 1) * part] = scaled

    def key_tile(s):
        return keys_ref[pl.ds(pl.multiple_of(s * tile, tile), tile), :]

    def products(buffer, s, g, keys):
        dots[buffer, g] = lax.dot_general(
            q_all[g], keys, contract_last, preferred_element_type=jnp.float32
        )

    def first(buffer, s):
        keys = key_tile(s)
        for g in range(groups):
            products(buffer, s, g, keys)

    def step(buffer, s, following):
        if following is not None:
            keys = key_tile(following)
        for g in range(groups):
            if following is not None:
                products(1 - buffer, following, g, keys)
            for i in range(tile // lanes):
                total = None
                for j in range(nh):
                    at = slice(j * part, (j + 1) * part)
                    value = dots[buffer, g, at, i * lanes : (i + 1) * lanes]
                    value = jnp.maximum(value, 0.0) * wb[g, at, :]
                    total = value if total is None else total + value
                summed = jnp.sum(total.reshape(bt, hh, lanes), axis=1) * scale
                column = pl.multiple_of(s * tile + i * lanes, lanes)
                score_ref[g * bt : (g + 1) * bt, pl.ds(column, lanes)] = summed

    in_pairs(n * chunk // tile, first, step)

    limit = row_limits(meta_ref, rows_here)
    lane = lax.broadcasted_iota(jnp.int32, (rows_here, lanes), 1)
    out = jnp.zeros((rows_here, lanes), jnp.float32)

    def piece(i, k):
        if i == 0:
            return score_ref[:, k * chunk : (k + 1) * chunk]
        return logits_ref[meta_ref[1] ^ k].astype(jnp.float32)

    for i in range(2):
        peak = None
        for k in range(n):
            allowed = piece_allowed(meta_ref, limit, k, kc, chunk)
            here = jnp.max(jnp.where(allowed, piece(i, k), masked_value), axis=1, keepdims=True)
            peak = here if peak is None else jnp.maximum(peak, here)
        total = None
        for k in range(n):
            allowed = piece_allowed(meta_ref, limit, k, kc, chunk)
            here = jnp.where(allowed, jnp.exp(piece(i, k) - peak), 0.0)
            here = jnp.sum(here, axis=1, keepdims=True)
            total = here if total is None else total + here
        out = jnp.where(lane == 2 * i, peak, out)
        out = jnp.where(lane == 2 * i + 1, total, out)
    cols[...] = jnp.zeros_like(cols)
    cols[:rows_here, :] = out
    stats_ref[0] = cols[...].T[:stat_rows]


def score_gradient(cfg, meta_ref, stats, rw_ref, logits_ref, score_ref, cols, grad_ref):
    n, nh, rows_here, hh, depth, kc, chunk, scale = cfg
    for i in range(2):
        peak = functools.reduce(jnp.maximum, [st[2 * i : 2 * i + 1] for st in stats])
        total = functools.reduce(
            jnp.add,
            [st[2 * i + 1 : 2 * i + 2] * jnp.exp(st[2 * i : 2 * i + 1] - peak) for st in stats],
        )
        cols[2 * i : 2 * i + 1, :] = peak
        cols[2 * i + 1 : 2 * i + 2, :] = rw_ref[...] / total
    cols[4:, :] = jnp.zeros((cols.shape[0] - 4, cols.shape[1]), jnp.float32)
    st = cols[...].T[:rows_here]
    limit = row_limits(meta_ref, rows_here)
    for k in range(n):
        logits = logits_ref[meta_ref[1] ^ k].astype(jnp.float32)
        score = score_ref[:, k * chunk : (k + 1) * chunk]
        g = jnp.exp(score - st[:, 0:1]) * st[:, 1:2] - jnp.exp(logits - st[:, 2:3]) * st[:, 3:4]
        g = jnp.where(piece_allowed(meta_ref, limit, k, kc, chunk), g, 0.0)
        grad_ref[:, k * chunk : (k + 1) * chunk] = g.astype(jnp.bfloat16)


def backward_kernel(cfg, is_first, is_last, meta_ref, *refs):
    n, nh, rows_here, hh, depth, kc, chunk, scale = cfg
    refs = list(refs)
    take = lambda count: [refs.pop(0) for _ in range(count)]
    q_ref, qw_ref, keys_ref = take(3)
    if is_first:
        stat_refs = take(nh)
        rw_ref, logits_ref, score_ref = take(3)
    else:
        grad_ref, kg_in_ref = take(2)
    (u_ref,) = take(1)
    if is_last:
        even_refs = take(n // 2)
        odd_refs = take(1)
    else:
        (kg_ref,) = take(1)
    if is_first:
        (grad_ref,) = take(1)
    masks, u_acc = take(2)
    if is_first:
        (cols,) = take(1)
    if is_last:
        (kg_ref,) = take(1)
    tile = masks.shape[2]
    rows = rows_here * hh
    if is_first:
        stats = [ref[0] for ref in stat_refs]
        score_gradient(cfg, meta_ref, stats, rw_ref, logits_ref, score_ref, cols, grad_ref)

    def tile_at(s):
        return pl.ds(pl.multiple_of(s * tile, tile), tile)

    def mask(buffer, s):
        dotted = lax.dot_general(
            q_ref[:rows_here].reshape(rows, depth),
            keys_ref[tile_at(s), :],
            contract_last,
            preferred_element_type=jnp.float32,
        )
        g = grad_ref[:, tile_at(s)].astype(jnp.float32)
        wide = jnp.broadcast_to(g[:, None, :], (rows_here, hh, tile)).reshape(rows, tile)
        masks[buffer] = jnp.where(dotted > 0, wide, 0.0).astype(jnp.bfloat16)

    def step(buffer, s, following):
        if following is not None:
            mask(1 - buffer, following)
        masked = masks[buffer]
        u_acc[...] += jnp.dot(
            masked, keys_ref[tile_at(s), :], preferred_element_type=jnp.float32
        )
        more = jnp.dot(qw_ref[0], masked, preferred_element_type=jnp.float32)
        if is_first:
            kg_ref[:, tile_at(s)] = more
        else:
            kg_ref[:, tile_at(s)] = kg_in_ref[:, tile_at(s)] + more

    u_acc[...] = jnp.zeros_like(u_acc)
    in_pairs(n * chunk // tile, mask, step)
    u_ref[...] = u_acc[...].reshape(rows_here, hh, depth).astype(u_ref.dtype)
    if is_last:
        for i in range(n // 2):
            k = 2 * i
            even_refs[i][...] = kg_ref[:, k * chunk : (k + 1) * chunk]
            odd_refs[0][i] = kg_ref[:, (k + 1) * chunk : (k + 2) * chunk].astype(jnp.bfloat16)


def per_device(query, weights, keys, main_logits, row_weight, offset):
    n = lax.axis_size("ctx")
    nh = lax.axis_size("head")
    c = lax.axis_index("ctx")
    h = lax.axis_index("head")
    rows_here, hh, depth = query.shape
    kc = keys.shape[0]
    chunk = kc // nh
    rows = rows_here * hh
    scale = depth ** (-0.5)
    loss_scale = float(kc * n) ** 0.5
    bf16, f32 = jnp.bfloat16, jnp.float32

    w_slab = jnp.pad(weights, ((0, 0), (0, lanes - hh))).reshape(rows_here // hh, hh, lanes)
    message = jnp.concatenate([query, w_slab], axis=0)
    q_blocks = [message] + [swap(message, "head", j) for j in range(1, nh)]

    k_pieces = [None] * n
    k_pieces[0] = lax.dynamic_slice_in_dim(keys, h * chunk, chunk, 0)
    for k in range(0, n, 2):
        if k > 0:
            k_pieces[k] = swap(k_pieces[0], "ctx", k)
        k_pieces[k + 1] = swap(k_pieces[k], "ctx", 1)

    logits = lax.dynamic_slice_in_dim(main_logits, h * chunk, chunk, 1)
    logits = lax.all_to_all(logits.reshape(n, rows_here, chunk), "ctx", 0, 0, tiled=True)

    meta = jnp.concatenate([offset, jnp.stack([c, h]).astype(jnp.int32)])
    rw = lax.dynamic_slice_in_dim(row_weight, c * rows_here, rows_here, 0)[None, :]
    padded = -(-rows_here // lanes) * lanes
    rw = jnp.pad(rw * loss_scale, ((0, 0), (0, padded - rows_here)))

    cfg = (n, nh, rows_here, hh, depth, kc, chunk, scale)
    total_keys = n * chunk
    groups = max(1, rows_here // 16)
    smem = pl.BlockSpec(memory_space=pltpu.SMEM)
    vmem = pl.BlockSpec(memory_space=pltpu.VMEM)
    macs = rows * total_keys * depth
    params = pltpu.CompilerParams(vmem_limit_bytes=vmem_bytes)
    tile = 256
    score, keys_all, qw, stats = pl.pallas_call(
        functools.partial(forward_kernel, cfg),
        out_shape=[
            jax.ShapeDtypeStruct((rows_here, total_keys), f32),
            jax.ShapeDtypeStruct((total_keys, depth), bf16),
            jax.ShapeDtypeStruct((nh, depth, rows), bf16),
            jax.ShapeDtypeStruct((1, stat_rows, padded), f32),
        ],
        in_specs=[smem] + [vmem] * (nh + n + 1),
        out_specs=[vmem] * 4,
        scratch_shapes=[
            pltpu.VMEM((groups, nh * rows // groups, depth), bf16),
            pltpu.VMEM((groups, nh * rows // groups, lanes), f32),
            pltpu.VMEM((2, groups, nh * rows // groups, tile), f32),
            pltpu.VMEM((padded, lanes), f32),
        ],
        compiler_params=params,
        cost_estimate=pl.CostEstimate(
            flops=4 * nh * macs, bytes_accessed=6 * 1024 * 1024, transcendentals=0
        ),
        name="forward",
    )(meta, *q_blocks, *k_pieces, logits)

    all_stats = [stats] + [swap(stats, "head", j) for j in range(1, nh)]

    tile = 512
    grad = kg = None
    sent = []
    for j in reversed(range(nh)):
        is_first, is_last = j == nh - 1, j == 0
        operands = [meta, q_blocks[j], lax.slice_in_dim(qw, j, j + 1, axis=0), keys_all]
        u_type = f32 if is_last else bf16
        out_shape = [jax.ShapeDtypeStruct((rows_here, hh, depth), u_type)]
        scratch = [pltpu.VMEM((2, rows, tile), bf16), pltpu.VMEM((rows, depth), f32)]
        if is_first:
            operands += all_stats + [rw, logits, score]
        else:
            operands += [grad, kg]
        if is_last:
            out_shape += [jax.ShapeDtypeStruct((depth, chunk), f32) for _ in range(n // 2)]
            out_shape += [jax.ShapeDtypeStruct((n // 2, depth, chunk), bf16)]
            scratch += [pltpu.VMEM((depth, total_keys), f32)]
        else:
            out_shape += [jax.ShapeDtypeStruct((depth, total_keys), f32)]
        if is_first:
            out_shape += [jax.ShapeDtypeStruct((rows_here, total_keys), bf16)]
            scratch += [pltpu.VMEM((padded, lanes), f32)]
        outs = pl.pallas_call(
            functools.partial(backward_kernel, cfg, is_first, is_last),
            out_shape=out_shape,
            in_specs=[smem] + [vmem] * (len(operands) - 1),
            out_specs=[vmem] * len(out_shape),
            scratch_shapes=scratch,
            compiler_params=params,
            cost_estimate=pl.CostEstimate(
                flops=12 * macs, bytes_accessed=4 * 1024 * 1024, transcendentals=0
            ),
            name=f"backward{j}",
        )(*operands)
        if is_last:
            u_mine, even, odd = outs[0], outs[1 : 1 + n // 2], outs[1 + n // 2]
        else:
            sent.append(swap(outs[0], "head", j))
            kg = outs[1]
        if is_first:
            grad = outs[2]

    other = swap(odd, "ctx", 1)
    even = [even[i] + other[i].astype(f32) for i in range(n // 2)]
    key_grad = even[0]
    for i in range(1, n // 2):
        key_grad = key_grad + swap(even[i].astype(bf16), "ctx", 2 * i).astype(f32)
    key_grad = key_grad.T

    total = u_mine
    for value in sent:
        total = total + value.astype(f32)
    weight_f = weights.astype(f32)
    query_grad = total * (weight_f * scale)[:, :, None]
    weight_grad = jnp.sum(total * query.astype(f32), axis=-1) * scale
    return query_grad, key_grad, weight_grad


def solution(mesh):
    in_specs = (P("ctx", "head", None), P("ctx", "head"), P("ctx", None), P(None, "ctx"), P(), P())
    out_specs = (P("ctx", "head", None), P(("ctx", "head"), None), P("ctx", "head"))
    return jax.shard_map(
        per_device, mesh=mesh, in_specs=in_specs, out_specs=out_specs, check_vma=False
    )
```

time: 498 us -> 137 us (0.28)
  waiting for transfers between devices: 282 us -> 39.9 us
  blocking collectives: 90.1 us -> 0 us
  matrix products: 69.9 us -> 0 us
  Pallas kernels: 0 us -> 46.9 us
  starting transfers between devices: 0.42 us -> 33.4 us
  local copies, waits for them, and re-layouts: 22.4 us -> 8.55 us
  between operations: 14.5 us -> 1.43 us
  other arithmetic: 18.4 us -> 5.92 us
    psum x1 -> x0, waiting for transfers between devices: 151 us -> none  [per_device(): scores = lax.psum(partial_scores, 'head')]
    reduce_scatter x2 -> x0, waiting for transfers between devices: 82.7 us -> none  [the longest x1 54.2 us: per_device(): lax.psum_scatter(query_acc, 'ctx', scatter_dimension=0, tiled=True)]
    dot_general x16 -> x0, matrix products: 69.9 us -> none  [the longest x4 29.9 us: backward_block(): jnp.einsum('ths,sd->thd', pre_grad, key_block, preferred_element_type=jnp...]
    pallas_call x0 -> x5, Pallas kernels: none -> 46.9 us  [the longest x4 32 us: per_device(): pl.pallas_call(functools.partial(backward_kernel, cfg, is_first, is_last)...]
    psum x1 -> x0, blocking collectives: 40.2 us -> none  [global_stats(): lax.psum((exp_total(masked, peak, allowed), exp_total(tmasked, tpeak, all...]
    ppermute x0 -> x20, waiting for transfers between devices: none -> 39.9 us  [swap(): return lax.ppermute(value, axis, [(i, i ^ distance) for i in range(size)])]
    pmax x1 -> x0, blocking collectives: 39.3 us -> none  [global_stats(): peak, tpeak = lax.pmax((peak, tpeak), ('ctx', 'head'))]
    ppermute x0 -> x20, starting transfers between devices: none -> 29.9 us  [swap(): return lax.ppermute(value, axis, [(i, i ^ distance) for i in range(size)])]
  transfers between devices with their start and end apart: 5 -> 21, of which waited for: 5 -> 7; matrix products, arithmetic and copies ran while one was open for 2% -> 4% of each run, Pallas kernels for 0% -> 6%
where the time goes in v1:
time: 137 us; the launch traced here: 136 us
  Pallas kernels  46.9 us (34%)
  waiting for transfers between devices  39.9 us (29%)
  starting transfers between devices  33.4 us (24%)
  local copies, waits for them, and re-layouts  8.55 us (6%)
  other arithmetic  5.92 us (4%)
  between operations  1.43 us (1%)
    ppermute x20, waiting for transfers between devices, swap(): return lax.ppermute(value, axis, [(i, i ^ distance) for i in range(size)])  39.9 us
    pallas_call x4, Pallas kernels, per_device(): pl.pallas_call(functools.partial(backward_kernel, cfg, is_first, is_last)...  32 us
    ppermute x20, starting transfers between devices, swap(): return lax.ppermute(value, axis, [(i, i ^ distance) for i in range(size)])  29.9 us
    pallas_call x1, Pallas kernels, per_device(): pl.pallas_call(functools.partial(forward_kernel, cfg), out_shape=[jax.Sha...  14.9 us
    unnamed x26, local copies, waits for them, and re-layouts  6.4 us
    all_to_all x1, starting transfers between devices, per_device(): lax.all_to_all(logits.reshape(n, rows_here, chunk), 'ctx', 0, 0, tiled=True)  3.49 us
  transfers between devices with their start and end apart: 21, of which 7 were waited for; matrix products, arithmetic and copies ran while one was open for 4% of the time, Pallas kernels for 6%

profile of v1, /device:TPU:0, one launch (start us, length us, event | category | flops | bytes accessed | tf_op | source)
XLA Modules:
  0.0 136.1 jit_solution(7531616995679111098)
XLA Ops:
  1.7 3.0 %collective-permute-start.4 = (bf16[512,128]{1,0:T(8,128)(2,1)S(1)}, bf16[512,128]{1,0:T(8,128)(2,1)S(1)}, u32[]{:S(2)}, u32[]{:S(2)}) collective-permute-start(bf16[512,128]{1,0:T(8,128)(2,1)S(1)} %constant_dynamic-slice_fusion.1.refs_4_), channel_id=1, source_target_pairs={{0,8},{4,12},{8,0},{12,4},{16,24},{20,28},{24,16},{28,20},{1,9},{5... | collective-permute-start | bytes 393224 | tf_op jit(solution)/shard_map/ppermute | solution.py:19
  5.6 3.5 %all-to-all-start = ((bf16[8,64,512]{2,1,0:T(8,128)(2,1)}), bf16[8,64,512]{2,1,0:T(8,128)(2,1)S(1)}, u32[]{:S(2)}, u32[]{:S(2)}) async-start(bf16[8,64,512]{2,1,0:T(8,128)(2,1)} %bitcast.28), calls=%async_computation | async-start | bytes 1048576 | tf_op jit(solution)/shard_map/all_to_all | solution.py:245
  9.1 1.9 %collective-permute-start.6 = (bf16[512,128]{1,0:T(8,128)(2,1)S(1)}, bf16[512,128]{1,0:T(8,128)(2,1)}, u32[]{:S(2)}, u32[]{:S(2)}) collective-permute-start(bf16[512,128]{1,0:T(8,128)(2,1)S(1)} %constant_dynamic-slice_fusion.1.refs_4_), channel_id=1, source_target_pairs={{0,16},{4,20},{8,24},{12,28},{16,0},{20,4},{24,8},{28,12},{1,17},{... | collective-permute-start | bytes 393224 | tf_op jit(solution)/shard_map/ppermute | solution.py:19
  11.0 1.4 %collective-permute-start.8 = (bf16[512,128]{1,0:T(8,128)(2,1)S(1)}, bf16[512,128]{1,0:T(8,128)(2,1)}, u32[]{:S(2)}, u32[]{:S(2)}) collective-permute-start(bf16[512,128]{1,0:T(8,128)(2,1)S(1)} %constant_dynamic-slice_fusion.1.refs_4_), channel_id=1, source_target_pairs={{0,24},{4,28},{8,16},{12,20},{16,8},{20,12},{24,0},{28,4},{1,25},{... | collective-permute-start | bytes 393224 | tf_op jit(solution)/shard_map/ppermute | solution.py:19
  13.2 1.6 %collective-permute-start = (bf16[68,16,128]{2,1,0:T(8,128)(2,1)S(1)}, bf16[68,16,128]{2,1,0:T(8,128)(2,1)S(1)}, u32[]{:S(2)}, u32[]{:S(2)}) collective-permute-start(bf16[68,16,128]{2,1,0:T(8,128)(2,1)S(1)} %pad_maximum_fusion.refs_0_), channel_id=1, source_target_pairs={{0,1},{1,0},{2,3},{3,2},{4,5},{5,4},{6,7},{7,6},{8,9},{9,8},{10,11... | collective-permute-start | bytes 835592 | tf_op jit(solution)/shard_map/ppermute | solution.py:19
  14.9 8.7 %collective-permute-done.6.refs_8_ = bf16[512,128]{1,0:T(8,128)(2,1)} collective-permute-done((bf16[512,128]{1,0:T(8,128)(2,1)S(1)}, bf16[512,128]{1,0:T(8,128)(2,1)}, u32[]{:S(2)}, u32[]{:S(2)}) %collective-permute-start.6) | collective-permute-done | bytes 131104 | tf_op jit(solution)/shard_map/ppermute | solution.py:19
  23.6 2.6 %collective-permute-start.1 = (bf16[68,16,128]{2,1,0:T(8,128)(2,1)S(1)}, bf16[68,16,128]{2,1,0:T(8,128)(2,1)}, u32[]{:S(2)}, u32[]{:S(2)}) collective-permute-start(bf16[68,16,128]{2,1,0:T(8,128)(2,1)S(1)} %pad_maximum_fusion.refs_0_), channel_id=1, source_target_pairs={{0,2},{1,3},{2,0},{3,1},{4,6},{5,7},{6,4},{7,5},{8,10},{9,11},{10,... | collective-permute-start | bytes 835592 | tf_op jit(solution)/shard_map/ppermute | solution.py:19
  26.2 1.3 collective-permute-start.2
  30.9 15.0 %collective-permute-done.1.refs_2_.refs_0_ = bf16[68,16,128]{2,1,0:T(8,128)(2,1)} collective-permute-done((bf16[68,16,128]{2,1,0:T(8,128)(2,1)S(1)}, bf16[68,16,128]{2,1,0:T(8,128)(2,1)}, u32[]{:S(2)}, u32[]{:S(2)}) %collective-permute-start.1) | collective-permute-done | bytes 278560 | tf_op jit(solution)/shard_map/ppermute | solution.py:19
  48.6 14.9 %forward.1 = (f32[64,4096]{1,0:T(8,128)S(1)}, bf16[4096,128]{1,0:T(8,128)(2,1)S(1)}, bf16[4,128,1024]{2,1,0:T(8,128)(2,1)S(1)}, f32[1,8,128]{2,1,0:T(8,128)S(1)}) custom-call(s32[3]{0:T(128)S(1)} %pad_add_fusion.meta_ref, bf16[68,16,128]{2,1,0:T(8,128)(2,1)S(1)} %pad_maximum_fusion.refs_0_, bf16[68,16,128]{2,1,0:T(8,128)(2,1)S(1)} %collective-permute-done.refs_1_.refs_0_, ...), custom_call_target="tpu_custom_call" | custom-call | flops 8589934592 | bytes 6291456 | tf_op jit(solution)/shard_map/forward/pallas_call | solution.py:260
  63.5 5.4 %collective-permute-start.10 = (f32[1,8,128]{2,1,0:T(8,128)S(1)}, f32[1,8,128]{2,1,0:T(8,128)S(1)}, u32[]{:S(2)}, u32[]{:S(2)}) collective-permute-start(f32[1,8,128]{2,1,0:T(8,128)S(1)} %get-tuple-element.22.refs_3_), channel_id=1, source_target_pairs={{0,1},{1,0},{2,3},{3,2},{4,5},{5,4},{6,7},{7,6},{8,9},{9,8},{10,11... | collective-permute-start | bytes 12296 | tf_op jit(solution)/shard_map/ppermute | solution.py:19
  68.9 2.1 %collective-permute-start.11 = (f32[1,8,128]{2,1,0:T(8,128)S(1)}, f32[1,8,128]{2,1,0:T(8,128)S(1)}, u32[]{:S(2)}, u32[]{:S(2)}) collective-permute-start(f32[1,8,128]{2,1,0:T(8,128)S(1)} %get-tuple-element.22.refs_3_), channel_id=1, source_target_pairs={{0,2},{1,3},{2,0},{3,1},{4,6},{5,7},{6,4},{7,5},{8,10},{9,11},{10,... | collective-permute-start | bytes 12296 | tf_op jit(solution)/shard_map/ppermute | solution.py:19
  71.0 1.4 %collective-permute-start.12 = (f32[1,8,128]{2,1,0:T(8,128)S(1)}, f32[1,8,128]{2,1,0:T(8,128)S(1)}, u32[]{:S(2)}, u32[]{:S(2)}) collective-permute-start(f32[1,8,128]{2,1,0:T(8,128)S(1)} %get-tuple-element.22.refs_3_), channel_id=1, source_target_pairs={{0,3},{1,2},{2,1},{3,0},{4,7},{5,6},{6,5},{7,4},{8,11},{9,10},{10,... | collective-permute-start | bytes 12296 | tf_op jit(solution)/shard_map/ppermute | solution.py:19
  73.4 3.0 %collective-permute-done.12.refs_6_ = f32[1,8,128]{2,1,0:T(8,128)S(1)} collective-permute-done((f32[1,8,128]{2,1,0:T(8,128)S(1)}, f32[1,8,128]{2,1,0:T(8,128)S(1)}, u32[]{:S(2)}, u32[]{:S(2)}) %collective-permute-start.12) | collective-permute-done | bytes 4128 | tf_op jit(solution)/shard_map/ppermute | solution.py:19
  76.4 8.5 %backward3.1 = (bf16[64,16,128]{2,1,0:T(8,128)(2,1)}, f32[128,4096]{1,0:T(8,128)S(1)}, bf16[64,4096]{1,0:T(8,128)(2,1)S(1)}) custom-call(s32[3]{0:T(128)S(1)} %pad_add_fusion.meta_ref, bf16[68,16,128]{2,1,0:T(8,128)(2,1)} %collective-permute-done.2.refs_3_.refs_0_, bf16[1,128,1024]{2,1,0:T(8,128)(2,1)S(1)} %get-tuple-element.51.refs_1_, ...), custom_call_target="tpu_custom_call" | custom-call | flops 6442450944 | bytes 4194304 | tf_op jit(solution)/shard_map/backward3/pallas_call | solution.py:307
  85.0 8.1 %backward2.1 = (bf16[64,16,128]{2,1,0:T(8,128)(2,1)}, f32[128,4096]{1,0:T(8,128)S(1)}) custom-call(s32[3]{0:T(128)S(1)} %pad_add_fusion.meta_ref, bf16[68,16,128]{2,1,0:T(8,128)(2,1)} %collective-permute-done.1.refs_2_.refs_0_, bf16[1,128,1024]{2,1,0:T(8,128)(2,1)S(1)} %get-tuple-element.49.refs_1_, bf16[4096,128]{1,0:T(8,128)(2,1)S(1)} %get-tuple-element.21.refs_2_, ...), custom_call_target="tpu_custom_call" | custom-call | flops 6442450944 | bytes 4194304 | tf_op jit(solution)/shard_map/backward2/pallas_call | solution.py:307
  93.1 7.6 %backward1.1 = (bf16[64,16,128]{2,1,0:T(8,128)(2,1)}, f32[128,4096]{1,0:T(8,128)S(1)}) custom-call(s32[3]{0:T(128)S(1)} %pad_add_fusion.meta_ref, bf16[68,16,128]{2,1,0:T(8,128)(2,1)S(1)} %collective-permute-done.refs_1_.refs_0_, bf16[1,128,1024]{2,1,0:T(8,128)(2,1)S(1)} %get-tuple-element.50.refs_1_, bf16[4096,128]{1,0:T(8,128)(2,1)S(1)} %get-tuple-element.21.refs_2_, ...), custom_call_target="tpu_custom_call" | custom-call | flops 6442450944 | bytes 4194304 | tf_op jit(solution)/shard_map/backward1/pallas_call | solution.py:307
  100.8 1.8 %collective-permute-start.14 = (bf16[64,16,128]{2,1,0:T(8,128)(2,1)}, bf16[64,16,128]{2,1,0:T(8,128)(2,1)}, u32[]{:S(2)}, u32[]{:S(2)}) collective-permute-start(bf16[64,16,128]{2,1,0:T(8,128)(2,1)} %get-tuple-element.30), channel_id=1, source_target_pairs={{0,2},{1,3},{2,0},{3,1},{4,6},{5,7},{6,4},{7,5},{8,10},{9,11},{10,... | collective-permute-start | bytes 786440 | tf_op jit(solution)/shard_map/ppermute | solution.py:19
  102.7 2.4 %collective-permute-start.13 = (bf16[64,16,128]{2,1,0:T(8,128)(2,1)}, bf16[64,16,128]{2,1,0:T(8,128)(2,1)}, u32[]{:S(2)}, u32[]{:S(2)}) collective-permute-start(bf16[64,16,128]{2,1,0:T(8,128)(2,1)} %get-tuple-element.29), channel_id=1, source_target_pairs={{0,3},{1,2},{2,1},{3,0},{4,7},{5,6},{6,5},{7,4},{8,11},{9,10},{10,... | collective-permute-start | bytes 786440 | tf_op jit(solution)/shard_map/ppermute | solution.py:19
  105.1 7.7 %backward0.1 = (f32[64,16,128]{2,1,0:T(8,128)S(1)}, f32[128,512]{1,0:T(8,128)S(1)}, f32[128,512]{1,0:T(8,128)S(1)}, f32[128,512]{1,0:T(8,128)S(1)}, f32[128,512]...) custom-call(s32[3]{0:T(128)S(1)} %pad_add_fusion.meta_ref, bf16[68,16,128]{2,1,0:T(8,128)(2,1)S(1)} %pad_maximum_fusion.refs_0_, ...), custom_call_target="tpu_custom_call" | custom-call | flops 6442450944 | bytes 4194304 | tf_op jit(solution)/shard_map/backward0/pallas_call | solution.py:307
  114.3 8.0 %collective-permute-done.14 = bf16[64,16,128]{2,1,0:T(8,128)(2,1)} collective-permute-done((bf16[64,16,128]{2,1,0:T(8,128)(2,1)}, bf16[64,16,128]{2,1,0:T(8,128)(2,1)}, u32[]{:S(2)}, u32[]{:S(2)}) %collective-permute-start.14) | collective-permute-done | bytes 262176 | tf_op jit(solution)/shard_map/ppermute | solution.py:19
  122.4 2.2 %multiply_reduce_fusion = (f32[64,16]{1,0:T(8,128)S(1)}, f32[64,16,128]{2,1,0:T(8,128)}) fusion(bf16[64,16,128]{2,1,0:T(8,128)(2,1)} %param.6, bf16[64,16,128]{2,1,0:T(8,128)(2,1)} %collective-permute-done.15, bf16[64,16,128]{2,1,0:T(8,128)(2,1)} %collective-permute-done.14, f32[64,16,128]{2,1,0:T(8,128)S(1)} %get-tuple-element.28, ...), kind=kLoop, calls=%fused_computation | loop fusion | flops 1309696 | bytes 2105344 | tf_op jit(solution)/shard_map/reduce_sum | solution.py:339
  125.9 2.0 %collective-permute-start.17 = (bf16[128,512]{1,0:T(8,128)(2,1)S(1)}, bf16[128,512]{1,0:T(8,128)(2,1)S(1)}, u32[]{:S(2)}, u32[]{:S(2)}) collective-permute-start(bf16[128,512]{1,0:T(8,128)(2,1)S(1)} %get-tuple-element.52), channel_id=1, source_target_pairs={{0,8},{4,12},{8,0},{12,4},{16,24},{20,28},{24,16},{28,20},{1,9},{5... | collective-permute-start | bytes 393224 | tf_op jit(solution)/shard_map/ppermute | solution.py:19
  130.9 3.3 %collective-permute-done.18 = bf16[128,512]{1,0:T(8,128)(2,1)S(1)} collective-permute-done((bf16[128,512]{1,0:T(8,128)(2,1)S(1)}, bf16[128,512]{1,0:T(8,128)(2,1)S(1)}, u32[]{:S(2)}, u32[]{:S(2)}) %collective-permute-start.18) | collective-permute-done | bytes 131104 | tf_op jit(solution)/shard_map/ppermute | solution.py:19
  (64 shorter events, 16.9 us)
Async XLA Ops:
  0.6 11.8 %copy-start.11 = (bf16[64,16]{0,1:T(8,128)(2,1)S(1)}, bf16[64,16]{0,1:T(8,128)(2,1)}, u32[]{:S(2)}) copy-start(bf16[64,16]{0,1:T(8,128)(2,1)} %param.7) | copy-start | bytes 6148
  0.7 12.5 %copy-start.10 = (bf16[64,16,128]{2,1,0:T(8,128)(2,1)S(1)}, bf16[64,16,128]{2,1,0:T(8,128)(2,1)}, u32[]{:S(2)}) copy-start(bf16[64,16,128]{2,1,0:T(8,128)(2,1)} %param.6) | copy-start | bytes 786436
  1.7 10.9 %collective-permute-start.4 = (bf16[512,128]{1,0:T(8,128)(2,1)S(1)}, bf16[512,128]{1,0:T(8,128)(2,1)S(1)}, u32[]{:S(2)}, u32[]{:S(2)}) collective-permute-start(bf16[512,128]{1,0:T(8,128)(2,1)S(1)} %constant_dynamic-slice_fusion.1.refs_4_), channel_id=1, source_target_pairs={{0,8},{4,12},{8,0},{12,4},{16,24},{20,28},{24,16},{28,20},{1,9},{5... | collective-permute-start | bytes 393224 | tf_op jit(solution)/shard_map/ppermute | solution.py:19
  5.6 40.3 %all-to-all-start = ((bf16[8,64,512]{2,1,0:T(8,128)(2,1)}), bf16[8,64,512]{2,1,0:T(8,128)(2,1)S(1)}, u32[]{:S(2)}, u32[]{:S(2)}) async-start(bf16[8,64,512]{2,1,0:T(8,128)(2,1)} %bitcast.28), calls=%async_computation | async-start | bytes 1048576 | tf_op jit(solution)/shard_map/all_to_all | solution.py:245
  9.1 14.5 %collective-permute-start.6 = (bf16[512,128]{1,0:T(8,128)(2,1)S(1)}, bf16[512,128]{1,0:T(8,128)(2,1)}, u32[]{:S(2)}, u32[]{:S(2)}) collective-permute-start(bf16[512,128]{1,0:T(8,128)(2,1)S(1)} %constant_dynamic-slice_fusion.1.refs_4_), channel_id=1, source_target_pairs={{0,16},{4,20},{8,24},{12,28},{16,0},{20,4},{24,8},{28,12},{1,17},{... | collective-permute-start | bytes 393224 | tf_op jit(solution)/shard_map/ppermute | solution.py:19
  11.0 15.1 %collective-permute-start.8 = (bf16[512,128]{1,0:T(8,128)(2,1)S(1)}, bf16[512,128]{1,0:T(8,128)(2,1)}, u32[]{:S(2)}, u32[]{:S(2)}) collective-permute-start(bf16[512,128]{1,0:T(8,128)(2,1)S(1)} %constant_dynamic-slice_fusion.1.refs_4_), channel_id=1, source_target_pairs={{0,24},{4,28},{8,16},{12,20},{16,8},{20,12},{24,0},{28,4},{1,25},{... | collective-permute-start | bytes 393224 | tf_op jit(solution)/shard_map/ppermute | solution.py:19
  12.5 15.0 %collective-permute-start.3 = (bf16[512,128]{1,0:T(8,128)(2,1)S(1)}, bf16[512,128]{1,0:T(8,128)(2,1)}, u32[]{:S(2)}, u32[]{:S(2)}) collective-permute-start(bf16[512,128]{1,0:T(8,128)(2,1)S(1)} %constant_dynamic-slice_fusion.1.refs_4_), channel_id=1, source_target_pairs={{0,4},{4,0},{8,12},{12,8},{16,20},{20,16},{24,28},{28,24},{1,5},{5... | collective-permute-start | bytes 393224 | tf_op jit(solution)/shard_map/ppermute | solution.py:19
  12.6 16.9 %copy-start.4 = (bf16[512,128]{1,0:T(8,128)(2,1)}, bf16[512,128]{1,0:T(8,128)(2,1)S(1)}, u32[]{:S(2)}) copy-start(bf16[512,128]{1,0:T(8,128)(2,1)S(1)} %collective-permute-done.4.refs_6_) | copy-start | bytes 393220
  12.6 14.9 %collective-permute-start.5 = (bf16[512,128]{1,0:T(8,128)(2,1)S(1)}, bf16[512,128]{1,0:T(8,128)(2,1)}, u32[]{:S(2)}, u32[]{:S(2)}) collective-permute-start(bf16[512,128]{1,0:T(8,128)(2,1)S(1)} %collective-permute-done.4.refs_6_), channel_id=1, source_target_pairs={{0,4},{4,0},{8,12},{12,8},{16,20},{20,16},{24,28},{28,24},{1,5},{5... | collective-permute-start | bytes 393224 | tf_op jit(solution)/shard_map/ppermute | solution.py:19
  13.2 17.6 %collective-permute-start = (bf16[68,16,128]{2,1,0:T(8,128)(2,1)S(1)}, bf16[68,16,128]{2,1,0:T(8,128)(2,1)S(1)}, u32[]{:S(2)}, u32[]{:S(2)}) collective-permute-start(bf16[68,16,128]{2,1,0:T(8,128)(2,1)S(1)} %pad_maximum_fusion.refs_0_), channel_id=1, source_target_pairs={{0,1},{1,0},{2,3},{3,2},{4,5},{5,4},{6,7},{7,6},{8,9},{9,8},{10,11... | collective-permute-start | bytes 835592 | tf_op jit(solution)/shard_map/ppermute | solution.py:19
  23.6 22.3 %collective-permute-start.1 = (bf16[68,16,128]{2,1,0:T(8,128)(2,1)S(1)}, bf16[68,16,128]{2,1,0:T(8,128)(2,1)}, u32[]{:S(2)}, u32[]{:S(2)}) collective-permute-start(bf16[68,16,128]{2,1,0:T(8,128)(2,1)S(1)} %pad_maximum_fusion.refs_0_), channel_id=1, source_target_pairs={{0,2},{1,3},{2,0},{3,1},{4,6},{5,7},{6,4},{7,5},{8,10},{9,11},{10,... | collective-permute-start | bytes 835592 | tf_op jit(solution)/shard_map/ppermute | solution.py:19
  26.2 19.7 %collective-permute-start.2 = (bf16[68,16,128]{2,1,0:T(8,128)(2,1)S(1)}, bf16[68,16,128]{2,1,0:T(8,128)(2,1)}, u32[]{:S(2)}, u32[]{:S(2)}) collective-permute-start(bf16[68,16,128]{2,1,0:T(8,128)(2,1)S(1)} %pad_maximum_fusion.refs_0_), channel_id=1, source_target_pairs={{0,3},{1,2},{2,1},{3,0},{4,7},{5,6},{6,5},{7,4},{8,11},{9,10},{10,... | collective-permute-start | bytes 835592 | tf_op jit(solution)/shard_map/ppermute | solution.py:19
  27.5 2.0 %collective-permute-start.7 = (bf16[512,128]{1,0:T(8,128)(2,1)}, bf16[512,128]{1,0:T(8,128)(2,1)S(1)}, u32[]{:S(2)}, u32[]{:S(2)}) collective-permute-start(bf16[512,128]{1,0:T(8,128)(2,1)} %collective-permute-done.6.refs_8_), channel_id=1, source_target_pairs={{0,4},{4,0},{8,12},{12,8},{16,20},{20,16},{24,28},{28,24},{1,5},{5... | collective-permute-start | bytes 393224 | tf_op jit(solution)/shard_map/ppermute | solution.py:19
  27.5 2.7 %collective-permute-start.9 = (bf16[512,128]{1,0:T(8,128)(2,1)}, bf16[512,128]{1,0:T(8,128)(2,1)S(1)}, u32[]{:S(2)}, u32[]{:S(2)}) collective-permute-start(bf16[512,128]{1,0:T(8,128)(2,1)} %collective-permute-done.8.refs_10_), channel_id=1, source_target_pairs={{0,4},{4,0},{8,12},{12,8},{16,20},{20,16},{24,28},{28,24},{1,5},{5... | collective-permute-start | bytes 393224 | tf_op jit(solution)/shard_map/ppermute | solution.py:19
  63.5 9.0 %collective-permute-start.10 = (f32[1,8,128]{2,1,0:T(8,128)S(1)}, f32[1,8,128]{2,1,0:T(8,128)S(1)}, u32[]{:S(2)}, u32[]{:S(2)}) collective-permute-start(f32[1,8,128]{2,1,0:T(8,128)S(1)} %get-tuple-element.22.refs_3_), channel_id=1, source_target_pairs={{0,1},{1,0},{2,3},{3,2},{4,5},{5,4},{6,7},{7,6},{8,9},{9,8},{10,11... | collective-permute-start | bytes 12296 | tf_op jit(solution)/shard_map/ppermute | solution.py:19
  68.9 4.5 %collective-permute-start.11 = (f32[1,8,128]{2,1,0:T(8,128)S(1)}, f32[1,8,128]{2,1,0:T(8,128)S(1)}, u32[]{:S(2)}, u32[]{:S(2)}) collective-permute-start(f32[1,8,128]{2,1,0:T(8,128)S(1)} %get-tuple-element.22.refs_3_), channel_id=1, source_target_pairs={{0,2},{1,3},{2,0},{3,1},{4,6},{5,7},{6,4},{7,5},{8,10},{9,11},{10,... | collective-permute-start | bytes 12296 | tf_op jit(solution)/shard_map/ppermute | solution.py:19
  71.0 5.4 %collective-permute-start.12 = (f32[1,8,128]{2,1,0:T(8,128)S(1)}, f32[1,8,128]{2,1,0:T(8,128)S(1)}, u32[]{:S(2)}, u32[]{:S(2)}) collective-permute-start(f32[1,8,128]{2,1,0:T(8,128)S(1)} %get-tuple-element.22.refs_3_), channel_id=1, source_target_pairs={{0,3},{1,2},{2,1},{3,0},{4,7},{5,6},{6,5},{7,4},{8,11},{9,10},{10,... | collective-permute-start | bytes 12296 | tf_op jit(solution)/shard_map/ppermute | solution.py:19
  100.7 13.6 %collective-permute-start.15 = (bf16[64,16,128]{2,1,0:T(8,128)(2,1)}, bf16[64,16,128]{2,1,0:T(8,128)(2,1)}, u32[]{:S(2)}, u32[]{:S(2)}) collective-permute-start(bf16[64,16,128]{2,1,0:T(8,128)(2,1)} %get-tuple-element.31), channel_id=1, source_target_pairs={{0,1},{1,0},{2,3},{3,2},{4,5},{5,4},{6,7},{7,6},{8,9},{9,8},{10,11... | collective-permute-start | bytes 786440 | tf_op jit(solution)/shard_map/ppermute | solution.py:19
  100.8 21.5 %collective-permute-start.14 = (bf16[64,16,128]{2,1,0:T(8,128)(2,1)}, bf16[64,16,128]{2,1,0:T(8,128)(2,1)}, u32[]{:S(2)}, u32[]{:S(2)}) collective-permute-start(bf16[64,16,128]{2,1,0:T(8,128)(2,1)} %get-tuple-element.30), channel_id=1, source_target_pairs={{0,2},{1,3},{2,0},{3,1},{4,6},{5,7},{6,4},{7,5},{8,10},{9,11},{10,... | collective-permute-start | bytes 786440 | tf_op jit(solution)/shard_map/ppermute | solution.py:19
  102.7 19.7 %collective-permute-start.13 = (bf16[64,16,128]{2,1,0:T(8,128)(2,1)}, bf16[64,16,128]{2,1,0:T(8,128)(2,1)}, u32[]{:S(2)}, u32[]{:S(2)}) collective-permute-start(bf16[64,16,128]{2,1,0:T(8,128)(2,1)} %get-tuple-element.29), channel_id=1, source_target_pairs={{0,3},{1,2},{2,1},{3,0},{4,7},{5,6},{6,5},{7,4},{8,11},{9,10},{10,... | collective-permute-start | bytes 786440 | tf_op jit(solution)/shard_map/ppermute | solution.py:19
  114.3 10.4 %collective-permute-start.16 = (bf16[4,128,512]{2,1,0:T(8,128)(2,1)}, bf16[4,128,512]{2,1,0:T(8,128)(2,1)}, u32[]{:S(2)}, u32[]{:S(2)}) collective-permute-start(bf16[4,128,512]{2,1,0:T(8,128)(2,1)} %get-tuple-element.33), channel_id=1, source_target_pairs={{0,4},{4,0},{8,12},{12,8},{16,20},{20,16},{24,28},{28,24},{1,5},{5... | collective-permute-start | bytes 1572872 | tf_op jit(solution)/shard_map/ppermute | solution.py:19
  125.9 5.0 %collective-permute-start.17 = (bf16[128,512]{1,0:T(8,128)(2,1)S(1)}, bf16[128,512]{1,0:T(8,128)(2,1)S(1)}, u32[]{:S(2)}, u32[]{:S(2)}) collective-permute-start(bf16[128,512]{1,0:T(8,128)(2,1)S(1)} %get-tuple-element.52), channel_id=1, source_target_pairs={{0,8},{4,12},{8,0},{12,4},{16,24},{20,28},{24,16},{28,20},{1,9},{5... | collective-permute-start | bytes 393224 | tf_op jit(solution)/shard_map/ppermute | solution.py:19
  127.9 6.4 %collective-permute-start.18 = (bf16[128,512]{1,0:T(8,128)(2,1)S(1)}, bf16[128,512]{1,0:T(8,128)(2,1)S(1)}, u32[]{:S(2)}, u32[]{:S(2)}) collective-permute-start(bf16[128,512]{1,0:T(8,128)(2,1)S(1)} %get-tuple-element.54), channel_id=1, source_target_pairs={{0,16},{4,20},{8,24},{12,28},{16,0},{20,4},{24,8},{28,12},{1,17},{... | collective-permute-start | bytes 393224 | tf_op jit(solution)/shard_map/ppermute | solution.py:19
  128.2 6.0 %collective-permute-start.19 = (bf16[128,512]{1,0:T(8,128)(2,1)S(1)}, bf16[128,512]{1,0:T(8,128)(2,1)S(1)}, u32[]{:S(2)}, u32[]{:S(2)}) collective-permute-start(bf16[128,512]{1,0:T(8,128)(2,1)S(1)} %get-tuple-element.53), channel_id=1, source_target_pairs={{0,24},{4,28},{8,16},{12,20},{16,8},{20,12},{24,0},{28,4},{1,25},{... | collective-permute-start | bytes 393224 | tf_op jit(solution)/shard_map/ppermute | solution.py:19
  (9 other events, 19.9 us)

commit v2 on v1

v2 whole, which is shorter than its diff:
```python
import functools

import jax
import jax.numpy as jnp
from jax import lax
from jax.experimental import pallas as pl
from jax.experimental.pallas import tpu as pltpu
from jax.sharding import PartitionSpec as P

masked_value = -1e30
lanes = 128
stat_rows = 8
vmem_bytes = 14 * 1024 * 1024
contract_last = (((1,), (1,)), ((), ()))


def swap(value, axis, distance):
    size = lax.axis_size(axis)
    return lax.ppermute(value, axis, [(i, i ^ distance) for i in range(size)])


def ring_next(value, axis):
    size = lax.axis_size(axis)
    ring = list(range(0, size, 2)) + list(range(1, size, 2))[::-1]
    return lax.ppermute(value, axis, [(ring[i], ring[(i + 1) % size]) for i in range(size)])


def in_pairs(count, first, step):
    first(0, 0)

    def body(i, _):
        step(0, 2 * i, 2 * i + 1)
        step(1, 2 * i + 1, 2 * i + 2)
        return 0

    lax.fori_loop(0, count // 2 - 1, body, 0)
    step(0, count - 2, count - 1)
    step(1, count - 1, None)


def row_limits(meta_ref, rows_here):
    row = lax.broadcasted_iota(jnp.int32, (rows_here, 1), 0)
    return meta_ref[0] + meta_ref[1] * rows_here + row


def piece_allowed(meta_ref, limit, k, kc, chunk):
    first = (meta_ref[1] ^ k) * kc + meta_ref[2] * chunk
    position = first + lax.broadcasted_iota(jnp.int32, (limit.shape[0], chunk), 1)
    return position <= limit


def forward_kernel(cfg, count, is_first, is_last, meta_ref, *refs):
    order, nh, rows_here, hh, depth, kc, chunk, scale = cfg
    n = len(order)
    rows = rows_here * hh
    refs = list(refs)
    take = lambda count: [refs.pop(0) for _ in range(count)]
    q_refs = take(count)
    if is_first:
        k_refs = take(n)
    else:
        keys_ref, before_ref = take(2)
    if is_last:
        (logits_ref,) = take(1)
    (score_ref,) = take(1)
    qw_refs = take(count)
    if is_first:
        (keys_ref,) = take(1)
    if is_last:
        (stats_ref,) = take(1)
    q_all, wb, dots = take(3)
    tile = dots.shape[3]
    tiles = n * chunk // tile
    wide_by = tile // lanes
    if is_first:
        for i in range(n):
            keys_ref[i * chunk : (i + 1) * chunk, :] = k_refs[i][...]

    eye = (
        lax.broadcasted_iota(jnp.int32, (rows_here, lanes), 0)
        == lax.broadcasted_iota(jnp.int32, (rows_here, lanes), 1)
    ).astype(jnp.float32)
    for j, q_ref in enumerate(q_refs):
        q_all[j] = q_ref[:rows, :]
        slab = q_ref[rows:, :].astype(jnp.float32)
        for head in range(hh):
            picked = jnp.sum(slab[head : head + 1] * eye, axis=1, keepdims=True)
            wb[j, head] = jnp.broadcast_to(picked, (rows_here, lanes))
        for head in range(0, hh, 2):
            at = slice(head * rows_here, (head + 2) * rows_here)
            q = q_ref[at, :].astype(jnp.float32)
            w = wb[j, head : head + 2].reshape(2 * rows_here, lanes) * scale
            qw_refs[j][:, at] = (q * w).T.astype(jnp.bfloat16)

    def dot_tile(buffer, s):
        j, s = s // tiles, s % tiles
        keys = keys_ref[pl.ds(pl.multiple_of(s * tile, tile), tile), :]
        dots[buffer] = lax.dot_general(
            q_all[j], keys, contract_last, preferred_element_type=jnp.float32
        ).reshape(hh, rows_here, tile)

    def step(buffer, s, following):
        if following is not None:
            dot_tile(1 - buffer, following)
        j, s = s // tiles, s % tiles
        columns = pl.ds(pl.multiple_of(s * tile, tile), tile)
        for t in range(0, rows_here, 8):
            total = None
            for head in range(hh):
                value = jnp.maximum(dots[buffer, head, t : t + 8, :], 0.0)
                w = wb[j, head, t : t + 8, :]
                value = value * jnp.concatenate([w] * wide_by, axis=1)
                total = value if total is None else total + value
            total = total * scale
            if is_first:
                score_ref[t : t + 8, columns] += total
            else:
                score_ref[t : t + 8, columns] = before_ref[t : t + 8, columns] + total

    if is_first:
        score_ref[...] = jnp.zeros_like(score_ref)
    in_pairs(count * tiles, dot_tile, step)
    if not is_last:
        return

    limit = row_limits(meta_ref, rows_here)
    lane = lax.broadcasted_iota(jnp.int32, (rows_here, lanes), 1)
    out = jnp.zeros((rows_here, lanes), jnp.float32)

    def piece(i, at):
        if i == 0:
            return score_ref[:, at * chunk : (at + 1) * chunk]
        return logits_ref[meta_ref[1] ^ order[at]].astype(jnp.float32)

    for i in range(2):
        peak = None
        for at, k in enumerate(order):
            allowed = piece_allowed(meta_ref, limit, k, kc, chunk)
            here = jnp.max(jnp.where(allowed, piece(i, at), masked_value), axis=1, keepdims=True)
            peak = here if peak is None else jnp.maximum(peak, here)
        total = None
        for at, k in enumerate(order):
            allowed = piece_allowed(meta_ref, limit, k, kc, chunk)
            here = jnp.where(allowed, jnp.exp(piece(i, at) - peak), 0.0)
            here = jnp.sum(here, axis=1, keepdims=True)
            total = here if total is None else total + here
        out = jnp.where(lane == 2 * i, peak, out)
        out = jnp.where(lane == 2 * i + 1, total, out)
    padded = stats_ref.shape[2]
    if padded > rows_here:
        out = jnp.concatenate([out, jnp.zeros((padded - rows_here, lanes), jnp.float32)], axis=0)
    stats_ref[0] = out.T[:stat_rows]


def score_gradient(cfg, meta_ref, stats, rw_ref, logits_ref, score_ref, cols, grad_ref):
    order, nh, rows_here, hh, depth, kc, chunk, scale = cfg
    for i in range(2):
        peak = functools.reduce(jnp.maximum, [st[2 * i : 2 * i + 1] for st in stats])
        total = functools.reduce(
            jnp.add,
            [st[2 * i + 1 : 2 * i + 2] * jnp.exp(st[2 * i : 2 * i + 1] - peak) for st in stats],
        )
        cols[2 * i : 2 * i + 1, :] = peak
        cols[2 * i + 1 : 2 * i + 2, :] = rw_ref[...] / total
    cols[4:, :] = jnp.zeros((cols.shape[0] - 4, cols.shape[1]), jnp.float32)
    st = cols[...].T[:rows_here]
    limit = row_limits(meta_ref, rows_here)
    for at, k in enumerate(order):
        logits = logits_ref[meta_ref[1] ^ k].astype(jnp.float32)
        score = score_ref[:, at * chunk : (at + 1) * chunk]
        g = jnp.exp(score - st[:, 0:1]) * st[:, 1:2] - jnp.exp(logits - st[:, 2:3]) * st[:, 3:4]
        g = jnp.where(piece_allowed(meta_ref, limit, k, kc, chunk), g, 0.0)
        grad_ref[:, at * chunk : (at + 1) * chunk] = g.astype(jnp.bfloat16)


def backward_kernel(cfg, is_first, half, meta_ref, *refs):
    order, nh, rows_here, hh, depth, kc, chunk, scale = cfg
    n = len(order)
    rows = rows_here * hh
    refs = list(refs)
    take = lambda count: [refs.pop(0) for _ in range(count)]
    q_ref, keys_ref = take(2)
    kg_in_ref = None
    (qw_ref,) = take(1)
    if is_first:
        stat_refs = take(nh)
        rw_ref, logits_ref, score_ref = take(3)
    else:
        (grad_ref,) = take(1)
        (kg_in_ref,) = take(1)
    if half == "second":
        (u_in_ref,) = take(1)
    (u_ref,) = take(1)
    if half in ("first", "second"):
        kg_refs = take(1) if half == "first" else take(n // 2)
    elif half == "all":
        (kg_ref,) = take(1)
    if is_first:
        (grad_ref,) = take(1)
    masks, u_acc = take(2)
    if half == "second":
        u_acc[...] = u_in_ref[...]
    else:
        u_acc[...] = jnp.zeros_like(u_acc)
    if half in ("first", "second"):
        (kg_acc,) = take(1)
    if is_first:
        (cols,) = take(1)
        stats = [ref[0] for ref in stat_refs]
        score_gradient(cfg, meta_ref, stats, rw_ref, logits_ref, score_ref, cols, grad_ref)
    tile = masks.shape[2]
    tiles = n * chunk // tile
    if half in ("first", "second"):
        tiles = tiles // 2
    offset = tiles if half == "second" else 0

    def tile_at(s):
        return pl.ds(pl.multiple_of((s + offset) * tile, tile), tile)

    def mask(buffer, s):
        dotted = lax.dot_general(
            q_ref[:rows, :],
            keys_ref[tile_at(s), :],
            contract_last,
            preferred_element_type=jnp.float32,
        )
        g = grad_ref[:, tile_at(s)].astype(jnp.float32)
        wide = jnp.broadcast_to(g[None], (hh, rows_here, tile)).reshape(rows, tile)
        masks[buffer] = jnp.where(dotted > 0, wide, 0.0).astype(jnp.bfloat16)

    def step(buffer, s, following):
        if following is not None:
            mask(1 - buffer, following)
        masked = masks[buffer]
        u_acc[...] += jnp.dot(
            masked, keys_ref[tile_at(s), :], preferred_element_type=jnp.float32
        )
        more = jnp.dot(qw_ref[...], masked, preferred_element_type=jnp.float32)
        if kg_in_ref is not None:
            more = kg_in_ref[:, tile_at(s)] + more
        if half == "all":
            kg_ref[:, tile_at(s)] = more
        else:
            kg_acc[:, pl.ds(pl.multiple_of(s * tile, tile), tile)] = more

    in_pairs(tiles, mask, step)
    u_ref[...] = u_acc[...].astype(u_ref.dtype)
    if half in ("first", "second"):
        for i in range(n // 2):
            value = kg_acc[:, i * chunk : (i + 1) * chunk].T
            if half == "first":
                kg_refs[0][i] = value.astype(kg_refs[0].dtype)
            else:
                kg_refs[i][...] = value


def finish_kernel(cfg, u_ref, moving_ref, q_ref, query_grad_ref, weight_grad_ref):
    order, nh, rows_here, hh, depth, kc, chunk, scale = cfg
    rows = rows_here * hh
    eye = (
        lax.broadcasted_iota(jnp.int32, (rows_here, lanes), 0)
        == lax.broadcasted_iota(jnp.int32, (rows_here, lanes), 1)
    ).astype(jnp.float32)
    lane = lax.broadcasted_iota(jnp.int32, (lanes, lanes), 1)[:rows_here]
    slab = q_ref[rows:, :].astype(jnp.float32)
    out = jnp.zeros((rows_here, lanes), jnp.float32)
    for head in range(hh):
        at = slice(head * rows_here, (head + 1) * rows_here)
        total = u_ref[at, :] + moving_ref[at, :].astype(jnp.float32)
        w = jnp.sum(slab[head : head + 1] * eye, axis=1, keepdims=True) * scale
        query_grad_ref[:, head, :] = total * w
        along = jnp.sum(total * q_ref[at, :].astype(jnp.float32), axis=1, keepdims=True)
        out = jnp.where(lane == head, along * scale, out)
    if rows_here < lanes:
        out = jnp.concatenate([out, jnp.zeros((lanes - rows_here, lanes), jnp.float32)], axis=0)
    weight_grad_ref[...] = out.T[:hh, :rows_here]


def per_device(query, weights, keys, main_logits, row_weight, offset):
    n = lax.axis_size("ctx")
    nh = lax.axis_size("head")
    c = lax.axis_index("ctx")
    h = lax.axis_index("head")
    rows_here, hh, depth = query.shape
    kc = keys.shape[0]
    chunk = kc // nh
    rows = rows_here * hh
    scale = depth ** (-0.5)
    loss_scale = float(kc * n) ** 0.5
    bf16, f32 = jnp.bfloat16, jnp.float32

    q_mine = jnp.swapaxes(query, 0, 1).reshape(rows, depth)
    slab_rows = -(-hh // 16) * 16
    w_slab = jnp.pad(weights.T, ((0, slab_rows - hh), (0, lanes - rows_here)))
    q_blocks = [jnp.concatenate([q_mine, w_slab], axis=0)]
    q_blocks.append(ring_next(q_blocks[0], "head"))

    k_mine = lax.dynamic_slice_in_dim(keys, h * chunk, chunk, 0)
    k_pieces = [None] * n
    k_pieces[0::2] = [k_mine] + [swap(k_mine, "ctx", k) for k in range(2, n, 2)]
    k_pieces[4], q_blocks[1] = lax.optimization_barrier((k_pieces[4], q_blocks[1]))
    k_pieces[1::2] = [swap(piece, "ctx", 1) for piece in k_pieces[0::2]]
    order = list(range(1, n, 2)) + list(range(0, n, 2))
    for j in range(2, nh):
        q_blocks.append(ring_next(q_blocks[-1], "head"))

    logits = lax.dynamic_slice_in_dim(main_logits, h * chunk, chunk, 1)
    logits = lax.optimization_barrier((logits, k_pieces[6]))[0]
    logits = lax.all_to_all(logits.reshape(n, rows_here, chunk), "ctx", 0, 0, tiled=True)
    logits, k_pieces[1] = lax.optimization_barrier((logits, k_pieces[1]))

    meta = jnp.concatenate([offset, jnp.stack([c, h]).astype(jnp.int32)])
    rw = lax.dynamic_slice_in_dim(row_weight, c * rows_here, rows_here, 0)[None, :]
    padded = -(-rows_here // lanes) * lanes
    rw = jnp.pad(rw * loss_scale, ((0, 0), (0, padded - rows_here)))

    cfg = (order, nh, rows_here, hh, depth, kc, chunk, scale)
    total_keys = n * chunk
    smem = pl.BlockSpec(memory_space=pltpu.SMEM)
    vmem = pl.BlockSpec(memory_space=pltpu.VMEM)
    macs = rows * total_keys * depth
    tile = 512

    def call(kernel, operands, out_shape, scratch, products, name, aliases={}):
        return pl.pallas_call(
            kernel,
            out_shape=out_shape,
            input_output_aliases=aliases,
            in_specs=[smem] + [vmem] * len(operands),
            out_specs=[vmem] * len(out_shape),
            scratch_shapes=scratch,
            compiler_params=pltpu.CompilerParams(vmem_limit_bytes=vmem_bytes),
            cost_estimate=pl.CostEstimate(
                flops=int(4 * products * macs), bytes_accessed=4 * 1024 * 1024, transcendentals=0
            ),
            name=name,
        )(meta, *operands)

    near = lambda x: pltpu.with_memory_space_constraint(x, pltpu.VMEM)

    score = keys_all = stats = None
    qw = []
    for js in (range(nh - 1), range(nh - 1, nh)):
        is_first, is_last = js[0] == 0, js[-1] == nh - 1
        operands = [q_blocks[j] for j in js]
        operands += [k_pieces[k] for k in order] if is_first else [near(keys_all), near(score)]
        operands += [logits] if is_last else []
        out_shape = [pltpu.VMEM((rows_here, total_keys), f32)]
        out_shape += [pltpu.VMEM((depth, rows), bf16)] * len(js)
        if is_first:
            out_shape += [pltpu.VMEM((total_keys, depth), bf16)]
        if is_last:
            out_shape += [jax.ShapeDtypeStruct((1, stat_rows, padded), f32)]
        scratch = [
            pltpu.VMEM((len(js), rows, depth), bf16),
            pltpu.VMEM((len(js), hh, rows_here, lanes), f32),
            pltpu.VMEM((2, hh, rows_here, tile), f32),
        ]
        kernel = functools.partial(forward_kernel, cfg, len(js), is_first, is_last)
        aliases = {} if is_first else {len(js) + 2: 0}
        outs = call(kernel, operands, out_shape, scratch, len(js), f"forward{js[0]}", aliases)
        score = outs[0]
        qw += outs[1 : 1 + len(js)]
        keys_all = outs[-1] if is_first else keys_all
        stats = outs[-1] if is_last else stats

    all_stats = [stats] + [swap(stats, "head", j) for j in range(1, nh)]

    grad = kg = moving = None
    mask_scratch = pltpu.VMEM((2, rows, tile), bf16)
    u_scratch = pltpu.VMEM((rows, depth), f32)
    u_shape = jax.ShapeDtypeStruct((rows, depth), f32)
    for j in range(1, nh):
        is_first = j == 1
        operands = [q_blocks[j], near(keys_all), near(qw[j])]
        if is_first:
            operands += all_stats + [rw, logits, near(score)]
        else:
            operands += [near(grad), near(kg)]
        out_shape = [
            jax.ShapeDtypeStruct((rows, depth), bf16) if is_first else u_shape,
            pltpu.VMEM((depth, total_keys), f32),
        ]
        scratch = [mask_scratch, u_scratch]
        if is_first:
            out_shape += [pltpu.VMEM((rows_here, total_keys), bf16)]
            scratch += [pltpu.VMEM((padded, lanes), f32)]
        kernel = functools.partial(backward_kernel, cfg, is_first, "all")
        aliases = {} if is_first else {5: 1}
        outs = call(kernel, operands, out_shape, scratch, 3, f"backward{j}", aliases)
        kg = outs[1]
        if is_first:
            grad = outs[2]
            part = outs[0]
        else:
            part = (outs[0] + moving.astype(f32)).astype(bf16)
            kg, part = lax.optimization_barrier((kg, part))
        moving = ring_next(part, "head")

    half_scratch = [mask_scratch, u_scratch, pltpu.VMEM((depth, total_keys // 2), f32)]
    operands = [q_blocks[0], near(keys_all), near(qw[0]), near(grad), near(kg)]
    u_mine, odd = call(
        functools.partial(backward_kernel, cfg, False, "first"),
        operands,
        [pltpu.VMEM((rows, depth), f32), jax.ShapeDtypeStruct((n // 2, chunk, depth), bf16)],
        half_scratch,
        1.5,
        "backward0_first",
    )
    other = swap(odd, "ctx", 1)
    u_mine, *even = call(
        functools.partial(backward_kernel, cfg, False, "second"),
        operands + [near(u_mine)],
        [u_shape] + [jax.ShapeDtypeStruct((chunk, depth), f32)] * (n // 2),
        half_scratch,
        1.5,
        "backward0_second",
    )

    even = [even[i] + other[i].astype(f32) for i in range(n // 2)]
    key_grad = even[0]
    sends = [even[i].astype(bf16) for i in range(1, n // 2)]
    u_mine, *sends = lax.optimization_barrier((u_mine, *sends))
    for i in range(1, n // 2):
        key_grad = key_grad + swap(sends[i - 1], "ctx", 2 * i).astype(f32)

    query_grad, weight_grad = pl.pallas_call(
        functools.partial(finish_kernel, cfg),
        out_shape=[
            jax.ShapeDtypeStruct((rows_here, hh, depth), f32),
            jax.ShapeDtypeStruct((hh, rows_here), f32),
        ],
        in_specs=[vmem] * 3,
        out_specs=[vmem] * 2,
        compiler_params=pltpu.CompilerParams(vmem_limit_bytes=vmem_bytes),
        cost_estimate=pl.CostEstimate(
            flops=8 * rows * depth, bytes_accessed=14 * rows * depth, transcendentals=0
        ),
        name="finish",
    )(u_mine, moving, q_blocks[0])
    return query_grad, key_grad, weight_grad.T


def solution(mesh):
    in_specs = (P("ctx", "head", None), P("ctx", "head"), P("ctx", None), P(None, "ctx"), P(), P())
    out_specs = (P("ctx", "head", None), P(("ctx", "head"), None), P("ctx", "head"))
    return jax.shard_map(
        per_device, mesh=mesh, in_specs=in_specs, out_specs=out_specs, check_vma=False
    )
```

time: 137 us -> 105 us (0.77)
  waiting for transfers between devices: 39.9 us -> 18.7 us
  local copies, waits for them, and re-layouts: 8.55 us -> 3.84 us
  other arithmetic: 5.92 us -> 2.53 us
    ppermute x20 -> x14, waiting for transfers between devices: 39.9 us -> 18.6 us  [swap(): return lax.ppermute(value, axis, [(i, i ^ distance) for i in range(size)])]
    ppermute x20 -> x14, starting transfers between devices: 29.9 us -> 16.4 us  [swap(): return lax.ppermute(value, axis, [(i, i ^ distance) for i in range(size)])]
    ppermute x0 -> x6, starting transfers between devices: none -> 12.2 us  [ring_next(): lax.ppermute(value, axis, [(ring[i], ring[(i + 1) % size]) for i in range...]
    unnamed x26 -> x6, local copies, waits for them, and re-layouts: 6.4 us -> 0.91 us
    reduce_sum x1 -> x0, other arithmetic: 2.19 us -> none  [per_device(): weight_grad = jnp.sum(total * query.astype(f32), axis=-1) * scale]
    pallas_call x5 -> x8, Pallas kernels: 46.9 us -> 45.9 us  [the longest x7 44.6 us: call(): pl.pallas_call(kernel, out_shape=out_shape, input_output_aliases=aliases,...]
  transfers between devices with their start and end apart: 21 -> 21, of which waited for: 7 -> 7; matrix products, arithmetic and copies ran while one was open for 4% -> 3% of each run, Pallas kernels for 6% -> 29%
where the time goes in v2:
time: 105 us
  Pallas kernels  45.9 us (44%)
  starting transfers between devices  32.1 us (31%)
  waiting for transfers between devices  18.7 us (18%)
  local copies, waits for them, and re-layouts  3.84 us (4%)
  other arithmetic  2.53 us (2%)
  between operations  1.45 us (1%)
    pallas_call x7, Pallas kernels, call(): pl.pallas_call(kernel, out_shape=out_shape, input_output_aliases=aliases,...  44.6 us
    ppermute x14, waiting for transfers between devices, swap(): return lax.ppermute(value, axis, [(i, i ^ distance) for i in range(size)])  18.6 us
    ppermute x14, starting transfers between devices, swap(): return lax.ppermute(value, axis, [(i, i ^ distance) for i in range(size)])  16.4 us
    ppermute x6, starting transfers between devices, ring_next(): lax.ppermute(value, axis, [(ring[i], ring[(i + 1) % size]) for i in range...  12.2 us
    all_to_all x1, starting transfers between devices, per_device(): lax.all_to_all(logits.reshape(n, rows_here, chunk), 'ctx', 0, 0, tiled=True)  3.5 us
  transfers between devices with their start and end apart: 21, of which 7 were waited for; matrix products, arithmetic and copies ran while one was open for 3% of the time, Pallas kernels for 29%

profile of v2, /device:TPU:0, one launch (start us, length us, event | category | flops | bytes accessed | tf_op | source)
XLA Modules:
  0.0 104.6 jit_solution(13436706204903089346)
XLA Ops:
  1.7 4.0 %collective-permute-start.3 = (bf16[512,128]{1,0:T(8,128)(2,1)S(1)}, bf16[512,128]{1,0:T(8,128)(2,1)S(1)}, u32[]{:S(2)}, u32[]{:S(2)}) collective-permute-start(bf16[512,128]{1,0:T(8,128)(2,1)S(1)} %constant_dynamic-slice_fusion.1.refs_7_), channel_id=1, source_target_pairs={{0,24},{4,28},{8,16},{12,20},{16,8},{20,12},{24,0},{28,4},{1,25},{... | collective-permute-start | bytes 393224 | tf_op jit(solution)/shard_map/ppermute | solution.py:19
  7.4 2.6 %collective-permute-start.1 = (bf16[1040,128]{1,0:T(8,128)(2,1)S(1)}, bf16[1040,128]{1,0:T(8,128)(2,1)S(1)}, u32[]{:S(2)}, u32[]{:S(2)}) collective-permute-start(bf16[1040,128]{1,0:T(8,128)(2,1)S(1)} %fusion.1.refs_0_.q_ref), channel_id=1, source_target_pairs={{0,2},{2,3},{3,1},{1,0},{4,6},{6,7},{7,5},{5,4},{8,10},{10,11},{11... | collective-permute-start | bytes 798728 | tf_op jit(solution)/shard_map/ppermute | solution.py:25
  10.9 3.5 %all-to-all-start = ((bf16[8,64,512]{2,1,0:T(8,128)(2,1)}), bf16[8,64,512]{2,1,0:T(8,128)(2,1)S(1)}, u32[]{:S(2)}, u32[]{:S(2)}) async-start(bf16[8,64,512]{2,1,0:T(8,128)(2,1)} %bitcast.29), calls=%async_computation | async-start | bytes 1048576 | tf_op jit(solution)/shard_map/all_to_all | solution.py:309
  14.4 1.9 %collective-permute-start = (bf16[512,128]{1,0:T(8,128)(2,1)S(1)}, bf16[512,128]{1,0:T(8,128)(2,1)}, u32[]{:S(2)}, u32[]{:S(2)}) collective-permute-start(bf16[512,128]{1,0:T(8,128)(2,1)S(1)} %constant_dynamic-slice_fusion.1.refs_7_), channel_id=1, source_target_pairs={{0,16},{4,20},{8,24},{12,28},{16,0},{20,4},{24,8},{28,12},{1,17},{... | collective-permute-start | bytes 393224 | tf_op jit(solution)/shard_map/ppermute | solution.py:19
  16.3 9.7 %collective-permute-done.refs_9_ = bf16[512,128]{1,0:T(8,128)(2,1)} collective-permute-done((bf16[512,128]{1,0:T(8,128)(2,1)S(1)}, bf16[512,128]{1,0:T(8,128)(2,1)}, u32[]{:S(2)}, u32[]{:S(2)}) %collective-permute-start) | collective-permute-done | bytes 131104 | tf_op jit(solution)/shard_map/ppermute | solution.py:19
  26.1 1.6 %collective-permute-start.2 = (bf16[1040,128]{1,0:T(8,128)(2,1)S(1)}, bf16[1040,128]{1,0:T(8,128)(2,1)S(1)}, u32[]{:S(2)}, u32[]{:S(2)}) collective-permute-start(bf16[1040,128]{1,0:T(8,128)(2,1)S(1)} %collective-permute-done.1.refs_1_.refs_0_), channel_id=1, source_target_pairs={{0,2},{2,3},{3,1},{1,0},{4,6},{6,7},{7,5},{5,4},{8,10},{10,11},{11... | collective-permute-start | bytes 798728 | tf_op jit(solution)/shard_map/ppermute | solution.py:25
  27.7 1.5 %collective-permute-start.5 = (bf16[512,128]{1,0:T(8,128)(2,1)S(1)}, bf16[512,128]{1,0:T(8,128)(2,1)}, u32[]{:S(2)}, u32[]{:S(2)}) collective-permute-start(bf16[512,128]{1,0:T(8,128)(2,1)S(1)} %constant_dynamic-slice_fusion.1.refs_7_), channel_id=1, source_target_pairs={{0,8},{4,12},{8,0},{12,4},{16,24},{20,28},{24,16},{28,20},{1,9},{5... | collective-permute-start | bytes 393224 | tf_op jit(solution)/shard_map/ppermute | solution.py:19
  29.6 3.1 %collective-permute-done.5.refs_8_ = bf16[512,128]{1,0:T(8,128)(2,1)} collective-permute-done((bf16[512,128]{1,0:T(8,128)(2,1)S(1)}, bf16[512,128]{1,0:T(8,128)(2,1)}, u32[]{:S(2)}, u32[]{:S(2)}) %collective-permute-start.5) | collective-permute-done | bytes 131104 | tf_op jit(solution)/shard_map/ppermute | solution.py:19
  34.0 2.5 %collective-permute-start.9 = (bf16[1040,128]{1,0:T(8,128)(2,1)S(1)}, bf16[1040,128]{1,0:T(8,128)(2,1)}, u32[]{:S(2)}, u32[]{:S(2)}) collective-permute-start(bf16[1040,128]{1,0:T(8,128)(2,1)S(1)} %collective-permute-done.2.refs_2_.refs_0_), channel_id=1, source_target_pairs={{0,2},{2,3},{3,1},{1,0},{4,6},{6,7},{7,5},{5,4},{8,10},{10,11},{11... | collective-permute-start | bytes 798728 | tf_op jit(solution)/shard_map/ppermute | solution.py:25
  37.4 10.7 %forward0.1 = (f32[64,4096]{1,0:T(8,128)S(1)}, bf16[128,1024]{1,0:T(8,128)(2,1)S(1)}, bf16[128,1024]{1,0:T(8,128)(2,1)S(1)}, bf16[128,1024]{1,0:T(8,128)(2,1)S(1)}, bf16[4096,128]{1,0:T(8,128)(2,1)S(1)}) custom-call(s32[3]{0:T(128)S(1)} %pad_add_fusion.meta_ref, bf16[1040,128]{1,0:T(8,128)(2,1)S(1)} %fusion.1.refs_0_.q_ref, ...), custom_call_target="tpu_custom_call" | custom-call | flops 6442450944 | bytes 4194304 | tf_op jit(solution)/shard_map/forward0/pallas_call | solution.py:325
  48.2 5.0 %forward3.1 = (f32[64,4096]{1,0:T(8,128)S(1)}, bf16[128,1024]{1,0:T(8,128)(2,1)S(1)}, f32[1,8,128]{2,1,0:T(8,128)S(1)}) custom-call(s32[3]{0:T(128)S(1)} %pad_add_fusion.meta_ref, bf16[1040,128]{1,0:T(8,128)(2,1)} %collective-permute-done.9.refs_0_, bf16[4096,128]{1,0:T(8,128)(2,1)S(1)} %get-tuple-element.44.refs_1_, ...), custom_call_target="tpu_custom_call", output_to_operand_aliasing={{0}: (3, {})} | custom-call | flops 2147483648 | bytes 4194304 | tf_op jit(solution)/shard_map/forward3/pallas_call | solution.py:325
  54.4 3.2 %collective-permute-start.10 = (f32[1,8,128]{2,1,0:T(8,128)S(1)}, f32[1,8,128]{2,1,0:T(8,128)S(1)}, u32[]{:S(2)}, u32[]{:S(2)}) collective-permute-start(f32[1,8,128]{2,1,0:T(8,128)S(1)} %get-tuple-element.49.refs_3_), channel_id=1, source_target_pairs={{0,1},{1,0},{2,3},{3,2},{4,5},{5,4},{6,7},{7,6},{8,9},{9,8},{10,11... | collective-permute-start | bytes 12296 | tf_op jit(solution)/shard_map/ppermute | solution.py:19
  59.2 7.4 %backward1.1 = (bf16[1024,128]{1,0:T(8,128)(2,1)S(1)}, f32[128,4096]{1,0:T(8,128)S(1)}, bf16[64,4096]{1,0:T(8,128)(2,1)S(1)}) custom-call(s32[3]{0:T(128)S(1)} %pad_add_fusion.meta_ref, bf16[1040,128]{1,0:T(8,128)(2,1)S(1)} %collective-permute-done.1.refs_1_.refs_0_, bf16[4096,128]{1,0:T(8,128)(2,1)S(1)} %get-tuple-element.44.refs_1_, ...), custom_call_target="tpu_custom_call" | custom-call | flops 6442450944 | bytes 4194304 | tf_op jit(solution)/shard_map/backward1/pallas_call | solution.py:325
  66.6 1.9 %collective-permute-start.13 = (bf16[1024,128]{1,0:T(8,128)(2,1)S(1)}, bf16[1024,128]{1,0:T(8,128)(2,1)S(1)}, u32[]{:S(2)}, u32[]{:S(2)}) collective-permute-start(bf16[1024,128]{1,0:T(8,128)(2,1)S(1)} %get-tuple-element.57), channel_id=1, source_target_pairs={{0,2},{2,3},{3,1},{1,0},{4,6},{6,7},{7,5},{5,4},{8,10},{10,11},{11... | collective-permute-start | bytes 786440 | tf_op jit(solution)/shard_map/ppermute | solution.py:25
  68.5 7.0 %backward2.1 = (f32[1024,128]{1,0:T(8,128)S(1)}, f32[128,4096]{1,0:T(8,128)S(1)}) custom-call(s32[3]{0:T(128)S(1)} %pad_add_fusion.meta_ref, bf16[1040,128]{1,0:T(8,128)(2,1)S(1)} %collective-permute-done.2.refs_2_.refs_0_, bf16[4096,128]{1,0:T(8,128)(2,1)S(1)} %get-tuple-element.44.refs_1_, ...), custom_call_target="tpu_custom_call", output_to_operand_aliasing={{1}: (5, {})} | custom-call | flops 6442450944 | bytes 4194304 | tf_op jit(solution)/shard_map/backward2/pallas_call | solution.py:325
  75.6 1.3 %collective-permute-start.14 = (bf16[1024,128]{1,0:T(8,128)(2,1)S(1)}, bf16[1024,128]{1,0:T(8,128)(2,1)S(1)}, u32[]{:S(2)}, u32[]{:S(2)}) collective-permute-start(bf16[1024,128]{1,0:T(8,128)(2,1)S(1)} %add_convert_fusion.1), channel_id=1, source_target_pairs={{0,2},{2,3},{3,1},{1,0},{4,6},{6,7},{7,5},{5,4},{8,10},{10,11},{11... | collective-permute-start | bytes 786440 | tf_op jit(solution)/shard_map/ppermute | solution.py:25
  76.9 7.4 %backward3.1 = (f32[1024,128]{1,0:T(8,128)S(1)}, f32[128,4096]{1,0:T(8,128)S(1)}) custom-call(s32[3]{0:T(128)S(1)} %pad_add_fusion.meta_ref, bf16[1040,128]{1,0:T(8,128)(2,1)} %collective-permute-done.9.refs_0_, bf16[4096,128]{1,0:T(8,128)(2,1)S(1)} %get-tuple-element.44.refs_1_, ...), custom_call_target="tpu_custom_call", output_to_operand_aliasing={{1}: (5, {})} | custom-call | flops 6442450944 | bytes 4194304 | tf_op jit(solution)/shard_map/backward3/pallas_call | solution.py:325
  84.4 3.5 %backward0_first.1 = (f32[1024,128]{1,0:T(8,128)S(1)}, bf16[4,512,128]{2,1,0:T(8,128)(2,1)S(1)}) custom-call(s32[3]{0:T(128)S(1)} %pad_add_fusion.meta_ref, bf16[1040,128]{1,0:T(8,128)(2,1)S(1)} %fusion.1.refs_0_.q_ref, bf16[4096,128]{1,0:T(8,128)(2,1)S(1)} %get-tuple-element.44.refs_1_, bf16[128,1024]{1,0:T(8,128)(2,1)S(1)} %get-tuple-element.45.refs_2_, ...), custom_call_target="tpu_custom_call" | custom-call | flops 3221225472 | bytes 4194304 | tf_op jit(solution)/shard_map/backward0_first/pallas_call | solution.py:325
  88.0 2.3 %collective-permute-start.16 = (bf16[1024,128]{1,0:T(8,128)(2,1)S(1)}, bf16[1024,128]{1,0:T(8,128)(2,1)S(1)}, u32[]{:S(2)}, u32[]{:S(2)}) collective-permute-start(bf16[1024,128]{1,0:T(8,128)(2,1)S(1)} %add_convert_fusion), channel_id=1, source_target_pairs={{0,2},{2,3},{3,1},{1,0},{4,6},{6,7},{7,5},{5,4},{8,10},{10,11},{11... | collective-permute-start | bytes 786440 | tf_op jit(solution)/shard_map/ppermute | solution.py:25
  90.3 3.5 %backward0_second.1 = (f32[1024,128]{1,0:T(8,128)S(1)}, f32[512,128]{1,0:T(8,128)S(1)}, f32[512,128]{1,0:T(8,128)S(1)}, f32[512,128]{1,0:T(8,128)S(1)}, f32[512,128]{1,0:T(8,128)S(1)}) custom-call(s32[3]{0:T(128)S(1)} %pad_add_fusion.meta_ref, bf16[1040,128]{1,0:T(8,128)(2,1)S(1)} %fusion.1.refs_0_.q_ref, bf16[4096,128]{1,0:T(8,128)(2,1)S(1)} %get-tuple-element.44.refs_1_, ...), custom_call_target="tpu_custom_call" | custom-call | flops 3221225472 | bytes 4194304 | tf_op jit(solution)/shard_map/backward0_second/pallas_call | solution.py:325
  93.9 2.0 %collective-permute-start.17 = (bf16[512,128]{1,0:T(8,128)(2,1)S(1)}, bf16[512,128]{1,0:T(8,128)(2,1)S(1)}, u32[]{:S(2)}, u32[]{:S(2)}) collective-permute-start(bf16[512,128]{1,0:T(8,128)(2,1)S(1)} %get-tuple-element.73), channel_id=1, source_target_pairs={{0,8},{4,12},{8,0},{12,4},{16,24},{20,28},{24,16},{28,20},{1,9},{5... | collective-permute-start | bytes 393224 | tf_op jit(solution)/shard_map/ppermute | solution.py:19
  96.2 1.3 %collective-permute-start.19 = (bf16[512,128]{1,0:T(8,128)(2,1)S(1)}, bf16[512,128]{1,0:T(8,128)(2,1)S(1)}, u32[]{:S(2)}, u32[]{:S(2)}) collective-permute-start(bf16[512,128]{1,0:T(8,128)(2,1)S(1)} %get-tuple-element.75), channel_id=1, source_target_pairs={{0,24},{4,28},{8,16},{12,20},{16,8},{20,12},{24,0},{28,4},{1,25},{... | collective-permute-start | bytes 393224 | tf_op jit(solution)/shard_map/ppermute | solution.py:19
  97.5 1.3 %finish.1 = (f32[64,16,128]{2,1,0:T(8,128)}, f32[16,64]{1,0:T(8,128)}) custom-call(f32[1024,128]{1,0:T(8,128)S(1)} %get-tuple-element.69.u_ref, bf16[1024,128]{1,0:T(8,128)(2,1)S(1)} %collective-permute-done.16.moving_ref, bf16[1040,128]{1,0:T(8,128)(2,1)S(1)} %fusion.1.refs_0_.q_ref), custom_call_target="tpu_custom_call" | custom-call | flops 1048576 | bytes 1835008 | tf_op jit(solution)/shard_map/finish/pallas_call | solution.py:427
  99.8 4.0 %collective-permute-done.18 = bf16[512,128]{1,0:T(8,128)(2,1)S(1)} collective-permute-done((bf16[512,128]{1,0:T(8,128)(2,1)S(1)}, bf16[512,128]{1,0:T(8,128)(2,1)S(1)}, u32[]{:S(2)}, u32[]{:S(2)}) %collective-permute-start.18) | collective-permute-done | bytes 131104 | tf_op jit(solution)/shard_map/ppermute | solution.py:19
  (43 shorter events, 10.8 us)
Async XLA Ops:
  0.6 9.4 %copy-start = (bf16[512,2048]{1,0:T(8,128)(2,1)S(1)}, bf16[512,2048]{1,0:T(8,128)(2,1)}, u32[]{:S(2)}) copy-start(bf16[512,2048]{1,0:T(8,128)(2,1)} %param.9) | copy-start | bytes 6291460
  1.7 9.2 %collective-permute-start.3 = (bf16[512,128]{1,0:T(8,128)(2,1)S(1)}, bf16[512,128]{1,0:T(8,128)(2,1)S(1)}, u32[]{:S(2)}, u32[]{:S(2)}) collective-permute-start(bf16[512,128]{1,0:T(8,128)(2,1)S(1)} %constant_dynamic-slice_fusion.1.refs_7_), channel_id=1, source_target_pairs={{0,24},{4,28},{8,16},{12,20},{16,8},{20,12},{24,0},{28,4},{1,25},{... | collective-permute-start | bytes 393224 | tf_op jit(solution)/shard_map/ppermute | solution.py:19
  7.4 18.7 %collective-permute-start.1 = (bf16[1040,128]{1,0:T(8,128)(2,1)S(1)}, bf16[1040,128]{1,0:T(8,128)(2,1)S(1)}, u32[]{:S(2)}, u32[]{:S(2)}) collective-permute-start(bf16[1040,128]{1,0:T(8,128)(2,1)S(1)} %fusion.1.refs_0_.q_ref), channel_id=1, source_target_pairs={{0,2},{2,3},{3,1},{1,0},{4,6},{6,7},{7,5},{5,4},{8,10},{10,11},{11... | collective-permute-start | bytes 798728 | tf_op jit(solution)/shard_map/ppermute | solution.py:25
  10.9 15.2 %copy-start.1 = (bf16[512,128]{1,0:T(8,128)(2,1)}, bf16[512,128]{1,0:T(8,128)(2,1)S(1)}, u32[]{:S(2)}) copy-start(bf16[512,128]{1,0:T(8,128)(2,1)S(1)} %collective-permute-done.3.refs_10_) | copy-start | bytes 393220
  10.9 25.6 %all-to-all-start = ((bf16[8,64,512]{2,1,0:T(8,128)(2,1)}), bf16[8,64,512]{2,1,0:T(8,128)(2,1)S(1)}, u32[]{:S(2)}, u32[]{:S(2)}) async-start(bf16[8,64,512]{2,1,0:T(8,128)(2,1)} %bitcast.29), calls=%async_computation | async-start | bytes 1048576 | tf_op jit(solution)/shard_map/all_to_all | solution.py:309
  14.4 11.7 %collective-permute-start = (bf16[512,128]{1,0:T(8,128)(2,1)S(1)}, bf16[512,128]{1,0:T(8,128)(2,1)}, u32[]{:S(2)}, u32[]{:S(2)}) collective-permute-start(bf16[512,128]{1,0:T(8,128)(2,1)S(1)} %constant_dynamic-slice_fusion.1.refs_7_), channel_id=1, source_target_pairs={{0,16},{4,20},{8,24},{12,28},{16,0},{20,4},{24,8},{28,12},{1,17},{... | collective-permute-start | bytes 393224 | tf_op jit(solution)/shard_map/ppermute | solution.py:19
  26.1 7.9 %collective-permute-start.2 = (bf16[1040,128]{1,0:T(8,128)(2,1)S(1)}, bf16[1040,128]{1,0:T(8,128)(2,1)S(1)}, u32[]{:S(2)}, u32[]{:S(2)}) collective-permute-start(bf16[1040,128]{1,0:T(8,128)(2,1)S(1)} %collective-permute-done.1.refs_1_.refs_0_), channel_id=1, source_target_pairs={{0,2},{2,3},{3,1},{1,0},{4,6},{6,7},{7,5},{5,4},{8,10},{10,11},{11... | collective-permute-start | bytes 798728 | tf_op jit(solution)/shard_map/ppermute | solution.py:25
  27.7 5.1 %collective-permute-start.5 = (bf16[512,128]{1,0:T(8,128)(2,1)S(1)}, bf16[512,128]{1,0:T(8,128)(2,1)}, u32[]{:S(2)}, u32[]{:S(2)}) collective-permute-start(bf16[512,128]{1,0:T(8,128)(2,1)S(1)} %constant_dynamic-slice_fusion.1.refs_7_), channel_id=1, source_target_pairs={{0,8},{4,12},{8,0},{12,4},{16,24},{20,28},{24,16},{28,20},{1,9},{5... | collective-permute-start | bytes 393224 | tf_op jit(solution)/shard_map/ppermute | solution.py:19
  29.1 7.4 %collective-permute-start.4 = (bf16[512,128]{1,0:T(8,128)(2,1)S(1)}, bf16[512,128]{1,0:T(8,128)(2,1)}, u32[]{:S(2)}, u32[]{:S(2)}) collective-permute-start(bf16[512,128]{1,0:T(8,128)(2,1)S(1)} %constant_dynamic-slice_fusion.1.refs_7_), channel_id=1, source_target_pairs={{0,4},{4,0},{8,12},{12,8},{16,20},{20,16},{24,28},{28,24},{1,5},{5... | collective-permute-start | bytes 393224 | tf_op jit(solution)/shard_map/ppermute | solution.py:19
  29.1 7.4 %collective-permute-start.8 = (bf16[512,128]{1,0:T(8,128)(2,1)}, bf16[512,128]{1,0:T(8,128)(2,1)}, u32[]{:S(2)}, u32[]{:S(2)}) collective-permute-start(bf16[512,128]{1,0:T(8,128)(2,1)} %copy-done.1), channel_id=1, source_target_pairs={{0,4},{4,0},{8,12},{12,8},{16,20},{20,16},{24,28},{28,24},{1,5},{5... | collective-permute-start | bytes 393224 | tf_op jit(solution)/shard_map/ppermute | solution.py:19
  32.7 3.8 %collective-permute-start.6 = (bf16[512,128]{1,0:T(8,128)(2,1)}, bf16[512,128]{1,0:T(8,128)(2,1)}, u32[]{:S(2)}, u32[]{:S(2)}) collective-permute-start(bf16[512,128]{1,0:T(8,128)(2,1)} %collective-permute-done.5.refs_8_), channel_id=1, source_target_pairs={{0,4},{4,0},{8,12},{12,8},{16,20},{20,16},{24,28},{28,24},{1,5},{5... | collective-permute-start | bytes 393224 | tf_op jit(solution)/shard_map/ppermute | solution.py:19
  32.7 3.8 %collective-permute-start.7 = (bf16[512,128]{1,0:T(8,128)(2,1)}, bf16[512,128]{1,0:T(8,128)(2,1)}, u32[]{:S(2)}, u32[]{:S(2)}) collective-permute-start(bf16[512,128]{1,0:T(8,128)(2,1)} %collective-permute-done.refs_9_), channel_id=1, source_target_pairs={{0,4},{4,0},{8,12},{12,8},{16,20},{20,16},{24,28},{28,24},{1,5},{5... | collective-permute-start | bytes 393224 | tf_op jit(solution)/shard_map/ppermute | solution.py:19
  34.0 14.1 %collective-permute-start.9 = (bf16[1040,128]{1,0:T(8,128)(2,1)S(1)}, bf16[1040,128]{1,0:T(8,128)(2,1)}, u32[]{:S(2)}, u32[]{:S(2)}) collective-permute-start(bf16[1040,128]{1,0:T(8,128)(2,1)S(1)} %collective-permute-done.2.refs_2_.refs_0_), channel_id=1, source_target_pairs={{0,2},{2,3},{3,1},{1,0},{4,6},{6,7},{7,5},{5,4},{8,10},{10,11},{11... | collective-permute-start | bytes 798728 | tf_op jit(solution)/shard_map/ppermute | solution.py:25
  36.5 0.9 copy-start.2
  53.2 5.4 %collective-permute-start.12 = (f32[1,8,128]{2,1,0:T(8,128)S(1)}, f32[1,8,128]{2,1,0:T(8,128)S(1)}, u32[]{:S(2)}, u32[]{:S(2)}) collective-permute-start(f32[1,8,128]{2,1,0:T(8,128)S(1)} %get-tuple-element.49.refs_3_), channel_id=1, source_target_pairs={{0,3},{1,2},{2,1},{3,0},{4,7},{5,6},{6,5},{7,4},{8,11},{9,10},{10,... | collective-permute-start | bytes 12296 | tf_op jit(solution)/shard_map/ppermute | solution.py:19
  54.4 4.5 %collective-permute-start.11 = (f32[1,8,128]{2,1,0:T(8,128)S(1)}, f32[1,8,128]{2,1,0:T(8,128)S(1)}, u32[]{:S(2)}, u32[]{:S(2)}) collective-permute-start(f32[1,8,128]{2,1,0:T(8,128)S(1)} %get-tuple-element.49.refs_3_), channel_id=1, source_target_pairs={{0,2},{1,3},{2,0},{3,1},{4,6},{5,7},{6,4},{7,5},{8,10},{9,11},{10,... | collective-permute-start | bytes 12296 | tf_op jit(solution)/shard_map/ppermute | solution.py:19
  54.4 4.8 %collective-permute-start.10 = (f32[1,8,128]{2,1,0:T(8,128)S(1)}, f32[1,8,128]{2,1,0:T(8,128)S(1)}, u32[]{:S(2)}, u32[]{:S(2)}) collective-permute-start(f32[1,8,128]{2,1,0:T(8,128)S(1)} %get-tuple-element.49.refs_3_), channel_id=1, source_target_pairs={{0,1},{1,0},{2,3},{3,2},{4,5},{5,4},{6,7},{7,6},{8,9},{9,8},{10,11... | collective-permute-start | bytes 12296 | tf_op jit(solution)/shard_map/ppermute | solution.py:19
  66.6 8.9 %collective-permute-start.13 = (bf16[1024,128]{1,0:T(8,128)(2,1)S(1)}, bf16[1024,128]{1,0:T(8,128)(2,1)S(1)}, u32[]{:S(2)}, u32[]{:S(2)}) collective-permute-start(bf16[1024,128]{1,0:T(8,128)(2,1)S(1)} %get-tuple-element.57), channel_id=1, source_target_pairs={{0,2},{2,3},{3,1},{1,0},{4,6},{6,7},{7,5},{5,4},{8,10},{10,11},{11... | collective-permute-start | bytes 786440 | tf_op jit(solution)/shard_map/ppermute | solution.py:25
  75.6 8.7 %collective-permute-start.14 = (bf16[1024,128]{1,0:T(8,128)(2,1)S(1)}, bf16[1024,128]{1,0:T(8,128)(2,1)S(1)}, u32[]{:S(2)}, u32[]{:S(2)}) collective-permute-start(bf16[1024,128]{1,0:T(8,128)(2,1)S(1)} %add_convert_fusion.1), channel_id=1, source_target_pairs={{0,2},{2,3},{3,1},{1,0},{4,6},{6,7},{7,5},{5,4},{8,10},{10,11},{11... | collective-permute-start | bytes 786440 | tf_op jit(solution)/shard_map/ppermute | solution.py:25
  87.9 5.9 %collective-permute-start.15 = (bf16[4,512,128]{2,1,0:T(8,128)(2,1)S(1)}, bf16[4,512,128]{2,1,0:T(8,128)(2,1)S(1)}, u32[]{:S(2)}, u32[]{:S(2)}) collective-permute-start(bf16[4,512,128]{2,1,0:T(8,128)(2,1)S(1)} %get-tuple-element.66), channel_id=1, source_target_pairs={{0,4},{4,0},{8,12},{12,8},{16,20},{20,16},{24,28},{28,24},{1,5},{5... | collective-permute-start | bytes 1572872 | tf_op jit(solution)/shard_map/ppermute | solution.py:19
  88.0 9.5 %collective-permute-start.16 = (bf16[1024,128]{1,0:T(8,128)(2,1)S(1)}, bf16[1024,128]{1,0:T(8,128)(2,1)S(1)}, u32[]{:S(2)}, u32[]{:S(2)}) collective-permute-start(bf16[1024,128]{1,0:T(8,128)(2,1)S(1)} %add_convert_fusion), channel_id=1, source_target_pairs={{0,2},{2,3},{3,1},{1,0},{4,6},{6,7},{7,5},{5,4},{8,10},{10,11},{11... | collective-permute-start | bytes 786440 | tf_op jit(solution)/shard_map/ppermute | solution.py:25
  93.9 5.8 %collective-permute-start.17 = (bf16[512,128]{1,0:T(8,128)(2,1)S(1)}, bf16[512,128]{1,0:T(8,128)(2,1)S(1)}, u32[]{:S(2)}, u32[]{:S(2)}) collective-permute-start(bf16[512,128]{1,0:T(8,128)(2,1)S(1)} %get-tuple-element.73), channel_id=1, source_target_pairs={{0,8},{4,12},{8,0},{12,4},{16,24},{20,28},{24,16},{28,20},{1,9},{5... | collective-permute-start | bytes 393224 | tf_op jit(solution)/shard_map/ppermute | solution.py:19
  95.9 7.9 %collective-permute-start.18 = (bf16[512,128]{1,0:T(8,128)(2,1)S(1)}, bf16[512,128]{1,0:T(8,128)(2,1)S(1)}, u32[]{:S(2)}, u32[]{:S(2)}) collective-permute-start(bf16[512,128]{1,0:T(8,128)(2,1)S(1)} %get-tuple-element.74), channel_id=1, source_target_pairs={{0,16},{4,20},{8,24},{12,28},{16,0},{20,4},{24,8},{28,12},{1,17},{... | collective-permute-start | bytes 393224 | tf_op jit(solution)/shard_map/ppermute | solution.py:19
  96.2 7.5 %collective-permute-start.19 = (bf16[512,128]{1,0:T(8,128)(2,1)S(1)}, bf16[512,128]{1,0:T(8,128)(2,1)S(1)}, u32[]{:S(2)}, u32[]{:S(2)}) collective-permute-start(bf16[512,128]{1,0:T(8,128)(2,1)S(1)} %get-tuple-element.75), channel_id=1, source_target_pairs={{0,24},{4,28},{8,16},{12,20},{16,8},{20,12},{24,0},{28,4},{1,25},{... | collective-permute-start | bytes 393224 | tf_op jit(solution)/shard_map/ppermute | solution.py:19

commit v3 on v2

v3 whole, which is shorter than its diff:
```python
import functools

import jax
import jax.numpy as jnp
from jax import lax
from jax.experimental import pallas as pl
from jax.experimental.pallas import tpu as pltpu
from jax.sharding import PartitionSpec as P

masked_value = -1e30
lanes = 128
stat_rows = 8
vmem_bytes = 6 * 1024 * 1024
contract_last = (((1,), (1,)), ((), ()))


def swap(value, axis, distance):
    size = lax.axis_size(axis)
    return lax.ppermute(value, axis, [(i, i ^ distance) for i in range(size)])


def ring_next(value, axis):
    size = lax.axis_size(axis)
    ring = list(range(0, size, 2)) + list(range(1, size, 2))[::-1]
    return lax.ppermute(value, axis, [(ring[i], ring[(i + 1) % size]) for i in range(size)])


def in_pairs(count, first, step):
    first(0, 0)

    def body(i, _):
        step(0, 2 * i, 2 * i + 1)
        step(1, 2 * i + 1, 2 * i + 2)
        return 0

    lax.fori_loop(0, count // 2 - 1, body, 0)
    step(0, count - 2, count - 1)
    step(1, count - 1, None)


def row_limits(meta_ref, rows_here):
    row = lax.broadcasted_iota(jnp.int32, (rows_here, 1), 0)
    return meta_ref[0] + meta_ref[1] * rows_here + row


def piece_allowed(meta_ref, limit, k, kc, chunk):
    first = (meta_ref[1] ^ k) * kc + meta_ref[2] * chunk
    position = first + lax.broadcasted_iota(jnp.int32, (limit.shape[0], chunk), 1)
    return position <= limit


def forward_kernel(cfg, count, is_first, is_last, meta_ref, *refs):
    order, nh, rows_here, hh, depth, kc, chunk, scale = cfg
    n = len(order)
    rows = rows_here * hh
    refs = list(refs)
    take = lambda count: [refs.pop(0) for _ in range(count)]
    q_refs = take(count)
    if is_first:
        message_refs = take(n)
    else:
        keys_ref, before_ref, logits_ref = take(3)
    (score_ref,) = take(1)
    qw_refs = take(count)
    active_refs = [None] * is_first + take(count - is_first)
    if is_first:
        keys_ref, logits_ref = take(2)
    if is_last:
        (stats_ref,) = take(1)
    (wb,) = take(1)
    side = min(256, n * chunk)
    tile = min(4 * side, n * chunk)
    tiles = n * chunk // tile
    if is_first:
        for at, k in enumerate(order):
            keys_ref[at * chunk : (at + 1) * chunk, :] = message_refs[at][:chunk, :]
            for i in range(chunk // lanes):
                first = chunk + (chunk // lanes * (k % 2) + i) * rows_here
                column = at * chunk + i * lanes
                logits_ref[:, column : column + lanes] = message_refs[at][
                    first : first + rows_here, :
                ]

    eye = (
        lax.broadcasted_iota(jnp.int32, (rows_here, lanes), 0)
        == lax.broadcasted_iota(jnp.int32, (rows_here, lanes), 1)
    ).astype(jnp.float32)
    for j, q_ref in enumerate(q_refs):
        slab = q_ref[rows:, :].astype(jnp.float32)
        for head in range(hh):
            picked = jnp.sum(slab[head : head + 1] * eye, axis=1, keepdims=True)
            wb[j, head] = jnp.broadcast_to(picked, (rows_here, lanes))
        for head in range(0, hh, 2):
            at = slice(head * rows_here, (head + 2) * rows_here)
            q = q_ref[at, :].astype(jnp.float32)
            w = wb[j, head : head + 2].reshape(2 * rows_here, lanes) * scale
            qw_refs[j][:, at] = (q * w).T.astype(jnp.bfloat16)

    def step(j, s):
        for first in range(0, tile, side):
            columns = pl.ds(pl.multiple_of(s * tile + first, side), side)
            dots = lax.dot_general(
                q_refs[j][:rows, :],
                keys_ref[columns, :],
                contract_last,
                preferred_element_type=jnp.float32,
            )
            total = [None] * (rows_here // 16)
            for head in range(hh):
                for t in range(rows_here // 16):
                    row = head * rows_here + t * 16
                    w = wb[j, head, t * 16 : t * 16 + 16, :]
                    w = jnp.concatenate([w] * (side // lanes), axis=1)
                    active = jnp.maximum(dots[row : row + 16, :], 0.0)
                    if active_refs[j] is not None:
                        active_refs[j][row : row + 16, columns] = active.astype(jnp.bfloat16)
                    value = active * w
                    total[t] = value if head == 0 else total[t] + value
            for t, value in enumerate(total):
                at = slice(t * 16, t * 16 + 16)
                value = value * scale
                if j > 0:
                    value = score_ref[at, columns] + value
                elif not is_first:
                    value = before_ref[at, columns] + value
                score_ref[at, columns] = value
        return 0

    for j in range(count):
        lax.fori_loop(0, tiles, lambda s, _, j=j: step(j, s), 0)
    if not is_last:
        return

    limit = row_limits(meta_ref, rows_here)
    lane = lax.broadcasted_iota(jnp.int32, (rows_here, lanes), 1)
    out = jnp.zeros((rows_here, lanes), jnp.float32)

    def piece(i, at):
        if i == 0:
            return score_ref[:, at * chunk : (at + 1) * chunk]
        return logits_ref[:, at * chunk : (at + 1) * chunk].astype(jnp.float32)

    for i in range(2):
        peak = None
        for at, k in enumerate(order):
            allowed = piece_allowed(meta_ref, limit, k, kc, chunk)
            here = jnp.max(jnp.where(allowed, piece(i, at), masked_value), axis=1, keepdims=True)
            peak = here if peak is None else jnp.maximum(peak, here)
        total = None
        for at, k in enumerate(order):
            allowed = piece_allowed(meta_ref, limit, k, kc, chunk)
            here = jnp.where(allowed, jnp.exp(piece(i, at) - peak), 0.0)
            here = jnp.sum(here, axis=1, keepdims=True)
            total = here if total is None else total + here
        out = jnp.where(lane == 2 * i, peak, out)
        out = jnp.where(lane == 2 * i + 1, total, out)
    padded = stats_ref.shape[2]
    if padded > rows_here:
        out = jnp.concatenate([out, jnp.zeros((padded - rows_here, lanes), jnp.float32)], axis=0)
    stats_ref[0] = out.T[:stat_rows]


def score_gradient(cfg, meta_ref, stats, rw_ref, logits_ref, score_ref, cols, grad_ref):
    order, nh, rows_here, hh, depth, kc, chunk, scale = cfg
    for i in range(2):
        peak = functools.reduce(jnp.maximum, [st[2 * i : 2 * i + 1] for st in stats])
        total = functools.reduce(
            jnp.add,
            [st[2 * i + 1 : 2 * i + 2] * jnp.exp(st[2 * i : 2 * i + 1] - peak) for st in stats],
        )
        cols[2 * i : 2 * i + 1, :] = peak
        cols[2 * i + 1 : 2 * i + 2, :] = rw_ref[...] / total
    cols[4:, :] = jnp.zeros((cols.shape[0] - 4, cols.shape[1]), jnp.float32)
    st = cols[...].T[:rows_here]
    limit = row_limits(meta_ref, rows_here)
    for at, k in enumerate(order):
        logits = logits_ref[:, at * chunk : (at + 1) * chunk].astype(jnp.float32)
        score = score_ref[:, at * chunk : (at + 1) * chunk]
        g = jnp.exp(score - st[:, 0:1]) * st[:, 1:2] - jnp.exp(logits - st[:, 2:3]) * st[:, 3:4]
        g = jnp.where(piece_allowed(meta_ref, limit, k, kc, chunk), g, 0.0)
        grad_ref[:, at * chunk : (at + 1) * chunk] = g.astype(jnp.bfloat16)


def backward_kernel(cfg, items, has_before, meta_ref, *refs):
    order, nh, rows_here, hh, depth, kc, chunk, scale = cfg
    n = len(order)
    rows = rows_here * hh
    refs = list(refs)
    take = lambda count: [refs.pop(0) for _ in range(count)]
    is_first = items[0][0] == 1 and items[0][2] is None
    makes_u = any(item[1] for item in items)
    ranges = [item[2] for item in items if item[2] is not None]
    half = ranges[0] if ranges and ranges[0] != "all" else None
    source_refs = take(len(items))
    qw_refs = [take(1)[0] if item[2] is not None else None for item in items]
    (keys_ref,) = take(1)
    if is_first:
        stat_refs = take(nh)
        rw_ref, logits_ref, score_ref = take(3)
    else:
        (grad_ref,) = take(1)
    before_ref = take(1)[0] if has_before else None
    if makes_u:
        (u_ref,) = take(1)
    if ranges:
        kg_refs = take(n // 2 if half == "second" else 1)
    if is_first:
        (grad_ref,) = take(1)
    if half is not None:
        mask_ref, kg_acc = take(2)
    else:
        masks = take(2)
        (u_acc,) = take(1)
    if is_first:
        (cols,) = take(1)
        stats = [ref[0] for ref in stat_refs]
        score_gradient(cfg, meta_ref, stats, rw_ref, logits_ref, score_ref, cols, grad_ref)
    tile = min(512, n * chunk // 4)
    chunks = max(1, min(4, hh))
    heads = hh // chunks
    part = heads * rows_here
    side = tile // 2

    for index, (_, is_u, keys_range) in enumerate(items):
        tiles = n * chunk // tile
        if half is not None:
            tiles = tiles // 2
        offset = tiles if half == "second" else 0
        source_ref, qw_ref = source_refs[index], qw_refs[index]
        is_start = index == 0 or items[index - 1][2] is None

        def tile_at(s, first=0, size=tile, offset=offset):
            return pl.ds(pl.multiple_of((s + offset) * tile + first, size), size)

        def mask_at(buffer, s, at, first=0, size=tile):
            if half is None:
                return masks[buffer].at[at, first : first + size]
            return mask_ref.at[at, pl.ds(pl.multiple_of(s * tile + first, size), size)]

        def mask_part(buffer, s, i, source_ref=source_ref):
            at = slice(i * part, (i + 1) * part)
            if half is None:
                g = grad_ref[:, tile_at(s)]
                value = source_ref[at, tile_at(s)]
            else:
                g = grad_ref[:, tile_at(s)].astype(jnp.float32)
                value = lax.dot_general(
                    source_ref[at, :],
                    keys_ref[tile_at(s), :],
                    contract_last,
                    preferred_element_type=jnp.float32,
                )
            wide = jnp.broadcast_to(g[None], (heads, rows_here, tile)).reshape(part, tile)
            value = jnp.where(value > 0, wide, jnp.zeros_like(wide))
            mask_at(buffer, s, at)[...] = value.astype(jnp.bfloat16)

        def mask(buffer, s):
            for i in range(chunks):
                mask_part(buffer, s, i)

        def step(buffer, s, following):
            for i in range(chunks):
                if following is not None:
                    mask_part(1 - buffer, following, i)
                if is_u:
                    at = slice(i * part, (i + 1) * part)
                    u_acc[at, :] += jnp.dot(
                        mask_at(buffer, s, at)[...],
                        keys_ref[tile_at(s), :],
                        preferred_element_type=jnp.float32,
                    )
                if keys_range is None or i % (chunks // 2) != chunks // 2 - 1:
                    continue
                first = i // (chunks // 2) * side
                more = jnp.dot(
                    qw_ref[...],
                    mask_at(buffer, s, slice(0, rows), first, side)[...],
                    preferred_element_type=jnp.float32,
                )
                here = tile_at(s, first, side)
                if not is_start:
                    more = kg_refs[0][:, here] + more
                elif before_ref is not None:
                    more = before_ref[:, here] + more
                if half is None:
                    kg_refs[0][:, here] = more
                else:
                    kg_acc[:, pl.ds(pl.multiple_of(s * tile + first, side), side)] = more

        if is_u:
            u_acc[...] = jnp.zeros_like(u_acc)
        in_pairs(tiles, mask, step)
        if is_u:
            u_ref[...] = u_acc[...].astype(u_ref.dtype)

    if half is not None:
        for i in range(n // 2):
            value = kg_acc[:, i * chunk : (i + 1) * chunk].T
            if half == "first":
                kg_refs[0][i] = value.astype(kg_refs[0].dtype)
            else:
                kg_refs[i][...] = value


def query_kernel(cfg, mask_refs, keys_ref, u_ref, u_acc):
    count = mask_refs[0].shape[1]
    tile = min(512, count)
    u_acc[...] = jnp.zeros_like(u_acc)
    for half, mask_ref in enumerate(mask_refs):

        def step(s, _, half=half, mask_ref=mask_ref):
            at = pl.multiple_of(s * tile, tile)
            u_acc[...] += jnp.dot(
                mask_ref[:, pl.ds(at, tile)],
                keys_ref[pl.ds(half * count + at, tile), :],
                preferred_element_type=jnp.float32,
            )
            return 0

        lax.fori_loop(0, count // tile, step, 0)
    u_ref[...] = u_acc[...]


def prepare_kernel(cfg, meta_ref, query_ref, weights_ref, rw_ref, keys_ref, logits_ref, *refs):
    order, nh, rows_here, hh, depth, kc, chunk, scale = cfg
    sends = len(order) // 2
    rows = rows_here * hh
    parts = chunk // lanes
    message_ref, rw_out_ref, key_refs = refs[0], refs[1], refs[2 : 2 + sends]
    wide, sems = refs[-2], refs[-1]
    share = pl.multiple_of(meta_ref[2] * chunk, chunk)
    copies = []

    def copy(source, target):
        copies.append(pltpu.make_async_copy(source, target, sems.at[len(copies)]))
        copies[-1].start()

    for i in reversed(range(sends)):
        copy(keys_ref.at[pl.ds(share, chunk), :], key_refs[i].at[:chunk, :])
        for core in range(2):
            row = pl.multiple_of((meta_ref[1] ^ (2 * i) ^ core) * rows_here, rows_here)
            for part in range(parts):
                first = chunk + (parts * core + part) * rows_here
                copy(
                    logits_ref.at[pl.ds(row, rows_here), pl.ds(share + part * lanes, lanes)],
                    key_refs[i].at[first : first + rows_here, :],
                )
    every = jnp.broadcast_to(rw_ref[...], (8, rw_ref.shape[1]))
    shift = every.shape[1] - meta_ref[1] * rows_here
    here = pltpu.roll(every, shift, 1)[:1, : rw_out_ref.shape[1]]
    rw_out_ref[...] = here * float(kc * len(order)) ** 0.5
    wide[...] = query_ref[...].astype(jnp.float32)
    for head in range(hh):
        at = slice(head * rows_here, (head + 1) * rows_here)
        message_ref[at, :] = wide[:, head, :].astype(jnp.bfloat16)
    message_ref[rows:, :] = jnp.zeros((message_ref.shape[0] - rows, lanes), jnp.bfloat16)
    message_ref[rows : rows + hh, :rows_here] = weights_ref[...]
    for item in copies:
        item.wait()


def add_kernel(u_ref, moving_ref, out_ref):
    out_ref[...] = (u_ref[...] + moving_ref[...].astype(jnp.float32)).astype(out_ref.dtype)


def finish_kernel(cfg, u_ref, moving_ref, q_ref, query_grad_ref, weight_grad_ref):
    order, nh, rows_here, hh, depth, kc, chunk, scale = cfg
    rows = rows_here * hh
    eye = (
        lax.broadcasted_iota(jnp.int32, (rows_here, lanes), 0)
        == lax.broadcasted_iota(jnp.int32, (rows_here, lanes), 1)
    ).astype(jnp.float32)
    lane = lax.broadcasted_iota(jnp.int32, (lanes, lanes), 1)[:rows_here]
    slab = q_ref[rows:, :].astype(jnp.float32)
    out = jnp.zeros((rows_here, lanes), jnp.float32)
    for head in range(hh):
        at = slice(head * rows_here, (head + 1) * rows_here)
        total = u_ref[at, :] + moving_ref[at, :].astype(jnp.float32)
        w = jnp.sum(slab[head : head + 1] * eye, axis=1, keepdims=True) * scale
        query_grad_ref[:, head, :] = total * w
        along = jnp.sum(total * q_ref[at, :].astype(jnp.float32), axis=1, keepdims=True)
        out = jnp.where(lane == head, along * scale, out)
    if rows_here < lanes:
        out = jnp.concatenate([out, jnp.zeros((lanes - rows_here, lanes), jnp.float32)], axis=0)
    weight_grad_ref[...] = out.T[:hh, :rows_here]


def per_device(query, weights, keys, main_logits, row_weight, offset):
    n = lax.axis_size("ctx")
    nh = lax.axis_size("head")
    c = lax.axis_index("ctx")
    h = lax.axis_index("head")
    rows_here, hh, depth = query.shape
    kc = keys.shape[0]
    chunk = kc // nh
    rows = rows_here * hh
    scale = depth ** (-0.5)
    bf16, f32 = jnp.bfloat16, jnp.float32

    order = list(range(1, n, 2)) + list(range(0, n, 2))
    cfg = (order, nh, rows_here, hh, depth, kc, chunk, scale)
    smem = pl.BlockSpec(memory_space=pltpu.SMEM)
    vmem = pl.BlockSpec(memory_space=pltpu.VMEM)
    padded = -(-rows_here // lanes) * lanes
    meta = jnp.concatenate([offset, jnp.stack([c, h]).astype(jnp.int32)])

    far = lambda x: pltpu.with_memory_space_constraint(x, pltpu.HBM)

    slab_rows = -(-hh // 16) * 16
    parts = chunk // lanes
    message, rw, *key_messages = pl.pallas_call(
        functools.partial(prepare_kernel, cfg),
        out_shape=[
            jax.ShapeDtypeStruct((rows + slab_rows, depth), bf16),
            jax.ShapeDtypeStruct((1, padded), f32),
        ]
        + [jax.ShapeDtypeStruct((chunk + 2 * parts * rows_here, depth), bf16)] * (n // 2),
        in_specs=[smem, vmem, vmem, vmem] + [pl.BlockSpec(memory_space=pltpu.HBM)] * 2,
        out_specs=[vmem] * (2 + n // 2),
        scratch_shapes=[
            pltpu.VMEM((rows_here, hh, depth), f32),
            pltpu.SemaphoreType.DMA((n // 2 * (1 + 2 * parts),)),
        ],
        compiler_params=pltpu.CompilerParams(vmem_limit_bytes=vmem_bytes),
        cost_estimate=pl.CostEstimate(
            flops=rows * depth, bytes_accessed=4 * 1024 * 1024, transcendentals=0
        ),
        name="prepare",
    )(meta, far(query), far(weights.T), row_weight[None, :], far(keys), far(main_logits))
    q_blocks = [message, ring_next(message, "head")]

    k_pieces = [None] * n
    k_pieces[0::2] = [key_messages[0]] + [
        swap(key_messages[k // 2], "ctx", k) for k in range(2, n, 2)
    ]
    k_pieces[4], q_blocks[1] = lax.optimization_barrier((k_pieces[4], q_blocks[1]))
    k_pieces[1::2] = [swap(piece, "ctx", 1) for piece in k_pieces[0::2]]
    for j in range(2, nh):
        q_blocks.append(ring_next(q_blocks[-1], "head"))

    total_keys = n * chunk
    macs = rows * total_keys * depth
    tile = 512

    def call(kernel, operands, out_shape, scratch, products, name, aliases={}):
        return pl.pallas_call(
            kernel,
            out_shape=out_shape,
            input_output_aliases=aliases,
            in_specs=[smem] + [vmem] * len(operands),
            out_specs=[vmem] * len(out_shape),
            scratch_shapes=scratch,
            compiler_params=pltpu.CompilerParams(vmem_limit_bytes=vmem_bytes),
            cost_estimate=pl.CostEstimate(
                flops=int(4 * products * macs), bytes_accessed=4 * 1024 * 1024, transcendentals=0
            ),
            name=name,
        )(meta, *operands)

    near = lambda x: pltpu.with_memory_space_constraint(x, pltpu.VMEM)

    score = keys_all = stats = None
    qw, active = [], []
    for js in (range(nh - 1), range(nh - 1, nh)):
        is_first, is_last = js[0] == 0, js[-1] == nh - 1
        operands = [q_blocks[j] for j in js]
        if is_first:
            operands += [k_pieces[k] for k in order]
        else:
            operands += [near(keys_all), near(score), near(logits)]
        out_shape = [pltpu.VMEM((rows_here, total_keys), f32)]
        out_shape += [pltpu.VMEM((depth, rows), bf16)] * len(js)
        kept = len(js) - is_first
        out_shape += [pltpu.VMEM((rows, total_keys), bf16)] * kept
        if is_first:
            out_shape += [pltpu.VMEM((total_keys, depth), bf16)]
            out_shape += [pltpu.VMEM((rows_here, total_keys), bf16)]
        if is_last:
            out_shape += [jax.ShapeDtypeStruct((1, stat_rows, padded), f32)]
        scratch = [
            pltpu.VMEM((len(js), hh, rows_here, lanes), f32),
        ]
        kernel = functools.partial(forward_kernel, cfg, len(js), is_first, is_last)
        aliases = {} if is_first else {len(js) + 2: 0}
        outs = call(kernel, operands, out_shape, scratch, len(js), f"forward{js[0]}", aliases)
        score = outs[0]
        qw += outs[1 : 1 + len(js)]
        active += [None] * is_first + list(outs[1 + len(js) : 1 + len(js) + kept])
        if is_first:
            keys_all, logits = outs[-2:]
        stats = outs[-1] if is_last else stats

    all_stats = [stats] + [swap(stats, "head", j) for j in range(1, nh)]

    grad = kg = None

    def backward(items, name):
        nonlocal grad, kg
        is_first = grad is None
        ranges = [item[2] for item in items if item[2] is not None]
        makes_u = any(item[1] for item in items)
        has_before = bool(ranges) and kg is not None
        halved = ranges != [] and ranges[0] != "all"
        operands = [q_blocks[0] if halved else near(active[item[0]]) for item in items]
        operands += [near(qw[item[0]]) for item in items if item[2] is not None]
        operands += [near(keys_all)]
        operands += all_stats + [rw, near(logits), near(score)] if is_first else [near(grad)]
        aliases = {}
        out_shape = [jax.ShapeDtypeStruct((rows, depth), bf16 if is_first else f32)]
        out_shape = out_shape if makes_u else []
        scratch = [pltpu.VMEM((rows, tile), bf16)] * 2 + [pltpu.VMEM((rows, depth), f32)]
        if not halved:
            if ranges:
                if has_before:
                    aliases = {len(operands) + 1: len(out_shape)}
                out_shape += [pltpu.VMEM((depth, total_keys), f32)]
        else:
            if ranges[0] == "first":
                out_shape += [jax.ShapeDtypeStruct((n // 2, chunk, depth), bf16)]
            else:
                out_shape += [jax.ShapeDtypeStruct((chunk, depth), f32)] * (n // 2)
            out_shape += [pltpu.VMEM((rows, total_keys // 2), bf16)]
            scratch = [pltpu.VMEM((depth, total_keys // 2), f32)]
        if has_before:
            operands += [near(kg)]
        if is_first:
            out_shape += [pltpu.VMEM((rows_here, total_keys), bf16)]
            scratch += [pltpu.VMEM((padded, lanes), f32)]
        kernel = functools.partial(backward_kernel, cfg, items, has_before)
        products = 1 if halved else makes_u + len(ranges)
        outs = call(kernel, operands, out_shape, scratch, products, name, aliases)
        if is_first:
            grad = outs[-1]
        if ranges and ranges[0] == "all":
            kg = outs[1 if makes_u else 0]
        return outs

    part = backward([(1, True, None)], "backward_1")[0]
    moving = ring_next(part, "head")
    for j in range(2, nh):
        items = [(j - 1, False, "all"), (j, True, "all" if j == nh - 1 else None)]
        part = backward(items, f"backward_{j}")[0]
        part = pl.pallas_call(
            add_kernel,
            out_shape=jax.ShapeDtypeStruct((rows, depth), bf16),
            in_specs=[vmem] * 2,
            out_specs=vmem,
            compiler_params=pltpu.CompilerParams(vmem_limit_bytes=vmem_bytes),
            cost_estimate=pl.CostEstimate(
                flops=rows * depth, bytes_accessed=8 * rows * depth, transcendentals=0
            ),
            name=f"add_{j}",
        )(part, moving)
        kg, part = lax.optimization_barrier((kg, part))
        moving = ring_next(part, "head")

    odd, mask_first = backward([(0, False, "first")], "backward_0_first")
    other = swap(odd, "ctx", 1)
    *even, mask_second = backward([(0, False, "second")], "backward_0_second")
    even = [even[i] + other[i].astype(f32) for i in range(n // 2)]
    key_grad = even[0]
    sends = [even[i].astype(bf16) for i in range(1, n // 2)]
    keys_all, *sends = lax.optimization_barrier((keys_all, *sends))
    for i in range(1, n // 2):
        key_grad = key_grad + swap(sends[i - 1], "ctx", 2 * i).astype(f32)
    (u_mine,) = call(
        lambda meta_ref, *refs: query_kernel(cfg, refs[:2], *refs[2:]),
        [near(mask_first), near(mask_second), near(keys_all)],
        [jax.ShapeDtypeStruct((rows, depth), f32)],
        [pltpu.VMEM((rows, depth), f32)],
        1,
        "backward_0",
    )

    query_grad, weight_grad = pl.pallas_call(
        functools.partial(finish_kernel, cfg),
        out_shape=[
            jax.ShapeDtypeStruct((rows_here, hh, depth), f32),
            jax.ShapeDtypeStruct((hh, rows_here), f32),
        ],
        in_specs=[vmem] * 3,
        out_specs=[vmem] * 2,
        compiler_params=pltpu.CompilerParams(vmem_limit_bytes=vmem_bytes),
        cost_estimate=pl.CostEstimate(
            flops=8 * rows * depth, bytes_accessed=14 * rows * depth, transcendentals=0
        ),
        name="finish",
    )(u_mine, moving, q_blocks[0])
    return query_grad, key_grad, weight_grad.T


def solution(mesh):
    in_specs = (P("ctx", "head", None), P("ctx", "head"), P("ctx", None), P(None, "ctx"), P(), P())
    out_specs = (P("ctx", "head", None), P(("ctx", "head"), None), P("ctx", "head"))
    return jax.shard_map(
        per_device, mesh=mesh, in_specs=in_specs, out_specs=out_specs, check_vma=False
    )
```

time: 105 us -> 87 us (0.83)
  starting transfers between devices: 32.1 us -> 25.1 us
  waiting for transfers between devices: 18.7 us -> 11.7 us
  local copies, waits for them, and re-layouts: 3.84 us -> 0.68 us
  other arithmetic: 2.53 us -> 0.93 us
    ppermute x14, waiting for transfers between devices: 18.6 us -> 11.7 us  [swap(): return lax.ppermute(value, axis, [(i, i ^ distance) for i in range(size)])]
    ppermute x14, starting transfers between devices: 16.4 us -> 12 us  [swap(): return lax.ppermute(value, axis, [(i, i ^ distance) for i in range(size)])]
    all_to_all x1 -> x0, starting transfers between devices: 3.5 us -> none  [per_device(): lax.all_to_all(logits.reshape(n, rows_here, chunk), 'ctx', 0, 0, tiled=True)]
    pallas_call x0 -> x3, Pallas kernels: none -> 2.69 us  [the longest x1 2.59 us: per_device(): pl.pallas_call(functools.partial(prepare_kernel, cfg), out_shape=[jax.Sha...]
    dynamic_slice x2 -> x0, local copies, waits for them, and re-layouts: 1.9 us -> none  [the longest x1 1.06 us: per_device(): k_mine = lax.dynamic_slice_in_dim(keys, h * chunk, chunk, 0)]
    pallas_call x7 -> x8, Pallas kernels: 44.6 us -> 42.8 us  [call(): pl.pallas_call(kernel, out_shape=out_shape, input_output_aliases=aliases,...]
  transfers between devices with their start and end apart: 21 -> 20, of which waited for: 7 -> 7; matrix products, arithmetic and copies ran while one was open for 3% -> 0% of each run, Pallas kernels for 29% -> 37%
where the time goes in v3:
time: 87 us; the launch traced here: 86.8 us
  Pallas kernels  46.8 us (54%)
  starting transfers between devices  25.1 us (29%)
  waiting for transfers between devices  11.7 us (13%)
  between operations  1.44 us (2%)
  other arithmetic  0.93 us (1%)
    pallas_call x8, Pallas kernels, call(): pl.pallas_call(kernel, out_shape=out_shape, input_output_aliases=aliases,...  42.8 us
    ppermute x6, starting transfers between devices, ring_next(): lax.ppermute(value, axis, [(ring[i], ring[(i + 1) % size]) for i in range...  13.1 us
    ppermute x14, starting transfers between devices, swap(): return lax.ppermute(value, axis, [(i, i ^ distance) for i in range(size)])  12 us
    ppermute x14, waiting for transfers between devices, swap(): return lax.ppermute(value, axis, [(i, i ^ distance) for i in range(size)])  11.7 us
    pallas_call x1, Pallas kernels, per_device(): pl.pallas_call(functools.partial(prepare_kernel, cfg), out_shape=[jax.Sha...  2.59 us
  transfers between devices with their start and end apart: 20, of which 7 were waited for; matrix products, arithmetic and copies ran while one was open for 0% of the time, Pallas kernels for 37%

profile of v3, /device:TPU:0, one launch (start us, length us, event | category | flops | bytes accessed | tf_op | source)
XLA Modules:
  0.0 86.8 jit_solution(3436561519823071345)
XLA Ops:
  2.0 2.6 %prepare.1 = (bf16[1040,128]{1,0:T(8,128)(2,1)S(1)}, f32[1,128]{1,0:T(1,128)S(1)}, bf16[1024,128]{1,0:T(8,128)(2,1)S(1)}, bf16[1024,128]{1,0:T(8,128)(2,1)S(1)},...) custom-call(s32[3]{0:T(128)S(1)} %pad_add_fusion.meta_ref, bf16[64,16,128]{2,1,0:T(8,128)(2,1)} %query_ref.1, ...), custom_call_target="tpu_custom_call" | custom-call | flops 131072 | bytes 4194304 | tf_op jit(solution)/shard_map/prepare/pallas_call | solution.py:411
  4.6 4.1 %collective-permute-start.1 = (bf16[1040,128]{1,0:T(8,128)(2,1)S(1)}, bf16[1040,128]{1,0:T(8,128)(2,1)S(1)}, u32[]{:S(2)}, u32[]{:S(2)}) collective-permute-start(bf16[1040,128]{1,0:T(8,128)(2,1)S(1)} %get-tuple-element.46.refs_0_.q_ref), channel_id=1, source_target_pairs={{0,2},{2,3},{3,1},{1,0},{4,6},{6,7},{7,5},{5,4},{8,10},{10,11},{11... | collective-permute-start | bytes 798728 | tf_op jit(solution)/shard_map/ppermute | solution.py:25
  8.7 1.5 %collective-permute-start = (bf16[1024,128]{1,0:T(8,128)(2,1)S(1)}, bf16[1024,128]{1,0:T(8,128)(2,1)S(1)}, u32[]{:S(2)}, u32[]{:S(2)}) collective-permute-start(bf16[1024,128]{1,0:T(8,128)(2,1)S(1)} %get-tuple-element.47), channel_id=1, source_target_pairs={{0,16},{4,20},{8,24},{12,28},{16,0},{20,4},{24,8},{28,12},{1,17},{... | collective-permute-start | bytes 786440 | tf_op jit(solution)/shard_map/ppermute | solution.py:19
  10.2 1.5 %collective-permute-start.4 = (bf16[1024,128]{1,0:T(8,128)(2,1)S(1)}, bf16[1024,128]{1,0:T(8,128)(2,1)S(1)}, u32[]{:S(2)}, u32[]{:S(2)}) collective-permute-start(bf16[1024,128]{1,0:T(8,128)(2,1)S(1)} %get-tuple-element.50), channel_id=1, source_target_pairs={{0,8},{4,12},{8,0},{12,4},{16,24},{20,28},{24,16},{28,20},{1,9},{5... | collective-permute-start | bytes 786440 | tf_op jit(solution)/shard_map/ppermute | solution.py:19
  12.2 4.9 %collective-permute-done.refs_9_ = bf16[1024,128]{1,0:T(8,128)(2,1)S(1)} collective-permute-done((bf16[1024,128]{1,0:T(8,128)(2,1)S(1)}, bf16[1024,128]{1,0:T(8,128)(2,1)S(1)}, u32[]{:S(2)}, u32[]{:S(2)}) %collective-permute-start) | collective-permute-done | bytes 262176 | tf_op jit(solution)/shard_map/ppermute | solution.py:19
  17.1 1.6 %collective-permute-start.2 = (bf16[1040,128]{1,0:T(8,128)(2,1)S(1)}, bf16[1040,128]{1,0:T(8,128)(2,1)S(1)}, u32[]{:S(2)}, u32[]{:S(2)}) collective-permute-start(bf16[1040,128]{1,0:T(8,128)(2,1)S(1)} %collective-permute-done.1.refs_1_), channel_id=1, source_target_pairs={{0,2},{2,3},{3,1},{1,0},{4,6},{6,7},{7,5},{5,4},{8,10},{10,11},{11... | collective-permute-start | bytes 798728 | tf_op jit(solution)/shard_map/ppermute | solution.py:25
  19.5 3.8 %collective-permute-done.7.refs_10_ = bf16[1024,128]{1,0:T(8,128)(2,1)S(1)} collective-permute-done((bf16[1024,128]{1,0:T(8,128)(2,1)S(1)}, bf16[1024,128]{1,0:T(8,128)(2,1)S(1)}, u32[]{:S(2)}, u32[]{:S(2)}) %collective-permute-start.7) | collective-permute-done | bytes 262176 | tf_op jit(solution)/shard_map/ppermute | solution.py:19
  23.8 2.2 %collective-permute-start.9 = (bf16[1040,128]{1,0:T(8,128)(2,1)S(1)}, bf16[1040,128]{1,0:T(8,128)(2,1)S(1)}, u32[]{:S(2)}, u32[]{:S(2)}) collective-permute-start(bf16[1040,128]{1,0:T(8,128)(2,1)S(1)} %collective-permute-done.2.refs_2_), channel_id=1, source_target_pairs={{0,2},{2,3},{3,1},{1,0},{4,6},{6,7},{7,5},{5,4},{8,10},{10,11},{11... | collective-permute-start | bytes 798728 | tf_op jit(solution)/shard_map/ppermute | solution.py:25
  26.0 11.5 %forward0.1 = (f32[64,4096]{1,0:T(8,128)S(1)}, bf16[128,1024]{1,0:T(8,128)(2,1)S(1)}, bf16[128,1024]{1,0:T(8,128)(2,1)S(1)}, bf16[128,1024]{1,0:T(8,128)(2,1)S(1...) custom-call(s32[3]{0:T(128)S(1)} %pad_add_fusion.meta_ref, ...), custom_call_target="tpu_custom_call" | custom-call | flops 6442450944 | bytes 4194304 | tf_op jit(solution)/shard_map/forward0/pallas_call | solution.py:446
  37.5 5.4 %forward3.1 = (f32[64,4096]{1,0:T(8,128)S(1)}, bf16[128,1024]{1,0:T(8,128)(2,1)S(1)}, bf16[1024,4096]{1,0:T(8,128)(2,1)S(1)}, f32[1,8,128]{2,1,0:T(8,128)S(1)}) custom-call(s32[3]{0:T(128)S(1)} %pad_add_fusion.meta_ref, bf16[1040,128]{1,0:T(8,128)(2,1)S(1)} %collective-permute-done.9.refs_0_, ...), custom_call_target="tpu_custom_call", output_to_operand_aliasing={{0}: (3, {})} | custom-call | flops 2147483648 | bytes 4194304 | tf_op jit(solution)/shard_map/forward3/pallas_call | solution.py:446
  42.9 1.3 %collective-permute-start.12 = (f32[1,8,128]{2,1,0:T(8,128)S(1)}, f32[1,8,128]{2,1,0:T(8,128)S(1)}, u32[]{:S(2)}, u32[]{:S(2)}) collective-permute-start(f32[1,8,128]{2,1,0:T(8,128)S(1)} %get-tuple-element.58.refs_2_), channel_id=1, source_target_pairs={{0,3},{1,2},{2,1},{3,0},{4,7},{5,6},{6,5},{7,4},{8,11},{9,10},{10,... | collective-permute-start | bytes 12296 | tf_op jit(solution)/shard_map/ppermute | solution.py:19
  44.3 3.1 %collective-permute-start.10 = (f32[1,8,128]{2,1,0:T(8,128)S(1)}, f32[1,8,128]{2,1,0:T(8,128)S(1)}, u32[]{:S(2)}, u32[]{:S(2)}) collective-permute-start(f32[1,8,128]{2,1,0:T(8,128)S(1)} %get-tuple-element.58.refs_2_), channel_id=1, source_target_pairs={{0,1},{1,0},{2,3},{3,2},{4,5},{5,4},{6,7},{7,6},{8,9},{9,8},{10,11... | collective-permute-start | bytes 12296 | tf_op jit(solution)/shard_map/ppermute | solution.py:19
  48.9 4.2 %backward_1.1 = (bf16[1024,128]{1,0:T(8,128)(2,1)S(1)}, bf16[64,4096]{1,0:T(8,128)(2,1)S(1)}) custom-call(s32[3]{0:T(128)S(1)} %pad_add_fusion.meta_ref, bf16[1024,4096]{1,0:T(8,128)(2,1)S(1)} %get-tuple-element.55.refs_0_, bf16[4096,128]{1,0:T(8,128)(2,1)S(1)} %get-tuple-element.81.refs_1_.refs_3_.refs_4_.refs_2_, ...), custom_call_target="tpu_custom_call" | custom-call | flops 2147483648 | bytes 4194304 | tf_op jit(solution)/shard_map/backward_1/pallas_call | solution.py:446
  53.1 1.9 %collective-permute-start.13 = (bf16[1024,128]{1,0:T(8,128)(2,1)S(1)}, bf16[1024,128]{1,0:T(8,128)(2,1)S(1)}, u32[]{:S(2)}, u32[]{:S(2)}) collective-permute-start(bf16[1024,128]{1,0:T(8,128)(2,1)S(1)} %get-tuple-element.69), channel_id=1, source_target_pairs={{0,2},{2,3},{3,1},{1,0},{4,6},{6,7},{7,5},{5,4},{8,10},{10,11},{11... | collective-permute-start | bytes 786440 | tf_op jit(solution)/shard_map/ppermute | solution.py:25
  55.0 5.6 %backward_2.1 = (f32[1024,128]{1,0:T(8,128)S(1)}, f32[128,4096]{1,0:T(8,128)S(1)}) custom-call(s32[3]{0:T(128)S(1)} %pad_add_fusion.meta_ref, bf16[1024,4096]{1,0:T(8,128)(2,1)S(1)} %get-tuple-element.55.refs_0_, bf16[1024,4096]{1,0:T(8,128)(2,1)S(1)} %get-tuple-element.62.refs_1_.refs_0_, bf16[128,1024]{1,0:T(8,128)(2,1)S(1)} %get-tuple-element.66.refs_2_, ...), custom_call_target="tpu_custom_call" | custom-call | flops 4294967296 | bytes 4194304 | tf_op jit(solution)/shard_map/backward_2/pallas_call | solution.py:446
  60.6 1.9 %collective-permute-start.14 = (bf16[1024,128]{1,0:T(8,128)(2,1)S(1)}, bf16[1024,128]{1,0:T(8,128)(2,1)S(1)}, u32[]{:S(2)}, u32[]{:S(2)}) collective-permute-start(bf16[1024,128]{1,0:T(8,128)(2,1)S(1)} %add_2.1), channel_id=1, source_target_pairs={{0,2},{2,3},{3,1},{1,0},{4,6},{6,7},{7,5},{5,4},{8,10},{10,11},{11... | collective-permute-start | bytes 786440 | tf_op jit(solution)/shard_map/ppermute | solution.py:25
  62.6 7.0 %backward_3.1 = (f32[1024,128]{1,0:T(8,128)S(1)}, f32[128,4096]{1,0:T(8,128)S(1)}) custom-call(s32[3]{0:T(128)S(1)} %pad_add_fusion.meta_ref, bf16[1024,4096]{1,0:T(8,128)(2,1)S(1)} %get-tuple-element.62.refs_1_.refs_0_, bf16[1024,4096]{1,0:T(8,128)(2,1)S(1)} %get-tuple-element.63.refs_1_, ...), custom_call_target="tpu_custom_call", output_to_operand_aliasing={{1}: (7, {})} | custom-call | flops 6442450944 | bytes 4194304 | tf_op jit(solution)/shard_map/backward_3/pallas_call | solution.py:446
  69.7 2.5 %backward_0_first.1 = (bf16[4,512,128]{2,1,0:T(8,128)(2,1)S(1)}, bf16[1024,2048]{1,0:T(8,128)(2,1)S(1)}) custom-call(s32[3]{0:T(128)S(1)} %pad_add_fusion.meta_ref, bf16[1040,128]{1,0:T(8,128)(2,1)S(1)} %get-tuple-element.46.refs_0_.q_ref, bf16[128,1024]{1,0:T(8,128)(2,1)S(1)} %get-tuple-element.53.refs_1_, ...), custom_call_target="tpu_custom_call" | custom-call | flops 2147483648 | bytes 4194304 | tf_op jit(solution)/shard_map/backward_0_first/pallas_call | solution.py:446
  72.3 1.5 %collective-permute-start.16 = (bf16[1024,128]{1,0:T(8,128)(2,1)S(1)}, bf16[1024,128]{1,0:T(8,128)(2,1)S(1)}, u32[]{:S(2)}, u32[]{:S(2)}) collective-permute-start(bf16[1024,128]{1,0:T(8,128)(2,1)S(1)} %add_3.1), channel_id=1, source_target_pairs={{0,2},{2,3},{3,1},{1,0},{4,6},{6,7},{7,5},{5,4},{8,10},{10,11},{11... | collective-permute-start | bytes 786440 | tf_op jit(solution)/shard_map/ppermute | solution.py:25
  73.7 2.5 %backward_0_second.1 = (f32[512,128]{1,0:T(8,128)S(1)}, f32[512,128]{1,0:T(8,128)S(1)}, f32[512,128]{1,0:T(8,128)S(1)}, f32[512,128]{1,0:T(8,128)S(1)}, bf16[1024,2048]{1,0:T(8,128)(2,1)S(1)}) custom-call(s32[3]{0:T(128)S(1)} %pad_add_fusion.meta_ref, bf16[1040,128]{1,0:T(8,128)(2,1)S(1)} %get-tuple-element.46.refs_0_.q_ref, ...), custom_call_target="tpu_custom_call" | custom-call | flops 2147483648 | bytes 4194304 | tf_op jit(solution)/shard_map/backward_0_second/pallas_call | solution.py:446
  76.3 1.6 %collective-permute-start.17 = (bf16[512,128]{1,0:T(8,128)(2,1)S(1)}, bf16[512,128]{1,0:T(8,128)(2,1)S(1)}, u32[]{:S(2)}, u32[]{:S(2)}) collective-permute-start(bf16[512,128]{1,0:T(8,128)(2,1)S(1)} %get-tuple-element.85), channel_id=1, source_target_pairs={{0,8},{4,12},{8,0},{12,4},{16,24},{20,28},{24,16},{28,20},{1,9},{5... | collective-permute-start | bytes 393224 | tf_op jit(solution)/shard_map/ppermute | solution.py:19
  77.9 1.5 %collective-permute-start.18 = (bf16[512,128]{1,0:T(8,128)(2,1)S(1)}, bf16[512,128]{1,0:T(8,128)(2,1)S(1)}, u32[]{:S(2)}, u32[]{:S(2)}) collective-permute-start(bf16[512,128]{1,0:T(8,128)(2,1)S(1)} %get-tuple-element.86), channel_id=1, source_target_pairs={{0,16},{4,20},{8,24},{12,28},{16,0},{20,4},{24,8},{28,12},{1,17},{... | collective-permute-start | bytes 393224 | tf_op jit(solution)/shard_map/ppermute | solution.py:19
  79.9 4.1 %backward_0.1.u_ref = f32[1024,128]{1,0:T(8,128)S(1)} custom-call(s32[3]{0:T(128)S(1)} %pad_add_fusion.meta_ref, bf16[1024,2048]{1,0:T(8,128)(2,1)S(1)} %get-tuple-element.75.refs_0_, bf16[1024,2048]{1,0:T(8,128)(2,1)S(1)} %get-tuple-element.76.refs_1_, bf16[4096,128]{1,0:T(8,128)(2,1)S(1)} %get-tuple-element.81.refs_1_.refs_3_.refs_4_.refs_2_), custom_call_target="tpu_custom_call" | custom-call | flops 2147483648 | bytes 4194304 | tf_op jit(solution)/shard_map/backward_0/pallas_call | solution.py:446
  84.0 1.3 %finish.1 = (f32[64,16,128]{2,1,0:T(8,128)}, f32[16,64]{1,0:T(8,128)}) custom-call(f32[1024,128]{1,0:T(8,128)S(1)} %backward_0.1.u_ref, bf16[1024,128]{1,0:T(8,128)(2,1)S(1)} %collective-permute-done.16.moving_ref, bf16[1040,128]{1,0:T(8,128)(2,1)S(1)} %get-tuple-element.46.refs_0_.q_ref), custom_call_target="tpu_custom_call" | custom-call | flops 1048576 | bytes 1835008 | tf_op jit(solution)/shard_map/finish/pallas_call | solution.py:575
  (33 shorter events, 6.4 us)
Async XLA Ops:
  1.4 0.7 copy-start
  4.6 12.4 %collective-permute-start.1 = (bf16[1040,128]{1,0:T(8,128)(2,1)S(1)}, bf16[1040,128]{1,0:T(8,128)(2,1)S(1)}, u32[]{:S(2)}, u32[]{:S(2)}) collective-permute-start(bf16[1040,128]{1,0:T(8,128)(2,1)S(1)} %get-tuple-element.46.refs_0_.q_ref), channel_id=1, source_target_pairs={{0,2},{2,3},{3,1},{1,0},{4,6},{6,7},{7,5},{5,4},{8,10},{10,11},{11... | collective-permute-start | bytes 798728 | tf_op jit(solution)/shard_map/ppermute | solution.py:25
  8.7 8.3 %collective-permute-start = (bf16[1024,128]{1,0:T(8,128)(2,1)S(1)}, bf16[1024,128]{1,0:T(8,128)(2,1)S(1)}, u32[]{:S(2)}, u32[]{:S(2)}) collective-permute-start(bf16[1024,128]{1,0:T(8,128)(2,1)S(1)} %get-tuple-element.47), channel_id=1, source_target_pairs={{0,16},{4,20},{8,24},{12,28},{16,0},{20,4},{24,8},{28,12},{1,17},{... | collective-permute-start | bytes 786440 | tf_op jit(solution)/shard_map/ppermute | solution.py:19
  10.2 9.2 %collective-permute-start.4 = (bf16[1024,128]{1,0:T(8,128)(2,1)S(1)}, bf16[1024,128]{1,0:T(8,128)(2,1)S(1)}, u32[]{:S(2)}, u32[]{:S(2)}) collective-permute-start(bf16[1024,128]{1,0:T(8,128)(2,1)S(1)} %get-tuple-element.50), channel_id=1, source_target_pairs={{0,8},{4,12},{8,0},{12,4},{16,24},{20,28},{24,16},{28,20},{1,9},{5... | collective-permute-start | bytes 786440 | tf_op jit(solution)/shard_map/ppermute | solution.py:19
  11.7 11.6 %collective-permute-start.7 = (bf16[1024,128]{1,0:T(8,128)(2,1)S(1)}, bf16[1024,128]{1,0:T(8,128)(2,1)S(1)}, u32[]{:S(2)}, u32[]{:S(2)}) collective-permute-start(bf16[1024,128]{1,0:T(8,128)(2,1)S(1)} %get-tuple-element.52), channel_id=1, source_target_pairs={{0,24},{4,28},{8,16},{12,20},{16,8},{20,12},{24,0},{28,4},{1,25},{... | collective-permute-start | bytes 786440 | tf_op jit(solution)/shard_map/ppermute | solution.py:19
  17.1 6.7 %collective-permute-start.2 = (bf16[1040,128]{1,0:T(8,128)(2,1)S(1)}, bf16[1040,128]{1,0:T(8,128)(2,1)S(1)}, u32[]{:S(2)}, u32[]{:S(2)}) collective-permute-start(bf16[1040,128]{1,0:T(8,128)(2,1)S(1)} %collective-permute-done.1.refs_1_), channel_id=1, source_target_pairs={{0,2},{2,3},{3,1},{1,0},{4,6},{6,7},{7,5},{5,4},{8,10},{10,11},{11... | collective-permute-start | bytes 798728 | tf_op jit(solution)/shard_map/ppermute | solution.py:25
  18.7 7.3 %collective-permute-start.3 = (bf16[1024,128]{1,0:T(8,128)(2,1)S(1)}, bf16[1024,128]{1,0:T(8,128)(2,1)S(1)}, u32[]{:S(2)}, u32[]{:S(2)}) collective-permute-start(bf16[1024,128]{1,0:T(8,128)(2,1)S(1)} %get-tuple-element.49.refs_7_), channel_id=1, source_target_pairs={{0,4},{4,0},{8,12},{12,8},{16,20},{20,16},{24,28},{28,24},{1,5},{5... | collective-permute-start | bytes 786440 | tf_op jit(solution)/shard_map/ppermute | solution.py:19
  19.5 6.5 %collective-permute-start.5 = (bf16[1024,128]{1,0:T(8,128)(2,1)S(1)}, bf16[1024,128]{1,0:T(8,128)(2,1)S(1)}, u32[]{:S(2)}, u32[]{:S(2)}) collective-permute-start(bf16[1024,128]{1,0:T(8,128)(2,1)S(1)} %collective-permute-done.4.refs_8_), channel_id=1, source_target_pairs={{0,4},{4,0},{8,12},{12,8},{16,20},{20,16},{24,28},{28,24},{1,5},{5... | collective-permute-start | bytes 786440 | tf_op jit(solution)/shard_map/ppermute | solution.py:19
  23.3 2.7 %collective-permute-start.8 = (bf16[1024,128]{1,0:T(8,128)(2,1)S(1)}, bf16[1024,128]{1,0:T(8,128)(2,1)S(1)}, u32[]{:S(2)}, u32[]{:S(2)}) collective-permute-start(bf16[1024,128]{1,0:T(8,128)(2,1)S(1)} %collective-permute-done.7.refs_10_), channel_id=1, source_target_pairs={{0,4},{4,0},{8,12},{12,8},{16,20},{20,16},{24,28},{28,24},{1,5},{5... | collective-permute-start | bytes 786440 | tf_op jit(solution)/shard_map/ppermute | solution.py:19
  23.3 2.7 %collective-permute-start.6 = (bf16[1024,128]{1,0:T(8,128)(2,1)S(1)}, bf16[1024,128]{1,0:T(8,128)(2,1)S(1)}, u32[]{:S(2)}, u32[]{:S(2)}) collective-permute-start(bf16[1024,128]{1,0:T(8,128)(2,1)S(1)} %collective-permute-done.refs_9_), channel_id=1, source_target_pairs={{0,4},{4,0},{8,12},{12,8},{16,20},{20,16},{24,28},{28,24},{1,5},{5... | collective-permute-start | bytes 786440 | tf_op jit(solution)/shard_map/ppermute | solution.py:19
  23.8 13.7 %collective-permute-start.9 = (bf16[1040,128]{1,0:T(8,128)(2,1)S(1)}, bf16[1040,128]{1,0:T(8,128)(2,1)S(1)}, u32[]{:S(2)}, u32[]{:S(2)}) collective-permute-start(bf16[1040,128]{1,0:T(8,128)(2,1)S(1)} %collective-permute-done.2.refs_2_), channel_id=1, source_target_pairs={{0,2},{2,3},{3,1},{1,0},{4,6},{6,7},{7,5},{5,4},{8,10},{10,11},{11... | collective-permute-start | bytes 798728 | tf_op jit(solution)/shard_map/ppermute | solution.py:25
  42.9 5.4 %collective-permute-start.12 = (f32[1,8,128]{2,1,0:T(8,128)S(1)}, f32[1,8,128]{2,1,0:T(8,128)S(1)}, u32[]{:S(2)}, u32[]{:S(2)}) collective-permute-start(f32[1,8,128]{2,1,0:T(8,128)S(1)} %get-tuple-element.58.refs_2_), channel_id=1, source_target_pairs={{0,3},{1,2},{2,1},{3,0},{4,7},{5,6},{6,5},{7,4},{8,11},{9,10},{10,... | collective-permute-start | bytes 12296 | tf_op jit(solution)/shard_map/ppermute | solution.py:19
  44.2 4.5 %collective-permute-start.11 = (f32[1,8,128]{2,1,0:T(8,128)S(1)}, f32[1,8,128]{2,1,0:T(8,128)S(1)}, u32[]{:S(2)}, u32[]{:S(2)}) collective-permute-start(f32[1,8,128]{2,1,0:T(8,128)S(1)} %get-tuple-element.58.refs_2_), channel_id=1, source_target_pairs={{0,2},{1,3},{2,0},{3,1},{4,6},{5,7},{6,4},{7,5},{8,10},{9,11},{10,... | collective-permute-start | bytes 12296 | tf_op jit(solution)/shard_map/ppermute | solution.py:19
  44.3 4.6 %collective-permute-start.10 = (f32[1,8,128]{2,1,0:T(8,128)S(1)}, f32[1,8,128]{2,1,0:T(8,128)S(1)}, u32[]{:S(2)}, u32[]{:S(2)}) collective-permute-start(f32[1,8,128]{2,1,0:T(8,128)S(1)} %get-tuple-element.58.refs_2_), channel_id=1, source_target_pairs={{0,1},{1,0},{2,3},{3,2},{4,5},{5,4},{6,7},{7,6},{8,9},{9,8},{10,11... | collective-permute-start | bytes 12296 | tf_op jit(solution)/shard_map/ppermute | solution.py:19
  53.1 7.5 %collective-permute-start.13 = (bf16[1024,128]{1,0:T(8,128)(2,1)S(1)}, bf16[1024,128]{1,0:T(8,128)(2,1)S(1)}, u32[]{:S(2)}, u32[]{:S(2)}) collective-permute-start(bf16[1024,128]{1,0:T(8,128)(2,1)S(1)} %get-tuple-element.69), channel_id=1, source_target_pairs={{0,2},{2,3},{3,1},{1,0},{4,6},{6,7},{7,5},{5,4},{8,10},{10,11},{11... | collective-permute-start | bytes 786440 | tf_op jit(solution)/shard_map/ppermute | solution.py:25
  60.6 9.0 %collective-permute-start.14 = (bf16[1024,128]{1,0:T(8,128)(2,1)S(1)}, bf16[1024,128]{1,0:T(8,128)(2,1)S(1)}, u32[]{:S(2)}, u32[]{:S(2)}) collective-permute-start(bf16[1024,128]{1,0:T(8,128)(2,1)S(1)} %add_2.1), channel_id=1, source_target_pairs={{0,2},{2,3},{3,1},{1,0},{4,6},{6,7},{7,5},{5,4},{8,10},{10,11},{11... | collective-permute-start | bytes 786440 | tf_op jit(solution)/shard_map/ppermute | solution.py:25
  72.2 4.1 %collective-permute-start.15 = (bf16[4,512,128]{2,1,0:T(8,128)(2,1)S(1)}, bf16[4,512,128]{2,1,0:T(8,128)(2,1)S(1)}, u32[]{:S(2)}, u32[]{:S(2)}) collective-permute-start(bf16[4,512,128]{2,1,0:T(8,128)(2,1)S(1)} %get-tuple-element.78), channel_id=1, source_target_pairs={{0,4},{4,0},{8,12},{12,8},{16,20},{20,16},{24,28},{28,24},{1,5},{5... | collective-permute-start | bytes 1572872 | tf_op jit(solution)/shard_map/ppermute | solution.py:19
  72.3 11.8 %collective-permute-start.16 = (bf16[1024,128]{1,0:T(8,128)(2,1)S(1)}, bf16[1024,128]{1,0:T(8,128)(2,1)S(1)}, u32[]{:S(2)}, u32[]{:S(2)}) collective-permute-start(bf16[1024,128]{1,0:T(8,128)(2,1)S(1)} %add_3.1), channel_id=1, source_target_pairs={{0,2},{2,3},{3,1},{1,0},{4,6},{6,7},{7,5},{5,4},{8,10},{10,11},{11... | collective-permute-start | bytes 786440 | tf_op jit(solution)/shard_map/ppermute | solution.py:25
  76.3 9.0 %collective-permute-start.17 = (bf16[512,128]{1,0:T(8,128)(2,1)S(1)}, bf16[512,128]{1,0:T(8,128)(2,1)S(1)}, u32[]{:S(2)}, u32[]{:S(2)}) collective-permute-start(bf16[512,128]{1,0:T(8,128)(2,1)S(1)} %get-tuple-element.85), channel_id=1, source_target_pairs={{0,8},{4,12},{8,0},{12,4},{16,24},{20,28},{24,16},{28,20},{1,9},{5... | collective-permute-start | bytes 393224 | tf_op jit(solution)/shard_map/ppermute | solution.py:19
  77.9 8.1 %collective-permute-start.18 = (bf16[512,128]{1,0:T(8,128)(2,1)S(1)}, bf16[512,128]{1,0:T(8,128)(2,1)S(1)}, u32[]{:S(2)}, u32[]{:S(2)}) collective-permute-start(bf16[512,128]{1,0:T(8,128)(2,1)S(1)} %get-tuple-element.86), channel_id=1, source_target_pairs={{0,16},{4,20},{8,24},{12,28},{16,0},{20,4},{24,8},{28,12},{1,17},{... | collective-permute-start | bytes 393224 | tf_op jit(solution)/shard_map/ppermute | solution.py:19
  79.4 6.6 %collective-permute-start.19 = (bf16[512,128]{1,0:T(8,128)(2,1)S(1)}, bf16[512,128]{1,0:T(8,128)(2,1)S(1)}, u32[]{:S(2)}, u32[]{:S(2)}) collective-permute-start(bf16[512,128]{1,0:T(8,128)(2,1)S(1)} %get-tuple-element.87), channel_id=1, source_target_pairs={{0,24},{4,28},{8,16},{12,20},{16,8},{20,12},{24,0},{28,4},{1,25},{... | collective-permute-start | bytes 393224 | tf_op jit(solution)/shard_map/ppermute | solution.py:19

commit v4 on v3

--- a/solution.py
+++ b/solution.py
@@ -59,12 +59,12 @@
     if is_first:
         message_refs = take(n)
     else:
-        keys_ref, before_ref, logits_ref = take(3)
+        keys_t_ref, before_ref, logits_ref = take(3)
     (score_ref,) = take(1)
     qw_refs = take(count)
     active_refs = [None] * is_first + take(count - is_first)
     if is_first:
-        keys_ref, logits_ref = take(2)
+        keys_t_ref, logits_ref = take(2)
     if is_last:
         (stats_ref,) = take(1)
     (wb,) = take(1)
@@ -73,7 +73,8 @@
     tiles = n * chunk // tile
     if is_first:
         for at, k in enumerate(order):
-            keys_ref[at * chunk : (at + 1) * chunk, :] = message_refs[at][:chunk, :]
+            keys = message_refs[at][:chunk, :].astype(jnp.float32)
+            keys_t_ref[:, at * chunk : (at + 1) * chunk] = keys.T.astype(jnp.bfloat16)
             for i in range(chunk // lanes):
                 first = chunk + (chunk // lanes * (k % 2) + i) * rows_here
                 column = at * chunk + i * lanes
@@ -99,11 +100,8 @@
     def step(j, s):
         for first in range(0, tile, side):
             columns = pl.ds(pl.multiple_of(s * tile + first, side), side)
-            dots = lax.dot_general(
-                q_refs[j][:rows, :],
-                keys_ref[columns, :],
-                contract_last,
-                preferred_element_type=jnp.float32,
+            dots = jnp.dot(
+                q_refs[j][:rows, :], keys_t_ref[:, columns], preferred_element_type=jnp.float32
             )
             total = [None] * (rows_here // 16)
             for head in range(hh):
@@ -193,7 +191,7 @@
     half = ranges[0] if ranges and ranges[0] != "all" else None
     source_refs = take(len(items))
     qw_refs = [take(1)[0] if item[2] is not None else None for item in items]
-    (keys_ref,) = take(1)
+    (keys_t_ref,) = take(1)
     if is_first:
         stat_refs = take(nh)
         rw_ref, logits_ref, score_ref = take(3)
@@ -244,11 +242,8 @@
                 value = source_ref[at, tile_at(s)]
             else:
                 g = grad_ref[:, tile_at(s)].astype(jnp.float32)
-                value = lax.dot_general(
-                    source_ref[at, :],
-                    keys_ref[tile_at(s), :],
-                    contract_last,
-                    preferred_element_type=jnp.float32,
+                value = jnp.dot(
+                    source_ref[at, :], keys_t_ref[:, tile_at(s)], preferred_element_type=jnp.float32
                 )
             wide = jnp.broadcast_to(g[None], (heads, rows_here, tile)).reshape(part, tile)
             value = jnp.where(value > 0, wide, jnp.zeros_like(wide))
@@ -264,9 +259,10 @@
                     mask_part(1 - buffer, following, i)
                 if is_u:
                     at = slice(i * part, (i + 1) * part)
-                    u_acc[at, :] += jnp.dot(
+                    u_acc[:, at] += lax.dot_general(
+                        keys_t_ref[:, tile_at(s)],
                         mask_at(buffer, s, at)[...],
-                        keys_ref[tile_at(s), :],
+                        contract_last,
                         preferred_element_type=jnp.float32,
                     )
                 if keys_range is None or i % (chunks // 2) != chunks // 2 - 1:
@@ -291,7 +287,7 @@
             u_acc[...] = jnp.zeros_like(u_acc)
         in_pairs(tiles, mask, step)
         if is_u:
-            u_ref[...] = u_acc[...].astype(u_ref.dtype)
+            u_ref[...] = u_acc[...].T.astype(u_ref.dtype)
 
     if half is not None:
         for i in range(n // 2):
@@ -302,7 +298,7 @@
                 kg_refs[i][...] = value
 
 
-def query_kernel(cfg, mask_refs, keys_ref, u_ref, u_acc):
+def query_kernel(cfg, mask_refs, keys_t_ref, u_ref, u_acc):
     count = mask_refs[0].shape[1]
     tile = min(512, count)
     u_acc[...] = jnp.zeros_like(u_acc)
@@ -310,15 +306,16 @@
 
         def step(s, _, half=half, mask_ref=mask_ref):
             at = pl.multiple_of(s * tile, tile)
-            u_acc[...] += jnp.dot(
+            u_acc[...] += lax.dot_general(
+                keys_t_ref[:, pl.ds(pl.multiple_of(half * count + at, tile), tile)],
                 mask_ref[:, pl.ds(at, tile)],
-                keys_ref[pl.ds(half * count + at, tile), :],
+                contract_last,
                 preferred_element_type=jnp.float32,
             )
             return 0
 
         lax.fori_loop(0, count // tile, step, 0)
-    u_ref[...] = u_acc[...]
+    u_ref[...] = u_acc[...].T
 
 
 def prepare_kernel(cfg, meta_ref, query_ref, weights_ref, rw_ref, keys_ref, logits_ref, *refs):
@@ -426,7 +423,7 @@
             flops=rows * depth, bytes_accessed=4 * 1024 * 1024, transcendentals=0
         ),
         name="prepare",
-    )(meta, far(query), far(weights.T), row_weight[None, :], far(keys), far(main_logits))
+    )(meta, far(query), far(weights.T), far(row_weight[None, :]), far(keys), far(main_logits))
     q_blocks = [message, ring_next(message, "head")]
 
     k_pieces = [None] * n
@@ -459,7 +456,7 @@
 
     near = lambda x: pltpu.with_memory_space_constraint(x, pltpu.VMEM)
 
-    score = keys_all = stats = None
+    score = keys_t = stats = None
     qw, active = [], []
     for js in (range(nh - 1), range(nh - 1, nh)):
         is_first, is_last = js[0] == 0, js[-1] == nh - 1
@@ -467,13 +464,13 @@
         if is_first:
             operands += [k_pieces[k] for k in order]
         else:
-            operands += [near(keys_all), near(score), near(logits)]
+            operands += [near(keys_t), near(score), near(logits)]
         out_shape = [pltpu.VMEM((rows_here, total_keys), f32)]
         out_shape += [pltpu.VMEM((depth, rows), bf16)] * len(js)
         kept = len(js) - is_first
         out_shape += [pltpu.VMEM((rows, total_keys), bf16)] * kept
         if is_first:
-            out_shape += [pltpu.VMEM((total_keys, depth), bf16)]
+            out_shape += [pltpu.VMEM((depth, total_keys), bf16)]
             out_shape += [pltpu.VMEM((rows_here, total_keys), bf16)]
         if is_last:
             out_shape += [jax.ShapeDtypeStruct((1, stat_rows, padded), f32)]
@@ -487,7 +484,7 @@
         qw += outs[1 : 1 + len(js)]
         active += [None] * is_first + list(outs[1 + len(js) : 1 + len(js) + kept])
         if is_first:
-            keys_all, logits = outs[-2:]
+            keys_t, logits = outs[-2:]
         stats = outs[-1] if is_last else stats
 
     all_stats = [stats] + [swap(stats, "head", j) for j in range(1, nh)]
@@ -503,12 +500,12 @@
         halved = ranges != [] and ranges[0] != "all"
         operands = [q_blocks[0] if halved else near(active[item[0]]) for item in items]
         operands += [near(qw[item[0]]) for item in items if item[2] is not None]
-        operands += [near(keys_all)]
+        operands += [near(keys_t)]
         operands += all_stats + [rw, near(logits), near(score)] if is_first else [near(grad)]
         aliases = {}
         out_shape = [jax.ShapeDtypeStruct((rows, depth), bf16 if is_first else f32)]
         out_shape = out_shape if makes_u else []
-        scratch = [pltpu.VMEM((rows, tile), bf16)] * 2 + [pltpu.VMEM((rows, depth), f32)]
+        scratch = [pltpu.VMEM((rows, tile), bf16)] * 2 + [pltpu.VMEM((depth, rows), f32)]
         if not halved:
             if ranges:
                 if has_before:
@@ -560,14 +557,14 @@
     even = [even[i] + other[i].astype(f32) for i in range(n // 2)]
     key_grad = even[0]
     sends = [even[i].astype(bf16) for i in range(1, n // 2)]
-    keys_all, *sends = lax.optimization_barrier((keys_all, *sends))
+    keys_t, *sends = lax.optimization_barrier((keys_t, *sends))
     for i in range(1, n // 2):
         key_grad = key_grad + swap(sends[i - 1], "ctx", 2 * i).astype(f32)
     (u_mine,) = call(
         lambda meta_ref, *refs: query_kernel(cfg, refs[:2], *refs[2:]),
-        [near(mask_first), near(mask_second), near(keys_all)],
+        [near(mask_first), near(mask_second), near(keys_t)],
         [jax.ShapeDtypeStruct((rows, depth), f32)],
-        [pltpu.VMEM((rows, depth), f32)],
+        [pltpu.VMEM((depth, rows), f32)],
         1,
         "backward_0",
     )

time: 87 us -> 88 us (1.011)
  Pallas kernels: 46.8 us -> 49.1 us
    pallas_call x8, Pallas kernels: 42.8 us -> 45.1 us  [call(): pl.pallas_call(kernel, out_shape=out_shape, input_output_aliases=aliases,...]
  transfers between devices with their start and end apart: 20 -> 20, of which waited for: 7 -> 7; matrix products, arithmetic and copies ran while one was open for 0% -> 0% of each run, Pallas kernels for 37% -> 38%
where the time goes in v4:
time: 88 us; the launch traced here: 87.8 us
  Pallas kernels  49.1 us (56%)
  starting transfers between devices  25.1 us (29%)
  waiting for transfers between devices  11.2 us (13%)
  between operations  1.44 us (2%)
  other arithmetic  0.93 us (1%)
    pallas_call x8, Pallas kernels, call(): pl.pallas_call(kernel, out_shape=out_shape, input_output_aliases=aliases,...  45.1 us
    ppermute x6, starting transfers between devices, ring_next(): lax.ppermute(value, axis, [(ring[i], ring[(i + 1) % size]) for i in range...  13.1 us
    ppermute x14, starting transfers between devices, swap(): return lax.ppermute(value, axis, [(i, i ^ distance) for i in range(size)])  12 us
    ppermute x14, waiting for transfers between devices, swap(): return lax.ppermute(value, axis, [(i, i ^ distance) for i in range(size)])  11.2 us
    pallas_call x1, Pallas kernels, per_device(): pl.pallas_call(functools.partial(prepare_kernel, cfg), out_shape=[jax.Sha...  2.61 us
  transfers between devices with their start and end apart: 20, of which 7 were waited for; matrix products, arithmetic and copies ran while one was open for 0% of the time, Pallas kernels for 38%

profile of v4, /device:TPU:0, one launch (start us, length us, event | category | flops | bytes accessed | tf_op | source)
XLA Modules:
  0.0 87.8 jit_solution(2132456699917584570)
XLA Ops:
  1.4 2.6 %prepare.1 = (bf16[1040,128]{1,0:T(8,128)(2,1)S(1)}, f32[1,128]{1,0:T(1,128)S(1)}, bf16[1024,128]{1,0:T(8,128)(2,1)S(1)}, bf16[1024,128]{1,0:T(8,128)(2,1)S(1)},...) custom-call(s32[3]{0:T(128)S(1)} %pad_add_fusion.meta_ref, bf16[64,16,128]{2,1,0:T(8,128)(2,1)} %query_ref.1, ...), custom_call_target="tpu_custom_call" | custom-call | flops 131072 | bytes 4194304 | tf_op jit(solution)/shard_map/prepare/pallas_call | solution.py:408
  4.0 4.1 %collective-permute-start.1 = (bf16[1040,128]{1,0:T(8,128)(2,1)S(1)}, bf16[1040,128]{1,0:T(8,128)(2,1)S(1)}, u32[]{:S(2)}, u32[]{:S(2)}) collective-permute-start(bf16[1040,128]{1,0:T(8,128)(2,1)S(1)} %get-tuple-element.46.refs_0_.q_ref), channel_id=1, source_target_pairs={{0,2},{2,3},{3,1},{1,0},{4,6},{6,7},{7,5},{5,4},{8,10},{10,11},{11... | collective-permute-start | bytes 798728 | tf_op jit(solution)/shard_map/ppermute | solution.py:25
  8.1 1.5 %collective-permute-start = (bf16[1024,128]{1,0:T(8,128)(2,1)S(1)}, bf16[1024,128]{1,0:T(8,128)(2,1)S(1)}, u32[]{:S(2)}, u32[]{:S(2)}) collective-permute-start(bf16[1024,128]{1,0:T(8,128)(2,1)S(1)} %get-tuple-element.47), channel_id=1, source_target_pairs={{0,16},{4,20},{8,24},{12,28},{16,0},{20,4},{24,8},{28,12},{1,17},{... | collective-permute-start | bytes 786440 | tf_op jit(solution)/shard_map/ppermute | solution.py:19
  9.6 1.5 %collective-permute-start.4 = (bf16[1024,128]{1,0:T(8,128)(2,1)S(1)}, bf16[1024,128]{1,0:T(8,128)(2,1)S(1)}, u32[]{:S(2)}, u32[]{:S(2)}) collective-permute-start(bf16[1024,128]{1,0:T(8,128)(2,1)S(1)} %get-tuple-element.50), channel_id=1, source_target_pairs={{0,8},{4,12},{8,0},{12,4},{16,24},{20,28},{24,16},{28,20},{1,9},{5... | collective-permute-start | bytes 786440 | tf_op jit(solution)/shard_map/ppermute | solution.py:19
  11.6 4.9 %collective-permute-done.refs_9_ = bf16[1024,128]{1,0:T(8,128)(2,1)S(1)} collective-permute-done((bf16[1024,128]{1,0:T(8,128)(2,1)S(1)}, bf16[1024,128]{1,0:T(8,128)(2,1)S(1)}, u32[]{:S(2)}, u32[]{:S(2)}) %collective-permute-start) | collective-permute-done | bytes 262176 | tf_op jit(solution)/shard_map/ppermute | solution.py:19
  16.4 1.6 %collective-permute-start.2 = (bf16[1040,128]{1,0:T(8,128)(2,1)S(1)}, bf16[1040,128]{1,0:T(8,128)(2,1)S(1)}, u32[]{:S(2)}, u32[]{:S(2)}) collective-permute-start(bf16[1040,128]{1,0:T(8,128)(2,1)S(1)} %collective-permute-done.1.refs_1_), channel_id=1, source_target_pairs={{0,2},{2,3},{3,1},{1,0},{4,6},{6,7},{7,5},{5,4},{8,10},{10,11},{11... | collective-permute-start | bytes 798728 | tf_op jit(solution)/shard_map/ppermute | solution.py:25
  18.8 3.8 %collective-permute-done.7.refs_10_ = bf16[1024,128]{1,0:T(8,128)(2,1)S(1)} collective-permute-done((bf16[1024,128]{1,0:T(8,128)(2,1)S(1)}, bf16[1024,128]{1,0:T(8,128)(2,1)S(1)}, u32[]{:S(2)}, u32[]{:S(2)}) %collective-permute-start.7) | collective-permute-done | bytes 262176 | tf_op jit(solution)/shard_map/ppermute | solution.py:19
  23.1 2.2 %collective-permute-start.9 = (bf16[1040,128]{1,0:T(8,128)(2,1)S(1)}, bf16[1040,128]{1,0:T(8,128)(2,1)S(1)}, u32[]{:S(2)}, u32[]{:S(2)}) collective-permute-start(bf16[1040,128]{1,0:T(8,128)(2,1)S(1)} %collective-permute-done.2.refs_2_), channel_id=1, source_target_pairs={{0,2},{2,3},{3,1},{1,0},{4,6},{6,7},{7,5},{5,4},{8,10},{10,11},{11... | collective-permute-start | bytes 798728 | tf_op jit(solution)/shard_map/ppermute | solution.py:25
  25.3 11.5 %forward0.1 = (f32[64,4096]{1,0:T(8,128)S(1)}, bf16[128,1024]{1,0:T(8,128)(2,1)S(1)}, bf16[128,1024]{1,0:T(8,128)(2,1)S(1)}, bf16[128,1024]{1,0:T(8,128)(2,1)S(1...) custom-call(s32[3]{0:T(128)S(1)} %pad_add_fusion.meta_ref, ...), custom_call_target="tpu_custom_call" | custom-call | flops 6442450944 | bytes 4194304 | tf_op jit(solution)/shard_map/forward0/pallas_call | solution.py:443
  36.9 5.3 %forward3.1 = (f32[64,4096]{1,0:T(8,128)S(1)}, bf16[128,1024]{1,0:T(8,128)(2,1)S(1)}, bf16[1024,4096]{1,0:T(8,128)(2,1)S(1)}, f32[1,8,128]{2,1,0:T(8,128)S(1)}) custom-call(s32[3]{0:T(128)S(1)} %pad_add_fusion.meta_ref, bf16[1040,128]{1,0:T(8,128)(2,1)S(1)} %collective-permute-done.9.refs_0_, ...), custom_call_target="tpu_custom_call", output_to_operand_aliasing={{0}: (3, {})} | custom-call | flops 2147483648 | bytes 4194304 | tf_op jit(solution)/shard_map/forward3/pallas_call | solution.py:443
  42.2 1.3 %collective-permute-start.12 = (f32[1,8,128]{2,1,0:T(8,128)S(1)}, f32[1,8,128]{2,1,0:T(8,128)S(1)}, u32[]{:S(2)}, u32[]{:S(2)}) collective-permute-start(f32[1,8,128]{2,1,0:T(8,128)S(1)} %get-tuple-element.58.refs_2_), channel_id=1, source_target_pairs={{0,3},{1,2},{2,1},{3,0},{4,7},{5,6},{6,5},{7,4},{8,11},{9,10},{10,... | collective-permute-start | bytes 12296 | tf_op jit(solution)/shard_map/ppermute | solution.py:19
  43.6 3.1 %collective-permute-start.10 = (f32[1,8,128]{2,1,0:T(8,128)S(1)}, f32[1,8,128]{2,1,0:T(8,128)S(1)}, u32[]{:S(2)}, u32[]{:S(2)}) collective-permute-start(f32[1,8,128]{2,1,0:T(8,128)S(1)} %get-tuple-element.58.refs_2_), channel_id=1, source_target_pairs={{0,1},{1,0},{2,3},{3,2},{4,5},{5,4},{6,7},{7,6},{8,9},{9,8},{10,11... | collective-permute-start | bytes 12296 | tf_op jit(solution)/shard_map/ppermute | solution.py:19
  48.2 5.0 %backward_1.1 = (bf16[1024,128]{1,0:T(8,128)(2,1)S(1)}, bf16[64,4096]{1,0:T(8,128)(2,1)S(1)}) custom-call(s32[3]{0:T(128)S(1)} %pad_add_fusion.meta_ref, bf16[1024,4096]{1,0:T(8,128)(2,1)S(1)} %get-tuple-element.55.refs_0_, bf16[128,4096]{1,0:T(8,128)(2,1)S(1)} %get-tuple-element.81.refs_1_.refs_3_.refs_4_.refs_2_, ...), custom_call_target="tpu_custom_call" | custom-call | flops 2147483648 | bytes 4194304 | tf_op jit(solution)/shard_map/backward_1/pallas_call | solution.py:443
  53.2 1.9 %collective-permute-start.13 = (bf16[1024,128]{1,0:T(8,128)(2,1)S(1)}, bf16[1024,128]{1,0:T(8,128)(2,1)S(1)}, u32[]{:S(2)}, u32[]{:S(2)}) collective-permute-start(bf16[1024,128]{1,0:T(8,128)(2,1)S(1)} %get-tuple-element.69), channel_id=1, source_target_pairs={{0,2},{2,3},{3,1},{1,0},{4,6},{6,7},{7,5},{5,4},{8,10},{10,11},{11... | collective-permute-start | bytes 786440 | tf_op jit(solution)/shard_map/ppermute | solution.py:25
  55.1 6.4 %backward_2.1 = (f32[1024,128]{1,0:T(8,128)S(1)}, f32[128,4096]{1,0:T(8,128)S(1)}) custom-call(s32[3]{0:T(128)S(1)} %pad_add_fusion.meta_ref, bf16[1024,4096]{1,0:T(8,128)(2,1)S(1)} %get-tuple-element.55.refs_0_, bf16[1024,4096]{1,0:T(8,128)(2,1)S(1)} %get-tuple-element.62.refs_1_.refs_0_, bf16[128,1024]{1,0:T(8,128)(2,1)S(1)} %get-tuple-element.66.refs_2_, ...), custom_call_target="tpu_custom_call" | custom-call | flops 4294967296 | bytes 4194304 | tf_op jit(solution)/shard_map/backward_2/pallas_call | solution.py:443
  61.5 1.3 %collective-permute-start.14 = (bf16[1024,128]{1,0:T(8,128)(2,1)S(1)}, bf16[1024,128]{1,0:T(8,128)(2,1)S(1)}, u32[]{:S(2)}, u32[]{:S(2)}) collective-permute-start(bf16[1024,128]{1,0:T(8,128)(2,1)S(1)} %add_2.1), channel_id=1, source_target_pairs={{0,2},{2,3},{3,1},{1,0},{4,6},{6,7},{7,5},{5,4},{8,10},{10,11},{11... | collective-permute-start | bytes 786440 | tf_op jit(solution)/shard_map/ppermute | solution.py:25
  62.8 7.3 %backward_3.1 = (f32[1024,128]{1,0:T(8,128)S(1)}, f32[128,4096]{1,0:T(8,128)S(1)}) custom-call(s32[3]{0:T(128)S(1)} %pad_add_fusion.meta_ref, bf16[1024,4096]{1,0:T(8,128)(2,1)S(1)} %get-tuple-element.62.refs_1_.refs_0_, bf16[1024,4096]{1,0:T(8,128)(2,1)S(1)} %get-tuple-element.63.refs_1_, ...), custom_call_target="tpu_custom_call", output_to_operand_aliasing={{1}: (7, {})} | custom-call | flops 6442450944 | bytes 4194304 | tf_op jit(solution)/shard_map/backward_3/pallas_call | solution.py:443
  70.2 2.5 %backward_0_first.1 = (bf16[4,512,128]{2,1,0:T(8,128)(2,1)S(1)}, bf16[1024,2048]{1,0:T(8,128)(2,1)S(1)}) custom-call(s32[3]{0:T(128)S(1)} %pad_add_fusion.meta_ref, bf16[1040,128]{1,0:T(8,128)(2,1)S(1)} %get-tuple-element.46.refs_0_.q_ref, bf16[128,1024]{1,0:T(8,128)(2,1)S(1)} %get-tuple-element.53.refs_1_, ...), custom_call_target="tpu_custom_call" | custom-call | flops 2147483648 | bytes 4194304 | tf_op jit(solution)/shard_map/backward_0_first/pallas_call | solution.py:443
  72.7 2.1 %collective-permute-start.16 = (bf16[1024,128]{1,0:T(8,128)(2,1)S(1)}, bf16[1024,128]{1,0:T(8,128)(2,1)S(1)}, u32[]{:S(2)}, u32[]{:S(2)}) collective-permute-start(bf16[1024,128]{1,0:T(8,128)(2,1)S(1)} %add_3.1), channel_id=1, source_target_pairs={{0,2},{2,3},{3,1},{1,0},{4,6},{6,7},{7,5},{5,4},{8,10},{10,11},{11... | collective-permute-start | bytes 786440 | tf_op jit(solution)/shard_map/ppermute | solution.py:25
  74.8 2.5 %backward_0_second.1 = (f32[512,128]{1,0:T(8,128)S(1)}, f32[512,128]{1,0:T(8,128)S(1)}, f32[512,128]{1,0:T(8,128)S(1)}, f32[512,128]{1,0:T(8,128)S(1)}, bf16[1024,2048]{1,0:T(8,128)(2,1)S(1)}) custom-call(s32[3]{0:T(128)S(1)} %pad_add_fusion.meta_ref, bf16[1040,128]{1,0:T(8,128)(2,1)S(1)} %get-tuple-element.46.refs_0_.q_ref, ...), custom_call_target="tpu_custom_call" | custom-call | flops 2147483648 | bytes 4194304 | tf_op jit(solution)/shard_map/backward_0_second/pallas_call | solution.py:443
  77.4 1.6 %collective-permute-start.17 = (bf16[512,128]{1,0:T(8,128)(2,1)S(1)}, bf16[512,128]{1,0:T(8,128)(2,1)S(1)}, u32[]{:S(2)}, u32[]{:S(2)}) collective-permute-start(bf16[512,128]{1,0:T(8,128)(2,1)S(1)} %get-tuple-element.85), channel_id=1, source_target_pairs={{0,8},{4,12},{8,0},{12,4},{16,24},{20,28},{24,16},{28,20},{1,9},{5... | collective-permute-start | bytes 393224 | tf_op jit(solution)/shard_map/ppermute | solution.py:19
  79.0 1.5 %collective-permute-start.18 = (bf16[512,128]{1,0:T(8,128)(2,1)S(1)}, bf16[512,128]{1,0:T(8,128)(2,1)S(1)}, u32[]{:S(2)}, u32[]{:S(2)}) collective-permute-start(bf16[512,128]{1,0:T(8,128)(2,1)S(1)} %get-tuple-element.86), channel_id=1, source_target_pairs={{0,16},{4,20},{8,24},{12,28},{16,0},{20,4},{24,8},{28,12},{1,17},{... | collective-permute-start | bytes 393224 | tf_op jit(solution)/shard_map/ppermute | solution.py:19
  81.0 4.6 %backward_0.1.u_ref = f32[1024,128]{1,0:T(8,128)S(1)} custom-call(s32[3]{0:T(128)S(1)} %pad_add_fusion.meta_ref, bf16[1024,2048]{1,0:T(8,128)(2,1)S(1)} %get-tuple-element.75.refs_0_, bf16[1024,2048]{1,0:T(8,128)(2,1)S(1)} %get-tuple-element.76.refs_1_, bf16[128,4096]{1,0:T(8,128)(2,1)S(1)} %get-tuple-element.81.refs_1_.refs_3_.refs_4_.refs_2_), custom_call_target="tpu_custom_call" | custom-call | flops 2147483648 | bytes 4194304 | tf_op jit(solution)/shard_map/backward_0/pallas_call | solution.py:443
  85.6 1.3 %finish.1 = (f32[64,16,128]{2,1,0:T(8,128)}, f32[16,64]{1,0:T(8,128)}) custom-call(f32[1024,128]{1,0:T(8,128)S(1)} %backward_0.1.u_ref, bf16[1024,128]{1,0:T(8,128)(2,1)S(1)} %collective-permute-done.16.moving_ref, bf16[1040,128]{1,0:T(8,128)(2,1)S(1)} %get-tuple-element.46.refs_0_.q_ref), custom_call_target="tpu_custom_call" | custom-call | flops 1048576 | bytes 1835008 | tf_op jit(solution)/shard_map/finish/pallas_call | solution.py:572
  (31 shorter events, 5.1 us)
Async XLA Ops:
  4.0 12.4 %collective-permute-start.1 = (bf16[1040,128]{1,0:T(8,128)(2,1)S(1)}, bf16[1040,128]{1,0:T(8,128)(2,1)S(1)}, u32[]{:S(2)}, u32[]{:S(2)}) collective-permute-start(bf16[1040,128]{1,0:T(8,128)(2,1)S(1)} %get-tuple-element.46.refs_0_.q_ref), channel_id=1, source_target_pairs={{0,2},{2,3},{3,1},{1,0},{4,6},{6,7},{7,5},{5,4},{8,10},{10,11},{11... | collective-permute-start | bytes 798728 | tf_op jit(solution)/shard_map/ppermute | solution.py:25
  8.1 8.3 %collective-permute-start = (bf16[1024,128]{1,0:T(8,128)(2,1)S(1)}, bf16[1024,128]{1,0:T(8,128)(2,1)S(1)}, u32[]{:S(2)}, u32[]{:S(2)}) collective-permute-start(bf16[1024,128]{1,0:T(8,128)(2,1)S(1)} %get-tuple-element.47), channel_id=1, source_target_pairs={{0,16},{4,20},{8,24},{12,28},{16,0},{20,4},{24,8},{28,12},{1,17},{... | collective-permute-start | bytes 786440 | tf_op jit(solution)/shard_map/ppermute | solution.py:19
  9.6 9.2 %collective-permute-start.4 = (bf16[1024,128]{1,0:T(8,128)(2,1)S(1)}, bf16[1024,128]{1,0:T(8,128)(2,1)S(1)}, u32[]{:S(2)}, u32[]{:S(2)}) collective-permute-start(bf16[1024,128]{1,0:T(8,128)(2,1)S(1)} %get-tuple-element.50), channel_id=1, source_target_pairs={{0,8},{4,12},{8,0},{12,4},{16,24},{20,28},{24,16},{28,20},{1,9},{5... | collective-permute-start | bytes 786440 | tf_op jit(solution)/shard_map/ppermute | solution.py:19
  11.1 11.6 %collective-permute-start.7 = (bf16[1024,128]{1,0:T(8,128)(2,1)S(1)}, bf16[1024,128]{1,0:T(8,128)(2,1)S(1)}, u32[]{:S(2)}, u32[]{:S(2)}) collective-permute-start(bf16[1024,128]{1,0:T(8,128)(2,1)S(1)} %get-tuple-element.52), channel_id=1, source_target_pairs={{0,24},{4,28},{8,16},{12,20},{16,8},{20,12},{24,0},{28,4},{1,25},{... | collective-permute-start | bytes 786440 | tf_op jit(solution)/shard_map/ppermute | solution.py:19
  16.4 6.7 %collective-permute-start.2 = (bf16[1040,128]{1,0:T(8,128)(2,1)S(1)}, bf16[1040,128]{1,0:T(8,128)(2,1)S(1)}, u32[]{:S(2)}, u32[]{:S(2)}) collective-permute-start(bf16[1040,128]{1,0:T(8,128)(2,1)S(1)} %collective-permute-done.1.refs_1_), channel_id=1, source_target_pairs={{0,2},{2,3},{3,1},{1,0},{4,6},{6,7},{7,5},{5,4},{8,10},{10,11},{11... | collective-permute-start | bytes 798728 | tf_op jit(solution)/shard_map/ppermute | solution.py:25
  18.0 7.3 %collective-permute-start.3 = (bf16[1024,128]{1,0:T(8,128)(2,1)S(1)}, bf16[1024,128]{1,0:T(8,128)(2,1)S(1)}, u32[]{:S(2)}, u32[]{:S(2)}) collective-permute-start(bf16[1024,128]{1,0:T(8,128)(2,1)S(1)} %get-tuple-element.49.refs_7_), channel_id=1, source_target_pairs={{0,4},{4,0},{8,12},{12,8},{16,20},{20,16},{24,28},{28,24},{1,5},{5... | collective-permute-start | bytes 786440 | tf_op jit(solution)/shard_map/ppermute | solution.py:19
  18.8 6.5 %collective-permute-start.5 = (bf16[1024,128]{1,0:T(8,128)(2,1)S(1)}, bf16[1024,128]{1,0:T(8,128)(2,1)S(1)}, u32[]{:S(2)}, u32[]{:S(2)}) collective-permute-start(bf16[1024,128]{1,0:T(8,128)(2,1)S(1)} %collective-permute-done.4.refs_8_), channel_id=1, source_target_pairs={{0,4},{4,0},{8,12},{12,8},{16,20},{20,16},{24,28},{28,24},{1,5},{5... | collective-permute-start | bytes 786440 | tf_op jit(solution)/shard_map/ppermute | solution.py:19
  22.6 2.7 %collective-permute-start.8 = (bf16[1024,128]{1,0:T(8,128)(2,1)S(1)}, bf16[1024,128]{1,0:T(8,128)(2,1)S(1)}, u32[]{:S(2)}, u32[]{:S(2)}) collective-permute-start(bf16[1024,128]{1,0:T(8,128)(2,1)S(1)} %collective-permute-done.7.refs_10_), channel_id=1, source_target_pairs={{0,4},{4,0},{8,12},{12,8},{16,20},{20,16},{24,28},{28,24},{1,5},{5... | collective-permute-start | bytes 786440 | tf_op jit(solution)/shard_map/ppermute | solution.py:19
  22.6 2.7 %collective-permute-start.6 = (bf16[1024,128]{1,0:T(8,128)(2,1)S(1)}, bf16[1024,128]{1,0:T(8,128)(2,1)S(1)}, u32[]{:S(2)}, u32[]{:S(2)}) collective-permute-start(bf16[1024,128]{1,0:T(8,128)(2,1)S(1)} %collective-permute-done.refs_9_), channel_id=1, source_target_pairs={{0,4},{4,0},{8,12},{12,8},{16,20},{20,16},{24,28},{28,24},{1,5},{5... | collective-permute-start | bytes 786440 | tf_op jit(solution)/shard_map/ppermute | solution.py:19
  23.1 13.7 %collective-permute-start.9 = (bf16[1040,128]{1,0:T(8,128)(2,1)S(1)}, bf16[1040,128]{1,0:T(8,128)(2,1)S(1)}, u32[]{:S(2)}, u32[]{:S(2)}) collective-permute-start(bf16[1040,128]{1,0:T(8,128)(2,1)S(1)} %collective-permute-done.2.refs_2_), channel_id=1, source_target_pairs={{0,2},{2,3},{3,1},{1,0},{4,6},{6,7},{7,5},{5,4},{8,10},{10,11},{11... | collective-permute-start | bytes 798728 | tf_op jit(solution)/shard_map/ppermute | solution.py:25
  42.2 5.4 %collective-permute-start.12 = (f32[1,8,128]{2,1,0:T(8,128)S(1)}, f32[1,8,128]{2,1,0:T(8,128)S(1)}, u32[]{:S(2)}, u32[]{:S(2)}) collective-permute-start(f32[1,8,128]{2,1,0:T(8,128)S(1)} %get-tuple-element.58.refs_2_), channel_id=1, source_target_pairs={{0,3},{1,2},{2,1},{3,0},{4,7},{5,6},{6,5},{7,4},{8,11},{9,10},{10,... | collective-permute-start | bytes 12296 | tf_op jit(solution)/shard_map/ppermute | solution.py:19
  43.5 4.5 %collective-permute-start.11 = (f32[1,8,128]{2,1,0:T(8,128)S(1)}, f32[1,8,128]{2,1,0:T(8,128)S(1)}, u32[]{:S(2)}, u32[]{:S(2)}) collective-permute-start(f32[1,8,128]{2,1,0:T(8,128)S(1)} %get-tuple-element.58.refs_2_), channel_id=1, source_target_pairs={{0,2},{1,3},{2,0},{3,1},{4,6},{5,7},{6,4},{7,5},{8,10},{9,11},{10,... | collective-permute-start | bytes 12296 | tf_op jit(solution)/shard_map/ppermute | solution.py:19
  43.6 4.6 %collective-permute-start.10 = (f32[1,8,128]{2,1,0:T(8,128)S(1)}, f32[1,8,128]{2,1,0:T(8,128)S(1)}, u32[]{:S(2)}, u32[]{:S(2)}) collective-permute-start(f32[1,8,128]{2,1,0:T(8,128)S(1)} %get-tuple-element.58.refs_2_), channel_id=1, source_target_pairs={{0,1},{1,0},{2,3},{3,2},{4,5},{5,4},{6,7},{7,6},{8,9},{9,8},{10,11... | collective-permute-start | bytes 12296 | tf_op jit(solution)/shard_map/ppermute | solution.py:19
  53.2 8.3 %collective-permute-start.13 = (bf16[1024,128]{1,0:T(8,128)(2,1)S(1)}, bf16[1024,128]{1,0:T(8,128)(2,1)S(1)}, u32[]{:S(2)}, u32[]{:S(2)}) collective-permute-start(bf16[1024,128]{1,0:T(8,128)(2,1)S(1)} %get-tuple-element.69), channel_id=1, source_target_pairs={{0,2},{2,3},{3,1},{1,0},{4,6},{6,7},{7,5},{5,4},{8,10},{10,11},{11... | collective-permute-start | bytes 786440 | tf_op jit(solution)/shard_map/ppermute | solution.py:25
  61.5 8.6 %collective-permute-start.14 = (bf16[1024,128]{1,0:T(8,128)(2,1)S(1)}, bf16[1024,128]{1,0:T(8,128)(2,1)S(1)}, u32[]{:S(2)}, u32[]{:S(2)}) collective-permute-start(bf16[1024,128]{1,0:T(8,128)(2,1)S(1)} %add_2.1), channel_id=1, source_target_pairs={{0,2},{2,3},{3,1},{1,0},{4,6},{6,7},{7,5},{5,4},{8,10},{10,11},{11... | collective-permute-start | bytes 786440 | tf_op jit(solution)/shard_map/ppermute | solution.py:25
  72.7 4.6 %collective-permute-start.15 = (bf16[4,512,128]{2,1,0:T(8,128)(2,1)S(1)}, bf16[4,512,128]{2,1,0:T(8,128)(2,1)S(1)}, u32[]{:S(2)}, u32[]{:S(2)}) collective-permute-start(bf16[4,512,128]{2,1,0:T(8,128)(2,1)S(1)} %get-tuple-element.78), channel_id=1, source_target_pairs={{0,4},{4,0},{8,12},{12,8},{16,20},{20,16},{24,28},{28,24},{1,5},{5... | collective-permute-start | bytes 1572872 | tf_op jit(solution)/shard_map/ppermute | solution.py:19
  72.7 12.9 %collective-permute-start.16 = (bf16[1024,128]{1,0:T(8,128)(2,1)S(1)}, bf16[1024,128]{1,0:T(8,128)(2,1)S(1)}, u32[]{:S(2)}, u32[]{:S(2)}) collective-permute-start(bf16[1024,128]{1,0:T(8,128)(2,1)S(1)} %add_3.1), channel_id=1, source_target_pairs={{0,2},{2,3},{3,1},{1,0},{4,6},{6,7},{7,5},{5,4},{8,10},{10,11},{11... | collective-permute-start | bytes 786440 | tf_op jit(solution)/shard_map/ppermute | solution.py:25
  77.4 9.6 %collective-permute-start.17 = (bf16[512,128]{1,0:T(8,128)(2,1)S(1)}, bf16[512,128]{1,0:T(8,128)(2,1)S(1)}, u32[]{:S(2)}, u32[]{:S(2)}) collective-permute-start(bf16[512,128]{1,0:T(8,128)(2,1)S(1)} %get-tuple-element.85), channel_id=1, source_target_pairs={{0,8},{4,12},{8,0},{12,4},{16,24},{20,28},{24,16},{28,20},{1,9},{5... | collective-permute-start | bytes 393224 | tf_op jit(solution)/shard_map/ppermute | solution.py:19
  79.0 8.1 %collective-permute-start.18 = (bf16[512,128]{1,0:T(8,128)(2,1)S(1)}, bf16[512,128]{1,0:T(8,128)(2,1)S(1)}, u32[]{:S(2)}, u32[]{:S(2)}) collective-permute-start(bf16[512,128]{1,0:T(8,128)(2,1)S(1)} %get-tuple-element.86), channel_id=1, source_target_pairs={{0,16},{4,20},{8,24},{12,28},{16,0},{20,4},{24,8},{28,12},{1,17},{... | collective-permute-start | bytes 393224 | tf_op jit(solution)/shard_map/ppermute | solution.py:19
  80.5 6.6 %collective-permute-start.19 = (bf16[512,128]{1,0:T(8,128)(2,1)S(1)}, bf16[512,128]{1,0:T(8,128)(2,1)S(1)}, u32[]{:S(2)}, u32[]{:S(2)}) collective-permute-start(bf16[512,128]{1,0:T(8,128)(2,1)S(1)} %get-tuple-element.87), channel_id=1, source_target_pairs={{0,24},{4,28},{8,16},{12,20},{16,8},{20,12},{24,0},{28,4},{1,25},{... | collective-permute-start | bytes 393224 | tf_op jit(solution)/shard_map/ppermute | solution.py:19

commit v5 on v4

--- a/solution.py
+++ b/solution.py
@@ -64,7 +64,7 @@
     qw_refs = take(count)
     active_refs = [None] * is_first + take(count - is_first)
     if is_first:
-        keys_t_ref, logits_ref = take(2)
+        keys_t_ref, keys_ref, logits_ref = take(3)
     if is_last:
         (stats_ref,) = take(1)
     (wb,) = take(1)
@@ -73,7 +73,10 @@
     tiles = n * chunk // tile
     if is_first:
         for at, k in enumerate(order):
-            keys = message_refs[at][:chunk, :].astype(jnp.float32)
+            keys = message_refs[at][:chunk, :]
+            keys_ref[at * chunk : (at + 1) * chunk, :depth] = keys
+            keys_ref[at * chunk : (at + 1) * chunk, depth:] = jnp.zeros_like(keys)
+            keys = keys.astype(jnp.float32)
             keys_t_ref[:, at * chunk : (at + 1) * chunk] = keys.T.astype(jnp.bfloat16)
             for i in range(chunk // lanes):
                 first = chunk + (chunk // lanes * (k % 2) + i) * rows_here
@@ -191,7 +194,7 @@
     half = ranges[0] if ranges and ranges[0] != "all" else None
     source_refs = take(len(items))
     qw_refs = [take(1)[0] if item[2] is not None else None for item in items]
-    (keys_t_ref,) = take(1)
+    (keys_ref,) = take(1)
     if is_first:
         stat_refs = take(nh)
         rw_ref, logits_ref, score_ref = take(3)
@@ -243,7 +246,7 @@
             else:
                 g = grad_ref[:, tile_at(s)].astype(jnp.float32)
                 value = jnp.dot(
-                    source_ref[at, :], keys_t_ref[:, tile_at(s)], preferred_element_type=jnp.float32
+                    source_ref[at, :], keys_ref[:, tile_at(s)], preferred_element_type=jnp.float32
                 )
             wide = jnp.broadcast_to(g[None], (heads, rows_here, tile)).reshape(part, tile)
             value = jnp.where(value > 0, wide, jnp.zeros_like(wide))
@@ -259,12 +262,11 @@
                     mask_part(1 - buffer, following, i)
                 if is_u:
                     at = slice(i * part, (i + 1) * part)
-                    u_acc[:, at] += lax.dot_general(
-                        keys_t_ref[:, tile_at(s)],
+                    u_acc[at, :] += jnp.dot(
                         mask_at(buffer, s, at)[...],
-                        contract_last,
+                        keys_ref[tile_at(s), :],
                         preferred_element_type=jnp.float32,
-                    )
+                    )[:, :depth]
                 if keys_range is None or i % (chunks // 2) != chunks // 2 - 1:
                     continue
                 first = i // (chunks // 2) * side
@@ -287,7 +289,7 @@
             u_acc[...] = jnp.zeros_like(u_acc)
         in_pairs(tiles, mask, step)
         if is_u:
-            u_ref[...] = u_acc[...].T.astype(u_ref.dtype)
+            u_ref[...] = u_acc[...].astype(u_ref.dtype)
 
     if half is not None:
         for i in range(n // 2):
@@ -298,7 +300,7 @@
                 kg_refs[i][...] = value
 
 
-def query_kernel(cfg, mask_refs, keys_t_ref, u_ref, u_acc):
+def query_kernel(cfg, mask_refs, keys_ref, u_ref, u_acc):
     count = mask_refs[0].shape[1]
     tile = min(512, count)
     u_acc[...] = jnp.zeros_like(u_acc)
@@ -306,16 +308,15 @@
 
         def step(s, _, half=half, mask_ref=mask_ref):
             at = pl.multiple_of(s * tile, tile)
-            u_acc[...] += lax.dot_general(
-                keys_t_ref[:, pl.ds(pl.multiple_of(half * count + at, tile), tile)],
+            u_acc[...] += jnp.dot(
                 mask_ref[:, pl.ds(at, tile)],
-                contract_last,
+                keys_ref[pl.ds(pl.multiple_of(half * count + at, tile), tile), :],
                 preferred_element_type=jnp.float32,
-            )
+            )[:, : u_acc.shape[1]]
             return 0
 
         lax.fori_loop(0, count // tile, step, 0)
-    u_ref[...] = u_acc[...].T
+    u_ref[...] = u_acc[...]
 
 
 def prepare_kernel(cfg, meta_ref, query_ref, weights_ref, rw_ref, keys_ref, logits_ref, *refs):
@@ -456,7 +457,7 @@
 
     near = lambda x: pltpu.with_memory_space_constraint(x, pltpu.VMEM)
 
-    score = keys_t = stats = None
+    score = keys_t = keys_wide = stats = None
     qw, active = [], []
     for js in (range(nh - 1), range(nh - 1, nh)):
         is_first, is_last = js[0] == 0, js[-1] == nh - 1
@@ -471,6 +472,7 @@
         out_shape += [pltpu.VMEM((rows, total_keys), bf16)] * kept
         if is_first:
             out_shape += [pltpu.VMEM((depth, total_keys), bf16)]
+            out_shape += [pltpu.VMEM((total_keys, 2 * depth), bf16)]
             out_shape += [pltpu.VMEM((rows_here, total_keys), bf16)]
         if is_last:
             out_shape += [jax.ShapeDtypeStruct((1, stat_rows, padded), f32)]
@@ -484,7 +486,7 @@
         qw += outs[1 : 1 + len(js)]
         active += [None] * is_first + list(outs[1 + len(js) : 1 + len(js) + kept])
         if is_first:
-            keys_t, logits = outs[-2:]
+            keys_t, keys_wide, logits = outs[-3:]
         stats = outs[-1] if is_last else stats
 
     all_stats = [stats] + [swap(stats, "head", j) for j in range(1, nh)]
@@ -500,12 +502,12 @@
         halved = ranges != [] and ranges[0] != "all"
         operands = [q_blocks[0] if halved else near(active[item[0]]) for item in items]
         operands += [near(qw[item[0]]) for item in items if item[2] is not None]
-        operands += [near(keys_t)]
+        operands += [near(keys_t if halved else keys_wide)]
         operands += all_stats + [rw, near(logits), near(score)] if is_first else [near(grad)]
         aliases = {}
         out_shape = [jax.ShapeDtypeStruct((rows, depth), bf16 if is_first else f32)]
         out_shape = out_shape if makes_u else []
-        scratch = [pltpu.VMEM((rows, tile), bf16)] * 2 + [pltpu.VMEM((depth, rows), f32)]
+        scratch = [pltpu.VMEM((rows, tile), bf16)] * 2 + [pltpu.VMEM((rows, depth), f32)]
         if not halved:
             if ranges:
                 if has_before:
@@ -557,14 +559,14 @@
     even = [even[i] + other[i].astype(f32) for i in range(n // 2)]
     key_grad = even[0]
     sends = [even[i].astype(bf16) for i in range(1, n // 2)]
-    keys_t, *sends = lax.optimization_barrier((keys_t, *sends))
+    keys_wide, *sends = lax.optimization_barrier((keys_wide, *sends))
     for i in range(1, n // 2):
         key_grad = key_grad + swap(sends[i - 1], "ctx", 2 * i).astype(f32)
     (u_mine,) = call(
         lambda meta_ref, *refs: query_kernel(cfg, refs[:2], *refs[2:]),
-        [near(mask_first), near(mask_second), near(keys_t)],
+        [near(mask_first), near(mask_second), near(keys_wide)],
         [jax.ShapeDtypeStruct((rows, depth), f32)],
-        [pltpu.VMEM((depth, rows), f32)],
+        [pltpu.VMEM((rows, depth), f32)],
         1,
         "backward_0",
     )

time: 88 us -> 86.8 us (0.986)
  Pallas kernels: 49.1 us -> 47.4 us
    pallas_call x8, Pallas kernels: 45.1 us -> 43.3 us  [call(): pl.pallas_call(kernel, out_shape=out_shape, input_output_aliases=aliases,...]
where the time goes in v5:
time: 86.8 us; the launch traced here: 86.6 us
  Pallas kernels  47.4 us (55%)
  starting transfers between devices  25.1 us (29%)
  waiting for transfers between devices  11.7 us (13%)
  between operations  1.43 us (2%)
  other arithmetic  0.94 us (1%)
    pallas_call x8, Pallas kernels, call(): pl.pallas_call(kernel, out_shape=out_shape, input_output_aliases=aliases,...  43.3 us
    ppermute x6, starting transfers between devices, ring_next(): lax.ppermute(value, axis, [(ring[i], ring[(i + 1) % size]) for i in range...  13.1 us
    ppermute x14, starting transfers between devices, swap(): return lax.ppermute(value, axis, [(i, i ^ distance) for i in range(size)])  12 us
    ppermute x14, waiting for transfers between devices, swap(): return lax.ppermute(value, axis, [(i, i ^ distance) for i in range(size)])  11.7 us
    pallas_call x1, Pallas kernels, per_device(): pl.pallas_call(functools.partial(prepare_kernel, cfg), out_shape=[jax.Sha...  2.61 us
  transfers between devices with their start and end apart: 20, of which 7 were waited for; matrix products, arithmetic and copies ran while one was open for 0% of the time, Pallas kernels for 38%

profile of v5, /device:TPU:0, one launch (start us, length us, event | category | flops | bytes accessed | tf_op | source)
XLA Modules:
  0.0 86.6 jit_solution(9183104530508805440)
XLA Ops:
  1.4 2.6 %prepare.1 = (bf16[1040,128]{1,0:T(8,128)(2,1)S(1)}, f32[1,128]{1,0:T(1,128)S(1)}, bf16[1024,128]{1,0:T(8,128)(2,1)S(1)}, bf16[1024,128]{1,0:T(8,128)(2,1)S(1)},...) custom-call(s32[3]{0:T(128)S(1)} %pad_add_fusion.meta_ref, bf16[64,16,128]{2,1,0:T(8,128)(2,1)} %query_ref.1, ...), custom_call_target="tpu_custom_call" | custom-call | flops 131072 | bytes 4194304 | tf_op jit(solution)/shard_map/prepare/pallas_call | solution.py:409
  4.0 4.1 %collective-permute-start.1 = (bf16[1040,128]{1,0:T(8,128)(2,1)S(1)}, bf16[1040,128]{1,0:T(8,128)(2,1)S(1)}, u32[]{:S(2)}, u32[]{:S(2)}) collective-permute-start(bf16[1040,128]{1,0:T(8,128)(2,1)S(1)} %get-tuple-element.47.refs_0_.q_ref), channel_id=1, source_target_pairs={{0,2},{2,3},{3,1},{1,0},{4,6},{6,7},{7,5},{5,4},{8,10},{10,11},{11... | collective-permute-start | bytes 798728 | tf_op jit(solution)/shard_map/ppermute | solution.py:25
  8.1 1.5 %collective-permute-start = (bf16[1024,128]{1,0:T(8,128)(2,1)S(1)}, bf16[1024,128]{1,0:T(8,128)(2,1)S(1)}, u32[]{:S(2)}, u32[]{:S(2)}) collective-permute-start(bf16[1024,128]{1,0:T(8,128)(2,1)S(1)} %get-tuple-element.48), channel_id=1, source_target_pairs={{0,16},{4,20},{8,24},{12,28},{16,0},{20,4},{24,8},{28,12},{1,17},{... | collective-permute-start | bytes 786440 | tf_op jit(solution)/shard_map/ppermute | solution.py:19
  9.6 1.5 %collective-permute-start.4 = (bf16[1024,128]{1,0:T(8,128)(2,1)S(1)}, bf16[1024,128]{1,0:T(8,128)(2,1)S(1)}, u32[]{:S(2)}, u32[]{:S(2)}) collective-permute-start(bf16[1024,128]{1,0:T(8,128)(2,1)S(1)} %get-tuple-element.51), channel_id=1, source_target_pairs={{0,8},{4,12},{8,0},{12,4},{16,24},{20,28},{24,16},{28,20},{1,9},{5... | collective-permute-start | bytes 786440 | tf_op jit(solution)/shard_map/ppermute | solution.py:19
  11.6 4.9 %collective-permute-done.refs_9_ = bf16[1024,128]{1,0:T(8,128)(2,1)S(1)} collective-permute-done((bf16[1024,128]{1,0:T(8,128)(2,1)S(1)}, bf16[1024,128]{1,0:T(8,128)(2,1)S(1)}, u32[]{:S(2)}, u32[]{:S(2)}) %collective-permute-start) | collective-permute-done | bytes 262176 | tf_op jit(solution)/shard_map/ppermute | solution.py:19
  16.4 1.6 %collective-permute-start.2 = (bf16[1040,128]{1,0:T(8,128)(2,1)S(1)}, bf16[1040,128]{1,0:T(8,128)(2,1)S(1)}, u32[]{:S(2)}, u32[]{:S(2)}) collective-permute-start(bf16[1040,128]{1,0:T(8,128)(2,1)S(1)} %collective-permute-done.1.refs_1_), channel_id=1, source_target_pairs={{0,2},{2,3},{3,1},{1,0},{4,6},{6,7},{7,5},{5,4},{8,10},{10,11},{11... | collective-permute-start | bytes 798728 | tf_op jit(solution)/shard_map/ppermute | solution.py:25
  18.8 3.8 %collective-permute-done.7.refs_10_ = bf16[1024,128]{1,0:T(8,128)(2,1)S(1)} collective-permute-done((bf16[1024,128]{1,0:T(8,128)(2,1)S(1)}, bf16[1024,128]{1,0:T(8,128)(2,1)S(1)}, u32[]{:S(2)}, u32[]{:S(2)}) %collective-permute-start.7) | collective-permute-done | bytes 262176 | tf_op jit(solution)/shard_map/ppermute | solution.py:19
  23.1 2.2 %collective-permute-start.9 = (bf16[1040,128]{1,0:T(8,128)(2,1)S(1)}, bf16[1040,128]{1,0:T(8,128)(2,1)S(1)}, u32[]{:S(2)}, u32[]{:S(2)}) collective-permute-start(bf16[1040,128]{1,0:T(8,128)(2,1)S(1)} %collective-permute-done.2.refs_2_), channel_id=1, source_target_pairs={{0,2},{2,3},{3,1},{1,0},{4,6},{6,7},{7,5},{5,4},{8,10},{10,11},{11... | collective-permute-start | bytes 798728 | tf_op jit(solution)/shard_map/ppermute | solution.py:25
  25.3 11.7 %forward0.1 = (f32[64,4096]{1,0:T(8,128)S(1)}, bf16[128,1024]{1,0:T(8,128)(2,1)S(1)}, bf16[128,1024]{1,0:T(8,128)(2,1)S(1)}, bf16[128,1024]{1,0:T(8,128)(2,1)S(1...) custom-call(s32[3]{0:T(128)S(1)} %pad_add_fusion.meta_ref, ...), custom_call_target="tpu_custom_call" | custom-call | flops 6442450944 | bytes 4194304 | tf_op jit(solution)/shard_map/forward0/pallas_call | solution.py:444
  37.1 5.3 %forward3.1 = (f32[64,4096]{1,0:T(8,128)S(1)}, bf16[128,1024]{1,0:T(8,128)(2,1)S(1)}, bf16[1024,4096]{1,0:T(8,128)(2,1)S(1)}, f32[1,8,128]{2,1,0:T(8,128)S(1)}) custom-call(s32[3]{0:T(128)S(1)} %pad_add_fusion.meta_ref, bf16[1040,128]{1,0:T(8,128)(2,1)S(1)} %collective-permute-done.9.refs_0_, ...), custom_call_target="tpu_custom_call", output_to_operand_aliasing={{0}: (3, {})} | custom-call | flops 2147483648 | bytes 4194304 | tf_op jit(solution)/shard_map/forward3/pallas_call | solution.py:444
  42.4 1.3 %collective-permute-start.12 = (f32[1,8,128]{2,1,0:T(8,128)S(1)}, f32[1,8,128]{2,1,0:T(8,128)S(1)}, u32[]{:S(2)}, u32[]{:S(2)}) collective-permute-start(f32[1,8,128]{2,1,0:T(8,128)S(1)} %get-tuple-element.60.refs_2_), channel_id=1, source_target_pairs={{0,3},{1,2},{2,1},{3,0},{4,7},{5,6},{6,5},{7,4},{8,11},{9,10},{10,... | collective-permute-start | bytes 12296 | tf_op jit(solution)/shard_map/ppermute | solution.py:19
  43.8 3.1 %collective-permute-start.10 = (f32[1,8,128]{2,1,0:T(8,128)S(1)}, f32[1,8,128]{2,1,0:T(8,128)S(1)}, u32[]{:S(2)}, u32[]{:S(2)}) collective-permute-start(f32[1,8,128]{2,1,0:T(8,128)S(1)} %get-tuple-element.60.refs_2_), channel_id=1, source_target_pairs={{0,1},{1,0},{2,3},{3,2},{4,5},{5,4},{6,7},{7,6},{8,9},{9,8},{10,11... | collective-permute-start | bytes 12296 | tf_op jit(solution)/shard_map/ppermute | solution.py:19
  48.4 4.3 %backward_1.1 = (bf16[1024,128]{1,0:T(8,128)(2,1)S(1)}, bf16[64,4096]{1,0:T(8,128)(2,1)S(1)}) custom-call(s32[3]{0:T(128)S(1)} %pad_add_fusion.meta_ref, bf16[1024,4096]{1,0:T(8,128)(2,1)S(1)} %get-tuple-element.56.refs_0_, bf16[4096,256]{1,0:T(8,128)(2,1)S(1)} %get-tuple-element.83.refs_1_.refs_3_.refs_4_.refs_2_, ...), custom_call_target="tpu_custom_call" | custom-call | flops 2147483648 | bytes 4194304 | tf_op jit(solution)/shard_map/backward_1/pallas_call | solution.py:444
  52.7 1.9 %collective-permute-start.13 = (bf16[1024,128]{1,0:T(8,128)(2,1)S(1)}, bf16[1024,128]{1,0:T(8,128)(2,1)S(1)}, u32[]{:S(2)}, u32[]{:S(2)}) collective-permute-start(bf16[1024,128]{1,0:T(8,128)(2,1)S(1)} %get-tuple-element.71), channel_id=1, source_target_pairs={{0,2},{2,3},{3,1},{1,0},{4,6},{6,7},{7,5},{5,4},{8,10},{10,11},{11... | collective-permute-start | bytes 786440 | tf_op jit(solution)/shard_map/ppermute | solution.py:25
  54.6 5.7 %backward_2.1 = (f32[1024,128]{1,0:T(8,128)S(1)}, f32[128,4096]{1,0:T(8,128)S(1)}) custom-call(s32[3]{0:T(128)S(1)} %pad_add_fusion.meta_ref, bf16[1024,4096]{1,0:T(8,128)(2,1)S(1)} %get-tuple-element.56.refs_0_, bf16[1024,4096]{1,0:T(8,128)(2,1)S(1)} %get-tuple-element.64.refs_1_.refs_0_, bf16[128,1024]{1,0:T(8,128)(2,1)S(1)} %get-tuple-element.68.refs_2_, ...), custom_call_target="tpu_custom_call" | custom-call | flops 4294967296 | bytes 4194304 | tf_op jit(solution)/shard_map/backward_2/pallas_call | solution.py:444
  60.5 1.8 %collective-permute-start.14 = (bf16[1024,128]{1,0:T(8,128)(2,1)S(1)}, bf16[1024,128]{1,0:T(8,128)(2,1)S(1)}, u32[]{:S(2)}, u32[]{:S(2)}) collective-permute-start(bf16[1024,128]{1,0:T(8,128)(2,1)S(1)} %add_2.1), channel_id=1, source_target_pairs={{0,2},{2,3},{3,1},{1,0},{4,6},{6,7},{7,5},{5,4},{8,10},{10,11},{11... | collective-permute-start | bytes 786440 | tf_op jit(solution)/shard_map/ppermute | solution.py:25
  62.2 7.1 %backward_3.1 = (f32[1024,128]{1,0:T(8,128)S(1)}, f32[128,4096]{1,0:T(8,128)S(1)}) custom-call(s32[3]{0:T(128)S(1)} %pad_add_fusion.meta_ref, bf16[1024,4096]{1,0:T(8,128)(2,1)S(1)} %get-tuple-element.64.refs_1_.refs_0_, bf16[1024,4096]{1,0:T(8,128)(2,1)S(1)} %get-tuple-element.65.refs_1_, ...), custom_call_target="tpu_custom_call", output_to_operand_aliasing={{1}: (7, {})} | custom-call | flops 6442450944 | bytes 4194304 | tf_op jit(solution)/shard_map/backward_3/pallas_call | solution.py:444
  69.4 2.5 %backward_0_first.1 = (bf16[4,512,128]{2,1,0:T(8,128)(2,1)S(1)}, bf16[1024,2048]{1,0:T(8,128)(2,1)S(1)}) custom-call(s32[3]{0:T(128)S(1)} %pad_add_fusion.meta_ref, bf16[1040,128]{1,0:T(8,128)(2,1)S(1)} %get-tuple-element.47.refs_0_.q_ref, bf16[128,1024]{1,0:T(8,128)(2,1)S(1)} %get-tuple-element.54.refs_1_, ...), custom_call_target="tpu_custom_call" | custom-call | flops 2147483648 | bytes 4194304 | tf_op jit(solution)/shard_map/backward_0_first/pallas_call | solution.py:444
  71.9 1.6 %collective-permute-start.16 = (bf16[1024,128]{1,0:T(8,128)(2,1)S(1)}, bf16[1024,128]{1,0:T(8,128)(2,1)S(1)}, u32[]{:S(2)}, u32[]{:S(2)}) collective-permute-start(bf16[1024,128]{1,0:T(8,128)(2,1)S(1)} %add_3.1), channel_id=1, source_target_pairs={{0,2},{2,3},{3,1},{1,0},{4,6},{6,7},{7,5},{5,4},{8,10},{10,11},{11... | collective-permute-start | bytes 786440 | tf_op jit(solution)/shard_map/ppermute | solution.py:25
  73.6 2.5 %backward_0_second.1 = (f32[512,128]{1,0:T(8,128)S(1)}, f32[512,128]{1,0:T(8,128)S(1)}, f32[512,128]{1,0:T(8,128)S(1)}, f32[512,128]{1,0:T(8,128)S(1)}, bf16[1024,2048]{1,0:T(8,128)(2,1)S(1)}) custom-call(s32[3]{0:T(128)S(1)} %pad_add_fusion.meta_ref, bf16[1040,128]{1,0:T(8,128)(2,1)S(1)} %get-tuple-element.47.refs_0_.q_ref, ...), custom_call_target="tpu_custom_call" | custom-call | flops 2147483648 | bytes 4194304 | tf_op jit(solution)/shard_map/backward_0_second/pallas_call | solution.py:444
  76.2 1.6 %collective-permute-start.17 = (bf16[512,128]{1,0:T(8,128)(2,1)S(1)}, bf16[512,128]{1,0:T(8,128)(2,1)S(1)}, u32[]{:S(2)}, u32[]{:S(2)}) collective-permute-start(bf16[512,128]{1,0:T(8,128)(2,1)S(1)} %get-tuple-element.87), channel_id=1, source_target_pairs={{0,8},{4,12},{8,0},{12,4},{16,24},{20,28},{24,16},{28,20},{1,9},{5... | collective-permute-start | bytes 393224 | tf_op jit(solution)/shard_map/ppermute | solution.py:19
  77.7 1.5 %collective-permute-start.18 = (bf16[512,128]{1,0:T(8,128)(2,1)S(1)}, bf16[512,128]{1,0:T(8,128)(2,1)S(1)}, u32[]{:S(2)}, u32[]{:S(2)}) collective-permute-start(bf16[512,128]{1,0:T(8,128)(2,1)S(1)} %get-tuple-element.88), channel_id=1, source_target_pairs={{0,16},{4,20},{8,24},{12,28},{16,0},{20,4},{24,8},{28,12},{1,17},{... | collective-permute-start | bytes 393224 | tf_op jit(solution)/shard_map/ppermute | solution.py:19
  79.7 4.1 %backward_0.1.u_ref = f32[1024,128]{1,0:T(8,128)S(1)} custom-call(s32[3]{0:T(128)S(1)} %pad_add_fusion.meta_ref, bf16[1024,2048]{1,0:T(8,128)(2,1)S(1)} %get-tuple-element.77.refs_0_, bf16[1024,2048]{1,0:T(8,128)(2,1)S(1)} %get-tuple-element.78.refs_1_, bf16[4096,256]{1,0:T(8,128)(2,1)S(1)} %get-tuple-element.83.refs_1_.refs_3_.refs_4_.refs_2_), custom_call_target="tpu_custom_call" | custom-call | flops 2147483648 | bytes 4194304 | tf_op jit(solution)/shard_map/backward_0/pallas_call | solution.py:444
  83.9 1.3 %finish.1 = (f32[64,16,128]{2,1,0:T(8,128)}, f32[16,64]{1,0:T(8,128)}) custom-call(f32[1024,128]{1,0:T(8,128)S(1)} %backward_0.1.u_ref, bf16[1024,128]{1,0:T(8,128)(2,1)S(1)} %collective-permute-done.16.moving_ref, bf16[1040,128]{1,0:T(8,128)(2,1)S(1)} %get-tuple-element.47.refs_0_.q_ref), custom_call_target="tpu_custom_call" | custom-call | flops 1048576 | bytes 1835008 | tf_op jit(solution)/shard_map/finish/pallas_call | solution.py:574
  (31 shorter events, 5.7 us)
Async XLA Ops:
  4.0 12.4 %collective-permute-start.1 = (bf16[1040,128]{1,0:T(8,128)(2,1)S(1)}, bf16[1040,128]{1,0:T(8,128)(2,1)S(1)}, u32[]{:S(2)}, u32[]{:S(2)}) collective-permute-start(bf16[1040,128]{1,0:T(8,128)(2,1)S(1)} %get-tuple-element.47.refs_0_.q_ref), channel_id=1, source_target_pairs={{0,2},{2,3},{3,1},{1,0},{4,6},{6,7},{7,5},{5,4},{8,10},{10,11},{11... | collective-permute-start | bytes 798728 | tf_op jit(solution)/shard_map/ppermute | solution.py:25
  8.1 8.3 %collective-permute-start = (bf16[1024,128]{1,0:T(8,128)(2,1)S(1)}, bf16[1024,128]{1,0:T(8,128)(2,1)S(1)}, u32[]{:S(2)}, u32[]{:S(2)}) collective-permute-start(bf16[1024,128]{1,0:T(8,128)(2,1)S(1)} %get-tuple-element.48), channel_id=1, source_target_pairs={{0,16},{4,20},{8,24},{12,28},{16,0},{20,4},{24,8},{28,12},{1,17},{... | collective-permute-start | bytes 786440 | tf_op jit(solution)/shard_map/ppermute | solution.py:19
  9.6 9.2 %collective-permute-start.4 = (bf16[1024,128]{1,0:T(8,128)(2,1)S(1)}, bf16[1024,128]{1,0:T(8,128)(2,1)S(1)}, u32[]{:S(2)}, u32[]{:S(2)}) collective-permute-start(bf16[1024,128]{1,0:T(8,128)(2,1)S(1)} %get-tuple-element.51), channel_id=1, source_target_pairs={{0,8},{4,12},{8,0},{12,4},{16,24},{20,28},{24,16},{28,20},{1,9},{5... | collective-permute-start | bytes 786440 | tf_op jit(solution)/shard_map/ppermute | solution.py:19
  11.1 11.6 %collective-permute-start.7 = (bf16[1024,128]{1,0:T(8,128)(2,1)S(1)}, bf16[1024,128]{1,0:T(8,128)(2,1)S(1)}, u32[]{:S(2)}, u32[]{:S(2)}) collective-permute-start(bf16[1024,128]{1,0:T(8,128)(2,1)S(1)} %get-tuple-element.53), channel_id=1, source_target_pairs={{0,24},{4,28},{8,16},{12,20},{16,8},{20,12},{24,0},{28,4},{1,25},{... | collective-permute-start | bytes 786440 | tf_op jit(solution)/shard_map/ppermute | solution.py:19
  16.4 6.7 %collective-permute-start.2 = (bf16[1040,128]{1,0:T(8,128)(2,1)S(1)}, bf16[1040,128]{1,0:T(8,128)(2,1)S(1)}, u32[]{:S(2)}, u32[]{:S(2)}) collective-permute-start(bf16[1040,128]{1,0:T(8,128)(2,1)S(1)} %collective-permute-done.1.refs_1_), channel_id=1, source_target_pairs={{0,2},{2,3},{3,1},{1,0},{4,6},{6,7},{7,5},{5,4},{8,10},{10,11},{11... | collective-permute-start | bytes 798728 | tf_op jit(solution)/shard_map/ppermute | solution.py:25
  18.0 7.3 %collective-permute-start.3 = (bf16[1024,128]{1,0:T(8,128)(2,1)S(1)}, bf16[1024,128]{1,0:T(8,128)(2,1)S(1)}, u32[]{:S(2)}, u32[]{:S(2)}) collective-permute-start(bf16[1024,128]{1,0:T(8,128)(2,1)S(1)} %get-tuple-element.50.refs_7_), channel_id=1, source_target_pairs={{0,4},{4,0},{8,12},{12,8},{16,20},{20,16},{24,28},{28,24},{1,5},{5... | collective-permute-start | bytes 786440 | tf_op jit(solution)/shard_map/ppermute | solution.py:19
  18.8 6.5 %collective-permute-start.5 = (bf16[1024,128]{1,0:T(8,128)(2,1)S(1)}, bf16[1024,128]{1,0:T(8,128)(2,1)S(1)}, u32[]{:S(2)}, u32[]{:S(2)}) collective-permute-start(bf16[1024,128]{1,0:T(8,128)(2,1)S(1)} %collective-permute-done.4.refs_8_), channel_id=1, source_target_pairs={{0,4},{4,0},{8,12},{12,8},{16,20},{20,16},{24,28},{28,24},{1,5},{5... | collective-permute-start | bytes 786440 | tf_op jit(solution)/shard_map/ppermute | solution.py:19
  22.6 2.7 %collective-permute-start.8 = (bf16[1024,128]{1,0:T(8,128)(2,1)S(1)}, bf16[1024,128]{1,0:T(8,128)(2,1)S(1)}, u32[]{:S(2)}, u32[]{:S(2)}) collective-permute-start(bf16[1024,128]{1,0:T(8,128)(2,1)S(1)} %collective-permute-done.7.refs_10_), channel_id=1, source_target_pairs={{0,4},{4,0},{8,12},{12,8},{16,20},{20,16},{24,28},{28,24},{1,5},{5... | collective-permute-start | bytes 786440 | tf_op jit(solution)/shard_map/ppermute | solution.py:19
  22.6 2.7 %collective-permute-start.6 = (bf16[1024,128]{1,0:T(8,128)(2,1)S(1)}, bf16[1024,128]{1,0:T(8,128)(2,1)S(1)}, u32[]{:S(2)}, u32[]{:S(2)}) collective-permute-start(bf16[1024,128]{1,0:T(8,128)(2,1)S(1)} %collective-permute-done.refs_9_), channel_id=1, source_target_pairs={{0,4},{4,0},{8,12},{12,8},{16,20},{20,16},{24,28},{28,24},{1,5},{5... | collective-permute-start | bytes 786440 | tf_op jit(solution)/shard_map/ppermute | solution.py:19
  23.1 13.9 %collective-permute-start.9 = (bf16[1040,128]{1,0:T(8,128)(2,1)S(1)}, bf16[1040,128]{1,0:T(8,128)(2,1)S(1)}, u32[]{:S(2)}, u32[]{:S(2)}) collective-permute-start(bf16[1040,128]{1,0:T(8,128)(2,1)S(1)} %collective-permute-done.2.refs_2_), channel_id=1, source_target_pairs={{0,2},{2,3},{3,1},{1,0},{4,6},{6,7},{7,5},{5,4},{8,10},{10,11},{11... | collective-permute-start | bytes 798728 | tf_op jit(solution)/shard_map/ppermute | solution.py:25
  42.4 5.4 %collective-permute-start.12 = (f32[1,8,128]{2,1,0:T(8,128)S(1)}, f32[1,8,128]{2,1,0:T(8,128)S(1)}, u32[]{:S(2)}, u32[]{:S(2)}) collective-permute-start(f32[1,8,128]{2,1,0:T(8,128)S(1)} %get-tuple-element.60.refs_2_), channel_id=1, source_target_pairs={{0,3},{1,2},{2,1},{3,0},{4,7},{5,6},{6,5},{7,4},{8,11},{9,10},{10,... | collective-permute-start | bytes 12296 | tf_op jit(solution)/shard_map/ppermute | solution.py:19
  43.7 4.5 %collective-permute-start.11 = (f32[1,8,128]{2,1,0:T(8,128)S(1)}, f32[1,8,128]{2,1,0:T(8,128)S(1)}, u32[]{:S(2)}, u32[]{:S(2)}) collective-permute-start(f32[1,8,128]{2,1,0:T(8,128)S(1)} %get-tuple-element.60.refs_2_), channel_id=1, source_target_pairs={{0,2},{1,3},{2,0},{3,1},{4,6},{5,7},{6,4},{7,5},{8,10},{9,11},{10,... | collective-permute-start | bytes 12296 | tf_op jit(solution)/shard_map/ppermute | solution.py:19
  43.8 4.6 %collective-permute-start.10 = (f32[1,8,128]{2,1,0:T(8,128)S(1)}, f32[1,8,128]{2,1,0:T(8,128)S(1)}, u32[]{:S(2)}, u32[]{:S(2)}) collective-permute-start(f32[1,8,128]{2,1,0:T(8,128)S(1)} %get-tuple-element.60.refs_2_), channel_id=1, source_target_pairs={{0,1},{1,0},{2,3},{3,2},{4,5},{5,4},{6,7},{7,6},{8,9},{9,8},{10,11... | collective-permute-start | bytes 12296 | tf_op jit(solution)/shard_map/ppermute | solution.py:19
  52.7 7.7 %collective-permute-start.13 = (bf16[1024,128]{1,0:T(8,128)(2,1)S(1)}, bf16[1024,128]{1,0:T(8,128)(2,1)S(1)}, u32[]{:S(2)}, u32[]{:S(2)}) collective-permute-start(bf16[1024,128]{1,0:T(8,128)(2,1)S(1)} %get-tuple-element.71), channel_id=1, source_target_pairs={{0,2},{2,3},{3,1},{1,0},{4,6},{6,7},{7,5},{5,4},{8,10},{10,11},{11... | collective-permute-start | bytes 786440 | tf_op jit(solution)/shard_map/ppermute | solution.py:25
  60.5 8.8 %collective-permute-start.14 = (bf16[1024,128]{1,0:T(8,128)(2,1)S(1)}, bf16[1024,128]{1,0:T(8,128)(2,1)S(1)}, u32[]{:S(2)}, u32[]{:S(2)}) collective-permute-start(bf16[1024,128]{1,0:T(8,128)(2,1)S(1)} %add_2.1), channel_id=1, source_target_pairs={{0,2},{2,3},{3,1},{1,0},{4,6},{6,7},{7,5},{5,4},{8,10},{10,11},{11... | collective-permute-start | bytes 786440 | tf_op jit(solution)/shard_map/ppermute | solution.py:25
  71.9 4.2 %collective-permute-start.15 = (bf16[4,512,128]{2,1,0:T(8,128)(2,1)S(1)}, bf16[4,512,128]{2,1,0:T(8,128)(2,1)S(1)}, u32[]{:S(2)}, u32[]{:S(2)}) collective-permute-start(bf16[4,512,128]{2,1,0:T(8,128)(2,1)S(1)} %get-tuple-element.80), channel_id=1, source_target_pairs={{0,4},{4,0},{8,12},{12,8},{16,20},{20,16},{24,28},{28,24},{1,5},{5... | collective-permute-start | bytes 1572872 | tf_op jit(solution)/shard_map/ppermute | solution.py:19
  71.9 11.9 %collective-permute-start.16 = (bf16[1024,128]{1,0:T(8,128)(2,1)S(1)}, bf16[1024,128]{1,0:T(8,128)(2,1)S(1)}, u32[]{:S(2)}, u32[]{:S(2)}) collective-permute-start(bf16[1024,128]{1,0:T(8,128)(2,1)S(1)} %add_3.1), channel_id=1, source_target_pairs={{0,2},{2,3},{3,1},{1,0},{4,6},{6,7},{7,5},{5,4},{8,10},{10,11},{11... | collective-permute-start | bytes 786440 | tf_op jit(solution)/shard_map/ppermute | solution.py:25
  76.2 9.0 %collective-permute-start.17 = (bf16[512,128]{1,0:T(8,128)(2,1)S(1)}, bf16[512,128]{1,0:T(8,128)(2,1)S(1)}, u32[]{:S(2)}, u32[]{:S(2)}) collective-permute-start(bf16[512,128]{1,0:T(8,128)(2,1)S(1)} %get-tuple-element.87), channel_id=1, source_target_pairs={{0,8},{4,12},{8,0},{12,4},{16,24},{20,28},{24,16},{28,20},{1,9},{5... | collective-permute-start | bytes 393224 | tf_op jit(solution)/shard_map/ppermute | solution.py:19
  77.7 8.1 %collective-permute-start.18 = (bf16[512,128]{1,0:T(8,128)(2,1)S(1)}, bf16[512,128]{1,0:T(8,128)(2,1)S(1)}, u32[]{:S(2)}, u32[]{:S(2)}) collective-permute-start(bf16[512,128]{1,0:T(8,128)(2,1)S(1)} %get-tuple-element.88), channel_id=1, source_target_pairs={{0,16},{4,20},{8,24},{12,28},{16,0},{20,4},{24,8},{28,12},{1,17},{... | collective-permute-start | bytes 393224 | tf_op jit(solution)/shard_map/ppermute | solution.py:19
  79.2 6.6 %collective-permute-start.19 = (bf16[512,128]{1,0:T(8,128)(2,1)S(1)}, bf16[512,128]{1,0:T(8,128)(2,1)S(1)}, u32[]{:S(2)}, u32[]{:S(2)}) collective-permute-start(bf16[512,128]{1,0:T(8,128)(2,1)S(1)} %get-tuple-element.89), channel_id=1, source_target_pairs={{0,24},{4,28},{8,16},{12,20},{16,8},{20,12},{24,0},{28,4},{1,25},{... | collective-permute-start | bytes 393224 | tf_op jit(solution)/shard_map/ppermute | solution.py:19

commit v6 on v5

--- a/solution.py
+++ b/solution.py
@@ -49,88 +49,129 @@
     return position <= limit
 
 
-def forward_kernel(cfg, count, is_first, is_last, meta_ref, *refs):
-    order, nh, rows_here, hh, depth, kc, chunk, scale = cfg
-    n = len(order)
+def spread_weights(cfg, q_ref, wide_ref, qw_ref):
+    order, nh, rows_here, hh, depth, kc, chunk, scale = cfg
     rows = rows_here * hh
-    refs = list(refs)
-    take = lambda count: [refs.pop(0) for _ in range(count)]
-    q_refs = take(count)
-    if is_first:
-        message_refs = take(n)
-    else:
-        keys_t_ref, before_ref, logits_ref = take(3)
-    (score_ref,) = take(1)
-    qw_refs = take(count)
-    active_refs = [None] * is_first + take(count - is_first)
-    if is_first:
-        keys_t_ref, keys_ref, logits_ref = take(3)
-    if is_last:
-        (stats_ref,) = take(1)
-    (wb,) = take(1)
-    side = min(256, n * chunk)
-    tile = min(4 * side, n * chunk)
-    tiles = n * chunk // tile
-    if is_first:
-        for at, k in enumerate(order):
-            keys = message_refs[at][:chunk, :]
-            keys_ref[at * chunk : (at + 1) * chunk, :depth] = keys
-            keys_ref[at * chunk : (at + 1) * chunk, depth:] = jnp.zeros_like(keys)
-            keys = keys.astype(jnp.float32)
-            keys_t_ref[:, at * chunk : (at + 1) * chunk] = keys.T.astype(jnp.bfloat16)
-            for i in range(chunk // lanes):
-                first = chunk + (chunk // lanes * (k % 2) + i) * rows_here
-                column = at * chunk + i * lanes
-                logits_ref[:, column : column + lanes] = message_refs[at][
-                    first : first + rows_here, :
-                ]
-
     eye = (
         lax.broadcasted_iota(jnp.int32, (rows_here, lanes), 0)
         == lax.broadcasted_iota(jnp.int32, (rows_here, lanes), 1)
     ).astype(jnp.float32)
-    for j, q_ref in enumerate(q_refs):
-        slab = q_ref[rows:, :].astype(jnp.float32)
-        for head in range(hh):
-            picked = jnp.sum(slab[head : head + 1] * eye, axis=1, keepdims=True)
-            wb[j, head] = jnp.broadcast_to(picked, (rows_here, lanes))
-        for head in range(0, hh, 2):
-            at = slice(head * rows_here, (head + 2) * rows_here)
-            q = q_ref[at, :].astype(jnp.float32)
-            w = wb[j, head : head + 2].reshape(2 * rows_here, lanes) * scale
-            qw_refs[j][:, at] = (q * w).T.astype(jnp.bfloat16)
-
-    def step(j, s):
+    slab = q_ref[rows:, :].astype(jnp.float32)
+    for head in range(hh):
+        picked = jnp.sum(slab[head : head + 1] * eye, axis=1, keepdims=True)
+        wide_ref[head] = jnp.broadcast_to(picked, (rows_here, lanes))
+    for head in range(0, hh, 2):
+        at = slice(head * rows_here, (head + 2) * rows_here)
+        q = q_ref[at, :].astype(jnp.float32)
+        w = wide_ref[head : head + 2].reshape(2 * rows_here, lanes) * scale
+        qw_ref[:, at] = (q * w).T.astype(jnp.bfloat16)
+
+
+def unpack(cfg, message_ref, k, at, keys_ref, keys_t_ref, logits_ref):
+    order, nh, rows_here, hh, depth, kc, chunk, scale = cfg
+    keys = message_ref[:chunk, :]
+    keys_ref[at : at + chunk, :] = keys
+    keys_t_ref[:, at : at + chunk] = keys.astype(jnp.float32).T.astype(jnp.bfloat16)
+    for i in range(chunk // lanes):
+        first = chunk + (chunk // lanes * (k % 2) + i) * rows_here
+        column = at + i * lanes
+        logits_ref[:, column : column + lanes] = message_ref[first : first + rows_here, :]
+
+
+def add_scores(cfg, q_ref, wide_ref, keys_t_ref, score_ref, before_ref, start, count, active_ref):
+    order, nh, rows_here, hh, depth, kc, chunk, scale = cfg
+    rows = rows_here * hh
+    side = min(256, count)
+    tile = min(4 * side, count)
+
+    def step(s, _):
         for first in range(0, tile, side):
-            columns = pl.ds(pl.multiple_of(s * tile + first, side), side)
+            local = pl.ds(pl.multiple_of(s * tile + first, side), side)
+            columns = pl.ds(pl.multiple_of(start + s * tile + first, side), side)
             dots = jnp.dot(
-                q_refs[j][:rows, :], keys_t_ref[:, columns], preferred_element_type=jnp.float32
+                q_ref[:rows, :], keys_t_ref[:, columns], preferred_element_type=jnp.float32
             )
             total = [None] * (rows_here // 16)
             for head in range(hh):
                 for t in range(rows_here // 16):
                     row = head * rows_here + t * 16
-                    w = wb[j, head, t * 16 : t * 16 + 16, :]
+                    w = wide_ref[head, t * 16 : t * 16 + 16, :]
                     w = jnp.concatenate([w] * (side // lanes), axis=1)
                     active = jnp.maximum(dots[row : row + 16, :], 0.0)
-                    if active_refs[j] is not None:
-                        active_refs[j][row : row + 16, columns] = active.astype(jnp.bfloat16)
+                    if active_ref is not None:
+                        active_ref[row : row + 16, local] = active.astype(jnp.bfloat16)
                     value = active * w
                     total[t] = value if head == 0 else total[t] + value
             for t, value in enumerate(total):
                 at = slice(t * 16, t * 16 + 16)
                 value = value * scale
-                if j > 0:
-                    value = score_ref[at, columns] + value
-                elif not is_first:
+                if before_ref is not None:
                     value = before_ref[at, columns] + value
                 score_ref[at, columns] = value
         return 0
 
-    for j in range(count):
-        lax.fori_loop(0, tiles, lambda s, _, j=j: step(j, s), 0)
-    if not is_last:
-        return
+    lax.fori_loop(0, count // tile, step, 0)
+
+
+def forward_early_kernel(cfg, pieces, is_first, meta_ref, *refs):
+    chunk = cfg[6]
+    refs = list(refs)
+    take = lambda count: [refs.pop(0) for _ in range(count)]
+    q_refs = take(2)
+    wide_refs = None if is_first else take(2)
+    message_refs = take(len(pieces))
+    score_ref, keys_ref, keys_t_ref, logits_ref, active_ref = take(5)
+    if is_first:
+        qw_refs, wide_refs = take(2), take(2)
+        for j in range(2):
+            spread_weights(cfg, q_refs[j], wide_refs[j], qw_refs[j])
+    for at, k in enumerate(pieces):
+        unpack(cfg, message_refs[at], k, at * chunk, keys_ref, keys_t_ref, logits_ref)
+    count = len(pieces) * chunk
+    add_scores(cfg, q_refs[0], wide_refs[0], keys_t_ref, score_ref, None, 0, count, None)
+    add_scores(cfg, q_refs[1], wide_refs[1], keys_t_ref, score_ref, score_ref, 0, count, active_ref)
+
+
+def forward_middle_kernel(cfg, groups, meta_ref, *refs):
+    order, nh, rows_here, hh, depth, kc, chunk, scale = cfg
+    refs = list(refs)
+    take = lambda count: [refs.pop(0) for _ in range(count)]
+    q_refs, wide_refs = take(2), take(2)
+    new_q_refs = take(nh - 3)
+    parts = [take(4) for _ in groups[:-1]]
+    message_refs = take(len(groups[-1]))
+    whole = take(4)
+    score_ref, keys_ref, keys_t_ref, logits_ref = whole
+    (last_active_ref,) = take(1)
+    active_refs, qw_refs = take(nh - 3), take(nh - 3)
+    (wide,) = take(1)
+    start = 0
+    for group, part in zip(groups, parts):
+        end = start + len(group) * chunk
+        score_ref[:, start:end] = part[0][...]
+        keys_ref[start:end, :] = part[1][...]
+        keys_t_ref[:, start:end] = part[2][...]
+        logits_ref[:, start:end] = part[3][...]
+        start = end
+    for i, k in enumerate(groups[-1]):
+        unpack(cfg, message_refs[i], k, start + i * chunk, keys_ref, keys_t_ref, logits_ref)
+    count = len(groups[-1]) * chunk
+    add_scores(cfg, q_refs[0], wide_refs[0], keys_t_ref, score_ref, None, start, count, None)
+    add_scores(
+        cfg, q_refs[1], wide_refs[1], keys_t_ref, score_ref, score_ref, start, count, last_active_ref
+    )
+    for q_ref, active_ref, qw_ref in zip(new_q_refs, active_refs, qw_refs):
+        spread_weights(cfg, q_ref, wide, qw_ref)
+        every = len(order) * chunk
+        add_scores(cfg, q_ref, wide, keys_t_ref, score_ref, score_ref, 0, every, active_ref)
+
+
+def forward_last_kernel(cfg, meta_ref, *refs):
+    order, nh, rows_here, hh, depth, kc, chunk, scale = cfg
+    q_ref, keys_t_ref, before_ref, logits_ref, score_ref, active_ref, qw_ref, stats_ref, wide = refs
+    spread_weights(cfg, q_ref, wide, qw_ref)
+    every = len(order) * chunk
+    add_scores(cfg, q_ref, wide, keys_t_ref, score_ref, before_ref, 0, every, active_ref)
 
     limit = row_limits(meta_ref, rows_here)
     lane = lax.broadcasted_iota(jnp.int32, (rows_here, lanes), 1)
@@ -192,7 +233,7 @@
     makes_u = any(item[1] for item in items)
     ranges = [item[2] for item in items if item[2] is not None]
     half = ranges[0] if ranges and ranges[0] != "all" else None
-    source_refs = take(len(items))
+    sources = [take(3 if item[0] == 1 else 1) for item in items]
     qw_refs = [take(1)[0] if item[2] is not None else None for item in items]
     (keys_ref,) = take(1)
     if is_first:
@@ -216,33 +257,44 @@
         (cols,) = take(1)
         stats = [ref[0] for ref in stat_refs]
         score_gradient(cfg, meta_ref, stats, rw_ref, logits_ref, score_ref, cols, grad_ref)
-    tile = min(512, n * chunk // 4)
+    tile = chunk
     chunks = max(1, min(4, hh))
     heads = hh // chunks
     part = heads * rows_here
     side = tile // 2
 
+    todo = []
     for index, (_, is_u, keys_range) in enumerate(items):
-        tiles = n * chunk // tile
-        if half is not None:
-            tiles = tiles // 2
-        offset = tiles if half == "second" else 0
-        source_ref, qw_ref = source_refs[index], qw_refs[index]
+        base = 0
+        for ref in sources[index]:
+            tiles = n // 2 if half is not None else ref.shape[1] // tile
+            todo.append((index, is_u, keys_range, ref, base, tiles))
+            base += tiles
+
+    for index, is_u, keys_range, source_ref, base, tiles in todo:
+        qw_ref = qw_refs[index]
         is_start = index == 0 or items[index - 1][2] is None
 
-        def tile_at(s, first=0, size=tile, offset=offset):
-            return pl.ds(pl.multiple_of((s + offset) * tile + first, size), size)
+        def tile_at(s, first=0, size=tile, base=base):
+            if half is None:
+                position = s + base
+            else:
+                position = meta_ref[3 + (n // 2 if half == "second" else 0) + s]
+            return pl.ds(pl.multiple_of(position * tile + first, size), size)
+
+        def local(s, first=0, size=tile):
+            return pl.ds(pl.multiple_of(s * tile + first, size), size)
 
         def mask_at(buffer, s, at, first=0, size=tile):
             if half is None:
                 return masks[buffer].at[at, first : first + size]
-            return mask_ref.at[at, pl.ds(pl.multiple_of(s * tile + first, size), size)]
+            return mask_ref.at[at, local(s, first, size)]
 
         def mask_part(buffer, s, i, source_ref=source_ref):
             at = slice(i * part, (i + 1) * part)
             if half is None:
                 g = grad_ref[:, tile_at(s)]
-                value = source_ref[at, tile_at(s)]
+                value = source_ref[at, local(s)]
             else:
                 g = grad_ref[:, tile_at(s)].astype(jnp.float32)
                 value = jnp.dot(
@@ -266,7 +318,7 @@
                         mask_at(buffer, s, at)[...],
                         keys_ref[tile_at(s), :],
                         preferred_element_type=jnp.float32,
-                    )[:, :depth]
+                    )
                 if keys_range is None or i % (chunks // 2) != chunks // 2 - 1:
                     continue
                 first = i // (chunks // 2) * side
@@ -283,12 +335,12 @@
                 if half is None:
                     kg_refs[0][:, here] = more
                 else:
-                    kg_acc[:, pl.ds(pl.multiple_of(s * tile + first, side), side)] = more
-
-        if is_u:
+                    kg_acc[:, local(s, first, side)] = more
+
+        if is_u and base == 0:
             u_acc[...] = jnp.zeros_like(u_acc)
         in_pairs(tiles, mask, step)
-        if is_u:
+        if is_u and (base + tiles) == n:
             u_ref[...] = u_acc[...].astype(u_ref.dtype)
 
     if half is not None:
@@ -300,22 +352,21 @@
                 kg_refs[i][...] = value
 
 
-def query_kernel(cfg, mask_refs, keys_ref, u_ref, u_acc):
-    count = mask_refs[0].shape[1]
-    tile = min(512, count)
+def query_kernel(cfg, meta_ref, first_ref, second_ref, keys_ref, u_ref, u_acc):
+    chunk, pieces = cfg[6], len(cfg[0]) // 2
     u_acc[...] = jnp.zeros_like(u_acc)
-    for half, mask_ref in enumerate(mask_refs):
+    for half, mask_ref in enumerate((first_ref, second_ref)):
 
         def step(s, _, half=half, mask_ref=mask_ref):
-            at = pl.multiple_of(s * tile, tile)
+            position = meta_ref[3 + half * pieces + s]
             u_acc[...] += jnp.dot(
-                mask_ref[:, pl.ds(at, tile)],
-                keys_ref[pl.ds(pl.multiple_of(half * count + at, tile), tile), :],
+                mask_ref[:, pl.ds(pl.multiple_of(s * chunk, chunk), chunk)],
+                keys_ref[pl.ds(pl.multiple_of(position * chunk, chunk), chunk), :],
                 preferred_element_type=jnp.float32,
-            )[:, : u_acc.shape[1]]
+            )
             return 0
 
-        lax.fori_loop(0, count // tile, step, 0)
+        lax.fori_loop(0, pieces, step, 0)
     u_ref[...] = u_acc[...]
 
 
@@ -395,12 +446,20 @@
     scale = depth ** (-0.5)
     bf16, f32 = jnp.bfloat16, jnp.float32
 
-    order = list(range(1, n, 2)) + list(range(0, n, 2))
+    groups = [
+        [1, 0],
+        list(range(3, n - 2, 2)) + list(range(2, n - 2, 2)),
+        [n - 1, n - 2],
+    ]
+    order = sum(groups, [])
     cfg = (order, nh, rows_here, hh, depth, kc, chunk, scale)
     smem = pl.BlockSpec(memory_space=pltpu.SMEM)
     vmem = pl.BlockSpec(memory_space=pltpu.VMEM)
     padded = -(-rows_here // lanes) * lanes
-    meta = jnp.concatenate([offset, jnp.stack([c, h]).astype(jnp.int32)])
+    table = [order.index(k) for k in list(range(1, n, 2)) + list(range(0, n, 2))]
+    meta = jnp.concatenate(
+        [offset, jnp.stack([c, h]).astype(jnp.int32), jnp.array(table, jnp.int32)]
+    )
 
     far = lambda x: pltpu.with_memory_space_constraint(x, pltpu.HBM)
 
@@ -431,14 +490,13 @@
     k_pieces[0::2] = [key_messages[0]] + [
         swap(key_messages[k // 2], "ctx", k) for k in range(2, n, 2)
     ]
-    k_pieces[4], q_blocks[1] = lax.optimization_barrier((k_pieces[4], q_blocks[1]))
-    k_pieces[1::2] = [swap(piece, "ctx", 1) for piece in k_pieces[0::2]]
+    k_pieces[1] = swap(k_pieces[0], "ctx", 1)
     for j in range(2, nh):
         q_blocks.append(ring_next(q_blocks[-1], "head"))
 
     total_keys = n * chunk
     macs = rows * total_keys * depth
-    tile = 512
+    tile = chunk
 
     def call(kernel, operands, out_shape, scratch, products, name, aliases={}):
         return pl.pallas_call(
@@ -450,44 +508,87 @@
             scratch_shapes=scratch,
             compiler_params=pltpu.CompilerParams(vmem_limit_bytes=vmem_bytes),
             cost_estimate=pl.CostEstimate(
-                flops=int(4 * products * macs), bytes_accessed=4 * 1024 * 1024, transcendentals=0
+                flops=int(4 * products * macs),
+                bytes_accessed=int(4 * products * 2**20),
+                transcendentals=0,
             ),
             name=name,
         )(meta, *operands)
 
     near = lambda x: pltpu.with_memory_space_constraint(x, pltpu.VMEM)
 
-    score = keys_t = keys_wide = stats = None
-    qw, active = [], []
-    for js in (range(nh - 1), range(nh - 1, nh)):
-        is_first, is_last = js[0] == 0, js[-1] == nh - 1
-        operands = [q_blocks[j] for j in js]
-        if is_first:
-            operands += [k_pieces[k] for k in order]
-        else:
-            operands += [near(keys_t), near(score), near(logits)]
-        out_shape = [pltpu.VMEM((rows_here, total_keys), f32)]
-        out_shape += [pltpu.VMEM((depth, rows), bf16)] * len(js)
-        kept = len(js) - is_first
-        out_shape += [pltpu.VMEM((rows, total_keys), bf16)] * kept
-        if is_first:
-            out_shape += [pltpu.VMEM((depth, total_keys), bf16)]
-            out_shape += [pltpu.VMEM((total_keys, 2 * depth), bf16)]
-            out_shape += [pltpu.VMEM((rows_here, total_keys), bf16)]
-        if is_last:
-            out_shape += [jax.ShapeDtypeStruct((1, stat_rows, padded), f32)]
-        scratch = [
-            pltpu.VMEM((len(js), hh, rows_here, lanes), f32),
+    wide_shape = pltpu.VMEM((hh, rows_here, lanes), f32)
+    qw_shape = pltpu.VMEM((depth, rows), bf16)
+
+    def keys_shapes(count):
+        return [
+            pltpu.VMEM((rows_here, count), f32),
+            pltpu.VMEM((count, depth), bf16),
+            pltpu.VMEM((depth, count), bf16),
+            pltpu.VMEM((rows_here, count), bf16),
         ]
-        kernel = functools.partial(forward_kernel, cfg, len(js), is_first, is_last)
-        aliases = {} if is_first else {len(js) + 2: 0}
-        outs = call(kernel, operands, out_shape, scratch, len(js), f"forward{js[0]}", aliases)
-        score = outs[0]
-        qw += outs[1 : 1 + len(js)]
-        active += [None] * is_first + list(outs[1 + len(js) : 1 + len(js) + kept])
-        if is_first:
-            keys_t, keys_wide, logits = outs[-3:]
-        stats = outs[-1] if is_last else stats
+
+    nears = lambda xs: [near(x) for x in xs]
+    early, early_active, qw, wides = [], [], [], []
+    for i, group in enumerate(groups[:2]):
+        count = len(group) * chunk
+        if i == 1:
+            far_even = range(2, n - 2, 2)
+            wides[0], *came = lax.optimization_barrier((wides[0], *(k_pieces[k] for k in far_even)))
+            for k, piece in zip(far_even, came):
+                k_pieces[k], k_pieces[k + 1] = piece, swap(piece, "ctx", 1)
+        outs = call(
+            functools.partial(forward_early_kernel, cfg, group, i == 0),
+            q_blocks[:2] + nears(wides) + [k_pieces[k] for k in group],
+            keys_shapes(count)
+            + [pltpu.VMEM((rows, count), bf16)]
+            + ([qw_shape] * 2 + [wide_shape] * 2 if i == 0 else []),
+            [],
+            0.001,
+            f"forward_early_{i}",
+        )
+        early += outs[:4]
+        early_active += [outs[4]]
+        if i == 0:
+            qw, wides = list(outs[5:7]), list(outs[7:9])
+    early[4], came = lax.optimization_barrier((early[4], k_pieces[n - 2]))
+    k_pieces[n - 2], k_pieces[n - 1] = came, swap(came, "ctx", 1)
+    last = len(groups[2]) * chunk
+    outs = call(
+        functools.partial(forward_middle_kernel, cfg, groups),
+        q_blocks[:2]
+        + nears(wides)
+        + q_blocks[2 : nh - 1]
+        + nears(early)
+        + [k_pieces[k] for k in groups[2]],
+        keys_shapes(total_keys)
+        + [pltpu.VMEM((rows, last), bf16)]
+        + [pltpu.VMEM((rows, total_keys), bf16)] * (nh - 3)
+        + [qw_shape] * (nh - 3),
+        [pltpu.VMEM((hh, rows_here, lanes), f32)],
+        nh - 2.5,
+        "forward_middle",
+    )
+    score, keys_all, keys_t, logits = outs[:4]
+    active = [None, early_active + [outs[4]]]
+    active += [[value] for value in outs[5 : 5 + nh - 3]]
+    qw += list(outs[5 + nh - 3 :])
+    score, last_active, last_qw, stats = call(
+        functools.partial(forward_last_kernel, cfg),
+        [q_blocks[nh - 1], near(keys_t), near(score), near(logits)],
+        [
+            pltpu.VMEM((rows_here, total_keys), f32),
+            pltpu.VMEM((rows, total_keys), bf16),
+            qw_shape,
+            jax.ShapeDtypeStruct((1, stat_rows, padded), f32),
+        ],
+        [pltpu.VMEM((hh, rows_here, lanes), f32)],
+        1,
+        "forward_last",
+        {3: 0},
+    )
+    active.append([last_active])
+    qw.append(last_qw)
 
     all_stats = [stats] + [swap(stats, "head", j) for j in range(1, nh)]
 
@@ -500,9 +601,11 @@
         makes_u = any(item[1] for item in items)
         has_before = bool(ranges) and kg is not None
         halved = ranges != [] and ranges[0] != "all"
-        operands = [q_blocks[0] if halved else near(active[item[0]]) for item in items]
+        operands = []
+        for item in items:
+            operands += [q_blocks[0]] if halved else nears(active[item[0]])
         operands += [near(qw[item[0]]) for item in items if item[2] is not None]
-        operands += [near(keys_t if halved else keys_wide)]
+        operands += [near(keys_t if halved else keys_all)]
         operands += all_stats + [rw, near(logits), near(score)] if is_first else [near(grad)]
         aliases = {}
         out_shape = [jax.ShapeDtypeStruct((rows, depth), bf16 if is_first else f32)]
@@ -559,12 +662,12 @@
     even = [even[i] + other[i].astype(f32) for i in range(n // 2)]
     key_grad = even[0]
     sends = [even[i].astype(bf16) for i in range(1, n // 2)]
-    keys_wide, *sends = lax.optimization_barrier((keys_wide, *sends))
+    keys_all, *sends = lax.optimization_barrier((keys_all, *sends))
     for i in range(1, n // 2):
         key_grad = key_grad + swap(sends[i - 1], "ctx", 2 * i).astype(f32)
     (u_mine,) = call(
-        lambda meta_ref, *refs: query_kernel(cfg, refs[:2], *refs[2:]),
-        [near(mask_first), near(mask_second), near(keys_wide)],
+        functools.partial(query_kernel, cfg),
+        [near(mask_first), near(mask_second), near(keys_all)],
         [jax.ShapeDtypeStruct((rows, depth), f32)],
         [pltpu.VMEM((rows, depth), f32)],
         1,

time: 86.8 us -> 86.6 us (level)
  waiting for transfers between devices: 11.7 us -> 8.61 us
  starting transfers between devices: 25.1 us -> 27.5 us
    ppermute x14, waiting for transfers between devices: 11.7 us -> 5.57 us  [swap(): return lax.ppermute(value, axis, [(i, i ^ distance) for i in range(size)])]
    ppermute x6, waiting for transfers between devices: 0.02 us -> 3.04 us  [ring_next(): lax.ppermute(value, axis, [(ring[i], ring[(i + 1) % size]) for i in range...]
    ppermute x6, starting transfers between devices: 13.1 us -> 14.5 us  [ring_next(): lax.ppermute(value, axis, [(ring[i], ring[(i + 1) % size]) for i in range...]
    ppermute x14, starting transfers between devices: 12 us -> 13 us  [swap(): return lax.ppermute(value, axis, [(i, i ^ distance) for i in range(size)])]
    pallas_call x8 -> x10, Pallas kernels: 43.3 us -> 43.2 us  [call(): pl.pallas_call(kernel, out_shape=out_shape, input_output_aliases=aliases,...]
  transfers between devices with their start and end apart: 20 -> 20, of which waited for: 7 -> 8; matrix products, arithmetic and copies ran while one was open for 0% -> 0% of each run, Pallas kernels for 38% -> 39%
where the time goes in v6:
time: 86.6 us; the launch traced here: 86.4 us
  Pallas kernels  47.3 us (55%)
  starting transfers between devices  27.5 us (32%)
  waiting for transfers between devices  8.61 us (10%)
  other arithmetic  1.62 us (2%)
  between operations  1.43 us (2%)
    pallas_call x10, Pallas kernels, call(): pl.pallas_call(kernel, out_shape=out_shape, input_output_aliases=aliases,...  43.2 us
    ppermute x6, starting transfers between devices, ring_next(): lax.ppermute(value, axis, [(ring[i], ring[(i + 1) % size]) for i in range...  14.5 us
    ppermute x14, starting transfers between devices, swap(): return lax.ppermute(value, axis, [(i, i ^ distance) for i in range(size)])  13 us
    ppermute x14, waiting for transfers between devices, swap(): return lax.ppermute(value, axis, [(i, i ^ distance) for i in range(size)])  5.57 us
    ppermute x6, waiting for transfers between devices, ring_next(): lax.ppermute(value, axis, [(ring[i], ring[(i + 1) % size]) for i in range...  3.04 us
    pallas_call x1, Pallas kernels, per_device(): pl.pallas_call(functools.partial(prepare_kernel, cfg), out_shape=[jax.Sha...  2.61 us
  transfers between devices with their start and end apart: 20, of which 8 were waited for; matrix products, arithmetic and copies ran while one was open for 0% of the time, Pallas kernels for 39%

profile of v6, /device:TPU:0, one launch (start us, length us, event | category | flops | bytes accessed | tf_op | source)
XLA Modules:
  0.0 86.4 jit_solution(12445882557139323434)
XLA Ops:
  2.0 2.6 %prepare.1 = (bf16[1040,128]{1,0:T(8,128)(2,1)S(1)}, f32[1,128]{1,0:T(1,128)S(1)}, bf16[1024,128]{1,0:T(8,128)(2,1)S(1)}, bf16[1024,128]{1,0:T(8,128)(2,1)S(1)},...) custom-call(s32[11]{0:T(128)S(1)} %pad_add_fusion.meta_ref, bf16[64,16,128]{2,1,0:T(8,128)(2,1)} %query_ref.1, ...), custom_call_target="tpu_custom_call" | custom-call | flops 131072 | bytes 4194304 | tf_op jit(solution)/shard_map/prepare/pallas_call | solution.py:468
  4.6 4.1 %collective-permute-start = (bf16[1040,128]{1,0:T(8,128)(2,1)S(1)}, bf16[1040,128]{1,0:T(8,128)(2,1)S(1)}, u32[]{:S(2)}, u32[]{:S(2)}) collective-permute-start(bf16[1040,128]{1,0:T(8,128)(2,1)S(1)} %get-tuple-element.62.refs_0_.q_ref), channel_id=1, source_target_pairs={{0,2},{2,3},{3,1},{1,0},{4,6},{6,7},{7,5},{5,4},{8,10},{10,11},{11... | collective-permute-start | bytes 798728 | tf_op jit(solution)/shard_map/ppermute | solution.py:25
  8.7 1.5 %collective-permute-start.2 = (bf16[1024,128]{1,0:T(8,128)(2,1)S(1)}, bf16[1024,128]{1,0:T(8,128)(2,1)S(1)}, u32[]{:S(2)}, u32[]{:S(2)}) collective-permute-start(bf16[1024,128]{1,0:T(8,128)(2,1)S(1)} %get-tuple-element.66), channel_id=1, source_target_pairs={{0,8},{4,12},{8,0},{12,4},{16,24},{20,28},{24,16},{28,20},{1,9},{5... | collective-permute-start | bytes 786440 | tf_op jit(solution)/shard_map/ppermute | solution.py:19
  10.2 1.5 %collective-permute-start.3 = (bf16[1024,128]{1,0:T(8,128)(2,1)S(1)}, bf16[1024,128]{1,0:T(8,128)(2,1)S(1)}, u32[]{:S(2)}, u32[]{:S(2)}) collective-permute-start(bf16[1024,128]{1,0:T(8,128)(2,1)S(1)} %get-tuple-element.67), channel_id=1, source_target_pairs={{0,16},{4,20},{8,24},{12,28},{16,0},{20,4},{24,8},{28,12},{1,17},{... | collective-permute-start | bytes 786440 | tf_op jit(solution)/shard_map/ppermute | solution.py:19
  11.7 2.6 %collective-permute-done.refs_1_ = bf16[1040,128]{1,0:T(8,128)(2,1)S(1)} collective-permute-done((bf16[1040,128]{1,0:T(8,128)(2,1)S(1)}, bf16[1040,128]{1,0:T(8,128)(2,1)S(1)}, u32[]{:S(2)}, u32[]{:S(2)}) %collective-permute-start) | collective-permute-done | bytes 266272 | tf_op jit(solution)/shard_map/ppermute | solution.py:25
  14.4 2.1 %forward_early_0.1 = (f32[64,1024]{1,0:T(8,128)S(1)}, bf16[1024,128]{1,0:T(8,128)(2,1)S(1)}, bf16[128,1024]{1,0:T(8,128)(2,1)S(1)}, bf16[64,1024]{1,0:T(8,128)(2...) custom-call(s32[11]{0:T(128)S(1)} %pad_add_fusion.meta_ref, ...), custom_call_target="tpu_custom_call" | custom-call | flops 2147483 | bytes 4194 | tf_op jit(solution)/shard_map/forward_early_0/pallas_call | solution.py:502
  19.2 1.5 %collective-permute-start.7 = (bf16[1024,128]{1,0:T(8,128)(2,1)S(1)}, bf16[1024,128]{1,0:T(8,128)(2,1)S(1)}, u32[]{:S(2)}, u32[]{:S(2)}) collective-permute-start(bf16[1024,128]{1,0:T(8,128)(2,1)S(1)} %get-tuple-element.77), channel_id=1, source_target_pairs={{0,24},{4,28},{8,16},{12,20},{16,8},{20,12},{24,0},{28,4},{1,25},{... | collective-permute-start | bytes 786440 | tf_op jit(solution)/shard_map/ppermute | solution.py:19
  20.7 2.3 %collective-permute-start.4 = (bf16[1040,128]{1,0:T(8,128)(2,1)S(1)}, bf16[1040,128]{1,0:T(8,128)(2,1)S(1)}, u32[]{:S(2)}, u32[]{:S(2)}) collective-permute-start(bf16[1040,128]{1,0:T(8,128)(2,1)S(1)} %collective-permute-done.refs_1_), channel_id=1, source_target_pairs={{0,2},{2,3},{3,1},{1,0},{4,6},{6,7},{7,5},{5,4},{8,10},{10,11},{11... | collective-permute-start | bytes 798728 | tf_op jit(solution)/shard_map/ppermute | solution.py:25
  22.9 4.0 %forward_early_1.1 = (f32[64,2048]{1,0:T(8,128)S(1)}, bf16[2048,128]{1,0:T(8,128)(2,1)S(1)}, bf16[128,2048]{1,0:T(8,128)(2,1)S(1)}, bf16[64,2048]{1,0:T(8,128)(2,1)S(1)}, bf16[1024,2048]{1,0:T(8,128)(2,1)S(1)}) custom-call(s32[11]{0:T(128)S(1)} %pad_add_fusion.meta_ref, bf16[1040,128]{1,0:T(8,128)(2,1)S(1)} %get-tuple-element.62.refs_0_.q_ref, ...), custom_call_target="tpu_custom_call" | custom-call | flops 2147483 | bytes 4194 | tf_op jit(solution)/shard_map/forward_early_1/pallas_call | solution.py:502
  28.7 3.2 %collective-permute-start.9 = (bf16[1040,128]{1,0:T(8,128)(2,1)S(1)}, bf16[1040,128]{1,0:T(8,128)(2,1)S(1)}, u32[]{:S(2)}, u32[]{:S(2)}) collective-permute-start(bf16[1040,128]{1,0:T(8,128)(2,1)S(1)} %collective-permute-done.4.refs_4_), channel_id=1, source_target_pairs={{0,2},{2,3},{3,1},{1,0},{4,6},{6,7},{7,5},{5,4},{8,10},{10,11},{11... | collective-permute-start | bytes 798728 | tf_op jit(solution)/shard_map/ppermute | solution.py:25
  31.9 5.7 %forward_middle.1 = (f32[64,4096]{1,0:T(8,128)S(1)}, bf16[4096,128]{1,0:T(8,128)(2,1)S(1)}, bf16[128,4096]{1,0:T(8,128)(2,1)S(1)}, bf16[64,4096]{1,0:T(8,128)(2,...) custom-call(s32[11]{0:T(128)S(1)} %pad_add_fusion.meta_ref, ...), custom_call_target="tpu_custom_call" | custom-call | flops 3221225472 | bytes 6291456 | tf_op jit(solution)/shard_map/forward_middle/pallas_call | solution.py:502
  37.7 5.3 %forward_last.1 = (f32[64,4096]{1,0:T(8,128)S(1)}, bf16[1024,4096]{1,0:T(8,128)(2,1)S(1)}, bf16[128,1024]{1,0:T(8,128)(2,1)S(1)}, f32[1,8,128]{2,1,0:T(8,128)S(1)}) custom-call(s32[11]{0:T(128)S(1)} %pad_add_fusion.meta_ref, bf16[1040,128]{1,0:T(8,128)(2,1)S(1)} %collective-permute-done.9.refs_0_, ...), custom_call_target="tpu_custom_call", output_to_operand_aliasing={{0}: (3, {})} | custom-call | flops 2147483648 | bytes 4194304 | tf_op jit(solution)/shard_map/forward_last/pallas_call | solution.py:502
  44.3 1.5 %collective-permute-start.11 = (f32[1,8,128]{2,1,0:T(8,128)S(1)}, f32[1,8,128]{2,1,0:T(8,128)S(1)}, u32[]{:S(2)}, u32[]{:S(2)}) collective-permute-start(f32[1,8,128]{2,1,0:T(8,128)S(1)} %get-tuple-element.90.refs_4_), channel_id=1, source_target_pairs={{0,2},{1,3},{2,0},{3,1},{4,6},{5,7},{6,4},{7,5},{8,10},{9,11},{10,... | collective-permute-start | bytes 12296 | tf_op jit(solution)/shard_map/ppermute | solution.py:19
  45.8 1.6 %collective-permute-start.10 = (f32[1,8,128]{2,1,0:T(8,128)S(1)}, f32[1,8,128]{2,1,0:T(8,128)S(1)}, u32[]{:S(2)}, u32[]{:S(2)}) collective-permute-start(f32[1,8,128]{2,1,0:T(8,128)S(1)} %get-tuple-element.90.refs_4_), channel_id=1, source_target_pairs={{0,1},{1,0},{2,3},{3,2},{4,5},{5,4},{6,7},{7,6},{8,9},{9,8},{10,11... | collective-permute-start | bytes 12296 | tf_op jit(solution)/shard_map/ppermute | solution.py:19
  49.4 3.4 %backward_1.1 = (bf16[1024,128]{1,0:T(8,128)(2,1)S(1)}, bf16[64,4096]{1,0:T(8,128)(2,1)S(1)}) custom-call(s32[11]{0:T(128)S(1)} %pad_add_fusion.meta_ref, bf16[1024,1024]{1,0:T(8,128)(2,1)S(1)} %get-tuple-element.84.refs_0_, bf16[1024,2048]{1,0:T(8,128)(2,1)S(1)} %get-tuple-element.85.refs_1_, bf16[1024,1024]{1,0:T(8,128)(2,1)S(1)} %get-tuple-element.86.refs_2_, ...), custom_call_target="tpu_custom_call" | custom-call | flops 2147483648 | bytes 4194304 | tf_op jit(solution)/shard_map/backward_1/pallas_call | solution.py:502
  52.9 1.5 %collective-permute-start.13 = (bf16[1024,128]{1,0:T(8,128)(2,1)S(1)}, bf16[1024,128]{1,0:T(8,128)(2,1)S(1)}, u32[]{:S(2)}, u32[]{:S(2)}) collective-permute-start(bf16[1024,128]{1,0:T(8,128)(2,1)S(1)} %get-tuple-element.101), channel_id=1, source_target_pairs={{0,2},{2,3},{3,1},{1,0},{4,6},{6,7},{7,5},{5,4},{8,10},{10,11},{11... | collective-permute-start | bytes 786440 | tf_op jit(solution)/shard_map/ppermute | solution.py:25
  54.4 6.0 %backward_2.1 = (f32[1024,128]{1,0:T(8,128)S(1)}, f32[128,4096]{1,0:T(8,128)S(1)}) custom-call(s32[11]{0:T(128)S(1)} %pad_add_fusion.meta_ref, bf16[1024,1024]{1,0:T(8,128)(2,1)S(1)} %get-tuple-element.84.refs_0_, bf16[1024,2048]{1,0:T(8,128)(2,1)S(1)} %get-tuple-element.85.refs_1_, bf16[1024,1024]{1,0:T(8,128)(2,1)S(1)} %get-tuple-element.86.refs_2_, ...), custom_call_target="tpu_custom_call" | custom-call | flops 4294967296 | bytes 8388608 | tf_op jit(solution)/shard_map/backward_2/pallas_call | solution.py:502
  60.4 1.9 %collective-permute-start.14 = (bf16[1024,128]{1,0:T(8,128)(2,1)S(1)}, bf16[1024,128]{1,0:T(8,128)(2,1)S(1)}, u32[]{:S(2)}, u32[]{:S(2)}) collective-permute-start(bf16[1024,128]{1,0:T(8,128)(2,1)S(1)} %add_2.1), channel_id=1, source_target_pairs={{0,2},{2,3},{3,1},{1,0},{4,6},{6,7},{7,5},{5,4},{8,10},{10,11},{11... | collective-permute-start | bytes 786440 | tf_op jit(solution)/shard_map/ppermute | solution.py:25
  62.3 7.5 %backward_3.1 = (f32[1024,128]{1,0:T(8,128)S(1)}, f32[128,4096]{1,0:T(8,128)S(1)}) custom-call(s32[11]{0:T(128)S(1)} %pad_add_fusion.meta_ref, bf16[1024,4096]{1,0:T(8,128)(2,1)S(1)} %get-tuple-element.94.refs_3_.refs_0_, bf16[1024,4096]{1,0:T(8,128)(2,1)S(1)} %get-tuple-element.95.refs_1_, ...), custom_call_target="tpu_custom_call", output_to_operand_aliasing={{1}: (7, {})} | custom-call | flops 6442450944 | bytes 12582912 | tf_op jit(solution)/shard_map/backward_3/pallas_call | solution.py:502
  69.9 2.5 %backward_0_first.1 = (bf16[4,512,128]{2,1,0:T(8,128)(2,1)S(1)}, bf16[1024,2048]{1,0:T(8,128)(2,1)S(1)}) custom-call(s32[11]{0:T(128)S(1)} %pad_add_fusion.meta_ref, bf16[1040,128]{1,0:T(8,128)(2,1)S(1)} %get-tuple-element.62.refs_0_.q_ref, bf16[128,1024]{1,0:T(8,128)(2,1)S(1)} %get-tuple-element.64.refs_1_, ...), custom_call_target="tpu_custom_call" | custom-call | flops 2147483648 | bytes 4194304 | tf_op jit(solution)/shard_map/backward_0_first/pallas_call | solution.py:502
  72.5 1.5 %collective-permute-start.16 = (bf16[1024,128]{1,0:T(8,128)(2,1)S(1)}, bf16[1024,128]{1,0:T(8,128)(2,1)S(1)}, u32[]{:S(2)}, u32[]{:S(2)}) collective-permute-start(bf16[1024,128]{1,0:T(8,128)(2,1)S(1)} %add_3.1), channel_id=1, source_target_pairs={{0,2},{2,3},{3,1},{1,0},{4,6},{6,7},{7,5},{5,4},{8,10},{10,11},{11... | collective-permute-start | bytes 786440 | tf_op jit(solution)/shard_map/ppermute | solution.py:25
  74.0 2.5 %backward_0_second.1 = (f32[512,128]{1,0:T(8,128)S(1)}, f32[512,128]{1,0:T(8,128)S(1)}, f32[512,128]{1,0:T(8,128)S(1)}, f32[512,128]{1,0:T(8,128)S(1)}, bf16[1024,2048]{1,0:T(8,128)(2,1)S(1)}) custom-call(s32[11]{0:T(128)S(1)} %pad_add_fusion.meta_ref, bf16[1040,128]{1,0:T(8,128)(2,1)S(1)} %get-tuple-element.62.refs_0_.q_ref, ...), custom_call_target="tpu_custom_call" | custom-call | flops 2147483648 | bytes 4194304 | tf_op jit(solution)/shard_map/backward_0_second/pallas_call | solution.py:502
  78.5 1.7 %collective-permute-start.19 = (bf16[512,128]{1,0:T(8,128)(2,1)S(1)}, bf16[512,128]{1,0:T(8,128)(2,1)S(1)}, u32[]{:S(2)}, u32[]{:S(2)}) collective-permute-start(bf16[512,128]{1,0:T(8,128)(2,1)S(1)} %get-tuple-element.119), channel_id=1, source_target_pairs={{0,24},{4,28},{8,16},{12,20},{16,8},{20,12},{24,0},{28,4},{1,25},{... | collective-permute-start | bytes 393224 | tf_op jit(solution)/shard_map/ppermute | solution.py:19
  80.2 4.1 %backward_0.1.u_ref = f32[1024,128]{1,0:T(8,128)S(1)} custom-call(s32[11]{0:T(128)S(1)} %pad_add_fusion.meta_ref, bf16[1024,2048]{1,0:T(8,128)(2,1)S(1)} %get-tuple-element.107.first_ref, bf16[1024,2048]{1,0:T(8,128)(2,1)S(1)} %get-tuple-element.108.second_ref, bf16[4096,128]{1,0:T(8,128)(2,1)S(1)} %get-tuple-element.113.refs_3_.refs_5_.refs_4_.keys_ref), custom_call_target="tpu_custom_call" | custom-call | flops 2147483648 | bytes 4194304 | tf_op jit(solution)/shard_map/backward_0/pallas_call | solution.py:502
  (33 shorter events, 12.9 us)
Async XLA Ops:
  4.6 9.7 %collective-permute-start = (bf16[1040,128]{1,0:T(8,128)(2,1)S(1)}, bf16[1040,128]{1,0:T(8,128)(2,1)S(1)}, u32[]{:S(2)}, u32[]{:S(2)}) collective-permute-start(bf16[1040,128]{1,0:T(8,128)(2,1)S(1)} %get-tuple-element.62.refs_0_.q_ref), channel_id=1, source_target_pairs={{0,2},{2,3},{3,1},{1,0},{4,6},{6,7},{7,5},{5,4},{8,10},{10,11},{11... | collective-permute-start | bytes 798728 | tf_op jit(solution)/shard_map/ppermute | solution.py:25
  8.7 3.0 %collective-permute-start.1 = (bf16[1024,128]{1,0:T(8,128)(2,1)S(1)}, bf16[1024,128]{1,0:T(8,128)(2,1)S(1)}, u32[]{:S(2)}, u32[]{:S(2)}) collective-permute-start(bf16[1024,128]{1,0:T(8,128)(2,1)S(1)} %get-tuple-element.63.refs_3_), channel_id=1, source_target_pairs={{0,4},{4,0},{8,12},{12,8},{16,20},{20,16},{24,28},{28,24},{1,5},{5... | collective-permute-start | bytes 786440 | tf_op jit(solution)/shard_map/ppermute | solution.py:19
  8.7 8.7 %collective-permute-start.2 = (bf16[1024,128]{1,0:T(8,128)(2,1)S(1)}, bf16[1024,128]{1,0:T(8,128)(2,1)S(1)}, u32[]{:S(2)}, u32[]{:S(2)}) collective-permute-start(bf16[1024,128]{1,0:T(8,128)(2,1)S(1)} %get-tuple-element.66), channel_id=1, source_target_pairs={{0,8},{4,12},{8,0},{12,4},{16,24},{20,28},{24,16},{28,20},{1,9},{5... | collective-permute-start | bytes 786440 | tf_op jit(solution)/shard_map/ppermute | solution.py:19
  10.2 8.4 %collective-permute-start.3 = (bf16[1024,128]{1,0:T(8,128)(2,1)S(1)}, bf16[1024,128]{1,0:T(8,128)(2,1)S(1)}, u32[]{:S(2)}, u32[]{:S(2)}) collective-permute-start(bf16[1024,128]{1,0:T(8,128)(2,1)S(1)} %get-tuple-element.67), channel_id=1, source_target_pairs={{0,16},{4,20},{8,24},{12,28},{16,0},{20,4},{24,8},{28,12},{1,17},{... | collective-permute-start | bytes 786440 | tf_op jit(solution)/shard_map/ppermute | solution.py:19
  18.7 4.3 %collective-permute-start.5 = (bf16[1024,128]{1,0:T(8,128)(2,1)S(1)}, bf16[1024,128]{1,0:T(8,128)(2,1)S(1)}, u32[]{:S(2)}, u32[]{:S(2)}) collective-permute-start(bf16[1024,128]{1,0:T(8,128)(2,1)S(1)} %collective-permute-done.2.refs_6_), channel_id=1, source_target_pairs={{0,4},{4,0},{8,12},{12,8},{16,20},{20,16},{24,28},{28,24},{1,5},{5... | collective-permute-start | bytes 786440 | tf_op jit(solution)/shard_map/ppermute | solution.py:19
  18.7 4.3 %collective-permute-start.6 = (bf16[1024,128]{1,0:T(8,128)(2,1)S(1)}, bf16[1024,128]{1,0:T(8,128)(2,1)S(1)}, u32[]{:S(2)}, u32[]{:S(2)}) collective-permute-start(bf16[1024,128]{1,0:T(8,128)(2,1)S(1)} %collective-permute-done.3.refs_7_), channel_id=1, source_target_pairs={{0,4},{4,0},{8,12},{12,8},{16,20},{20,16},{24,28},{28,24},{1,5},{5... | collective-permute-start | bytes 786440 | tf_op jit(solution)/shard_map/ppermute | solution.py:19
  19.2 9.1 %collective-permute-start.7 = (bf16[1024,128]{1,0:T(8,128)(2,1)S(1)}, bf16[1024,128]{1,0:T(8,128)(2,1)S(1)}, u32[]{:S(2)}, u32[]{:S(2)}) collective-permute-start(bf16[1024,128]{1,0:T(8,128)(2,1)S(1)} %get-tuple-element.77), channel_id=1, source_target_pairs={{0,24},{4,28},{8,16},{12,20},{16,8},{20,12},{24,0},{28,4},{1,25},{... | collective-permute-start | bytes 786440 | tf_op jit(solution)/shard_map/ppermute | solution.py:19
  20.7 8.0 %collective-permute-start.4 = (bf16[1040,128]{1,0:T(8,128)(2,1)S(1)}, bf16[1040,128]{1,0:T(8,128)(2,1)S(1)}, u32[]{:S(2)}, u32[]{:S(2)}) collective-permute-start(bf16[1040,128]{1,0:T(8,128)(2,1)S(1)} %collective-permute-done.refs_1_), channel_id=1, source_target_pairs={{0,2},{2,3},{3,1},{1,0},{4,6},{6,7},{7,5},{5,4},{8,10},{10,11},{11... | collective-permute-start | bytes 798728 | tf_op jit(solution)/shard_map/ppermute | solution.py:25
  28.3 3.6 %collective-permute-start.8 = (bf16[1024,128]{1,0:T(8,128)(2,1)S(1)}, bf16[1024,128]{1,0:T(8,128)(2,1)S(1)}, u32[]{:S(2)}, u32[]{:S(2)}) collective-permute-start(bf16[1024,128]{1,0:T(8,128)(2,1)S(1)} %collective-permute-done.7.refs_14_), channel_id=1, source_target_pairs={{0,4},{4,0},{8,12},{12,8},{16,20},{20,16},{24,28},{28,24},{1,5},{5... | collective-permute-start | bytes 786440 | tf_op jit(solution)/shard_map/ppermute | solution.py:19
  28.7 9.0 %collective-permute-start.9 = (bf16[1040,128]{1,0:T(8,128)(2,1)S(1)}, bf16[1040,128]{1,0:T(8,128)(2,1)S(1)}, u32[]{:S(2)}, u32[]{:S(2)}) collective-permute-start(bf16[1040,128]{1,0:T(8,128)(2,1)S(1)} %collective-permute-done.4.refs_4_), channel_id=1, source_target_pairs={{0,2},{2,3},{3,1},{1,0},{4,6},{6,7},{7,5},{5,4},{8,10},{10,11},{11... | collective-permute-start | bytes 798728 | tf_op jit(solution)/shard_map/ppermute | solution.py:25
  43.0 5.4 %collective-permute-start.12 = (f32[1,8,128]{2,1,0:T(8,128)S(1)}, f32[1,8,128]{2,1,0:T(8,128)S(1)}, u32[]{:S(2)}, u32[]{:S(2)}) collective-permute-start(f32[1,8,128]{2,1,0:T(8,128)S(1)} %get-tuple-element.90.refs_4_), channel_id=1, source_target_pairs={{0,3},{1,2},{2,1},{3,0},{4,7},{5,6},{6,5},{7,4},{8,11},{9,10},{10,... | collective-permute-start | bytes 12296 | tf_op jit(solution)/shard_map/ppermute | solution.py:19
  44.3 4.5 %collective-permute-start.11 = (f32[1,8,128]{2,1,0:T(8,128)S(1)}, f32[1,8,128]{2,1,0:T(8,128)S(1)}, u32[]{:S(2)}, u32[]{:S(2)}) collective-permute-start(f32[1,8,128]{2,1,0:T(8,128)S(1)} %get-tuple-element.90.refs_4_), channel_id=1, source_target_pairs={{0,2},{1,3},{2,0},{3,1},{4,6},{5,7},{6,4},{7,5},{8,10},{9,11},{10,... | collective-permute-start | bytes 12296 | tf_op jit(solution)/shard_map/ppermute | solution.py:19
  45.8 3.6 %collective-permute-start.10 = (f32[1,8,128]{2,1,0:T(8,128)S(1)}, f32[1,8,128]{2,1,0:T(8,128)S(1)}, u32[]{:S(2)}, u32[]{:S(2)}) collective-permute-start(f32[1,8,128]{2,1,0:T(8,128)S(1)} %get-tuple-element.90.refs_4_), channel_id=1, source_target_pairs={{0,1},{1,0},{2,3},{3,2},{4,5},{5,4},{6,7},{7,6},{8,9},{9,8},{10,11... | collective-permute-start | bytes 12296 | tf_op jit(solution)/shard_map/ppermute | solution.py:19
  52.9 7.5 %collective-permute-start.13 = (bf16[1024,128]{1,0:T(8,128)(2,1)S(1)}, bf16[1024,128]{1,0:T(8,128)(2,1)S(1)}, u32[]{:S(2)}, u32[]{:S(2)}) collective-permute-start(bf16[1024,128]{1,0:T(8,128)(2,1)S(1)} %get-tuple-element.101), channel_id=1, source_target_pairs={{0,2},{2,3},{3,1},{1,0},{4,6},{6,7},{7,5},{5,4},{8,10},{10,11},{11... | collective-permute-start | bytes 786440 | tf_op jit(solution)/shard_map/ppermute | solution.py:25
  60.4 9.4 %collective-permute-start.14 = (bf16[1024,128]{1,0:T(8,128)(2,1)S(1)}, bf16[1024,128]{1,0:T(8,128)(2,1)S(1)}, u32[]{:S(2)}, u32[]{:S(2)}) collective-permute-start(bf16[1024,128]{1,0:T(8,128)(2,1)S(1)} %add_2.1), channel_id=1, source_target_pairs={{0,2},{2,3},{3,1},{1,0},{4,6},{6,7},{7,5},{5,4},{8,10},{10,11},{11... | collective-permute-start | bytes 786440 | tf_op jit(solution)/shard_map/ppermute | solution.py:25
  72.4 4.1 %collective-permute-start.15 = (bf16[4,512,128]{2,1,0:T(8,128)(2,1)S(1)}, bf16[4,512,128]{2,1,0:T(8,128)(2,1)S(1)}, u32[]{:S(2)}, u32[]{:S(2)}) collective-permute-start(bf16[4,512,128]{2,1,0:T(8,128)(2,1)S(1)} %get-tuple-element.110), channel_id=1, source_target_pairs={{0,4},{4,0},{8,12},{12,8},{16,20},{20,16},{24,28},{28,24},{1,5},{5... | collective-permute-start | bytes 1572872 | tf_op jit(solution)/shard_map/ppermute | solution.py:19
  72.5 11.8 %collective-permute-start.16 = (bf16[1024,128]{1,0:T(8,128)(2,1)S(1)}, bf16[1024,128]{1,0:T(8,128)(2,1)S(1)}, u32[]{:S(2)}, u32[]{:S(2)}) collective-permute-start(bf16[1024,128]{1,0:T(8,128)(2,1)S(1)} %add_3.1), channel_id=1, source_target_pairs={{0,2},{2,3},{3,1},{1,0},{4,6},{6,7},{7,5},{5,4},{8,10},{10,11},{11... | collective-permute-start | bytes 786440 | tf_op jit(solution)/shard_map/ppermute | solution.py:25
  76.6 9.0 %collective-permute-start.17 = (bf16[512,128]{1,0:T(8,128)(2,1)S(1)}, bf16[512,128]{1,0:T(8,128)(2,1)S(1)}, u32[]{:S(2)}, u32[]{:S(2)}) collective-permute-start(bf16[512,128]{1,0:T(8,128)(2,1)S(1)} %get-tuple-element.117), channel_id=1, source_target_pairs={{0,8},{4,12},{8,0},{12,4},{16,24},{20,28},{24,16},{28,20},{1,9},{5... | collective-permute-start | bytes 393224 | tf_op jit(solution)/shard_map/ppermute | solution.py:19
  77.4 8.3 %collective-permute-start.18 = (bf16[512,128]{1,0:T(8,128)(2,1)S(1)}, bf16[512,128]{1,0:T(8,128)(2,1)S(1)}, u32[]{:S(2)}, u32[]{:S(2)}) collective-permute-start(bf16[512,128]{1,0:T(8,128)(2,1)S(1)} %get-tuple-element.118), channel_id=1, source_target_pairs={{0,16},{4,20},{8,24},{12,28},{16,0},{20,4},{24,8},{28,12},{1,17},{... | collective-permute-start | bytes 393224 | tf_op jit(solution)/shard_map/ppermute | solution.py:19
  78.5 7.2 %collective-permute-start.19 = (bf16[512,128]{1,0:T(8,128)(2,1)S(1)}, bf16[512,128]{1,0:T(8,128)(2,1)S(1)}, u32[]{:S(2)}, u32[]{:S(2)}) collective-permute-start(bf16[512,128]{1,0:T(8,128)(2,1)S(1)} %get-tuple-element.119), channel_id=1, source_target_pairs={{0,24},{4,28},{8,16},{12,20},{16,8},{20,12},{24,0},{28,4},{1,25},{... | collective-permute-start | bytes 393224 | tf_op jit(solution)/shard_map/ppermute | solution.py:19

commit v7 on v6

--- a/solution.py
+++ b/solution.py
@@ -19,10 +19,10 @@
     return lax.ppermute(value, axis, [(i, i ^ distance) for i in range(size)])
 
 
-def ring_next(value, axis):
+def ring_next(value, axis, hop=1):
     size = lax.axis_size(axis)
     ring = list(range(0, size, 2)) + list(range(1, size, 2))[::-1]
-    return lax.ppermute(value, axis, [(ring[i], ring[(i + 1) % size]) for i in range(size)])
+    return lax.ppermute(value, axis, [(ring[i], ring[(i + hop) % size]) for i in range(size)])
 
 
 def in_pairs(count, first, step):
@@ -82,7 +82,7 @@
     order, nh, rows_here, hh, depth, kc, chunk, scale = cfg
     rows = rows_here * hh
     side = min(256, count)
-    tile = min(4 * side, count)
+    tile = next(size for size in (4 * side, 2 * side, side) if count % size == 0)
 
     def step(s, _):
         for first in range(0, tile, side):
@@ -113,23 +113,33 @@
     lax.fori_loop(0, count // tile, step, 0)
 
 
-def forward_early_kernel(cfg, pieces, is_first, meta_ref, *refs):
+def forward_early_kernel(cfg, done, pieces, meta_ref, *refs):
     chunk = cfg[6]
     refs = list(refs)
     take = lambda count: [refs.pop(0) for _ in range(count)]
-    q_refs = take(2)
-    wide_refs = None if is_first else take(2)
+    q_refs = take(2 if done else 1)
+    start, count = len(done) * chunk, len(pieces) * chunk
+    if done:
+        (own_wide_ref,) = take(1)
+        part = take(4)
     message_refs = take(len(pieces))
-    score_ref, keys_ref, keys_t_ref, logits_ref, active_ref = take(5)
-    if is_first:
-        qw_refs, wide_refs = take(2), take(2)
-        for j in range(2):
-            spread_weights(cfg, q_refs[j], wide_refs[j], qw_refs[j])
-    for at, k in enumerate(pieces):
-        unpack(cfg, message_refs[at], k, at * chunk, keys_ref, keys_t_ref, logits_ref)
-    count = len(pieces) * chunk
-    add_scores(cfg, q_refs[0], wide_refs[0], keys_t_ref, score_ref, None, 0, count, None)
-    add_scores(cfg, q_refs[1], wide_refs[1], keys_t_ref, score_ref, score_ref, 0, count, active_ref)
+    score_ref, keys_ref, keys_t_ref, logits_ref = take(4)
+    active_ref = take(1)[0] if done else None
+    qw_ref, wide_ref = take(2)
+    spread_weights(cfg, q_refs[-1], wide_ref, qw_ref)
+    if done:
+        score_ref[:, :start] = part[0][...]
+        keys_ref[:start, :] = part[1][...]
+        keys_t_ref[:, :start] = part[2][...]
+        logits_ref[:, :start] = part[3][...]
+    else:
+        own_wide_ref = wide_ref
+    for i, k in enumerate(pieces):
+        unpack(cfg, message_refs[i], k, start + i * chunk, keys_ref, keys_t_ref, logits_ref)
+    add_scores(cfg, q_refs[0], own_wide_ref, keys_t_ref, score_ref, None, start, count, None)
+    if done:
+        count = start + count
+        add_scores(cfg, q_refs[1], wide_ref, keys_t_ref, score_ref, score_ref, 0, count, active_ref)
 
 
 def forward_middle_kernel(cfg, groups, meta_ref, *refs):
@@ -233,7 +243,7 @@
     makes_u = any(item[1] for item in items)
     ranges = [item[2] for item in items if item[2] is not None]
     half = ranges[0] if ranges and ranges[0] != "all" else None
-    sources = [take(3 if item[0] == 1 else 1) for item in items]
+    sources = [take(2 if item[0] == 1 else 1) for item in items]
     qw_refs = [take(1)[0] if item[2] is not None else None for item in items]
     (keys_ref,) = take(1)
     if is_first:
@@ -484,16 +494,20 @@
         ),
         name="prepare",
     )(meta, far(query), far(weights.T), far(row_weight[None, :]), far(keys), far(main_logits))
-    q_blocks = [message, ring_next(message, "head")]
+    q_blocks = [message] * nh
+    for hop in range(1, nh // 2 + 1):
+        q_blocks[hop] = ring_next(q_blocks[hop - 1], "head")
+        if nh - hop > hop:
+            q_blocks[nh - hop] = ring_next(q_blocks[(nh - hop + 1) % nh], "head", -1)
+    arrival = [1]
+    for hop in range(1, nh // 2 + 1):
+        arrival += [j for j in sorted({hop, nh - hop}) if j not in arrival]
 
     k_pieces = [None] * n
     k_pieces[0::2] = [key_messages[0]] + [
         swap(key_messages[k // 2], "ctx", k) for k in range(2, n, 2)
     ]
     k_pieces[1] = swap(k_pieces[0], "ctx", 1)
-    for j in range(2, nh):
-        q_blocks.append(ring_next(q_blocks[-1], "head"))
-
     total_keys = n * chunk
     macs = rows * total_keys * depth
     tile = chunk
@@ -529,36 +543,34 @@
         ]
 
     nears = lambda xs: [near(x) for x in xs]
-    early, early_active, qw, wides = [], [], [], []
+    early, qw, wides = [], [], []
     for i, group in enumerate(groups[:2]):
-        count = len(group) * chunk
         if i == 1:
             far_even = range(2, n - 2, 2)
             wides[0], *came = lax.optimization_barrier((wides[0], *(k_pieces[k] for k in far_even)))
             for k, piece in zip(far_even, came):
                 k_pieces[k], k_pieces[k + 1] = piece, swap(piece, "ctx", 1)
+        count = (len(group) + i * len(groups[0])) * chunk
         outs = call(
-            functools.partial(forward_early_kernel, cfg, group, i == 0),
-            q_blocks[:2] + nears(wides) + [k_pieces[k] for k in group],
-            keys_shapes(count)
-            + [pltpu.VMEM((rows, count), bf16)]
-            + ([qw_shape] * 2 + [wide_shape] * 2 if i == 0 else []),
+            functools.partial(forward_early_kernel, cfg, groups[0] if i == 1 else [], group),
+            q_blocks[: i + 1] + nears(wides) + nears(early) + [k_pieces[k] for k in group],
+            keys_shapes(count) + [pltpu.VMEM((rows, count), bf16)] * i + [qw_shape, wide_shape],
             [],
             0.001,
             f"forward_early_{i}",
         )
-        early += outs[:4]
-        early_active += [outs[4]]
-        if i == 0:
-            qw, wides = list(outs[5:7]), list(outs[7:9])
-    early[4], came = lax.optimization_barrier((early[4], k_pieces[n - 2]))
+        early = list(outs[:4])
+        qw.append(outs[-2])
+        wides.append(outs[-1])
+    early_active = outs[4]
+    early[0], came = lax.optimization_barrier((early[0], k_pieces[n - 2]))
     k_pieces[n - 2], k_pieces[n - 1] = came, swap(came, "ctx", 1)
     last = len(groups[2]) * chunk
     outs = call(
-        functools.partial(forward_middle_kernel, cfg, groups),
+        functools.partial(forward_middle_kernel, cfg, [groups[0] + groups[1], groups[2]]),
         q_blocks[:2]
         + nears(wides)
-        + q_blocks[2 : nh - 1]
+        + [q_blocks[j] for j in arrival[1:-1]]
         + nears(early)
         + [k_pieces[k] for k in groups[2]],
         keys_shapes(total_keys)
@@ -570,12 +582,13 @@
         "forward_middle",
     )
     score, keys_all, keys_t, logits = outs[:4]
-    active = [None, early_active + [outs[4]]]
-    active += [[value] for value in outs[5 : 5 + nh - 3]]
-    qw += list(outs[5 + nh - 3 :])
+    active = {1: [early_active, outs[4]]}
+    qw = dict(enumerate(qw))
+    for i, j in enumerate(arrival[1:-1]):
+        active[j], qw[j] = [outs[5 + i]], outs[5 + nh - 3 + i]
     score, last_active, last_qw, stats = call(
         functools.partial(forward_last_kernel, cfg),
-        [q_blocks[nh - 1], near(keys_t), near(score), near(logits)],
+        [q_blocks[arrival[-1]], near(keys_t), near(score), near(logits)],
         [
             pltpu.VMEM((rows_here, total_keys), f32),
             pltpu.VMEM((rows, total_keys), bf16),
@@ -587,8 +600,7 @@
         "forward_last",
         {3: 0},
     )
-    active.append([last_active])
-    qw.append(last_qw)
+    active[arrival[-1]], qw[arrival[-1]] = [last_active], last_qw
 
     all_stats = [stats] + [swap(stats, "head", j) for j in range(1, nh)]
 

time: 86.6 us -> 85.5 us (0.987)
  starting transfers between devices: 27.5 us -> 25.1 us
  Pallas kernels: 47.3 us -> 48.6 us
    ppermute x6, starting transfers between devices: 14.5 us -> 10.5 us  [ring_next(): lax.ppermute(value, axis, [(ring[i], ring[(i + hop) % size]) for i in ran...]
    ppermute x14, waiting for transfers between devices: 5.57 us -> 8.02 us  [swap(): return lax.ppermute(value, axis, [(i, i ^ distance) for i in range(size)])]
    ppermute x6, waiting for transfers between devices: 3.04 us -> 0.6 us  [ring_next(): lax.ppermute(value, axis, [(ring[i], ring[(i + hop) % size]) for i in ran...]
    ppermute x14, starting transfers between devices: 13 us -> 14.6 us  [swap(): return lax.ppermute(value, axis, [(i, i ^ distance) for i in range(size)])]
    pallas_call x10, Pallas kernels: 43.2 us -> 44.5 us  [call(): pl.pallas_call(kernel, out_shape=out_shape, input_output_aliases=aliases,...]
  transfers between devices with their start and end apart: 20 -> 20, of which waited for: 8 -> 7; matrix products, arithmetic and copies ran while one was open for 0% -> 0% of each run, Pallas kernels for 39% -> 40%
where the time goes in v7:
time: 85.5 us; the launch traced here: 85.3 us
  Pallas kernels  48.6 us (57%)
  starting transfers between devices  25.1 us (29%)
  waiting for transfers between devices  8.62 us (10%)
  other arithmetic  1.61 us (2%)
  between operations  1.43 us (2%)
    pallas_call x10, Pallas kernels, call(): pl.pallas_call(kernel, out_shape=out_shape, input_output_aliases=aliases,...  44.5 us
    ppermute x14, starting transfers between devices, swap(): return lax.ppermute(value, axis, [(i, i ^ distance) for i in range(size)])  14.6 us
    ppermute x6, starting transfers between devices, ring_next(): lax.ppermute(value, axis, [(ring[i], ring[(i + hop) % size]) for i in ran...  10.5 us
    ppermute x14, waiting for transfers between devices, swap(): return lax.ppermute(value, axis, [(i, i ^ distance) for i in range(size)])  8.02 us
    pallas_call x1, Pallas kernels, per_device(): pl.pallas_call(functools.partial(prepare_kernel, cfg), out_shape=[jax.Sha...  2.61 us
  transfers between devices with their start and end apart: 20, of which 7 were waited for; matrix products, arithmetic and copies ran while one was open for 0% of the time, Pallas kernels for 40%

profile of v7, /device:TPU:0, one launch (start us, length us, event | category | flops | bytes accessed | tf_op | source)
XLA Modules:
  0.0 85.3 jit_solution(13176611810338143752)
XLA Ops:
  2.0 2.6 %prepare.1 = (bf16[1040,128]{1,0:T(8,128)(2,1)S(1)}, f32[1,128]{1,0:T(1,128)S(1)}, bf16[1024,128]{1,0:T(8,128)(2,1)S(1)}, bf16[1024,128]{1,0:T(8,128)(2,1)S(1)},...) custom-call(s32[11]{0:T(128)S(1)} %pad_add_fusion.meta_ref, bf16[64,16,128]{2,1,0:T(8,128)(2,1)} %query_ref.1, ...), custom_call_target="tpu_custom_call" | custom-call | flops 131072 | bytes 4194304 | tf_op jit(solution)/shard_map/prepare/pallas_call | solution.py:478
  5.2 2.6 %collective-permute-start.2 = (bf16[1024,128]{1,0:T(8,128)(2,1)S(1)}, bf16[1024,128]{1,0:T(8,128)(2,1)S(1)}, u32[]{:S(2)}, u32[]{:S(2)}) collective-permute-start(bf16[1024,128]{1,0:T(8,128)(2,1)S(1)} %get-tuple-element.65), channel_id=1, source_target_pairs={{0,8},{4,12},{8,0},{12,4},{16,24},{20,28},{24,16},{28,20},{1,9},{5... | collective-permute-start | bytes 786440 | tf_op jit(solution)/shard_map/ppermute | solution.py:19
  7.7 1.5 %collective-permute-start.3 = (bf16[1024,128]{1,0:T(8,128)(2,1)S(1)}, bf16[1024,128]{1,0:T(8,128)(2,1)S(1)}, u32[]{:S(2)}, u32[]{:S(2)}) collective-permute-start(bf16[1024,128]{1,0:T(8,128)(2,1)S(1)} %get-tuple-element.66), channel_id=1, source_target_pairs={{0,16},{4,20},{8,24},{12,28},{16,0},{20,4},{24,8},{28,12},{1,17},{... | collective-permute-start | bytes 786440 | tf_op jit(solution)/shard_map/ppermute | solution.py:19
  9.2 2.6 %collective-permute-start.1 = (bf16[1040,128]{1,0:T(8,128)(2,1)S(1)}, bf16[1040,128]{1,0:T(8,128)(2,1)S(1)}, u32[]{:S(2)}, u32[]{:S(2)}) collective-permute-start(bf16[1040,128]{1,0:T(8,128)(2,1)S(1)} %get-tuple-element.61.refs_0_.q_ref), channel_id=1, source_target_pairs={{0,2},{2,3},{3,1},{1,0},{4,6},{6,7},{7,5},{5,4},{8,10},{10,11},{11... | collective-permute-start | bytes 798728 | tf_op jit(solution)/shard_map/ppermute | solution.py:25
  11.8 1.4 %forward_early_0.1 = (f32[64,1024]{1,0:T(8,128)S(1)}, bf16[1024,128]{1,0:T(8,128)(2,1)S(1)}, bf16[128,1024]{1,0:T(8,128)(2,1)S(1)}, bf16[64,1024]{1,0:T(8,128)(2...) custom-call(s32[11]{0:T(128)S(1)} %pad_add_fusion.meta_ref, ...), custom_call_target="tpu_custom_call" | custom-call | flops 2147483 | bytes 4194 | tf_op jit(solution)/shard_map/forward_early_0/pallas_call | solution.py:516
  13.2 1.4 %collective-permute-done.2.refs_9_ = bf16[1024,128]{1,0:T(8,128)(2,1)S(1)} collective-permute-done((bf16[1024,128]{1,0:T(8,128)(2,1)S(1)}, bf16[1024,128]{1,0:T(8,128)(2,1)S(1)}, u32[]{:S(2)}, u32[]{:S(2)}) %collective-permute-start.2) | collective-permute-done | bytes 262176 | tf_op jit(solution)/shard_map/ppermute | solution.py:19
  14.6 1.5 %collective-permute-done.3.refs_10_ = bf16[1024,128]{1,0:T(8,128)(2,1)S(1)} collective-permute-done((bf16[1024,128]{1,0:T(8,128)(2,1)S(1)}, bf16[1024,128]{1,0:T(8,128)(2,1)S(1)}, u32[]{:S(2)}, u32[]{:S(2)}) %collective-permute-start.3) | collective-permute-done | bytes 262176 | tf_op jit(solution)/shard_map/ppermute | solution.py:19
  16.6 1.5 %collective-permute-start.7 = (bf16[1024,128]{1,0:T(8,128)(2,1)S(1)}, bf16[1024,128]{1,0:T(8,128)(2,1)S(1)}, u32[]{:S(2)}, u32[]{:S(2)}) collective-permute-start(bf16[1024,128]{1,0:T(8,128)(2,1)S(1)} %get-tuple-element.76), channel_id=1, source_target_pairs={{0,24},{4,28},{8,16},{12,20},{16,8},{20,12},{24,0},{28,4},{1,25},{... | collective-permute-start | bytes 786440 | tf_op jit(solution)/shard_map/ppermute | solution.py:19
  18.1 1.6 %collective-permute-start.6 = (bf16[1040,128]{1,0:T(8,128)(2,1)S(1)}, bf16[1040,128]{1,0:T(8,128)(2,1)S(1)}, u32[]{:S(2)}, u32[]{:S(2)}) collective-permute-start(bf16[1040,128]{1,0:T(8,128)(2,1)S(1)} %get-tuple-element.61.refs_0_.q_ref), channel_id=1, source_target_pairs={{0,1},{2,0},{3,2},{1,3},{4,5},{6,4},{7,6},{5,7},{8,9},{10,8},{11,1... | collective-permute-start | bytes 798728 | tf_op jit(solution)/shard_map/ppermute | solution.py:25
  19.7 5.1 %forward_early_1.1 = (f32[64,3072]{1,0:T(8,128)S(1)}, bf16[3072,128]{1,0:T(8,128)(2,1)S(1)}, bf16[128,3072]{1,0:T(8,128)(2,1)S(1)}, bf16[64,3072]{1,0:T(8,128)(2...) custom-call(s32[11]{0:T(128)S(1)} %pad_add_fusion.meta_ref, ...), custom_call_target="tpu_custom_call" | custom-call | flops 2147483 | bytes 4194 | tf_op jit(solution)/shard_map/forward_early_1/pallas_call | solution.py:516
  25.7 2.6 %collective-permute-start.9 = (bf16[1040,128]{1,0:T(8,128)(2,1)S(1)}, bf16[1040,128]{1,0:T(8,128)(2,1)S(1)}, u32[]{:S(2)}, u32[]{:S(2)}) collective-permute-start(bf16[1040,128]{1,0:T(8,128)(2,1)S(1)} %collective-permute-done.1.refs_1_), channel_id=1, source_target_pairs={{0,2},{2,3},{3,1},{1,0},{4,6},{6,7},{7,5},{5,4},{8,10},{10,11},{11... | collective-permute-start | bytes 798728 | tf_op jit(solution)/shard_map/ppermute | solution.py:25
  28.3 5.7 %forward_middle.1 = (f32[64,4096]{1,0:T(8,128)S(1)}, bf16[4096,128]{1,0:T(8,128)(2,1)S(1)}, bf16[128,4096]{1,0:T(8,128)(2,1)S(1)}, bf16[64,4096]{1,0:T(8,128)(2,...) custom-call(s32[11]{0:T(128)S(1)} %pad_add_fusion.meta_ref, ...), custom_call_target="tpu_custom_call" | custom-call | flops 3221225472 | bytes 6291456 | tf_op jit(solution)/shard_map/forward_middle/pallas_call | solution.py:516
  34.6 5.3 %forward_last.1 = (f32[64,4096]{1,0:T(8,128)S(1)}, bf16[1024,4096]{1,0:T(8,128)(2,1)S(1)}, bf16[128,1024]{1,0:T(8,128)(2,1)S(1)}, f32[1,8,128]{2,1,0:T(8,128)S(1)}) custom-call(s32[11]{0:T(128)S(1)} %pad_add_fusion.meta_ref, bf16[1040,128]{1,0:T(8,128)(2,1)S(1)} %collective-permute-done.9.refs_0_, ...), custom_call_target="tpu_custom_call", output_to_operand_aliasing={{0}: (3, {})} | custom-call | flops 2147483648 | bytes 4194304 | tf_op jit(solution)/shard_map/forward_last/pallas_call | solution.py:516
  40.0 3.5 %collective-permute-start.12 = (f32[1,8,128]{2,1,0:T(8,128)S(1)}, f32[1,8,128]{2,1,0:T(8,128)S(1)}, u32[]{:S(2)}, u32[]{:S(2)}) collective-permute-start(f32[1,8,128]{2,1,0:T(8,128)S(1)} %get-tuple-element.88.refs_3_), channel_id=1, source_target_pairs={{0,3},{1,2},{2,1},{3,0},{4,7},{5,6},{6,5},{7,4},{8,11},{9,10},{10,... | collective-permute-start | bytes 12296 | tf_op jit(solution)/shard_map/ppermute | solution.py:19
  45.4 2.6 %collective-permute-done.11.refs_5_ = f32[1,8,128]{2,1,0:T(8,128)S(1)} collective-permute-done((f32[1,8,128]{2,1,0:T(8,128)S(1)}, f32[1,8,128]{2,1,0:T(8,128)S(1)}, u32[]{:S(2)}, u32[]{:S(2)}) %collective-permute-start.11) | collective-permute-done | bytes 4128 | tf_op jit(solution)/shard_map/ppermute | solution.py:19
  48.0 4.3 %backward_1.1 = (bf16[1024,128]{1,0:T(8,128)(2,1)S(1)}, bf16[64,4096]{1,0:T(8,128)(2,1)S(1)}) custom-call(s32[11]{0:T(128)S(1)} %pad_add_fusion.meta_ref, bf16[1024,3072]{1,0:T(8,128)(2,1)S(1)} %get-tuple-element.83.refs_0_, bf16[1024,1024]{1,0:T(8,128)(2,1)S(1)} %get-tuple-element.84.refs_1_, ...), custom_call_target="tpu_custom_call" | custom-call | flops 2147483648 | bytes 4194304 | tf_op jit(solution)/shard_map/backward_1/pallas_call | solution.py:516
  52.3 2.3 %collective-permute-start.13 = (bf16[1024,128]{1,0:T(8,128)(2,1)S(1)}, bf16[1024,128]{1,0:T(8,128)(2,1)S(1)}, u32[]{:S(2)}, u32[]{:S(2)}) collective-permute-start(bf16[1024,128]{1,0:T(8,128)(2,1)S(1)} %get-tuple-element.99), channel_id=1, source_target_pairs={{0,2},{2,3},{3,1},{1,0},{4,6},{6,7},{7,5},{5,4},{8,10},{10,11},{11... | collective-permute-start | bytes 786440 | tf_op jit(solution)/shard_map/ppermute | solution.py:25
  54.6 6.0 %backward_2.1 = (f32[1024,128]{1,0:T(8,128)S(1)}, f32[128,4096]{1,0:T(8,128)S(1)}) custom-call(s32[11]{0:T(128)S(1)} %pad_add_fusion.meta_ref, bf16[1024,3072]{1,0:T(8,128)(2,1)S(1)} %get-tuple-element.83.refs_0_, bf16[1024,1024]{1,0:T(8,128)(2,1)S(1)} %get-tuple-element.84.refs_1_, bf16[1024,4096]{1,0:T(8,128)(2,1)S(1)} %get-tuple-element.92.refs_2_.refs_0_, ...), custom_call_target="tpu_custom_call" | custom-call | flops 4294967296 | bytes 8388608 | tf_op jit(solution)/shard_map/backward_2/pallas_call | solution.py:516
  60.7 1.4 %collective-permute-start.14 = (bf16[1024,128]{1,0:T(8,128)(2,1)S(1)}, bf16[1024,128]{1,0:T(8,128)(2,1)S(1)}, u32[]{:S(2)}, u32[]{:S(2)}) collective-permute-start(bf16[1024,128]{1,0:T(8,128)(2,1)S(1)} %add_2.1), channel_id=1, source_target_pairs={{0,2},{2,3},{3,1},{1,0},{4,6},{6,7},{7,5},{5,4},{8,10},{10,11},{11... | collective-permute-start | bytes 786440 | tf_op jit(solution)/shard_map/ppermute | solution.py:25
  62.1 7.4 %backward_3.1 = (f32[1024,128]{1,0:T(8,128)S(1)}, f32[128,4096]{1,0:T(8,128)S(1)}) custom-call(s32[11]{0:T(128)S(1)} %pad_add_fusion.meta_ref, bf16[1024,4096]{1,0:T(8,128)(2,1)S(1)} %get-tuple-element.92.refs_2_.refs_0_, bf16[1024,4096]{1,0:T(8,128)(2,1)S(1)} %get-tuple-element.93.refs_1_, ...), custom_call_target="tpu_custom_call", output_to_operand_aliasing={{1}: (7, {})} | custom-call | flops 6442450944 | bytes 12582912 | tf_op jit(solution)/shard_map/backward_3/pallas_call | solution.py:516
  69.6 2.5 %backward_0_first.1 = (bf16[4,512,128]{2,1,0:T(8,128)(2,1)S(1)}, bf16[1024,2048]{1,0:T(8,128)(2,1)S(1)}) custom-call(s32[11]{0:T(128)S(1)} %pad_add_fusion.meta_ref, bf16[1040,128]{1,0:T(8,128)(2,1)S(1)} %get-tuple-element.61.refs_0_.q_ref, bf16[128,1024]{1,0:T(8,128)(2,1)S(1)} %get-tuple-element.63.refs_1_, ...), custom_call_target="tpu_custom_call" | custom-call | flops 2147483648 | bytes 4194304 | tf_op jit(solution)/shard_map/backward_0_first/pallas_call | solution.py:516
  72.2 2.5 %backward_0_second.1 = (f32[512,128]{1,0:T(8,128)S(1)}, f32[512,128]{1,0:T(8,128)S(1)}, f32[512,128]{1,0:T(8,128)S(1)}, f32[512,128]{1,0:T(8,128)S(1)}, bf16[1024,2048]{1,0:T(8,128)(2,1)S(1)}) custom-call(s32[11]{0:T(128)S(1)} %pad_add_fusion.meta_ref, bf16[1040,128]{1,0:T(8,128)(2,1)S(1)} %get-tuple-element.61.refs_0_.q_ref, ...), custom_call_target="tpu_custom_call" | custom-call | flops 2147483648 | bytes 4194304 | tf_op jit(solution)/shard_map/backward_0_second/pallas_call | solution.py:516
  77.0 1.4 %collective-permute-start.19 = (bf16[512,128]{1,0:T(8,128)(2,1)S(1)}, bf16[512,128]{1,0:T(8,128)(2,1)S(1)}, u32[]{:S(2)}, u32[]{:S(2)}) collective-permute-start(bf16[512,128]{1,0:T(8,128)(2,1)S(1)} %get-tuple-element.117), channel_id=1, source_target_pairs={{0,24},{4,28},{8,16},{12,20},{16,8},{20,12},{24,0},{28,4},{1,25},{... | collective-permute-start | bytes 393224 | tf_op jit(solution)/shard_map/ppermute | solution.py:19
  78.4 4.1 %backward_0.1.u_ref = f32[1024,128]{1,0:T(8,128)S(1)} custom-call(s32[11]{0:T(128)S(1)} %pad_add_fusion.meta_ref, bf16[1024,2048]{1,0:T(8,128)(2,1)S(1)} %get-tuple-element.105.first_ref, bf16[1024,2048]{1,0:T(8,128)(2,1)S(1)} %get-tuple-element.106.second_ref, bf16[4096,128]{1,0:T(8,128)(2,1)S(1)} %get-tuple-element.111.refs_2_.refs_4_.keys_ref), custom_call_target="tpu_custom_call" | custom-call | flops 2147483648 | bytes 4194304 | tf_op jit(solution)/shard_map/backward_0/pallas_call | solution.py:516
  (33 shorter events, 10.4 us)
Async XLA Ops:
  4.6 7.2 %collective-permute-start = (bf16[1024,128]{1,0:T(8,128)(2,1)S(1)}, bf16[1024,128]{1,0:T(8,128)(2,1)S(1)}, u32[]{:S(2)}, u32[]{:S(2)}) collective-permute-start(bf16[1024,128]{1,0:T(8,128)(2,1)S(1)} %get-tuple-element.62.refs_2_), channel_id=1, source_target_pairs={{0,4},{4,0},{8,12},{12,8},{16,20},{20,16},{24,28},{28,24},{1,5},{5... | collective-permute-start | bytes 786440 | tf_op jit(solution)/shard_map/ppermute | solution.py:19
  5.2 9.5 %collective-permute-start.2 = (bf16[1024,128]{1,0:T(8,128)(2,1)S(1)}, bf16[1024,128]{1,0:T(8,128)(2,1)S(1)}, u32[]{:S(2)}, u32[]{:S(2)}) collective-permute-start(bf16[1024,128]{1,0:T(8,128)(2,1)S(1)} %get-tuple-element.65), channel_id=1, source_target_pairs={{0,8},{4,12},{8,0},{12,4},{16,24},{20,28},{24,16},{28,20},{1,9},{5... | collective-permute-start | bytes 786440 | tf_op jit(solution)/shard_map/ppermute | solution.py:19
  7.7 8.4 %collective-permute-start.3 = (bf16[1024,128]{1,0:T(8,128)(2,1)S(1)}, bf16[1024,128]{1,0:T(8,128)(2,1)S(1)}, u32[]{:S(2)}, u32[]{:S(2)}) collective-permute-start(bf16[1024,128]{1,0:T(8,128)(2,1)S(1)} %get-tuple-element.66), channel_id=1, source_target_pairs={{0,16},{4,20},{8,24},{12,28},{16,0},{20,4},{24,8},{28,12},{1,17},{... | collective-permute-start | bytes 786440 | tf_op jit(solution)/shard_map/ppermute | solution.py:19
  9.2 10.4 %collective-permute-start.1 = (bf16[1040,128]{1,0:T(8,128)(2,1)S(1)}, bf16[1040,128]{1,0:T(8,128)(2,1)S(1)}, u32[]{:S(2)}, u32[]{:S(2)}) collective-permute-start(bf16[1040,128]{1,0:T(8,128)(2,1)S(1)} %get-tuple-element.61.refs_0_.q_ref), channel_id=1, source_target_pairs={{0,2},{2,3},{3,1},{1,0},{4,6},{6,7},{7,5},{5,4},{8,10},{10,11},{11... | collective-permute-start | bytes 798728 | tf_op jit(solution)/shard_map/ppermute | solution.py:25
  16.1 3.6 %collective-permute-start.4 = (bf16[1024,128]{1,0:T(8,128)(2,1)S(1)}, bf16[1024,128]{1,0:T(8,128)(2,1)S(1)}, u32[]{:S(2)}, u32[]{:S(2)}) collective-permute-start(bf16[1024,128]{1,0:T(8,128)(2,1)S(1)} %collective-permute-done.2.refs_9_), channel_id=1, source_target_pairs={{0,4},{4,0},{8,12},{12,8},{16,20},{20,16},{24,28},{28,24},{1,5},{5... | collective-permute-start | bytes 786440 | tf_op jit(solution)/shard_map/ppermute | solution.py:19
  16.1 3.6 %collective-permute-start.5 = (bf16[1024,128]{1,0:T(8,128)(2,1)S(1)}, bf16[1024,128]{1,0:T(8,128)(2,1)S(1)}, u32[]{:S(2)}, u32[]{:S(2)}) collective-permute-start(bf16[1024,128]{1,0:T(8,128)(2,1)S(1)} %collective-permute-done.3.refs_10_), channel_id=1, source_target_pairs={{0,4},{4,0},{8,12},{12,8},{16,20},{20,16},{24,28},{28,24},{1,5},{5... | collective-permute-start | bytes 786440 | tf_op jit(solution)/shard_map/ppermute | solution.py:19
  16.6 9.1 %collective-permute-start.7 = (bf16[1024,128]{1,0:T(8,128)(2,1)S(1)}, bf16[1024,128]{1,0:T(8,128)(2,1)S(1)}, u32[]{:S(2)}, u32[]{:S(2)}) collective-permute-start(bf16[1024,128]{1,0:T(8,128)(2,1)S(1)} %get-tuple-element.76), channel_id=1, source_target_pairs={{0,24},{4,28},{8,16},{12,20},{16,8},{20,12},{24,0},{28,4},{1,25},{... | collective-permute-start | bytes 786440 | tf_op jit(solution)/shard_map/ppermute | solution.py:19
  18.1 10.2 %collective-permute-start.6 = (bf16[1040,128]{1,0:T(8,128)(2,1)S(1)}, bf16[1040,128]{1,0:T(8,128)(2,1)S(1)}, u32[]{:S(2)}, u32[]{:S(2)}) collective-permute-start(bf16[1040,128]{1,0:T(8,128)(2,1)S(1)} %get-tuple-element.61.refs_0_.q_ref), channel_id=1, source_target_pairs={{0,1},{2,0},{3,2},{1,3},{4,5},{6,4},{7,6},{5,7},{8,9},{10,8},{11,1... | collective-permute-start | bytes 798728 | tf_op jit(solution)/shard_map/ppermute | solution.py:25
  25.7 2.6 %collective-permute-start.8 = (bf16[1024,128]{1,0:T(8,128)(2,1)S(1)}, bf16[1024,128]{1,0:T(8,128)(2,1)S(1)}, u32[]{:S(2)}, u32[]{:S(2)}) collective-permute-start(bf16[1024,128]{1,0:T(8,128)(2,1)S(1)} %collective-permute-done.7.refs_10_), channel_id=1, source_target_pairs={{0,4},{4,0},{8,12},{12,8},{16,20},{20,16},{24,28},{28,24},{1,5},{5... | collective-permute-start | bytes 786440 | tf_op jit(solution)/shard_map/ppermute | solution.py:19
  25.7 8.9 %collective-permute-start.9 = (bf16[1040,128]{1,0:T(8,128)(2,1)S(1)}, bf16[1040,128]{1,0:T(8,128)(2,1)S(1)}, u32[]{:S(2)}, u32[]{:S(2)}) collective-permute-start(bf16[1040,128]{1,0:T(8,128)(2,1)S(1)} %collective-permute-done.1.refs_1_), channel_id=1, source_target_pairs={{0,2},{2,3},{3,1},{1,0},{4,6},{6,7},{7,5},{5,4},{8,10},{10,11},{11... | collective-permute-start | bytes 798728 | tf_op jit(solution)/shard_map/ppermute | solution.py:25
  40.0 5.4 %collective-permute-start.12 = (f32[1,8,128]{2,1,0:T(8,128)S(1)}, f32[1,8,128]{2,1,0:T(8,128)S(1)}, u32[]{:S(2)}, u32[]{:S(2)}) collective-permute-start(f32[1,8,128]{2,1,0:T(8,128)S(1)} %get-tuple-element.88.refs_3_), channel_id=1, source_target_pairs={{0,3},{1,2},{2,1},{3,0},{4,7},{5,6},{6,5},{7,4},{8,11},{9,10},{10,... | collective-permute-start | bytes 12296 | tf_op jit(solution)/shard_map/ppermute | solution.py:19
  43.5 4.5 %collective-permute-start.11 = (f32[1,8,128]{2,1,0:T(8,128)S(1)}, f32[1,8,128]{2,1,0:T(8,128)S(1)}, u32[]{:S(2)}, u32[]{:S(2)}) collective-permute-start(f32[1,8,128]{2,1,0:T(8,128)S(1)} %get-tuple-element.88.refs_3_), channel_id=1, source_target_pairs={{0,2},{1,3},{2,0},{3,1},{4,6},{5,7},{6,4},{7,5},{8,10},{9,11},{10,... | collective-permute-start | bytes 12296 | tf_op jit(solution)/shard_map/ppermute | solution.py:19
  44.0 4.0 %collective-permute-start.10 = (f32[1,8,128]{2,1,0:T(8,128)S(1)}, f32[1,8,128]{2,1,0:T(8,128)S(1)}, u32[]{:S(2)}, u32[]{:S(2)}) collective-permute-start(f32[1,8,128]{2,1,0:T(8,128)S(1)} %get-tuple-element.88.refs_3_), channel_id=1, source_target_pairs={{0,1},{1,0},{2,3},{3,2},{4,5},{5,4},{6,7},{7,6},{8,9},{9,8},{10,11... | collective-permute-start | bytes 12296 | tf_op jit(solution)/shard_map/ppermute | solution.py:19
  52.3 8.3 %collective-permute-start.13 = (bf16[1024,128]{1,0:T(8,128)(2,1)S(1)}, bf16[1024,128]{1,0:T(8,128)(2,1)S(1)}, u32[]{:S(2)}, u32[]{:S(2)}) collective-permute-start(bf16[1024,128]{1,0:T(8,128)(2,1)S(1)} %get-tuple-element.99), channel_id=1, source_target_pairs={{0,2},{2,3},{3,1},{1,0},{4,6},{6,7},{7,5},{5,4},{8,10},{10,11},{11... | collective-permute-start | bytes 786440 | tf_op jit(solution)/shard_map/ppermute | solution.py:25
  60.7 8.8 %collective-permute-start.14 = (bf16[1024,128]{1,0:T(8,128)(2,1)S(1)}, bf16[1024,128]{1,0:T(8,128)(2,1)S(1)}, u32[]{:S(2)}, u32[]{:S(2)}) collective-permute-start(bf16[1024,128]{1,0:T(8,128)(2,1)S(1)} %add_2.1), channel_id=1, source_target_pairs={{0,2},{2,3},{3,1},{1,0},{4,6},{6,7},{7,5},{5,4},{8,10},{10,11},{11... | collective-permute-start | bytes 786440 | tf_op jit(solution)/shard_map/ppermute | solution.py:25
  72.1 2.7 %collective-permute-start.15 = (bf16[4,512,128]{2,1,0:T(8,128)(2,1)S(1)}, bf16[4,512,128]{2,1,0:T(8,128)(2,1)S(1)}, u32[]{:S(2)}, u32[]{:S(2)}) collective-permute-start(bf16[4,512,128]{2,1,0:T(8,128)(2,1)S(1)} %get-tuple-element.108), channel_id=1, source_target_pairs={{0,4},{4,0},{8,12},{12,8},{16,20},{20,16},{24,28},{28,24},{1,5},{5... | collective-permute-start | bytes 1572872 | tf_op jit(solution)/shard_map/ppermute | solution.py:19
  72.2 10.4 %collective-permute-start.16 = (bf16[1024,128]{1,0:T(8,128)(2,1)S(1)}, bf16[1024,128]{1,0:T(8,128)(2,1)S(1)}, u32[]{:S(2)}, u32[]{:S(2)}) collective-permute-start(bf16[1024,128]{1,0:T(8,128)(2,1)S(1)} %add_3.1), channel_id=1, source_target_pairs={{0,2},{2,3},{3,1},{1,0},{4,6},{6,7},{7,5},{5,4},{8,10},{10,11},{11... | collective-permute-start | bytes 786440 | tf_op jit(solution)/shard_map/ppermute | solution.py:25
  74.9 9.0 %collective-permute-start.17 = (bf16[512,128]{1,0:T(8,128)(2,1)S(1)}, bf16[512,128]{1,0:T(8,128)(2,1)S(1)}, u32[]{:S(2)}, u32[]{:S(2)}) collective-permute-start(bf16[512,128]{1,0:T(8,128)(2,1)S(1)} %get-tuple-element.115), channel_id=1, source_target_pairs={{0,8},{4,12},{8,0},{12,4},{16,24},{20,28},{24,16},{28,20},{1,9},{5... | collective-permute-start | bytes 393224 | tf_op jit(solution)/shard_map/ppermute | solution.py:19
  75.9 8.0 %collective-permute-start.18 = (bf16[512,128]{1,0:T(8,128)(2,1)S(1)}, bf16[512,128]{1,0:T(8,128)(2,1)S(1)}, u32[]{:S(2)}, u32[]{:S(2)}) collective-permute-start(bf16[512,128]{1,0:T(8,128)(2,1)S(1)} %get-tuple-element.116), channel_id=1, source_target_pairs={{0,16},{4,20},{8,24},{12,28},{16,0},{20,4},{24,8},{28,12},{1,17},{... | collective-permute-start | bytes 393224 | tf_op jit(solution)/shard_map/ppermute | solution.py:19
  77.0 7.6 %collective-permute-start.19 = (bf16[512,128]{1,0:T(8,128)(2,1)S(1)}, bf16[512,128]{1,0:T(8,128)(2,1)S(1)}, u32[]{:S(2)}, u32[]{:S(2)}) collective-permute-start(bf16[512,128]{1,0:T(8,128)(2,1)S(1)} %get-tuple-element.117), channel_id=1, source_target_pairs={{0,24},{4,28},{8,16},{12,20},{16,8},{20,12},{24,0},{28,4},{1,25},{... | collective-permute-start | bytes 393224 | tf_op jit(solution)/shard_map/ppermute | solution.py:19

commit v8 on v7

--- a/solution.py
+++ b/solution.py
@@ -302,14 +302,8 @@
 
         def mask_part(buffer, s, i, source_ref=source_ref):
             at = slice(i * part, (i + 1) * part)
-            if half is None:
-                g = grad_ref[:, tile_at(s)]
-                value = source_ref[at, local(s)]
-            else:
-                g = grad_ref[:, tile_at(s)].astype(jnp.float32)
-                value = jnp.dot(
-                    source_ref[at, :], keys_ref[:, tile_at(s)], preferred_element_type=jnp.float32
-                )
+            g = grad_ref[:, tile_at(s)]
+            value = source_ref[at, local(s)]
             wide = jnp.broadcast_to(g[None], (heads, rows_here, tile)).reshape(part, tile)
             value = jnp.where(value > 0, wide, jnp.zeros_like(wide))
             mask_at(buffer, s, at)[...] = value.astype(jnp.bfloat16)
@@ -362,6 +356,28 @@
                 kg_refs[i][...] = value
 
 
+def own_active_kernel(cfg, meta_ref, q_ref, keys_t_ref, first_ref, second_ref):
+    order, nh, rows_here, hh, depth, kc, chunk, scale = cfg
+    pieces = len(order) // 2
+    side = min(256, chunk)
+    for half, active_ref in enumerate((first_ref, second_ref)):
+
+        def step(s, _, half=half, active_ref=active_ref):
+            position = meta_ref[3 + half * pieces + s]
+            for first in range(0, chunk, side):
+                columns = pl.ds(pl.multiple_of(position * chunk + first, side), side)
+                local = pl.ds(pl.multiple_of(s * chunk + first, side), side)
+                dots = jnp.dot(
+                    q_ref[: rows_here * hh, :],
+                    keys_t_ref[:, columns],
+                    preferred_element_type=jnp.float32,
+                )
+                active_ref[:, local] = jnp.maximum(dots, 0.0).astype(jnp.bfloat16)
+            return 0
+
+        lax.fori_loop(0, pieces, step, 0)
+
+
 def query_kernel(cfg, meta_ref, first_ref, second_ref, keys_ref, u_ref, u_acc):
     chunk, pieces = cfg[6], len(cfg[0]) // 2
     u_acc[...] = jnp.zeros_like(u_acc)
@@ -380,14 +396,14 @@
     u_ref[...] = u_acc[...]
 
 
-def prepare_kernel(cfg, meta_ref, query_ref, weights_ref, rw_ref, keys_ref, logits_ref, *refs):
+def prepare_kernel(cfg, query_ref, weights_ref, rw_ref, keys_ref, logits_ref, *refs):
     order, nh, rows_here, hh, depth, kc, chunk, scale = cfg
     sends = len(order) // 2
     rows = rows_here * hh
     parts = chunk // lanes
     message_ref, rw_out_ref, key_refs = refs[0], refs[1], refs[2 : 2 + sends]
     wide, sems = refs[-2], refs[-1]
-    share = pl.multiple_of(meta_ref[2] * chunk, chunk)
+    share = pl.multiple_of(lax.axis_index("head") * chunk, chunk)
     copies = []
 
     def copy(source, target):
@@ -397,7 +413,7 @@
     for i in reversed(range(sends)):
         copy(keys_ref.at[pl.ds(share, chunk), :], key_refs[i].at[:chunk, :])
         for core in range(2):
-            row = pl.multiple_of((meta_ref[1] ^ (2 * i) ^ core) * rows_here, rows_here)
+            row = pl.multiple_of((lax.axis_index("ctx") ^ (2 * i) ^ core) * rows_here, rows_here)
             for part in range(parts):
                 first = chunk + (parts * core + part) * rows_here
                 copy(
@@ -405,7 +421,7 @@
                     key_refs[i].at[first : first + rows_here, :],
                 )
     every = jnp.broadcast_to(rw_ref[...], (8, rw_ref.shape[1]))
-    shift = every.shape[1] - meta_ref[1] * rows_here
+    shift = every.shape[1] - lax.axis_index("ctx") * rows_here
     here = pltpu.roll(every, shift, 1)[:1, : rw_out_ref.shape[1]]
     rw_out_ref[...] = here * float(kc * len(order)) ** 0.5
     wide[...] = query_ref[...].astype(jnp.float32)
@@ -482,7 +498,7 @@
             jax.ShapeDtypeStruct((1, padded), f32),
         ]
         + [jax.ShapeDtypeStruct((chunk + 2 * parts * rows_here, depth), bf16)] * (n // 2),
-        in_specs=[smem, vmem, vmem, vmem] + [pl.BlockSpec(memory_space=pltpu.HBM)] * 2,
+        in_specs=[vmem, vmem, vmem] + [pl.BlockSpec(memory_space=pltpu.HBM)] * 2,
         out_specs=[vmem] * (2 + n // 2),
         scratch_shapes=[
             pltpu.VMEM((rows_here, hh, depth), f32),
@@ -493,7 +509,7 @@
             flops=rows * depth, bytes_accessed=4 * 1024 * 1024, transcendentals=0
         ),
         name="prepare",
-    )(meta, far(query), far(weights.T), far(row_weight[None, :]), far(keys), far(main_logits))
+    )(far(query), far(weights.T), far(row_weight[None, :]), far(keys), far(main_logits))
     q_blocks = [message] * nh
     for hop in range(1, nh // 2 + 1):
         q_blocks[hop] = ring_next(q_blocks[hop - 1], "head")
@@ -604,6 +620,18 @@
 
     all_stats = [stats] + [swap(stats, "head", j) for j in range(1, nh)]
 
+    q_own, _ = lax.optimization_barrier((q_blocks[0], stats))
+    outs = call(
+        functools.partial(own_active_kernel, cfg),
+        [q_own, near(keys_t)],
+        [pltpu.VMEM((rows, total_keys // 2), bf16)] * 2,
+        [],
+        1,
+        "own_active",
+    )
+    rw, *outs = lax.optimization_barrier((rw, *outs))
+    own_active = {"first": outs[:1], "second": outs[1:]}
+
     grad = kg = None
 
     def backward(items, name):
@@ -615,9 +643,9 @@
         halved = ranges != [] and ranges[0] != "all"
         operands = []
         for item in items:
-            operands += [q_blocks[0]] if halved else nears(active[item[0]])
+            operands += nears(own_active[ranges[0]] if halved else active[item[0]])
         operands += [near(qw[item[0]]) for item in items if item[2] is not None]
-        operands += [near(keys_t if halved else keys_all)]
+        operands += [near(keys_all)]
         operands += all_stats + [rw, near(logits), near(score)] if is_first else [near(grad)]
         aliases = {}
         out_shape = [jax.ShapeDtypeStruct((rows, depth), bf16 if is_first else f32)]

time: 85.5 us -> 84.8 us (level)
  waiting for transfers between devices: 8.62 us -> 3.33 us
  Pallas kernels: 48.6 us -> 51.3 us
  starting transfers between devices: 25.1 us -> 26.9 us
    ppermute x14, waiting for transfers between devices: 8.02 us -> 2.72 us  [swap(): return lax.ppermute(value, axis, [(i, i ^ distance) for i in range(size)])]
    pallas_call x10 -> x11, Pallas kernels: 44.5 us -> 47.3 us  [call(): pl.pallas_call(kernel, out_shape=out_shape, input_output_aliases=aliases,...]
    ppermute x6, starting transfers between devices: 10.5 us -> 12.3 us  [ring_next(): lax.ppermute(value, axis, [(ring[i], ring[(i + hop) % size]) for i in ran...]
  transfers between devices with their start and end apart: 20 -> 20, of which waited for: 7 -> 4; matrix products, arithmetic and copies ran while one was open for 0% -> 1% of each run, Pallas kernels for 40% -> 44%
where the time goes in v8:
time: 84.8 us; the launch traced here: 84.6 us
  Pallas kernels  51.3 us (60%)
  starting transfers between devices  26.9 us (32%)
  waiting for transfers between devices  3.33 us (4%)
  other arithmetic  1.62 us (2%)
  between operations  1.47 us (2%)
    pallas_call x11, Pallas kernels, call(): pl.pallas_call(kernel, out_shape=out_shape, input_output_aliases=aliases,...  47.3 us
    ppermute x14, starting transfers between devices, swap(): return lax.ppermute(value, axis, [(i, i ^ distance) for i in range(size)])  14.6 us
    ppermute x6, starting transfers between devices, ring_next(): lax.ppermute(value, axis, [(ring[i], ring[(i + hop) % size]) for i in ran...  12.3 us
    ppermute x14, waiting for transfers between devices, swap(): return lax.ppermute(value, axis, [(i, i ^ distance) for i in range(size)])  2.72 us
    pallas_call x1, Pallas kernels, per_device(): pl.pallas_call(functools.partial(prepare_kernel, cfg), out_shape=[jax.Sha...  2.61 us
  transfers between devices with their start and end apart: 20, of which 4 were waited for; matrix products, arithmetic and copies ran while one was open for 1% of the time, Pallas kernels for 44%

profile of v8, /device:TPU:0, one launch (start us, length us, event | category | flops | bytes accessed | tf_op | source)
XLA Modules:
  0.0 84.6 jit_solution(994256394064438206)
XLA Ops:
  0.6 2.6 %prepare.1 = (bf16[1040,128]{1,0:T(8,128)(2,1)S(1)}, f32[1,128]{1,0:T(1,128)S(1)}, bf16[1024,128]{1,0:T(8,128)(2,1)S(1)}, bf16[1024,128]{1,0:T(8,128)(2,1)S(1)},...) custom-call(bf16[64,16,128]{2,1,0:T(8,128)(2,1)} %query_ref.1, bf16[16,64]{1,0:T(8,128)(2,1)} %bitcast.25, ...), custom_call_target="tpu_custom_call" | custom-call | flops 131072 | bytes 4194304 | tf_op jit(solution)/shard_map/prepare/pallas_call | solution.py:494
  3.8 2.6 %collective-permute-start.3 = (bf16[1024,128]{1,0:T(8,128)(2,1)S(1)}, bf16[1024,128]{1,0:T(8,128)(2,1)S(1)}, u32[]{:S(2)}, u32[]{:S(2)}) collective-permute-start(bf16[1024,128]{1,0:T(8,128)(2,1)S(1)} %get-tuple-element.71), channel_id=1, source_target_pairs={{0,8},{4,12},{8,0},{12,4},{16,24},{20,28},{24,16},{28,20},{1,9},{5... | collective-permute-start | bytes 786440 | tf_op jit(solution)/shard_map/ppermute | solution.py:19
  6.3 1.5 %collective-permute-start.4 = (bf16[1024,128]{1,0:T(8,128)(2,1)S(1)}, bf16[1024,128]{1,0:T(8,128)(2,1)S(1)}, u32[]{:S(2)}, u32[]{:S(2)}) collective-permute-start(bf16[1024,128]{1,0:T(8,128)(2,1)S(1)} %get-tuple-element.72), channel_id=1, source_target_pairs={{0,16},{4,20},{8,24},{12,28},{16,0},{20,4},{24,8},{28,12},{1,17},{... | collective-permute-start | bytes 786440 | tf_op jit(solution)/shard_map/ppermute | solution.py:19
  7.9 2.6 %collective-permute-start = (bf16[1040,128]{1,0:T(8,128)(2,1)S(1)}, bf16[1040,128]{1,0:T(8,128)(2,1)S(1)}, u32[]{:S(2)}, u32[]{:S(2)}) collective-permute-start(bf16[1040,128]{1,0:T(8,128)(2,1)S(1)} %get-tuple-element.92.refs_0_.q_ref), channel_id=1, source_target_pairs={{0,2},{2,3},{3,1},{1,0},{4,6},{6,7},{7,5},{5,4},{8,10},{10,11},{11... | collective-permute-start | bytes 798728 | tf_op jit(solution)/shard_map/ppermute | solution.py:25
  11.8 1.4 %forward_early_0.1 = (f32[64,1024]{1,0:T(8,128)S(1)}, bf16[1024,128]{1,0:T(8,128)(2,1)S(1)}, bf16[128,1024]{1,0:T(8,128)(2,1)S(1)}, bf16[64,1024]{1,0:T(8,128)(2...) custom-call(s32[11]{0:T(128)S(1)} %pad_add_fusion.meta_ref, ...), custom_call_target="tpu_custom_call" | custom-call | flops 2147483 | bytes 4194 | tf_op jit(solution)/shard_map/forward_early_0/pallas_call | solution.py:532
  13.2 1.5 %collective-permute-done.4.refs_10_ = bf16[1024,128]{1,0:T(8,128)(2,1)S(1)} collective-permute-done((bf16[1024,128]{1,0:T(8,128)(2,1)S(1)}, bf16[1024,128]{1,0:T(8,128)(2,1)S(1)}, u32[]{:S(2)}, u32[]{:S(2)}) %collective-permute-start.4) | collective-permute-done | bytes 262176 | tf_op jit(solution)/shard_map/ppermute | solution.py:19
  15.2 1.5 %collective-permute-start.8 = (bf16[1024,128]{1,0:T(8,128)(2,1)S(1)}, bf16[1024,128]{1,0:T(8,128)(2,1)S(1)}, u32[]{:S(2)}, u32[]{:S(2)}) collective-permute-start(bf16[1024,128]{1,0:T(8,128)(2,1)S(1)} %get-tuple-element.82), channel_id=1, source_target_pairs={{0,24},{4,28},{8,16},{12,20},{16,8},{20,12},{24,0},{28,4},{1,25},{... | collective-permute-start | bytes 786440 | tf_op jit(solution)/shard_map/ppermute | solution.py:19
  16.7 1.6 %collective-permute-start.7 = (bf16[1040,128]{1,0:T(8,128)(2,1)S(1)}, bf16[1040,128]{1,0:T(8,128)(2,1)S(1)}, u32[]{:S(2)}, u32[]{:S(2)}) collective-permute-start(bf16[1040,128]{1,0:T(8,128)(2,1)S(1)} %get-tuple-element.92.refs_0_.q_ref), channel_id=1, source_target_pairs={{0,1},{2,0},{3,2},{1,3},{4,5},{6,4},{7,6},{5,7},{8,9},{10,8},{11,1... | collective-permute-start | bytes 798728 | tf_op jit(solution)/shard_map/ppermute | solution.py:25
  18.3 5.2 %forward_early_1.1 = (f32[64,3072]{1,0:T(8,128)S(1)}, bf16[3072,128]{1,0:T(8,128)(2,1)S(1)}, bf16[128,3072]{1,0:T(8,128)(2,1)S(1)}, bf16[64,3072]{1,0:T(8,128)(2...) custom-call(s32[11]{0:T(128)S(1)} %pad_add_fusion.meta_ref, ...), custom_call_target="tpu_custom_call" | custom-call | flops 2147483 | bytes 4194 | tf_op jit(solution)/shard_map/forward_early_1/pallas_call | solution.py:532
  24.3 2.6 %collective-permute-start.1 = (bf16[1040,128]{1,0:T(8,128)(2,1)S(1)}, bf16[1040,128]{1,0:T(8,128)(2,1)S(1)}, u32[]{:S(2)}, u32[]{:S(2)}) collective-permute-start(bf16[1040,128]{1,0:T(8,128)(2,1)S(1)} %collective-permute-done.refs_1_), channel_id=1, source_target_pairs={{0,2},{2,3},{3,1},{1,0},{4,6},{6,7},{7,5},{5,4},{8,10},{10,11},{11... | collective-permute-start | bytes 798728 | tf_op jit(solution)/shard_map/ppermute | solution.py:25
  26.9 5.7 %forward_middle.1 = (f32[64,4096]{1,0:T(8,128)S(1)}, bf16[4096,128]{1,0:T(8,128)(2,1)S(1)}, bf16[128,4096]{1,0:T(8,128)(2,1)S(1)}, bf16[64,4096]{1,0:T(8,128)(2,...) custom-call(s32[11]{0:T(128)S(1)} %pad_add_fusion.meta_ref, ...), custom_call_target="tpu_custom_call" | custom-call | flops 3221225472 | bytes 6291456 | tf_op jit(solution)/shard_map/forward_middle/pallas_call | solution.py:532
  33.3 5.3 %forward_last.1 = (f32[64,4096]{1,0:T(8,128)S(1)}, bf16[1024,4096]{1,0:T(8,128)(2,1)S(1)}, bf16[128,1024]{1,0:T(8,128)(2,1)S(1)}, f32[1,8,128]{2,1,0:T(8,128)S(1)}) custom-call(s32[11]{0:T(128)S(1)} %pad_add_fusion.meta_ref, bf16[1040,128]{1,0:T(8,128)(2,1)S(1)} %collective-permute-done.1.refs_0_, ...), custom_call_target="tpu_custom_call", output_to_operand_aliasing={{0}: (3, {})} | custom-call | flops 2147483648 | bytes 4194304 | tf_op jit(solution)/shard_map/forward_last/pallas_call | solution.py:532
  38.6 3.5 %collective-permute-start.12 = (f32[1,8,128]{2,1,0:T(8,128)S(1)}, f32[1,8,128]{2,1,0:T(8,128)S(1)}, u32[]{:S(2)}, u32[]{:S(2)}) collective-permute-start(f32[1,8,128]{2,1,0:T(8,128)S(1)} %get-tuple-element.91.refs_3_), channel_id=1, source_target_pairs={{0,3},{1,2},{2,1},{3,0},{4,7},{5,6},{6,5},{7,4},{8,11},{9,10},{10,... | collective-permute-start | bytes 12296 | tf_op jit(solution)/shard_map/ppermute | solution.py:19
  43.0 4.5 %own_active.1 = (bf16[1024,2048]{1,0:T(8,128)(2,1)S(1)}, bf16[1024,2048]{1,0:T(8,128)(2,1)S(1)}) custom-call(s32[11]{0:T(128)S(1)} %pad_add_fusion.meta_ref, bf16[1040,128]{1,0:T(8,128)(2,1)S(1)} %get-tuple-element.92.refs_0_.q_ref, bf16[128,4096]{1,0:T(8,128)(2,1)S(1)} %get-tuple-element.88.refs_1_.keys_t_ref), custom_call_target="tpu_custom_call" | custom-call | flops 2147483648 | bytes 4194304 | tf_op jit(solution)/shard_map/own_active/pallas_call | solution.py:532
  47.5 4.3 %backward_1.1 = (bf16[1024,128]{1,0:T(8,128)(2,1)S(1)}, bf16[64,4096]{1,0:T(8,128)(2,1)S(1)}) custom-call(s32[11]{0:T(128)S(1)} %pad_add_fusion.meta_ref, bf16[1024,3072]{1,0:T(8,128)(2,1)S(1)} %get-tuple-element.98.refs_0_, bf16[1024,1024]{1,0:T(8,128)(2,1)S(1)} %get-tuple-element.99.refs_1_, ...), custom_call_target="tpu_custom_call" | custom-call | flops 2147483648 | bytes 4194304 | tf_op jit(solution)/shard_map/backward_1/pallas_call | solution.py:532
  51.8 2.5 %collective-permute-start.13 = (bf16[1024,128]{1,0:T(8,128)(2,1)S(1)}, bf16[1024,128]{1,0:T(8,128)(2,1)S(1)}, u32[]{:S(2)}, u32[]{:S(2)}) collective-permute-start(bf16[1024,128]{1,0:T(8,128)(2,1)S(1)} %get-tuple-element.110), channel_id=1, source_target_pairs={{0,2},{2,3},{3,1},{1,0},{4,6},{6,7},{7,5},{5,4},{8,10},{10,11},{11... | collective-permute-start | bytes 786440 | tf_op jit(solution)/shard_map/ppermute | solution.py:25
  54.3 6.0 %backward_2.1 = (f32[1024,128]{1,0:T(8,128)S(1)}, f32[128,4096]{1,0:T(8,128)S(1)}) custom-call(s32[11]{0:T(128)S(1)} %pad_add_fusion.meta_ref, bf16[1024,3072]{1,0:T(8,128)(2,1)S(1)} %get-tuple-element.98.refs_0_, bf16[1024,1024]{1,0:T(8,128)(2,1)S(1)} %get-tuple-element.99.refs_1_, bf16[1024,4096]{1,0:T(8,128)(2,1)S(1)} %get-tuple-element.103.refs_2_.refs_0_, ...), custom_call_target="tpu_custom_call" | custom-call | flops 4294967296 | bytes 8388608 | tf_op jit(solution)/shard_map/backward_2/pallas_call | solution.py:532
  60.4 2.2 %collective-permute-start.14 = (bf16[1024,128]{1,0:T(8,128)(2,1)S(1)}, bf16[1024,128]{1,0:T(8,128)(2,1)S(1)}, u32[]{:S(2)}, u32[]{:S(2)}) collective-permute-start(bf16[1024,128]{1,0:T(8,128)(2,1)S(1)} %add_2.1), channel_id=1, source_target_pairs={{0,2},{2,3},{3,1},{1,0},{4,6},{6,7},{7,5},{5,4},{8,10},{10,11},{11... | collective-permute-start | bytes 786440 | tf_op jit(solution)/shard_map/ppermute | solution.py:25
  62.6 7.5 %backward_3.1 = (f32[1024,128]{1,0:T(8,128)S(1)}, f32[128,4096]{1,0:T(8,128)S(1)}) custom-call(s32[11]{0:T(128)S(1)} %pad_add_fusion.meta_ref, bf16[1024,4096]{1,0:T(8,128)(2,1)S(1)} %get-tuple-element.103.refs_2_.refs_0_, bf16[1024,4096]{1,0:T(8,128)(2,1)S(1)} %get-tuple-element.104.refs_1_, ...), custom_call_target="tpu_custom_call", output_to_operand_aliasing={{1}: (7, {})} | custom-call | flops 6442450944 | bytes 12582912 | tf_op jit(solution)/shard_map/backward_3/pallas_call | solution.py:532
  70.2 1.6 %backward_0_first.1 = (bf16[4,512,128]{2,1,0:T(8,128)(2,1)S(1)}, bf16[1024,2048]{1,0:T(8,128)(2,1)S(1)}) custom-call(s32[11]{0:T(128)S(1)} %pad_add_fusion.meta_ref, bf16[1024,2048]{1,0:T(8,128)(2,1)S(1)} %get-tuple-element.95.refs_0_, bf16[128,1024]{1,0:T(8,128)(2,1)S(1)} %get-tuple-element.96.refs_1_, ...), custom_call_target="tpu_custom_call" | custom-call | flops 2147483648 | bytes 4194304 | tf_op jit(solution)/shard_map/backward_0_first/pallas_call | solution.py:532
  72.7 1.7 %backward_0_second.1 = (f32[512,128]{1,0:T(8,128)S(1)}, f32[512,128]{1,0:T(8,128)S(1)}, f32[512,128]{1,0:T(8,128)S(1)}, f32[512,128]{1,0:T(8,128)S(1)}, bf16[1024,2048]{1,0:T(8,128)(2,1)S(1)}) custom-call(s32[11]{0:T(128)S(1)} %pad_add_fusion.meta_ref, bf16[1024,2048]{1,0:T(8,128)(2,1)S(1)} %get-tuple-element.117.refs_0_, ...), custom_call_target="tpu_custom_call" | custom-call | flops 2147483648 | bytes 4194304 | tf_op jit(solution)/shard_map/backward_0_second/pallas_call | solution.py:532
  76.6 1.4 %collective-permute-start.19 = (bf16[512,128]{1,0:T(8,128)(2,1)S(1)}, bf16[512,128]{1,0:T(8,128)(2,1)S(1)}, u32[]{:S(2)}, u32[]{:S(2)}) collective-permute-start(bf16[512,128]{1,0:T(8,128)(2,1)S(1)} %get-tuple-element.129), channel_id=1, source_target_pairs={{0,24},{4,28},{8,16},{12,20},{16,8},{20,12},{24,0},{28,4},{1,25},{... | collective-permute-start | bytes 393224 | tf_op jit(solution)/shard_map/ppermute | solution.py:19
  78.0 4.1 %backward_0.1.u_ref = f32[1024,128]{1,0:T(8,128)S(1)} custom-call(s32[11]{0:T(128)S(1)} %pad_add_fusion.meta_ref, bf16[1024,2048]{1,0:T(8,128)(2,1)S(1)} %get-tuple-element.116.first_ref, bf16[1024,2048]{1,0:T(8,128)(2,1)S(1)} %get-tuple-element.118.second_ref, bf16[4096,128]{1,0:T(8,128)(2,1)S(1)} %get-tuple-element.123.refs_2_.refs_4_.keys_ref), custom_call_target="tpu_custom_call" | custom-call | flops 2147483648 | bytes 4194304 | tf_op jit(solution)/shard_map/backward_0/pallas_call | solution.py:532
  82.2 1.3 %finish.1 = (f32[64,16,128]{2,1,0:T(8,128)}, f32[16,64]{1,0:T(8,128)}) custom-call(f32[1024,128]{1,0:T(8,128)S(1)} %backward_0.1.u_ref, bf16[1024,128]{1,0:T(8,128)(2,1)S(1)} %collective-permute-done.16.moving_ref, bf16[1040,128]{1,0:T(8,128)(2,1)S(1)} %get-tuple-element.92.refs_0_.q_ref), custom_call_target="tpu_custom_call" | custom-call | flops 1048576 | bytes 1835008 | tf_op jit(solution)/shard_map/finish/pallas_call | solution.py:717
  (34 shorter events, 8.4 us)
Async XLA Ops:
  3.2 8.6 %collective-permute-start.2 = (bf16[1024,128]{1,0:T(8,128)(2,1)S(1)}, bf16[1024,128]{1,0:T(8,128)(2,1)S(1)}, u32[]{:S(2)}, u32[]{:S(2)}) collective-permute-start(bf16[1024,128]{1,0:T(8,128)(2,1)S(1)} %get-tuple-element.69.refs_2_), channel_id=1, source_target_pairs={{0,4},{4,0},{8,12},{12,8},{16,20},{20,16},{24,28},{28,24},{1,5},{5... | collective-permute-start | bytes 786440 | tf_op jit(solution)/shard_map/ppermute | solution.py:19
  3.8 9.5 %collective-permute-start.3 = (bf16[1024,128]{1,0:T(8,128)(2,1)S(1)}, bf16[1024,128]{1,0:T(8,128)(2,1)S(1)}, u32[]{:S(2)}, u32[]{:S(2)}) collective-permute-start(bf16[1024,128]{1,0:T(8,128)(2,1)S(1)} %get-tuple-element.71), channel_id=1, source_target_pairs={{0,8},{4,12},{8,0},{12,4},{16,24},{20,28},{24,16},{28,20},{1,9},{5... | collective-permute-start | bytes 786440 | tf_op jit(solution)/shard_map/ppermute | solution.py:19
  6.3 8.4 %collective-permute-start.4 = (bf16[1024,128]{1,0:T(8,128)(2,1)S(1)}, bf16[1024,128]{1,0:T(8,128)(2,1)S(1)}, u32[]{:S(2)}, u32[]{:S(2)}) collective-permute-start(bf16[1024,128]{1,0:T(8,128)(2,1)S(1)} %get-tuple-element.72), channel_id=1, source_target_pairs={{0,16},{4,20},{8,24},{12,28},{16,0},{20,4},{24,8},{28,12},{1,17},{... | collective-permute-start | bytes 786440 | tf_op jit(solution)/shard_map/ppermute | solution.py:19
  7.9 10.4 %collective-permute-start = (bf16[1040,128]{1,0:T(8,128)(2,1)S(1)}, bf16[1040,128]{1,0:T(8,128)(2,1)S(1)}, u32[]{:S(2)}, u32[]{:S(2)}) collective-permute-start(bf16[1040,128]{1,0:T(8,128)(2,1)S(1)} %get-tuple-element.92.refs_0_.q_ref), channel_id=1, source_target_pairs={{0,2},{2,3},{3,1},{1,0},{4,6},{6,7},{7,5},{5,4},{8,10},{10,11},{11... | collective-permute-start | bytes 798728 | tf_op jit(solution)/shard_map/ppermute | solution.py:25
  14.7 3.6 %collective-permute-start.5 = (bf16[1024,128]{1,0:T(8,128)(2,1)S(1)}, bf16[1024,128]{1,0:T(8,128)(2,1)S(1)}, u32[]{:S(2)}, u32[]{:S(2)}) collective-permute-start(bf16[1024,128]{1,0:T(8,128)(2,1)S(1)} %collective-permute-done.3.refs_9_), channel_id=1, source_target_pairs={{0,4},{4,0},{8,12},{12,8},{16,20},{20,16},{24,28},{28,24},{1,5},{5... | collective-permute-start | bytes 786440 | tf_op jit(solution)/shard_map/ppermute | solution.py:19
  14.7 3.6 %collective-permute-start.6 = (bf16[1024,128]{1,0:T(8,128)(2,1)S(1)}, bf16[1024,128]{1,0:T(8,128)(2,1)S(1)}, u32[]{:S(2)}, u32[]{:S(2)}) collective-permute-start(bf16[1024,128]{1,0:T(8,128)(2,1)S(1)} %collective-permute-done.4.refs_10_), channel_id=1, source_target_pairs={{0,4},{4,0},{8,12},{12,8},{16,20},{20,16},{24,28},{28,24},{1,5},{5... | collective-permute-start | bytes 786440 | tf_op jit(solution)/shard_map/ppermute | solution.py:19
  15.2 9.1 %collective-permute-start.8 = (bf16[1024,128]{1,0:T(8,128)(2,1)S(1)}, bf16[1024,128]{1,0:T(8,128)(2,1)S(1)}, u32[]{:S(2)}, u32[]{:S(2)}) collective-permute-start(bf16[1024,128]{1,0:T(8,128)(2,1)S(1)} %get-tuple-element.82), channel_id=1, source_target_pairs={{0,24},{4,28},{8,16},{12,20},{16,8},{20,12},{24,0},{28,4},{1,25},{... | collective-permute-start | bytes 786440 | tf_op jit(solution)/shard_map/ppermute | solution.py:19
  16.7 10.2 %collective-permute-start.7 = (bf16[1040,128]{1,0:T(8,128)(2,1)S(1)}, bf16[1040,128]{1,0:T(8,128)(2,1)S(1)}, u32[]{:S(2)}, u32[]{:S(2)}) collective-permute-start(bf16[1040,128]{1,0:T(8,128)(2,1)S(1)} %get-tuple-element.92.refs_0_.q_ref), channel_id=1, source_target_pairs={{0,1},{2,0},{3,2},{1,3},{4,5},{6,4},{7,6},{5,7},{8,9},{10,8},{11,1... | collective-permute-start | bytes 798728 | tf_op jit(solution)/shard_map/ppermute | solution.py:25
  24.3 2.6 %collective-permute-start.9 = (bf16[1024,128]{1,0:T(8,128)(2,1)S(1)}, bf16[1024,128]{1,0:T(8,128)(2,1)S(1)}, u32[]{:S(2)}, u32[]{:S(2)}) collective-permute-start(bf16[1024,128]{1,0:T(8,128)(2,1)S(1)} %collective-permute-done.8.refs_10_), channel_id=1, source_target_pairs={{0,4},{4,0},{8,12},{12,8},{16,20},{20,16},{24,28},{28,24},{1,5},{5... | collective-permute-start | bytes 786440 | tf_op jit(solution)/shard_map/ppermute | solution.py:19
  24.3 8.9 %collective-permute-start.1 = (bf16[1040,128]{1,0:T(8,128)(2,1)S(1)}, bf16[1040,128]{1,0:T(8,128)(2,1)S(1)}, u32[]{:S(2)}, u32[]{:S(2)}) collective-permute-start(bf16[1040,128]{1,0:T(8,128)(2,1)S(1)} %collective-permute-done.refs_1_), channel_id=1, source_target_pairs={{0,2},{2,3},{3,1},{1,0},{4,6},{6,7},{7,5},{5,4},{8,10},{10,11},{11... | collective-permute-start | bytes 798728 | tf_op jit(solution)/shard_map/ppermute | solution.py:25
  38.6 8.9 %collective-permute-start.12 = (f32[1,8,128]{2,1,0:T(8,128)S(1)}, f32[1,8,128]{2,1,0:T(8,128)S(1)}, u32[]{:S(2)}, u32[]{:S(2)}) collective-permute-start(f32[1,8,128]{2,1,0:T(8,128)S(1)} %get-tuple-element.91.refs_3_), channel_id=1, source_target_pairs={{0,3},{1,2},{2,1},{3,0},{4,7},{5,6},{6,5},{7,4},{8,11},{9,10},{10,... | collective-permute-start | bytes 12296 | tf_op jit(solution)/shard_map/ppermute | solution.py:19
  42.1 5.4 %collective-permute-start.11 = (f32[1,8,128]{2,1,0:T(8,128)S(1)}, f32[1,8,128]{2,1,0:T(8,128)S(1)}, u32[]{:S(2)}, u32[]{:S(2)}) collective-permute-start(f32[1,8,128]{2,1,0:T(8,128)S(1)} %get-tuple-element.91.refs_3_), channel_id=1, source_target_pairs={{0,2},{1,3},{2,0},{3,1},{4,6},{5,7},{6,4},{7,5},{8,10},{9,11},{10,... | collective-permute-start | bytes 12296 | tf_op jit(solution)/shard_map/ppermute | solution.py:19
  42.6 4.9 %collective-permute-start.10 = (f32[1,8,128]{2,1,0:T(8,128)S(1)}, f32[1,8,128]{2,1,0:T(8,128)S(1)}, u32[]{:S(2)}, u32[]{:S(2)}) collective-permute-start(f32[1,8,128]{2,1,0:T(8,128)S(1)} %get-tuple-element.91.refs_3_), channel_id=1, source_target_pairs={{0,1},{1,0},{2,3},{3,2},{4,5},{5,4},{6,7},{7,6},{8,9},{9,8},{10,11... | collective-permute-start | bytes 12296 | tf_op jit(solution)/shard_map/ppermute | solution.py:19
  51.8 8.5 %collective-permute-start.13 = (bf16[1024,128]{1,0:T(8,128)(2,1)S(1)}, bf16[1024,128]{1,0:T(8,128)(2,1)S(1)}, u32[]{:S(2)}, u32[]{:S(2)}) collective-permute-start(bf16[1024,128]{1,0:T(8,128)(2,1)S(1)} %get-tuple-element.110), channel_id=1, source_target_pairs={{0,2},{2,3},{3,1},{1,0},{4,6},{6,7},{7,5},{5,4},{8,10},{10,11},{11... | collective-permute-start | bytes 786440 | tf_op jit(solution)/shard_map/ppermute | solution.py:25
  60.4 9.8 %collective-permute-start.14 = (bf16[1024,128]{1,0:T(8,128)(2,1)S(1)}, bf16[1024,128]{1,0:T(8,128)(2,1)S(1)}, u32[]{:S(2)}, u32[]{:S(2)}) collective-permute-start(bf16[1024,128]{1,0:T(8,128)(2,1)S(1)} %add_2.1), channel_id=1, source_target_pairs={{0,2},{2,3},{3,1},{1,0},{4,6},{6,7},{7,5},{5,4},{8,10},{10,11},{11... | collective-permute-start | bytes 786440 | tf_op jit(solution)/shard_map/ppermute | solution.py:25
  71.9 2.5 %collective-permute-start.15 = (bf16[4,512,128]{2,1,0:T(8,128)(2,1)S(1)}, bf16[4,512,128]{2,1,0:T(8,128)(2,1)S(1)}, u32[]{:S(2)}, u32[]{:S(2)}) collective-permute-start(bf16[4,512,128]{2,1,0:T(8,128)(2,1)S(1)} %get-tuple-element.120), channel_id=1, source_target_pairs={{0,4},{4,0},{8,12},{12,8},{16,20},{20,16},{24,28},{28,24},{1,5},{5... | collective-permute-start | bytes 1572872 | tf_op jit(solution)/shard_map/ppermute | solution.py:19
  71.9 10.2 %collective-permute-start.16 = (bf16[1024,128]{1,0:T(8,128)(2,1)S(1)}, bf16[1024,128]{1,0:T(8,128)(2,1)S(1)}, u32[]{:S(2)}, u32[]{:S(2)}) collective-permute-start(bf16[1024,128]{1,0:T(8,128)(2,1)S(1)} %add_3.1), channel_id=1, source_target_pairs={{0,2},{2,3},{3,1},{1,0},{4,6},{6,7},{7,5},{5,4},{8,10},{10,11},{11... | collective-permute-start | bytes 786440 | tf_op jit(solution)/shard_map/ppermute | solution.py:25
  74.5 9.0 %collective-permute-start.17 = (bf16[512,128]{1,0:T(8,128)(2,1)S(1)}, bf16[512,128]{1,0:T(8,128)(2,1)S(1)}, u32[]{:S(2)}, u32[]{:S(2)}) collective-permute-start(bf16[512,128]{1,0:T(8,128)(2,1)S(1)} %get-tuple-element.127), channel_id=1, source_target_pairs={{0,8},{4,12},{8,0},{12,4},{16,24},{20,28},{24,16},{28,20},{1,9},{5... | collective-permute-start | bytes 393224 | tf_op jit(solution)/shard_map/ppermute | solution.py:19
  75.5 8.0 %collective-permute-start.18 = (bf16[512,128]{1,0:T(8,128)(2,1)S(1)}, bf16[512,128]{1,0:T(8,128)(2,1)S(1)}, u32[]{:S(2)}, u32[]{:S(2)}) collective-permute-start(bf16[512,128]{1,0:T(8,128)(2,1)S(1)} %get-tuple-element.128), channel_id=1, source_target_pairs={{0,16},{4,20},{8,24},{12,28},{16,0},{20,4},{24,8},{28,12},{1,17},{... | collective-permute-start | bytes 393224 | tf_op jit(solution)/shard_map/ppermute | solution.py:19
  76.6 7.3 %collective-permute-start.19 = (bf16[512,128]{1,0:T(8,128)(2,1)S(1)}, bf16[512,128]{1,0:T(8,128)(2,1)S(1)}, u32[]{:S(2)}, u32[]{:S(2)}) collective-permute-start(bf16[512,128]{1,0:T(8,128)(2,1)S(1)} %get-tuple-element.129), channel_id=1, source_target_pairs={{0,24},{4,28},{8,16},{12,20},{16,8},{20,12},{24,0},{28,4},{1,25},{... | collective-permute-start | bytes 393224 | tf_op jit(solution)/shard_map/ppermute | solution.py:19

commit v9 on v8

--- a/solution.py
+++ b/solution.py
@@ -27,6 +27,10 @@
 
 def in_pairs(count, first, step):
     first(0, 0)
+    if count <= 8:
+        for i in range(count):
+            step(i % 2, i, i + 1 if i + 1 < count else None)
+        return
 
     def body(i, _):
         step(0, 2 * i, 2 * i + 1)
@@ -82,7 +86,7 @@
     order, nh, rows_here, hh, depth, kc, chunk, scale = cfg
     rows = rows_here * hh
     side = min(256, count)
-    tile = next(size for size in (4 * side, 2 * side, side) if count % size == 0)
+    tile = next(size * side for size in (8, 6, 4, 2, 1) if count % (size * side) == 0)
 
     def step(s, _):
         for first in range(0, tile, side):
@@ -358,41 +362,34 @@
 
 def own_active_kernel(cfg, meta_ref, q_ref, keys_t_ref, first_ref, second_ref):
     order, nh, rows_here, hh, depth, kc, chunk, scale = cfg
-    pieces = len(order) // 2
     side = min(256, chunk)
     for half, active_ref in enumerate((first_ref, second_ref)):
-
-        def step(s, _, half=half, active_ref=active_ref):
-            position = meta_ref[3 + half * pieces + s]
+        for s, k in enumerate(range(1 - half, len(order), 2)):
             for first in range(0, chunk, side):
-                columns = pl.ds(pl.multiple_of(position * chunk + first, side), side)
-                local = pl.ds(pl.multiple_of(s * chunk + first, side), side)
+                column = order.index(k) * chunk + first
                 dots = jnp.dot(
                     q_ref[: rows_here * hh, :],
-                    keys_t_ref[:, columns],
+                    keys_t_ref[:, column : column + side],
                     preferred_element_type=jnp.float32,
                 )
-                active_ref[:, local] = jnp.maximum(dots, 0.0).astype(jnp.bfloat16)
-            return 0
-
-        lax.fori_loop(0, pieces, step, 0)
+                active = jnp.maximum(dots, 0.0).astype(jnp.bfloat16)
+                active_ref[:, s * chunk + first : s * chunk + first + side] = active
 
 
 def query_kernel(cfg, meta_ref, first_ref, second_ref, keys_ref, u_ref, u_acc):
-    chunk, pieces = cfg[6], len(cfg[0]) // 2
-    u_acc[...] = jnp.zeros_like(u_acc)
+    order, chunk = cfg[0], cfg[6]
     for half, mask_ref in enumerate((first_ref, second_ref)):
-
-        def step(s, _, half=half, mask_ref=mask_ref):
-            position = meta_ref[3 + half * pieces + s]
-            u_acc[...] += jnp.dot(
-                mask_ref[:, pl.ds(pl.multiple_of(s * chunk, chunk), chunk)],
-                keys_ref[pl.ds(pl.multiple_of(position * chunk, chunk), chunk), :],
+        for s, k in enumerate(range(1 - half, len(order), 2)):
+            position = order.index(k)
+            more = jnp.dot(
+                mask_ref[:, s * chunk : (s + 1) * chunk],
+                keys_ref[position * chunk : (position + 1) * chunk, :],
                 preferred_element_type=jnp.float32,
             )
-            return 0
-
-        lax.fori_loop(0, pieces, step, 0)
+            if half == 0 and s == 0:
+                u_acc[...] = more
+            else:
+                u_acc[...] += more
     u_ref[...] = u_acc[...]
 
 

time: 84.8 us -> 81 us (0.955)
  Pallas kernels: 51.3 us -> 42.6 us
  waiting for transfers between devices: 3.33 us -> 6.23 us
  starting transfers between devices: 26.9 us -> 29 us
    pallas_call x11, Pallas kernels: 47.3 us -> 38.5 us  [call(): pl.pallas_call(kernel, out_shape=out_shape, input_output_aliases=aliases,...]
    ppermute x14, waiting for transfers between devices: 2.72 us -> 5.06 us  [swap(): return lax.ppermute(value, axis, [(i, i ^ distance) for i in range(size)])]
    ppermute x6, starting transfers between devices: 12.3 us -> 14.3 us  [ring_next(): lax.ppermute(value, axis, [(ring[i], ring[(i + hop) % size]) for i in ran...]
  transfers between devices with their start and end apart: 20 -> 20, of which waited for: 4 -> 6; matrix products, arithmetic and copies ran while one was open for 1% -> 1% of each run, Pallas kernels for 44% -> 37%
where the time goes in v9:
time: 81 us; the launch traced here: 80.8 us
  Pallas kernels  42.6 us (53%)
  starting transfers between devices  29 us (36%)
  waiting for transfers between devices  6.23 us (8%)
  other arithmetic  1.62 us (2%)
  between operations  1.43 us (2%)
    pallas_call x11, Pallas kernels, call(): pl.pallas_call(kernel, out_shape=out_shape, input_output_aliases=aliases,...  38.5 us
    ppermute x14, starting transfers between devices, swap(): return lax.ppermute(value, axis, [(i, i ^ distance) for i in range(size)])  14.6 us
    ppermute x6, starting transfers between devices, ring_next(): lax.ppermute(value, axis, [(ring[i], ring[(i + hop) % size]) for i in ran...  14.3 us
    ppermute x14, waiting for transfers between devices, swap(): return lax.ppermute(value, axis, [(i, i ^ distance) for i in range(size)])  5.06 us
    pallas_call x1, Pallas kernels, per_device(): pl.pallas_call(functools.partial(prepare_kernel, cfg), out_shape=[jax.Sha...  2.61 us
  transfers between devices with their start and end apart: 20, of which 6 were waited for; matrix products, arithmetic and copies ran while one was open for 1% of the time, Pallas kernels for 37%

profile of v9, /device:TPU:0, one launch (start us, length us, event | category | flops | bytes accessed | tf_op | source)
XLA Modules:
  0.0 80.8 jit_solution(9050446945834633914)
XLA Ops:
  0.6 2.6 %prepare.1 = (bf16[1040,128]{1,0:T(8,128)(2,1)S(1)}, f32[1,128]{1,0:T(1,128)S(1)}, bf16[1024,128]{1,0:T(8,128)(2,1)S(1)}, bf16[1024,128]{1,0:T(8,128)(2,1)S(1)},...) custom-call(bf16[64,16,128]{2,1,0:T(8,128)(2,1)} %query_ref.1, bf16[16,64]{1,0:T(8,128)(2,1)} %bitcast.25, ...), custom_call_target="tpu_custom_call" | custom-call | flops 131072 | bytes 4194304 | tf_op jit(solution)/shard_map/prepare/pallas_call | solution.py:491
  3.8 2.6 %collective-permute-start.3 = (bf16[1024,128]{1,0:T(8,128)(2,1)S(1)}, bf16[1024,128]{1,0:T(8,128)(2,1)S(1)}, u32[]{:S(2)}, u32[]{:S(2)}) collective-permute-start(bf16[1024,128]{1,0:T(8,128)(2,1)S(1)} %get-tuple-element.71), channel_id=1, source_target_pairs={{0,8},{4,12},{8,0},{12,4},{16,24},{20,28},{24,16},{28,20},{1,9},{5... | collective-permute-start | bytes 786440 | tf_op jit(solution)/shard_map/ppermute | solution.py:19
  6.3 1.5 %collective-permute-start.4 = (bf16[1024,128]{1,0:T(8,128)(2,1)S(1)}, bf16[1024,128]{1,0:T(8,128)(2,1)S(1)}, u32[]{:S(2)}, u32[]{:S(2)}) collective-permute-start(bf16[1024,128]{1,0:T(8,128)(2,1)S(1)} %get-tuple-element.72), channel_id=1, source_target_pairs={{0,16},{4,20},{8,24},{12,28},{16,0},{20,4},{24,8},{28,12},{1,17},{... | collective-permute-start | bytes 786440 | tf_op jit(solution)/shard_map/ppermute | solution.py:19
  7.9 2.6 %collective-permute-start = (bf16[1040,128]{1,0:T(8,128)(2,1)S(1)}, bf16[1040,128]{1,0:T(8,128)(2,1)S(1)}, u32[]{:S(2)}, u32[]{:S(2)}) collective-permute-start(bf16[1040,128]{1,0:T(8,128)(2,1)S(1)} %get-tuple-element.92.refs_0_.q_ref), channel_id=1, source_target_pairs={{0,2},{2,3},{3,1},{1,0},{4,6},{6,7},{7,5},{5,4},{8,10},{10,11},{11... | collective-permute-start | bytes 798728 | tf_op jit(solution)/shard_map/ppermute | solution.py:25
  13.2 1.5 %collective-permute-done.4.refs_10_ = bf16[1024,128]{1,0:T(8,128)(2,1)S(1)} collective-permute-done((bf16[1024,128]{1,0:T(8,128)(2,1)S(1)}, bf16[1024,128]{1,0:T(8,128)(2,1)S(1)}, u32[]{:S(2)}, u32[]{:S(2)}) %collective-permute-start.4) | collective-permute-done | bytes 262176 | tf_op jit(solution)/shard_map/ppermute | solution.py:19
  15.2 1.5 %collective-permute-start.8 = (bf16[1024,128]{1,0:T(8,128)(2,1)S(1)}, bf16[1024,128]{1,0:T(8,128)(2,1)S(1)}, u32[]{:S(2)}, u32[]{:S(2)}) collective-permute-start(bf16[1024,128]{1,0:T(8,128)(2,1)S(1)} %get-tuple-element.82), channel_id=1, source_target_pairs={{0,24},{4,28},{8,16},{12,20},{16,8},{20,12},{24,0},{28,4},{1,25},{... | collective-permute-start | bytes 786440 | tf_op jit(solution)/shard_map/ppermute | solution.py:19
  16.7 1.6 %collective-permute-start.7 = (bf16[1040,128]{1,0:T(8,128)(2,1)S(1)}, bf16[1040,128]{1,0:T(8,128)(2,1)S(1)}, u32[]{:S(2)}, u32[]{:S(2)}) collective-permute-start(bf16[1040,128]{1,0:T(8,128)(2,1)S(1)} %get-tuple-element.92.refs_0_.q_ref), channel_id=1, source_target_pairs={{0,1},{2,0},{3,2},{1,3},{4,5},{6,4},{7,6},{5,7},{8,9},{10,8},{11,1... | collective-permute-start | bytes 798728 | tf_op jit(solution)/shard_map/ppermute | solution.py:25
  18.3 4.6 %forward_early_1.1 = (f32[64,3072]{1,0:T(8,128)S(1)}, bf16[3072,128]{1,0:T(8,128)(2,1)S(1)}, bf16[128,3072]{1,0:T(8,128)(2,1)S(1)}, bf16[64,3072]{1,0:T(8,128)(2...) custom-call(s32[11]{0:T(128)S(1)} %pad_add_fusion.meta_ref, ...), custom_call_target="tpu_custom_call" | custom-call | flops 2147483 | bytes 4194 | tf_op jit(solution)/shard_map/forward_early_1/pallas_call | solution.py:529
  22.9 1.5 %collective-permute-done.8.refs_10_ = bf16[1024,128]{1,0:T(8,128)(2,1)S(1)} collective-permute-done((bf16[1024,128]{1,0:T(8,128)(2,1)S(1)}, bf16[1024,128]{1,0:T(8,128)(2,1)S(1)}, u32[]{:S(2)}, u32[]{:S(2)}) %collective-permute-start.8) | collective-permute-done | bytes 262176 | tf_op jit(solution)/shard_map/ppermute | solution.py:19
  24.3 2.6 %collective-permute-start.1 = (bf16[1040,128]{1,0:T(8,128)(2,1)S(1)}, bf16[1040,128]{1,0:T(8,128)(2,1)S(1)}, u32[]{:S(2)}, u32[]{:S(2)}) collective-permute-start(bf16[1040,128]{1,0:T(8,128)(2,1)S(1)} %collective-permute-done.refs_1_), channel_id=1, source_target_pairs={{0,2},{2,3},{3,1},{1,0},{4,6},{6,7},{7,5},{5,4},{8,10},{10,11},{11... | collective-permute-start | bytes 798728 | tf_op jit(solution)/shard_map/ppermute | solution.py:25
  26.9 5.5 %forward_middle.1 = (f32[64,4096]{1,0:T(8,128)S(1)}, bf16[4096,128]{1,0:T(8,128)(2,1)S(1)}, bf16[128,4096]{1,0:T(8,128)(2,1)S(1)}, bf16[64,4096]{1,0:T(8,128)(2,...) custom-call(s32[11]{0:T(128)S(1)} %pad_add_fusion.meta_ref, ...), custom_call_target="tpu_custom_call" | custom-call | flops 3221225472 | bytes 6291456 | tf_op jit(solution)/shard_map/forward_middle/pallas_call | solution.py:529
  33.3 5.0 %forward_last.1 = (f32[64,4096]{1,0:T(8,128)S(1)}, bf16[1024,4096]{1,0:T(8,128)(2,1)S(1)}, bf16[128,1024]{1,0:T(8,128)(2,1)S(1)}, f32[1,8,128]{2,1,0:T(8,128)S(1)}) custom-call(s32[11]{0:T(128)S(1)} %pad_add_fusion.meta_ref, bf16[1040,128]{1,0:T(8,128)(2,1)S(1)} %collective-permute-done.1.refs_0_, ...), custom_call_target="tpu_custom_call", output_to_operand_aliasing={{0}: (3, {})} | custom-call | flops 2147483648 | bytes 4194304 | tf_op jit(solution)/shard_map/forward_last/pallas_call | solution.py:529
  38.3 3.5 %collective-permute-start.12 = (f32[1,8,128]{2,1,0:T(8,128)S(1)}, f32[1,8,128]{2,1,0:T(8,128)S(1)}, u32[]{:S(2)}, u32[]{:S(2)}) collective-permute-start(f32[1,8,128]{2,1,0:T(8,128)S(1)} %get-tuple-element.91.refs_3_), channel_id=1, source_target_pairs={{0,3},{1,2},{2,1},{3,0},{4,7},{5,6},{6,5},{7,4},{8,11},{9,10},{10,... | collective-permute-start | bytes 12296 | tf_op jit(solution)/shard_map/ppermute | solution.py:19
  42.7 2.9 %own_active.1 = (bf16[1024,2048]{1,0:T(8,128)(2,1)S(1)}, bf16[1024,2048]{1,0:T(8,128)(2,1)S(1)}) custom-call(s32[11]{0:T(128)S(1)} %pad_add_fusion.meta_ref, bf16[1040,128]{1,0:T(8,128)(2,1)S(1)} %get-tuple-element.92.refs_0_.q_ref, bf16[128,4096]{1,0:T(8,128)(2,1)S(1)} %get-tuple-element.88.refs_1_.keys_t_ref), custom_call_target="tpu_custom_call" | custom-call | flops 2147483648 | bytes 4194304 | tf_op jit(solution)/shard_map/own_active/pallas_call | solution.py:529
  46.3 3.3 %backward_1.1 = (bf16[1024,128]{1,0:T(8,128)(2,1)S(1)}, bf16[64,4096]{1,0:T(8,128)(2,1)S(1)}) custom-call(s32[11]{0:T(128)S(1)} %pad_add_fusion.meta_ref, bf16[1024,3072]{1,0:T(8,128)(2,1)S(1)} %get-tuple-element.98.refs_0_, bf16[1024,1024]{1,0:T(8,128)(2,1)S(1)} %get-tuple-element.99.refs_1_, ...), custom_call_target="tpu_custom_call" | custom-call | flops 2147483648 | bytes 4194304 | tf_op jit(solution)/shard_map/backward_1/pallas_call | solution.py:529
  49.6 2.3 %collective-permute-start.13 = (bf16[1024,128]{1,0:T(8,128)(2,1)S(1)}, bf16[1024,128]{1,0:T(8,128)(2,1)S(1)}, u32[]{:S(2)}, u32[]{:S(2)}) collective-permute-start(bf16[1024,128]{1,0:T(8,128)(2,1)S(1)} %get-tuple-element.110), channel_id=1, source_target_pairs={{0,2},{2,3},{3,1},{1,0},{4,6},{6,7},{7,5},{5,4},{8,10},{10,11},{11... | collective-permute-start | bytes 786440 | tf_op jit(solution)/shard_map/ppermute | solution.py:25
  51.9 4.1 %backward_2.1 = (f32[1024,128]{1,0:T(8,128)S(1)}, f32[128,4096]{1,0:T(8,128)S(1)}) custom-call(s32[11]{0:T(128)S(1)} %pad_add_fusion.meta_ref, bf16[1024,3072]{1,0:T(8,128)(2,1)S(1)} %get-tuple-element.98.refs_0_, bf16[1024,1024]{1,0:T(8,128)(2,1)S(1)} %get-tuple-element.99.refs_1_, bf16[1024,4096]{1,0:T(8,128)(2,1)S(1)} %get-tuple-element.103.refs_2_.refs_0_, ...), custom_call_target="tpu_custom_call" | custom-call | flops 4294967296 | bytes 8388608 | tf_op jit(solution)/shard_map/backward_2/pallas_call | solution.py:529
  56.5 3.3 %collective-permute-start.14 = (bf16[1024,128]{1,0:T(8,128)(2,1)S(1)}, bf16[1024,128]{1,0:T(8,128)(2,1)S(1)}, u32[]{:S(2)}, u32[]{:S(2)}) collective-permute-start(bf16[1024,128]{1,0:T(8,128)(2,1)S(1)} %add_2.1), channel_id=1, source_target_pairs={{0,2},{2,3},{3,1},{1,0},{4,6},{6,7},{7,5},{5,4},{8,10},{10,11},{11... | collective-permute-start | bytes 786440 | tf_op jit(solution)/shard_map/ppermute | solution.py:25
  59.8 5.6 %backward_3.1 = (f32[1024,128]{1,0:T(8,128)S(1)}, f32[128,4096]{1,0:T(8,128)S(1)}) custom-call(s32[11]{0:T(128)S(1)} %pad_add_fusion.meta_ref, bf16[1024,4096]{1,0:T(8,128)(2,1)S(1)} %get-tuple-element.103.refs_2_.refs_0_, bf16[1024,4096]{1,0:T(8,128)(2,1)S(1)} %get-tuple-element.104.refs_1_, ...), custom_call_target="tpu_custom_call", output_to_operand_aliasing={{1}: (7, {})} | custom-call | flops 6442450944 | bytes 12582912 | tf_op jit(solution)/shard_map/backward_3/pallas_call | solution.py:529
  65.5 1.6 %backward_0_first.1 = (bf16[4,512,128]{2,1,0:T(8,128)(2,1)S(1)}, bf16[1024,2048]{1,0:T(8,128)(2,1)S(1)}) custom-call(s32[11]{0:T(128)S(1)} %pad_add_fusion.meta_ref, bf16[1024,2048]{1,0:T(8,128)(2,1)S(1)} %get-tuple-element.95.refs_0_, bf16[128,1024]{1,0:T(8,128)(2,1)S(1)} %get-tuple-element.96.refs_1_, ...), custom_call_target="tpu_custom_call" | custom-call | flops 2147483648 | bytes 4194304 | tf_op jit(solution)/shard_map/backward_0_first/pallas_call | solution.py:529
  67.2 2.0 %collective-permute-start.16 = (bf16[1024,128]{1,0:T(8,128)(2,1)S(1)}, bf16[1024,128]{1,0:T(8,128)(2,1)S(1)}, u32[]{:S(2)}, u32[]{:S(2)}) collective-permute-start(bf16[1024,128]{1,0:T(8,128)(2,1)S(1)} %add_3.1), channel_id=1, source_target_pairs={{0,2},{2,3},{3,1},{1,0},{4,6},{6,7},{7,5},{5,4},{8,10},{10,11},{11... | collective-permute-start | bytes 786440 | tf_op jit(solution)/shard_map/ppermute | solution.py:25
  69.1 1.7 %backward_0_second.1 = (f32[512,128]{1,0:T(8,128)S(1)}, f32[512,128]{1,0:T(8,128)S(1)}, f32[512,128]{1,0:T(8,128)S(1)}, f32[512,128]{1,0:T(8,128)S(1)}, bf16[1024,2048]{1,0:T(8,128)(2,1)S(1)}) custom-call(s32[11]{0:T(128)S(1)} %pad_add_fusion.meta_ref, bf16[1024,2048]{1,0:T(8,128)(2,1)S(1)} %get-tuple-element.117.refs_0_, ...), custom_call_target="tpu_custom_call" | custom-call | flops 2147483648 | bytes 4194304 | tf_op jit(solution)/shard_map/backward_0_second/pallas_call | solution.py:529
  71.5 1.5 %collective-permute-start.18 = (bf16[512,128]{1,0:T(8,128)(2,1)S(1)}, bf16[512,128]{1,0:T(8,128)(2,1)S(1)}, u32[]{:S(2)}, u32[]{:S(2)}) collective-permute-start(bf16[512,128]{1,0:T(8,128)(2,1)S(1)} %get-tuple-element.128), channel_id=1, source_target_pairs={{0,16},{4,20},{8,24},{12,28},{16,0},{20,4},{24,8},{28,12},{1,17},{... | collective-permute-start | bytes 393224 | tf_op jit(solution)/shard_map/ppermute | solution.py:19
  74.5 2.9 %backward_0.1.u_ref = f32[1024,128]{1,0:T(8,128)S(1)} custom-call(s32[11]{0:T(128)S(1)} %pad_add_fusion.meta_ref, bf16[1024,2048]{1,0:T(8,128)(2,1)S(1)} %get-tuple-element.116.first_ref, bf16[1024,2048]{1,0:T(8,128)(2,1)S(1)} %get-tuple-element.118.second_ref, bf16[4096,128]{1,0:T(8,128)(2,1)S(1)} %get-tuple-element.123.refs_2_.refs_4_.keys_ref), custom_call_target="tpu_custom_call" | custom-call | flops 2147483648 | bytes 4194304 | tf_op jit(solution)/shard_map/backward_0/pallas_call | solution.py:529
  (34 shorter events, 11.8 us)
Async XLA Ops:
  3.2 8.6 %collective-permute-start.2 = (bf16[1024,128]{1,0:T(8,128)(2,1)S(1)}, bf16[1024,128]{1,0:T(8,128)(2,1)S(1)}, u32[]{:S(2)}, u32[]{:S(2)}) collective-permute-start(bf16[1024,128]{1,0:T(8,128)(2,1)S(1)} %get-tuple-element.69.refs_2_), channel_id=1, source_target_pairs={{0,4},{4,0},{8,12},{12,8},{16,20},{20,16},{24,28},{28,24},{1,5},{5... | collective-permute-start | bytes 786440 | tf_op jit(solution)/shard_map/ppermute | solution.py:19
  3.8 9.5 %collective-permute-start.3 = (bf16[1024,128]{1,0:T(8,128)(2,1)S(1)}, bf16[1024,128]{1,0:T(8,128)(2,1)S(1)}, u32[]{:S(2)}, u32[]{:S(2)}) collective-permute-start(bf16[1024,128]{1,0:T(8,128)(2,1)S(1)} %get-tuple-element.71), channel_id=1, source_target_pairs={{0,8},{4,12},{8,0},{12,4},{16,24},{20,28},{24,16},{28,20},{1,9},{5... | collective-permute-start | bytes 786440 | tf_op jit(solution)/shard_map/ppermute | solution.py:19
  6.3 8.4 %collective-permute-start.4 = (bf16[1024,128]{1,0:T(8,128)(2,1)S(1)}, bf16[1024,128]{1,0:T(8,128)(2,1)S(1)}, u32[]{:S(2)}, u32[]{:S(2)}) collective-permute-start(bf16[1024,128]{1,0:T(8,128)(2,1)S(1)} %get-tuple-element.72), channel_id=1, source_target_pairs={{0,16},{4,20},{8,24},{12,28},{16,0},{20,4},{24,8},{28,12},{1,17},{... | collective-permute-start | bytes 786440 | tf_op jit(solution)/shard_map/ppermute | solution.py:19
  7.9 10.4 %collective-permute-start = (bf16[1040,128]{1,0:T(8,128)(2,1)S(1)}, bf16[1040,128]{1,0:T(8,128)(2,1)S(1)}, u32[]{:S(2)}, u32[]{:S(2)}) collective-permute-start(bf16[1040,128]{1,0:T(8,128)(2,1)S(1)} %get-tuple-element.92.refs_0_.q_ref), channel_id=1, source_target_pairs={{0,2},{2,3},{3,1},{1,0},{4,6},{6,7},{7,5},{5,4},{8,10},{10,11},{11... | collective-permute-start | bytes 798728 | tf_op jit(solution)/shard_map/ppermute | solution.py:25
  14.7 3.6 %collective-permute-start.5 = (bf16[1024,128]{1,0:T(8,128)(2,1)S(1)}, bf16[1024,128]{1,0:T(8,128)(2,1)S(1)}, u32[]{:S(2)}, u32[]{:S(2)}) collective-permute-start(bf16[1024,128]{1,0:T(8,128)(2,1)S(1)} %collective-permute-done.3.refs_9_), channel_id=1, source_target_pairs={{0,4},{4,0},{8,12},{12,8},{16,20},{20,16},{24,28},{28,24},{1,5},{5... | collective-permute-start | bytes 786440 | tf_op jit(solution)/shard_map/ppermute | solution.py:19
  14.7 3.6 %collective-permute-start.6 = (bf16[1024,128]{1,0:T(8,128)(2,1)S(1)}, bf16[1024,128]{1,0:T(8,128)(2,1)S(1)}, u32[]{:S(2)}, u32[]{:S(2)}) collective-permute-start(bf16[1024,128]{1,0:T(8,128)(2,1)S(1)} %collective-permute-done.4.refs_10_), channel_id=1, source_target_pairs={{0,4},{4,0},{8,12},{12,8},{16,20},{20,16},{24,28},{28,24},{1,5},{5... | collective-permute-start | bytes 786440 | tf_op jit(solution)/shard_map/ppermute | solution.py:19
  15.2 9.1 %collective-permute-start.8 = (bf16[1024,128]{1,0:T(8,128)(2,1)S(1)}, bf16[1024,128]{1,0:T(8,128)(2,1)S(1)}, u32[]{:S(2)}, u32[]{:S(2)}) collective-permute-start(bf16[1024,128]{1,0:T(8,128)(2,1)S(1)} %get-tuple-element.82), channel_id=1, source_target_pairs={{0,24},{4,28},{8,16},{12,20},{16,8},{20,12},{24,0},{28,4},{1,25},{... | collective-permute-start | bytes 786440 | tf_op jit(solution)/shard_map/ppermute | solution.py:19
  16.7 10.2 %collective-permute-start.7 = (bf16[1040,128]{1,0:T(8,128)(2,1)S(1)}, bf16[1040,128]{1,0:T(8,128)(2,1)S(1)}, u32[]{:S(2)}, u32[]{:S(2)}) collective-permute-start(bf16[1040,128]{1,0:T(8,128)(2,1)S(1)} %get-tuple-element.92.refs_0_.q_ref), channel_id=1, source_target_pairs={{0,1},{2,0},{3,2},{1,3},{4,5},{6,4},{7,6},{5,7},{8,9},{10,8},{11,1... | collective-permute-start | bytes 798728 | tf_op jit(solution)/shard_map/ppermute | solution.py:25
  24.3 2.6 %collective-permute-start.9 = (bf16[1024,128]{1,0:T(8,128)(2,1)S(1)}, bf16[1024,128]{1,0:T(8,128)(2,1)S(1)}, u32[]{:S(2)}, u32[]{:S(2)}) collective-permute-start(bf16[1024,128]{1,0:T(8,128)(2,1)S(1)} %collective-permute-done.8.refs_10_), channel_id=1, source_target_pairs={{0,4},{4,0},{8,12},{12,8},{16,20},{20,16},{24,28},{28,24},{1,5},{5... | collective-permute-start | bytes 786440 | tf_op jit(solution)/shard_map/ppermute | solution.py:19
  24.3 8.9 %collective-permute-start.1 = (bf16[1040,128]{1,0:T(8,128)(2,1)S(1)}, bf16[1040,128]{1,0:T(8,128)(2,1)S(1)}, u32[]{:S(2)}, u32[]{:S(2)}) collective-permute-start(bf16[1040,128]{1,0:T(8,128)(2,1)S(1)} %collective-permute-done.refs_1_), channel_id=1, source_target_pairs={{0,2},{2,3},{3,1},{1,0},{4,6},{6,7},{7,5},{5,4},{8,10},{10,11},{11... | collective-permute-start | bytes 798728 | tf_op jit(solution)/shard_map/ppermute | solution.py:25
  38.3 7.3 %collective-permute-start.12 = (f32[1,8,128]{2,1,0:T(8,128)S(1)}, f32[1,8,128]{2,1,0:T(8,128)S(1)}, u32[]{:S(2)}, u32[]{:S(2)}) collective-permute-start(f32[1,8,128]{2,1,0:T(8,128)S(1)} %get-tuple-element.91.refs_3_), channel_id=1, source_target_pairs={{0,3},{1,2},{2,1},{3,0},{4,7},{5,6},{6,5},{7,4},{8,11},{9,10},{10,... | collective-permute-start | bytes 12296 | tf_op jit(solution)/shard_map/ppermute | solution.py:19
  41.8 4.5 %collective-permute-start.11 = (f32[1,8,128]{2,1,0:T(8,128)S(1)}, f32[1,8,128]{2,1,0:T(8,128)S(1)}, u32[]{:S(2)}, u32[]{:S(2)}) collective-permute-start(f32[1,8,128]{2,1,0:T(8,128)S(1)} %get-tuple-element.91.refs_3_), channel_id=1, source_target_pairs={{0,2},{1,3},{2,0},{3,1},{4,6},{5,7},{6,4},{7,5},{8,10},{9,11},{10,... | collective-permute-start | bytes 12296 | tf_op jit(solution)/shard_map/ppermute | solution.py:19
  42.1 4.2 %collective-permute-start.10 = (f32[1,8,128]{2,1,0:T(8,128)S(1)}, f32[1,8,128]{2,1,0:T(8,128)S(1)}, u32[]{:S(2)}, u32[]{:S(2)}) collective-permute-start(f32[1,8,128]{2,1,0:T(8,128)S(1)} %get-tuple-element.91.refs_3_), channel_id=1, source_target_pairs={{0,1},{1,0},{2,3},{3,2},{4,5},{5,4},{6,7},{7,6},{8,9},{9,8},{10,11... | collective-permute-start | bytes 12296 | tf_op jit(solution)/shard_map/ppermute | solution.py:19
  49.6 6.8 %collective-permute-start.13 = (bf16[1024,128]{1,0:T(8,128)(2,1)S(1)}, bf16[1024,128]{1,0:T(8,128)(2,1)S(1)}, u32[]{:S(2)}, u32[]{:S(2)}) collective-permute-start(bf16[1024,128]{1,0:T(8,128)(2,1)S(1)} %get-tuple-element.110), channel_id=1, source_target_pairs={{0,2},{2,3},{3,1},{1,0},{4,6},{6,7},{7,5},{5,4},{8,10},{10,11},{11... | collective-permute-start | bytes 786440 | tf_op jit(solution)/shard_map/ppermute | solution.py:25
  56.5 8.9 %collective-permute-start.14 = (bf16[1024,128]{1,0:T(8,128)(2,1)S(1)}, bf16[1024,128]{1,0:T(8,128)(2,1)S(1)}, u32[]{:S(2)}, u32[]{:S(2)}) collective-permute-start(bf16[1024,128]{1,0:T(8,128)(2,1)S(1)} %add_2.1), channel_id=1, source_target_pairs={{0,2},{2,3},{3,1},{1,0},{4,6},{6,7},{7,5},{5,4},{8,10},{10,11},{11... | collective-permute-start | bytes 786440 | tf_op jit(solution)/shard_map/ppermute | solution.py:25
  67.1 3.7 %collective-permute-start.15 = (bf16[4,512,128]{2,1,0:T(8,128)(2,1)S(1)}, bf16[4,512,128]{2,1,0:T(8,128)(2,1)S(1)}, u32[]{:S(2)}, u32[]{:S(2)}) collective-permute-start(bf16[4,512,128]{2,1,0:T(8,128)(2,1)S(1)} %get-tuple-element.120), channel_id=1, source_target_pairs={{0,4},{4,0},{8,12},{12,8},{16,20},{20,16},{24,28},{28,24},{1,5},{5... | collective-permute-start | bytes 1572872 | tf_op jit(solution)/shard_map/ppermute | solution.py:19
  67.2 10.2 %collective-permute-start.16 = (bf16[1024,128]{1,0:T(8,128)(2,1)S(1)}, bf16[1024,128]{1,0:T(8,128)(2,1)S(1)}, u32[]{:S(2)}, u32[]{:S(2)}) collective-permute-start(bf16[1024,128]{1,0:T(8,128)(2,1)S(1)} %add_3.1), channel_id=1, source_target_pairs={{0,2},{2,3},{3,1},{1,0},{4,6},{6,7},{7,5},{5,4},{8,10},{10,11},{11... | collective-permute-start | bytes 786440 | tf_op jit(solution)/shard_map/ppermute | solution.py:25
  70.9 7.8 %collective-permute-start.17 = (bf16[512,128]{1,0:T(8,128)(2,1)S(1)}, bf16[512,128]{1,0:T(8,128)(2,1)S(1)}, u32[]{:S(2)}, u32[]{:S(2)}) collective-permute-start(bf16[512,128]{1,0:T(8,128)(2,1)S(1)} %get-tuple-element.127), channel_id=1, source_target_pairs={{0,8},{4,12},{8,0},{12,4},{16,24},{20,28},{24,16},{28,20},{1,9},{5... | collective-permute-start | bytes 393224 | tf_op jit(solution)/shard_map/ppermute | solution.py:19
  71.5 7.2 %collective-permute-start.18 = (bf16[512,128]{1,0:T(8,128)(2,1)S(1)}, bf16[512,128]{1,0:T(8,128)(2,1)S(1)}, u32[]{:S(2)}, u32[]{:S(2)}) collective-permute-start(bf16[512,128]{1,0:T(8,128)(2,1)S(1)} %get-tuple-element.128), channel_id=1, source_target_pairs={{0,16},{4,20},{8,24},{12,28},{16,0},{20,4},{24,8},{28,12},{1,17},{... | collective-permute-start | bytes 393224 | tf_op jit(solution)/shard_map/ppermute | solution.py:19
  73.0 7.0 %collective-permute-start.19 = (bf16[512,128]{1,0:T(8,128)(2,1)S(1)}, bf16[512,128]{1,0:T(8,128)(2,1)S(1)}, u32[]{:S(2)}, u32[]{:S(2)}) collective-permute-start(bf16[512,128]{1,0:T(8,128)(2,1)S(1)} %get-tuple-element.129), channel_id=1, source_target_pairs={{0,24},{4,28},{8,16},{12,20},{16,8},{20,12},{24,0},{28,4},{1,25},{... | collective-permute-start | bytes 393224 | tf_op jit(solution)/shard_map/ppermute | solution.py:19

commit v10 on v9

--- a/solution.py
+++ b/solution.py
@@ -86,7 +86,7 @@
     order, nh, rows_here, hh, depth, kc, chunk, scale = cfg
     rows = rows_here * hh
     side = min(256, count)
-    tile = next(size * side for size in (8, 6, 4, 2, 1) if count % (size * side) == 0)
+    tile = next(size * side for size in (16, 12, 8, 6, 4, 2, 1) if count % (size * side) == 0)
 
     def step(s, _):
         for first in range(0, tile, side):
@@ -399,7 +399,7 @@
     rows = rows_here * hh
     parts = chunk // lanes
     message_ref, rw_out_ref, key_refs = refs[0], refs[1], refs[2 : 2 + sends]
-    wide, sems = refs[-2], refs[-1]
+    query_here, weights_here, rw_here, wide, sems = refs[-5:]
     share = pl.multiple_of(lax.axis_index("head") * chunk, chunk)
     copies = []
 
@@ -407,6 +407,9 @@
         copies.append(pltpu.make_async_copy(source, target, sems.at[len(copies)]))
         copies[-1].start()
 
+    copy(query_ref, query_here)
+    copy(rw_ref, rw_here)
+    copy(weights_ref, weights_here)
     for i in reversed(range(sends)):
         copy(keys_ref.at[pl.ds(share, chunk), :], key_refs[i].at[:chunk, :])
         for core in range(2):
@@ -417,17 +420,19 @@
                     logits_ref.at[pl.ds(row, rows_here), pl.ds(share + part * lanes, lanes)],
                     key_refs[i].at[first : first + rows_here, :],
                 )
-    every = jnp.broadcast_to(rw_ref[...], (8, rw_ref.shape[1]))
+    for item in copies[:3]:
+        item.wait()
+    every = jnp.broadcast_to(rw_here[...], (8, rw_here.shape[1]))
     shift = every.shape[1] - lax.axis_index("ctx") * rows_here
     here = pltpu.roll(every, shift, 1)[:1, : rw_out_ref.shape[1]]
     rw_out_ref[...] = here * float(kc * len(order)) ** 0.5
-    wide[...] = query_ref[...].astype(jnp.float32)
+    wide[...] = query_here[...].astype(jnp.float32)
     for head in range(hh):
         at = slice(head * rows_here, (head + 1) * rows_here)
         message_ref[at, :] = wide[:, head, :].astype(jnp.bfloat16)
     message_ref[rows:, :] = jnp.zeros((message_ref.shape[0] - rows, lanes), jnp.bfloat16)
-    message_ref[rows : rows + hh, :rows_here] = weights_ref[...]
-    for item in copies:
+    message_ref[rows : rows + hh, :rows_here] = weights_here[...]
+    for item in copies[3:]:
         item.wait()
 
 
@@ -495,11 +500,14 @@
             jax.ShapeDtypeStruct((1, padded), f32),
         ]
         + [jax.ShapeDtypeStruct((chunk + 2 * parts * rows_here, depth), bf16)] * (n // 2),
-        in_specs=[vmem, vmem, vmem] + [pl.BlockSpec(memory_space=pltpu.HBM)] * 2,
+        in_specs=[pl.BlockSpec(memory_space=pltpu.HBM)] * 5,
         out_specs=[vmem] * (2 + n // 2),
         scratch_shapes=[
+            pltpu.VMEM((rows_here, hh, depth), bf16),
+            pltpu.VMEM((hh, rows_here), bf16),
+            pltpu.VMEM((1, rows_here * n), f32),
             pltpu.VMEM((rows_here, hh, depth), f32),
-            pltpu.SemaphoreType.DMA((n // 2 * (1 + 2 * parts),)),
+            pltpu.SemaphoreType.DMA((3 + n // 2 * (1 + 2 * parts),)),
         ],
         compiler_params=pltpu.CompilerParams(vmem_limit_bytes=vmem_bytes),
         cost_estimate=pl.CostEstimate(

time: 81 us -> 79.6 us (0.983)
  Pallas kernels: 42.6 us -> 39.2 us
  waiting for transfers between devices: 6.23 us -> 8.35 us
    pallas_call x11, Pallas kernels: 38.5 us -> 35.8 us  [call(): pl.pallas_call(kernel, out_shape=out_shape, input_output_aliases=aliases,...]
    ppermute x6, waiting for transfers between devices: 1.18 us -> 2.44 us  [ring_next(): lax.ppermute(value, axis, [(ring[i], ring[(i + hop) % size]) for i in ran...]
    ppermute x14, waiting for transfers between devices: 5.06 us -> 5.91 us  [swap(): return lax.ppermute(value, axis, [(i, i ^ distance) for i in range(size)])]
  transfers between devices with their start and end apart: 20 -> 20, of which waited for: 6 -> 6; matrix products, arithmetic and copies ran while one was open for 1% -> 1% of each run, Pallas kernels for 37% -> 35%
where the time goes in v10:
time: 79.6 us; the launch traced here: 79.4 us
  Pallas kernels  39.2 us (49%)
  starting transfers between devices  28.8 us (36%)
  waiting for transfers between devices  8.35 us (10%)
  other arithmetic  1.62 us (2%)
  between operations  1.43 us (2%)
    pallas_call x11, Pallas kernels, call(): pl.pallas_call(kernel, out_shape=out_shape, input_output_aliases=aliases,...  35.8 us
    ppermute x14, starting transfers between devices, swap(): return lax.ppermute(value, axis, [(i, i ^ distance) for i in range(size)])  14.7 us
    ppermute x6, starting transfers between devices, ring_next(): lax.ppermute(value, axis, [(ring[i], ring[(i + hop) % size]) for i in ran...  14.1 us
    ppermute x14, waiting for transfers between devices, swap(): return lax.ppermute(value, axis, [(i, i ^ distance) for i in range(size)])  5.91 us
    ppermute x6, waiting for transfers between devices, ring_next(): lax.ppermute(value, axis, [(ring[i], ring[(i + hop) % size]) for i in ran...  2.44 us
    pallas_call x1, Pallas kernels, per_device(): pl.pallas_call(functools.partial(prepare_kernel, cfg), out_shape=[jax.Sha...  2.03 us
  transfers between devices with their start and end apart: 20, of which 6 were waited for; matrix products, arithmetic and copies ran while one was open for 1% of the time, Pallas kernels for 35%

profile of v10, /device:TPU:0, one launch (start us, length us, event | category | flops | bytes accessed | tf_op | source)
XLA Modules:
  0.0 79.4 jit_solution(17974878253919437987)
XLA Ops:
  0.6 2.0 %prepare.1 = (bf16[1040,128]{1,0:T(8,128)(2,1)S(1)}, f32[1,128]{1,0:T(1,128)S(1)}, bf16[1024,128]{1,0:T(8,128)(2,1)S(1)}, bf16[1024,128]{1,0:T(8,128)(2,1)S(1)},...) custom-call(bf16[64,16,128]{2,1,0:T(8,128)(2,1)} %query_ref.1, bf16[16,64]{1,0:T(8,128)(2,1)} %bitcast.25, ...), custom_call_target="tpu_custom_call" | custom-call | flops 131072 | bytes 4194304 | tf_op jit(solution)/shard_map/prepare/pallas_call | solution.py:496
  3.2 2.6 %collective-permute-start.3 = (bf16[1024,128]{1,0:T(8,128)(2,1)S(1)}, bf16[1024,128]{1,0:T(8,128)(2,1)S(1)}, u32[]{:S(2)}, u32[]{:S(2)}) collective-permute-start(bf16[1024,128]{1,0:T(8,128)(2,1)S(1)} %get-tuple-element.71), channel_id=1, source_target_pairs={{0,8},{4,12},{8,0},{12,4},{16,24},{20,28},{24,16},{28,20},{1,9},{5... | collective-permute-start | bytes 786440 | tf_op jit(solution)/shard_map/ppermute | solution.py:19
  5.8 1.5 %collective-permute-start.4 = (bf16[1024,128]{1,0:T(8,128)(2,1)S(1)}, bf16[1024,128]{1,0:T(8,128)(2,1)S(1)}, u32[]{:S(2)}, u32[]{:S(2)}) collective-permute-start(bf16[1024,128]{1,0:T(8,128)(2,1)S(1)} %get-tuple-element.72), channel_id=1, source_target_pairs={{0,16},{4,20},{8,24},{12,28},{16,0},{20,4},{24,8},{28,12},{1,17},{... | collective-permute-start | bytes 786440 | tf_op jit(solution)/shard_map/ppermute | solution.py:19
  7.3 2.6 %collective-permute-start = (bf16[1040,128]{1,0:T(8,128)(2,1)S(1)}, bf16[1040,128]{1,0:T(8,128)(2,1)S(1)}, u32[]{:S(2)}, u32[]{:S(2)}) collective-permute-start(bf16[1040,128]{1,0:T(8,128)(2,1)S(1)} %get-tuple-element.92.refs_0_.q_ref), channel_id=1, source_target_pairs={{0,2},{2,3},{3,1},{1,0},{4,6},{6,7},{7,5},{5,4},{8,10},{10,11},{11... | collective-permute-start | bytes 798728 | tf_op jit(solution)/shard_map/ppermute | solution.py:25
  14.6 1.5 %collective-permute-start.8 = (bf16[1024,128]{1,0:T(8,128)(2,1)S(1)}, bf16[1024,128]{1,0:T(8,128)(2,1)S(1)}, u32[]{:S(2)}, u32[]{:S(2)}) collective-permute-start(bf16[1024,128]{1,0:T(8,128)(2,1)S(1)} %get-tuple-element.82), channel_id=1, source_target_pairs={{0,24},{4,28},{8,16},{12,20},{16,8},{20,12},{24,0},{28,4},{1,25},{... | collective-permute-start | bytes 786440 | tf_op jit(solution)/shard_map/ppermute | solution.py:19
  16.1 1.6 %collective-permute-start.7 = (bf16[1040,128]{1,0:T(8,128)(2,1)S(1)}, bf16[1040,128]{1,0:T(8,128)(2,1)S(1)}, u32[]{:S(2)}, u32[]{:S(2)}) collective-permute-start(bf16[1040,128]{1,0:T(8,128)(2,1)S(1)} %get-tuple-element.92.refs_0_.q_ref), channel_id=1, source_target_pairs={{0,1},{2,0},{3,2},{1,3},{4,5},{6,4},{7,6},{5,7},{8,9},{10,8},{11,1... | collective-permute-start | bytes 798728 | tf_op jit(solution)/shard_map/ppermute | solution.py:25
  17.7 3.7 %forward_early_1.1 = (f32[64,3072]{1,0:T(8,128)S(1)}, bf16[3072,128]{1,0:T(8,128)(2,1)S(1)}, bf16[128,3072]{1,0:T(8,128)(2,1)S(1)}, bf16[64,3072]{1,0:T(8,128)(2...) custom-call(s32[11]{0:T(128)S(1)} %pad_add_fusion.meta_ref, ...), custom_call_target="tpu_custom_call" | custom-call | flops 2147483 | bytes 4194 | tf_op jit(solution)/shard_map/forward_early_1/pallas_call | solution.py:537
  21.4 2.3 %collective-permute-done.8.refs_10_ = bf16[1024,128]{1,0:T(8,128)(2,1)S(1)} collective-permute-done((bf16[1024,128]{1,0:T(8,128)(2,1)S(1)}, bf16[1024,128]{1,0:T(8,128)(2,1)S(1)}, u32[]{:S(2)}, u32[]{:S(2)}) %collective-permute-start.8) | collective-permute-done | bytes 262176 | tf_op jit(solution)/shard_map/ppermute | solution.py:19
  23.8 2.6 %collective-permute-start.1 = (bf16[1040,128]{1,0:T(8,128)(2,1)S(1)}, bf16[1040,128]{1,0:T(8,128)(2,1)S(1)}, u32[]{:S(2)}, u32[]{:S(2)}) collective-permute-start(bf16[1040,128]{1,0:T(8,128)(2,1)S(1)} %collective-permute-done.refs_1_), channel_id=1, source_target_pairs={{0,2},{2,3},{3,1},{1,0},{4,6},{6,7},{7,5},{5,4},{8,10},{10,11},{11... | collective-permute-start | bytes 798728 | tf_op jit(solution)/shard_map/ppermute | solution.py:25
  26.4 4.2 %forward_middle.1 = (f32[64,4096]{1,0:T(8,128)S(1)}, bf16[4096,128]{1,0:T(8,128)(2,1)S(1)}, bf16[128,4096]{1,0:T(8,128)(2,1)S(1)}, bf16[64,4096]{1,0:T(8,128)(2,...) custom-call(s32[11]{0:T(128)S(1)} %pad_add_fusion.meta_ref, ...), custom_call_target="tpu_custom_call" | custom-call | flops 3221225472 | bytes 6291456 | tf_op jit(solution)/shard_map/forward_middle/pallas_call | solution.py:537
  30.6 2.1 %collective-permute-done.1.refs_0_ = bf16[1040,128]{1,0:T(8,128)(2,1)S(1)} collective-permute-done((bf16[1040,128]{1,0:T(8,128)(2,1)S(1)}, bf16[1040,128]{1,0:T(8,128)(2,1)S(1)}, u32[]{:S(2)}, u32[]{:S(2)}) %collective-permute-start.1) | collective-permute-done | bytes 266272 | tf_op jit(solution)/shard_map/ppermute | solution.py:25
  32.7 4.1 %forward_last.1 = (f32[64,4096]{1,0:T(8,128)S(1)}, bf16[1024,4096]{1,0:T(8,128)(2,1)S(1)}, bf16[128,1024]{1,0:T(8,128)(2,1)S(1)}, f32[1,8,128]{2,1,0:T(8,128)S(1)}) custom-call(s32[11]{0:T(128)S(1)} %pad_add_fusion.meta_ref, bf16[1040,128]{1,0:T(8,128)(2,1)S(1)} %collective-permute-done.1.refs_0_, ...), custom_call_target="tpu_custom_call", output_to_operand_aliasing={{0}: (3, {})} | custom-call | flops 2147483648 | bytes 4194304 | tf_op jit(solution)/shard_map/forward_last/pallas_call | solution.py:537
  36.8 3.6 %collective-permute-start.12 = (f32[1,8,128]{2,1,0:T(8,128)S(1)}, f32[1,8,128]{2,1,0:T(8,128)S(1)}, u32[]{:S(2)}, u32[]{:S(2)}) collective-permute-start(f32[1,8,128]{2,1,0:T(8,128)S(1)} %get-tuple-element.91.refs_3_), channel_id=1, source_target_pairs={{0,3},{1,2},{2,1},{3,0},{4,7},{5,6},{6,5},{7,4},{8,11},{9,10},{10,... | collective-permute-start | bytes 12296 | tf_op jit(solution)/shard_map/ppermute | solution.py:19
  41.2 2.9 %own_active.1 = (bf16[1024,2048]{1,0:T(8,128)(2,1)S(1)}, bf16[1024,2048]{1,0:T(8,128)(2,1)S(1)}) custom-call(s32[11]{0:T(128)S(1)} %pad_add_fusion.meta_ref, bf16[1040,128]{1,0:T(8,128)(2,1)S(1)} %get-tuple-element.92.refs_0_.q_ref, bf16[128,4096]{1,0:T(8,128)(2,1)S(1)} %get-tuple-element.88.refs_1_.keys_t_ref), custom_call_target="tpu_custom_call" | custom-call | flops 2147483648 | bytes 4194304 | tf_op jit(solution)/shard_map/own_active/pallas_call | solution.py:537
  44.9 3.6 %backward_1.1 = (bf16[1024,128]{1,0:T(8,128)(2,1)S(1)}, bf16[64,4096]{1,0:T(8,128)(2,1)S(1)}) custom-call(s32[11]{0:T(128)S(1)} %pad_add_fusion.meta_ref, bf16[1024,3072]{1,0:T(8,128)(2,1)S(1)} %get-tuple-element.98.refs_0_, bf16[1024,1024]{1,0:T(8,128)(2,1)S(1)} %get-tuple-element.99.refs_1_, ...), custom_call_target="tpu_custom_call" | custom-call | flops 2147483648 | bytes 4194304 | tf_op jit(solution)/shard_map/backward_1/pallas_call | solution.py:537
  48.4 2.1 %collective-permute-start.13 = (bf16[1024,128]{1,0:T(8,128)(2,1)S(1)}, bf16[1024,128]{1,0:T(8,128)(2,1)S(1)}, u32[]{:S(2)}, u32[]{:S(2)}) collective-permute-start(bf16[1024,128]{1,0:T(8,128)(2,1)S(1)} %get-tuple-element.110), channel_id=1, source_target_pairs={{0,2},{2,3},{3,1},{1,0},{4,6},{6,7},{7,5},{5,4},{8,10},{10,11},{11... | collective-permute-start | bytes 786440 | tf_op jit(solution)/shard_map/ppermute | solution.py:25
  50.5 4.1 %backward_2.1 = (f32[1024,128]{1,0:T(8,128)S(1)}, f32[128,4096]{1,0:T(8,128)S(1)}) custom-call(s32[11]{0:T(128)S(1)} %pad_add_fusion.meta_ref, bf16[1024,3072]{1,0:T(8,128)(2,1)S(1)} %get-tuple-element.98.refs_0_, bf16[1024,1024]{1,0:T(8,128)(2,1)S(1)} %get-tuple-element.99.refs_1_, bf16[1024,4096]{1,0:T(8,128)(2,1)S(1)} %get-tuple-element.103.refs_2_.refs_0_, ...), custom_call_target="tpu_custom_call" | custom-call | flops 4294967296 | bytes 8388608 | tf_op jit(solution)/shard_map/backward_2/pallas_call | solution.py:537
  55.0 3.3 %collective-permute-start.14 = (bf16[1024,128]{1,0:T(8,128)(2,1)S(1)}, bf16[1024,128]{1,0:T(8,128)(2,1)S(1)}, u32[]{:S(2)}, u32[]{:S(2)}) collective-permute-start(bf16[1024,128]{1,0:T(8,128)(2,1)S(1)} %add_2.1), channel_id=1, source_target_pairs={{0,2},{2,3},{3,1},{1,0},{4,6},{6,7},{7,5},{5,4},{8,10},{10,11},{11... | collective-permute-start | bytes 786440 | tf_op jit(solution)/shard_map/ppermute | solution.py:25
  58.3 5.6 %backward_3.1 = (f32[1024,128]{1,0:T(8,128)S(1)}, f32[128,4096]{1,0:T(8,128)S(1)}) custom-call(s32[11]{0:T(128)S(1)} %pad_add_fusion.meta_ref, bf16[1024,4096]{1,0:T(8,128)(2,1)S(1)} %get-tuple-element.103.refs_2_.refs_0_, bf16[1024,4096]{1,0:T(8,128)(2,1)S(1)} %get-tuple-element.104.refs_1_, ...), custom_call_target="tpu_custom_call", output_to_operand_aliasing={{1}: (7, {})} | custom-call | flops 6442450944 | bytes 12582912 | tf_op jit(solution)/shard_map/backward_3/pallas_call | solution.py:537
  64.0 1.6 %backward_0_first.1 = (bf16[4,512,128]{2,1,0:T(8,128)(2,1)S(1)}, bf16[1024,2048]{1,0:T(8,128)(2,1)S(1)}) custom-call(s32[11]{0:T(128)S(1)} %pad_add_fusion.meta_ref, bf16[1024,2048]{1,0:T(8,128)(2,1)S(1)} %get-tuple-element.95.refs_0_, bf16[128,1024]{1,0:T(8,128)(2,1)S(1)} %get-tuple-element.96.refs_1_, ...), custom_call_target="tpu_custom_call" | custom-call | flops 2147483648 | bytes 4194304 | tf_op jit(solution)/shard_map/backward_0_first/pallas_call | solution.py:537
  65.7 2.0 %collective-permute-start.16 = (bf16[1024,128]{1,0:T(8,128)(2,1)S(1)}, bf16[1024,128]{1,0:T(8,128)(2,1)S(1)}, u32[]{:S(2)}, u32[]{:S(2)}) collective-permute-start(bf16[1024,128]{1,0:T(8,128)(2,1)S(1)} %add_3.1), channel_id=1, source_target_pairs={{0,2},{2,3},{3,1},{1,0},{4,6},{6,7},{7,5},{5,4},{8,10},{10,11},{11... | collective-permute-start | bytes 786440 | tf_op jit(solution)/shard_map/ppermute | solution.py:25
  67.7 1.7 %backward_0_second.1 = (f32[512,128]{1,0:T(8,128)S(1)}, f32[512,128]{1,0:T(8,128)S(1)}, f32[512,128]{1,0:T(8,128)S(1)}, f32[512,128]{1,0:T(8,128)S(1)}, bf16[1024,2048]{1,0:T(8,128)(2,1)S(1)}) custom-call(s32[11]{0:T(128)S(1)} %pad_add_fusion.meta_ref, bf16[1024,2048]{1,0:T(8,128)(2,1)S(1)} %get-tuple-element.117.refs_0_, ...), custom_call_target="tpu_custom_call" | custom-call | flops 2147483648 | bytes 4194304 | tf_op jit(solution)/shard_map/backward_0_second/pallas_call | solution.py:537
  70.1 1.5 %collective-permute-start.18 = (bf16[512,128]{1,0:T(8,128)(2,1)S(1)}, bf16[512,128]{1,0:T(8,128)(2,1)S(1)}, u32[]{:S(2)}, u32[]{:S(2)}) collective-permute-start(bf16[512,128]{1,0:T(8,128)(2,1)S(1)} %get-tuple-element.128), channel_id=1, source_target_pairs={{0,16},{4,20},{8,24},{12,28},{16,0},{20,4},{24,8},{28,12},{1,17},{... | collective-permute-start | bytes 393224 | tf_op jit(solution)/shard_map/ppermute | solution.py:19
  73.0 2.9 %backward_0.1.u_ref = f32[1024,128]{1,0:T(8,128)S(1)} custom-call(s32[11]{0:T(128)S(1)} %pad_add_fusion.meta_ref, bf16[1024,2048]{1,0:T(8,128)(2,1)S(1)} %get-tuple-element.116.first_ref, bf16[1024,2048]{1,0:T(8,128)(2,1)S(1)} %get-tuple-element.118.second_ref, bf16[4096,128]{1,0:T(8,128)(2,1)S(1)} %get-tuple-element.123.refs_2_.refs_4_.keys_ref), custom_call_target="tpu_custom_call" | custom-call | flops 2147483648 | bytes 4194304 | tf_op jit(solution)/shard_map/backward_0/pallas_call | solution.py:537
  (34 shorter events, 12.4 us)
Async XLA Ops:
  2.7 8.6 %collective-permute-start.2 = (bf16[1024,128]{1,0:T(8,128)(2,1)S(1)}, bf16[1024,128]{1,0:T(8,128)(2,1)S(1)}, u32[]{:S(2)}, u32[]{:S(2)}) collective-permute-start(bf16[1024,128]{1,0:T(8,128)(2,1)S(1)} %get-tuple-element.69.refs_2_), channel_id=1, source_target_pairs={{0,4},{4,0},{8,12},{12,8},{16,20},{20,16},{24,28},{28,24},{1,5},{5... | collective-permute-start | bytes 786440 | tf_op jit(solution)/shard_map/ppermute | solution.py:19
  3.2 9.5 %collective-permute-start.3 = (bf16[1024,128]{1,0:T(8,128)(2,1)S(1)}, bf16[1024,128]{1,0:T(8,128)(2,1)S(1)}, u32[]{:S(2)}, u32[]{:S(2)}) collective-permute-start(bf16[1024,128]{1,0:T(8,128)(2,1)S(1)} %get-tuple-element.71), channel_id=1, source_target_pairs={{0,8},{4,12},{8,0},{12,4},{16,24},{20,28},{24,16},{28,20},{1,9},{5... | collective-permute-start | bytes 786440 | tf_op jit(solution)/shard_map/ppermute | solution.py:19
  5.8 8.4 %collective-permute-start.4 = (bf16[1024,128]{1,0:T(8,128)(2,1)S(1)}, bf16[1024,128]{1,0:T(8,128)(2,1)S(1)}, u32[]{:S(2)}, u32[]{:S(2)}) collective-permute-start(bf16[1024,128]{1,0:T(8,128)(2,1)S(1)} %get-tuple-element.72), channel_id=1, source_target_pairs={{0,16},{4,20},{8,24},{12,28},{16,0},{20,4},{24,8},{28,12},{1,17},{... | collective-permute-start | bytes 786440 | tf_op jit(solution)/shard_map/ppermute | solution.py:19
  7.3 10.4 %collective-permute-start = (bf16[1040,128]{1,0:T(8,128)(2,1)S(1)}, bf16[1040,128]{1,0:T(8,128)(2,1)S(1)}, u32[]{:S(2)}, u32[]{:S(2)}) collective-permute-start(bf16[1040,128]{1,0:T(8,128)(2,1)S(1)} %get-tuple-element.92.refs_0_.q_ref), channel_id=1, source_target_pairs={{0,2},{2,3},{3,1},{1,0},{4,6},{6,7},{7,5},{5,4},{8,10},{10,11},{11... | collective-permute-start | bytes 798728 | tf_op jit(solution)/shard_map/ppermute | solution.py:25
  14.1 3.6 %collective-permute-start.5 = (bf16[1024,128]{1,0:T(8,128)(2,1)S(1)}, bf16[1024,128]{1,0:T(8,128)(2,1)S(1)}, u32[]{:S(2)}, u32[]{:S(2)}) collective-permute-start(bf16[1024,128]{1,0:T(8,128)(2,1)S(1)} %collective-permute-done.3.refs_9_), channel_id=1, source_target_pairs={{0,4},{4,0},{8,12},{12,8},{16,20},{20,16},{24,28},{28,24},{1,5},{5... | collective-permute-start | bytes 786440 | tf_op jit(solution)/shard_map/ppermute | solution.py:19
  14.1 3.6 %collective-permute-start.6 = (bf16[1024,128]{1,0:T(8,128)(2,1)S(1)}, bf16[1024,128]{1,0:T(8,128)(2,1)S(1)}, u32[]{:S(2)}, u32[]{:S(2)}) collective-permute-start(bf16[1024,128]{1,0:T(8,128)(2,1)S(1)} %collective-permute-done.4.refs_10_), channel_id=1, source_target_pairs={{0,4},{4,0},{8,12},{12,8},{16,20},{20,16},{24,28},{28,24},{1,5},{5... | collective-permute-start | bytes 786440 | tf_op jit(solution)/shard_map/ppermute | solution.py:19
  14.6 9.1 %collective-permute-start.8 = (bf16[1024,128]{1,0:T(8,128)(2,1)S(1)}, bf16[1024,128]{1,0:T(8,128)(2,1)S(1)}, u32[]{:S(2)}, u32[]{:S(2)}) collective-permute-start(bf16[1024,128]{1,0:T(8,128)(2,1)S(1)} %get-tuple-element.82), channel_id=1, source_target_pairs={{0,24},{4,28},{8,16},{12,20},{16,8},{20,12},{24,0},{28,4},{1,25},{... | collective-permute-start | bytes 786440 | tf_op jit(solution)/shard_map/ppermute | solution.py:19
  16.1 10.2 %collective-permute-start.7 = (bf16[1040,128]{1,0:T(8,128)(2,1)S(1)}, bf16[1040,128]{1,0:T(8,128)(2,1)S(1)}, u32[]{:S(2)}, u32[]{:S(2)}) collective-permute-start(bf16[1040,128]{1,0:T(8,128)(2,1)S(1)} %get-tuple-element.92.refs_0_.q_ref), channel_id=1, source_target_pairs={{0,1},{2,0},{3,2},{1,3},{4,5},{6,4},{7,6},{5,7},{8,9},{10,8},{11,1... | collective-permute-start | bytes 798728 | tf_op jit(solution)/shard_map/ppermute | solution.py:25
  23.8 2.6 %collective-permute-start.9 = (bf16[1024,128]{1,0:T(8,128)(2,1)S(1)}, bf16[1024,128]{1,0:T(8,128)(2,1)S(1)}, u32[]{:S(2)}, u32[]{:S(2)}) collective-permute-start(bf16[1024,128]{1,0:T(8,128)(2,1)S(1)} %collective-permute-done.8.refs_10_), channel_id=1, source_target_pairs={{0,4},{4,0},{8,12},{12,8},{16,20},{20,16},{24,28},{28,24},{1,5},{5... | collective-permute-start | bytes 786440 | tf_op jit(solution)/shard_map/ppermute | solution.py:19
  23.8 8.9 %collective-permute-start.1 = (bf16[1040,128]{1,0:T(8,128)(2,1)S(1)}, bf16[1040,128]{1,0:T(8,128)(2,1)S(1)}, u32[]{:S(2)}, u32[]{:S(2)}) collective-permute-start(bf16[1040,128]{1,0:T(8,128)(2,1)S(1)} %collective-permute-done.refs_1_), channel_id=1, source_target_pairs={{0,2},{2,3},{3,1},{1,0},{4,6},{6,7},{7,5},{5,4},{8,10},{10,11},{11... | collective-permute-start | bytes 798728 | tf_op jit(solution)/shard_map/ppermute | solution.py:25
  36.8 7.3 %collective-permute-start.12 = (f32[1,8,128]{2,1,0:T(8,128)S(1)}, f32[1,8,128]{2,1,0:T(8,128)S(1)}, u32[]{:S(2)}, u32[]{:S(2)}) collective-permute-start(f32[1,8,128]{2,1,0:T(8,128)S(1)} %get-tuple-element.91.refs_3_), channel_id=1, source_target_pairs={{0,3},{1,2},{2,1},{3,0},{4,7},{5,6},{6,5},{7,4},{8,11},{9,10},{10,... | collective-permute-start | bytes 12296 | tf_op jit(solution)/shard_map/ppermute | solution.py:19
  40.3 4.5 %collective-permute-start.11 = (f32[1,8,128]{2,1,0:T(8,128)S(1)}, f32[1,8,128]{2,1,0:T(8,128)S(1)}, u32[]{:S(2)}, u32[]{:S(2)}) collective-permute-start(f32[1,8,128]{2,1,0:T(8,128)S(1)} %get-tuple-element.91.refs_3_), channel_id=1, source_target_pairs={{0,2},{1,3},{2,0},{3,1},{4,6},{5,7},{6,4},{7,5},{8,10},{9,11},{10,... | collective-permute-start | bytes 12296 | tf_op jit(solution)/shard_map/ppermute | solution.py:19
  40.7 4.2 %collective-permute-start.10 = (f32[1,8,128]{2,1,0:T(8,128)S(1)}, f32[1,8,128]{2,1,0:T(8,128)S(1)}, u32[]{:S(2)}, u32[]{:S(2)}) collective-permute-start(f32[1,8,128]{2,1,0:T(8,128)S(1)} %get-tuple-element.91.refs_3_), channel_id=1, source_target_pairs={{0,1},{1,0},{2,3},{3,2},{4,5},{5,4},{6,7},{7,6},{8,9},{9,8},{10,11... | collective-permute-start | bytes 12296 | tf_op jit(solution)/shard_map/ppermute | solution.py:19
  48.4 6.6 %collective-permute-start.13 = (bf16[1024,128]{1,0:T(8,128)(2,1)S(1)}, bf16[1024,128]{1,0:T(8,128)(2,1)S(1)}, u32[]{:S(2)}, u32[]{:S(2)}) collective-permute-start(bf16[1024,128]{1,0:T(8,128)(2,1)S(1)} %get-tuple-element.110), channel_id=1, source_target_pairs={{0,2},{2,3},{3,1},{1,0},{4,6},{6,7},{7,5},{5,4},{8,10},{10,11},{11... | collective-permute-start | bytes 786440 | tf_op jit(solution)/shard_map/ppermute | solution.py:25
  55.0 8.9 %collective-permute-start.14 = (bf16[1024,128]{1,0:T(8,128)(2,1)S(1)}, bf16[1024,128]{1,0:T(8,128)(2,1)S(1)}, u32[]{:S(2)}, u32[]{:S(2)}) collective-permute-start(bf16[1024,128]{1,0:T(8,128)(2,1)S(1)} %add_2.1), channel_id=1, source_target_pairs={{0,2},{2,3},{3,1},{1,0},{4,6},{6,7},{7,5},{5,4},{8,10},{10,11},{11... | collective-permute-start | bytes 786440 | tf_op jit(solution)/shard_map/ppermute | solution.py:25
  65.7 3.7 %collective-permute-start.15 = (bf16[4,512,128]{2,1,0:T(8,128)(2,1)S(1)}, bf16[4,512,128]{2,1,0:T(8,128)(2,1)S(1)}, u32[]{:S(2)}, u32[]{:S(2)}) collective-permute-start(bf16[4,512,128]{2,1,0:T(8,128)(2,1)S(1)} %get-tuple-element.120), channel_id=1, source_target_pairs={{0,4},{4,0},{8,12},{12,8},{16,20},{20,16},{24,28},{28,24},{1,5},{5... | collective-permute-start | bytes 1572872 | tf_op jit(solution)/shard_map/ppermute | solution.py:19
  65.7 10.2 %collective-permute-start.16 = (bf16[1024,128]{1,0:T(8,128)(2,1)S(1)}, bf16[1024,128]{1,0:T(8,128)(2,1)S(1)}, u32[]{:S(2)}, u32[]{:S(2)}) collective-permute-start(bf16[1024,128]{1,0:T(8,128)(2,1)S(1)} %add_3.1), channel_id=1, source_target_pairs={{0,2},{2,3},{3,1},{1,0},{4,6},{6,7},{7,5},{5,4},{8,10},{10,11},{11... | collective-permute-start | bytes 786440 | tf_op jit(solution)/shard_map/ppermute | solution.py:25
  69.5 7.8 %collective-permute-start.17 = (bf16[512,128]{1,0:T(8,128)(2,1)S(1)}, bf16[512,128]{1,0:T(8,128)(2,1)S(1)}, u32[]{:S(2)}, u32[]{:S(2)}) collective-permute-start(bf16[512,128]{1,0:T(8,128)(2,1)S(1)} %get-tuple-element.127), channel_id=1, source_target_pairs={{0,8},{4,12},{8,0},{12,4},{16,24},{20,28},{24,16},{28,20},{1,9},{5... | collective-permute-start | bytes 393224 | tf_op jit(solution)/shard_map/ppermute | solution.py:19
  70.1 7.2 %collective-permute-start.18 = (bf16[512,128]{1,0:T(8,128)(2,1)S(1)}, bf16[512,128]{1,0:T(8,128)(2,1)S(1)}, u32[]{:S(2)}, u32[]{:S(2)}) collective-permute-start(bf16[512,128]{1,0:T(8,128)(2,1)S(1)} %get-tuple-element.128), channel_id=1, source_target_pairs={{0,16},{4,20},{8,24},{12,28},{16,0},{20,4},{24,8},{28,12},{1,17},{... | collective-permute-start | bytes 393224 | tf_op jit(solution)/shard_map/ppermute | solution.py:19
  71.6 7.0 %collective-permute-start.19 = (bf16[512,128]{1,0:T(8,128)(2,1)S(1)}, bf16[512,128]{1,0:T(8,128)(2,1)S(1)}, u32[]{:S(2)}, u32[]{:S(2)}) collective-permute-start(bf16[512,128]{1,0:T(8,128)(2,1)S(1)} %get-tuple-element.129), channel_id=1, source_target_pairs={{0,24},{4,28},{8,16},{12,20},{16,8},{20,12},{24,0},{28,4},{1,25},{... | collective-permute-start | bytes 393224 | tf_op jit(solution)/shard_map/ppermute | solution.py:19

commit v11 on v10

--- a/solution.py
+++ b/solution.py
@@ -599,7 +599,7 @@
         + [pltpu.VMEM((rows, total_keys), bf16)] * (nh - 3)
         + [qw_shape] * (nh - 3),
         [pltpu.VMEM((hh, rows_here, lanes), f32)],
-        nh - 2.5,
+        0.001,
         "forward_middle",
     )
     score, keys_all, keys_t, logits = outs[:4]

time: 79.6 us -> 83.6 us (1.050)
  starting transfers between devices: 28.8 us -> 31.7 us
  waiting for transfers between devices: 8.35 us -> 9.51 us
    ppermute x14, starting transfers between devices: 14.7 us -> 18.8 us  [swap(): return lax.ppermute(value, axis, [(i, i ^ distance) for i in range(size)])]
    ppermute x6, waiting for transfers between devices: 2.44 us -> 4.68 us  [ring_next(): lax.ppermute(value, axis, [(ring[i], ring[(i + hop) % size]) for i in ran...]
    ppermute x6, starting transfers between devices: 14.1 us -> 12.8 us  [ring_next(): lax.ppermute(value, axis, [(ring[i], ring[(i + hop) % size]) for i in ran...]
    ppermute x14, waiting for transfers between devices: 5.91 us -> 4.82 us  [swap(): return lax.ppermute(value, axis, [(i, i ^ distance) for i in range(size)])]
  transfers between devices with their start and end apart: 20 -> 20, of which waited for: 6 -> 7; matrix products, arithmetic and copies ran while one was open for 1% -> 1% of each run, Pallas kernels for 35% -> 34%
where the time goes in v11:
time: 83.6 us; the launch traced here: 83.4 us
  Pallas kernels  39.2 us (47%)
  starting transfers between devices  31.7 us (38%)
  waiting for transfers between devices  9.51 us (11%)
  other arithmetic  1.62 us (2%)
  between operations  1.43 us (2%)
    pallas_call x11, Pallas kernels, call(): pl.pallas_call(kernel, out_shape=out_shape, input_output_aliases=aliases,...  35.7 us
    ppermute x14, starting transfers between devices, swap(): return lax.ppermute(value, axis, [(i, i ^ distance) for i in range(size)])  18.8 us
    ppermute x6, starting transfers between devices, ring_next(): lax.ppermute(value, axis, [(ring[i], ring[(i + hop) % size]) for i in ran...  12.8 us
    ppermute x14, waiting for transfers between devices, swap(): return lax.ppermute(value, axis, [(i, i ^ distance) for i in range(size)])  4.82 us
    ppermute x6, waiting for transfers between devices, ring_next(): lax.ppermute(value, axis, [(ring[i], ring[(i + hop) % size]) for i in ran...  4.68 us
    pallas_call x1, Pallas kernels, per_device(): pl.pallas_call(functools.partial(prepare_kernel, cfg), out_shape=[jax.Sha...  2.03 us
  transfers between devices with their start and end apart: 20, of which 7 were waited for; matrix products, arithmetic and copies ran while one was open for 1% of the time, Pallas kernels for 34%

profile of v11, /device:TPU:0, one launch (start us, length us, event | category | flops | bytes accessed | tf_op | source)
XLA Modules:
  0.0 83.4 jit_solution(13350004922836271745)
XLA Ops:
  0.6 2.0 %prepare.1 = (bf16[1040,128]{1,0:T(8,128)(2,1)S(1)}, f32[1,128]{1,0:T(1,128)S(1)}, bf16[1024,128]{1,0:T(8,128)(2,1)S(1)}, bf16[1024,128]{1,0:T(8,128)(2,1)S(1)},...) custom-call(bf16[64,16,128]{2,1,0:T(8,128)(2,1)} %query_ref.1, bf16[16,64]{1,0:T(8,128)(2,1)} %bitcast.25, ...), custom_call_target="tpu_custom_call" | custom-call | flops 131072 | bytes 4194304 | tf_op jit(solution)/shard_map/prepare/pallas_call | solution.py:496
  3.2 2.6 %collective-permute-start.3 = (bf16[1024,128]{1,0:T(8,128)(2,1)S(1)}, bf16[1024,128]{1,0:T(8,128)(2,1)S(1)}, u32[]{:S(2)}, u32[]{:S(2)}) collective-permute-start(bf16[1024,128]{1,0:T(8,128)(2,1)S(1)} %get-tuple-element.71), channel_id=1, source_target_pairs={{0,8},{4,12},{8,0},{12,4},{16,24},{20,28},{24,16},{28,20},{1,9},{5... | collective-permute-start | bytes 786440 | tf_op jit(solution)/shard_map/ppermute | solution.py:19
  5.8 1.5 %collective-permute-start.4 = (bf16[1024,128]{1,0:T(8,128)(2,1)S(1)}, bf16[1024,128]{1,0:T(8,128)(2,1)S(1)}, u32[]{:S(2)}, u32[]{:S(2)}) collective-permute-start(bf16[1024,128]{1,0:T(8,128)(2,1)S(1)} %get-tuple-element.72), channel_id=1, source_target_pairs={{0,16},{4,20},{8,24},{12,28},{16,0},{20,4},{24,8},{28,12},{1,17},{... | collective-permute-start | bytes 786440 | tf_op jit(solution)/shard_map/ppermute | solution.py:19
  7.3 2.6 %collective-permute-start = (bf16[1040,128]{1,0:T(8,128)(2,1)S(1)}, bf16[1040,128]{1,0:T(8,128)(2,1)S(1)}, u32[]{:S(2)}, u32[]{:S(2)}) collective-permute-start(bf16[1040,128]{1,0:T(8,128)(2,1)S(1)} %get-tuple-element.92.refs_0_.q_ref), channel_id=1, source_target_pairs={{0,2},{2,3},{3,1},{1,0},{4,6},{6,7},{7,5},{5,4},{8,10},{10,11},{11... | collective-permute-start | bytes 798728 | tf_op jit(solution)/shard_map/ppermute | solution.py:25
  12.7 1.5 %collective-permute-done.4.refs_10_ = bf16[1024,128]{1,0:T(8,128)(2,1)S(1)} collective-permute-done((bf16[1024,128]{1,0:T(8,128)(2,1)S(1)}, bf16[1024,128]{1,0:T(8,128)(2,1)S(1)}, u32[]{:S(2)}, u32[]{:S(2)}) %collective-permute-start.4) | collective-permute-done | bytes 262176 | tf_op jit(solution)/shard_map/ppermute | solution.py:19
  14.6 1.5 %collective-permute-start.8 = (bf16[1024,128]{1,0:T(8,128)(2,1)S(1)}, bf16[1024,128]{1,0:T(8,128)(2,1)S(1)}, u32[]{:S(2)}, u32[]{:S(2)}) collective-permute-start(bf16[1024,128]{1,0:T(8,128)(2,1)S(1)} %get-tuple-element.82), channel_id=1, source_target_pairs={{0,24},{4,28},{8,16},{12,20},{16,8},{20,12},{24,0},{28,4},{1,25},{... | collective-permute-start | bytes 786440 | tf_op jit(solution)/shard_map/ppermute | solution.py:19
  16.1 1.6 %collective-permute-start.7 = (bf16[1040,128]{1,0:T(8,128)(2,1)S(1)}, bf16[1040,128]{1,0:T(8,128)(2,1)S(1)}, u32[]{:S(2)}, u32[]{:S(2)}) collective-permute-start(bf16[1040,128]{1,0:T(8,128)(2,1)S(1)} %get-tuple-element.92.refs_0_.q_ref), channel_id=1, source_target_pairs={{0,1},{2,0},{3,2},{1,3},{4,5},{6,4},{7,6},{5,7},{8,9},{10,8},{11,1... | collective-permute-start | bytes 798728 | tf_op jit(solution)/shard_map/ppermute | solution.py:25
  19.1 3.7 %forward_early_1.1 = (f32[64,3072]{1,0:T(8,128)S(1)}, bf16[3072,128]{1,0:T(8,128)(2,1)S(1)}, bf16[128,3072]{1,0:T(8,128)(2,1)S(1)}, bf16[64,3072]{1,0:T(8,128)(2...) custom-call(s32[11]{0:T(128)S(1)} %pad_add_fusion.meta_ref, ...), custom_call_target="tpu_custom_call" | custom-call | flops 2147483 | bytes 4194 | tf_op jit(solution)/shard_map/forward_early_1/pallas_call | solution.py:537
  23.8 1.5 %collective-permute-done.7.refs_4_ = bf16[1040,128]{1,0:T(8,128)(2,1)S(1)} collective-permute-done((bf16[1040,128]{1,0:T(8,128)(2,1)S(1)}, bf16[1040,128]{1,0:T(8,128)(2,1)S(1)}, u32[]{:S(2)}, u32[]{:S(2)}) %collective-permute-start.7) | collective-permute-done | bytes 266272 | tf_op jit(solution)/shard_map/ppermute | solution.py:25
  25.3 4.2 %forward_middle.1 = (f32[64,4096]{1,0:T(8,128)S(1)}, bf16[4096,128]{1,0:T(8,128)(2,1)S(1)}, bf16[128,4096]{1,0:T(8,128)(2,1)S(1)}, bf16[64,4096]{1,0:T(8,128)(2,...) custom-call(s32[11]{0:T(128)S(1)} %pad_add_fusion.meta_ref, ...), custom_call_target="tpu_custom_call" | custom-call | flops 2147483 | bytes 4194 | tf_op jit(solution)/shard_map/forward_middle/pallas_call | solution.py:537
  30.8 4.1 %forward_last.1 = (f32[64,4096]{1,0:T(8,128)S(1)}, bf16[1024,4096]{1,0:T(8,128)(2,1)S(1)}, bf16[128,1024]{1,0:T(8,128)(2,1)S(1)}, f32[1,8,128]{2,1,0:T(8,128)S(1)}) custom-call(s32[11]{0:T(128)S(1)} %pad_add_fusion.meta_ref, bf16[1040,128]{1,0:T(8,128)(2,1)S(1)} %collective-permute-done.1.refs_0_, ...), custom_call_target="tpu_custom_call", output_to_operand_aliasing={{0}: (3, {})} | custom-call | flops 2147483648 | bytes 4194304 | tf_op jit(solution)/shard_map/forward_last/pallas_call | solution.py:537
  34.9 8.0 %collective-permute-start.12 = (f32[1,8,128]{2,1,0:T(8,128)S(1)}, f32[1,8,128]{2,1,0:T(8,128)S(1)}, u32[]{:S(2)}, u32[]{:S(2)}) collective-permute-start(f32[1,8,128]{2,1,0:T(8,128)S(1)} %get-tuple-element.91.refs_3_), channel_id=1, source_target_pairs={{0,3},{1,2},{2,1},{3,0},{4,7},{5,6},{6,5},{7,4},{8,11},{9,10},{10,... | collective-permute-start | bytes 12296 | tf_op jit(solution)/shard_map/ppermute | solution.py:19
  43.5 3.1 %own_active.1 = (bf16[1024,2048]{1,0:T(8,128)(2,1)S(1)}, bf16[1024,2048]{1,0:T(8,128)(2,1)S(1)}) custom-call(s32[11]{0:T(128)S(1)} %pad_add_fusion.meta_ref, bf16[1040,128]{1,0:T(8,128)(2,1)S(1)} %get-tuple-element.92.refs_0_.q_ref, bf16[128,4096]{1,0:T(8,128)(2,1)S(1)} %get-tuple-element.88.refs_1_.keys_t_ref), custom_call_target="tpu_custom_call" | custom-call | flops 2147483648 | bytes 4194304 | tf_op jit(solution)/shard_map/own_active/pallas_call | solution.py:537
  47.3 3.3 %backward_1.1 = (bf16[1024,128]{1,0:T(8,128)(2,1)S(1)}, bf16[64,4096]{1,0:T(8,128)(2,1)S(1)}) custom-call(s32[11]{0:T(128)S(1)} %pad_add_fusion.meta_ref, bf16[1024,3072]{1,0:T(8,128)(2,1)S(1)} %get-tuple-element.98.refs_0_, bf16[1024,1024]{1,0:T(8,128)(2,1)S(1)} %get-tuple-element.99.refs_1_, ...), custom_call_target="tpu_custom_call" | custom-call | flops 2147483648 | bytes 4194304 | tf_op jit(solution)/shard_map/backward_1/pallas_call | solution.py:537
  50.7 2.1 %collective-permute-start.13 = (bf16[1024,128]{1,0:T(8,128)(2,1)S(1)}, bf16[1024,128]{1,0:T(8,128)(2,1)S(1)}, u32[]{:S(2)}, u32[]{:S(2)}) collective-permute-start(bf16[1024,128]{1,0:T(8,128)(2,1)S(1)} %get-tuple-element.110), channel_id=1, source_target_pairs={{0,2},{2,3},{3,1},{1,0},{4,6},{6,7},{7,5},{5,4},{8,10},{10,11},{11... | collective-permute-start | bytes 786440 | tf_op jit(solution)/shard_map/ppermute | solution.py:25
  52.8 4.1 %backward_2.1 = (f32[1024,128]{1,0:T(8,128)S(1)}, f32[128,4096]{1,0:T(8,128)S(1)}) custom-call(s32[11]{0:T(128)S(1)} %pad_add_fusion.meta_ref, bf16[1024,3072]{1,0:T(8,128)(2,1)S(1)} %get-tuple-element.98.refs_0_, bf16[1024,1024]{1,0:T(8,128)(2,1)S(1)} %get-tuple-element.99.refs_1_, bf16[1024,4096]{1,0:T(8,128)(2,1)S(1)} %get-tuple-element.103.refs_2_.refs_0_, ...), custom_call_target="tpu_custom_call" | custom-call | flops 4294967296 | bytes 8388608 | tf_op jit(solution)/shard_map/backward_2/pallas_call | solution.py:537
  56.9 1.9 %collective-permute-done.13.moving_ref = bf16[1024,128]{1,0:T(8,128)(2,1)S(1)} collective-permute-done((bf16[1024,128]{1,0:T(8,128)(2,1)S(1)}, bf16[1024,128]{1,0:T(8,128)(2,1)S(1)}, u32[]{:S(2)}, u32[]{:S(2)}) %collective-permute-start.13) | collective-permute-done | bytes 262176 | tf_op jit(solution)/shard_map/ppermute | solution.py:25
  58.9 3.4 %collective-permute-start.14 = (bf16[1024,128]{1,0:T(8,128)(2,1)S(1)}, bf16[1024,128]{1,0:T(8,128)(2,1)S(1)}, u32[]{:S(2)}, u32[]{:S(2)}) collective-permute-start(bf16[1024,128]{1,0:T(8,128)(2,1)S(1)} %add_2.1), channel_id=1, source_target_pairs={{0,2},{2,3},{3,1},{1,0},{4,6},{6,7},{7,5},{5,4},{8,10},{10,11},{11... | collective-permute-start | bytes 786440 | tf_op jit(solution)/shard_map/ppermute | solution.py:25
  62.3 5.6 %backward_3.1 = (f32[1024,128]{1,0:T(8,128)S(1)}, f32[128,4096]{1,0:T(8,128)S(1)}) custom-call(s32[11]{0:T(128)S(1)} %pad_add_fusion.meta_ref, bf16[1024,4096]{1,0:T(8,128)(2,1)S(1)} %get-tuple-element.103.refs_2_.refs_0_, bf16[1024,4096]{1,0:T(8,128)(2,1)S(1)} %get-tuple-element.104.refs_1_, ...), custom_call_target="tpu_custom_call", output_to_operand_aliasing={{1}: (7, {})} | custom-call | flops 6442450944 | bytes 12582912 | tf_op jit(solution)/shard_map/backward_3/pallas_call | solution.py:537
  68.0 1.6 %backward_0_first.1 = (bf16[4,512,128]{2,1,0:T(8,128)(2,1)S(1)}, bf16[1024,2048]{1,0:T(8,128)(2,1)S(1)}) custom-call(s32[11]{0:T(128)S(1)} %pad_add_fusion.meta_ref, bf16[1024,2048]{1,0:T(8,128)(2,1)S(1)} %get-tuple-element.95.refs_0_, bf16[128,1024]{1,0:T(8,128)(2,1)S(1)} %get-tuple-element.96.refs_1_, ...), custom_call_target="tpu_custom_call" | custom-call | flops 2147483648 | bytes 4194304 | tf_op jit(solution)/shard_map/backward_0_first/pallas_call | solution.py:537
  69.7 1.7 %collective-permute-start.16 = (bf16[1024,128]{1,0:T(8,128)(2,1)S(1)}, bf16[1024,128]{1,0:T(8,128)(2,1)S(1)}, u32[]{:S(2)}, u32[]{:S(2)}) collective-permute-start(bf16[1024,128]{1,0:T(8,128)(2,1)S(1)} %add_3.1), channel_id=1, source_target_pairs={{0,2},{2,3},{3,1},{1,0},{4,6},{6,7},{7,5},{5,4},{8,10},{10,11},{11... | collective-permute-start | bytes 786440 | tf_op jit(solution)/shard_map/ppermute | solution.py:25
  71.4 1.7 %backward_0_second.1 = (f32[512,128]{1,0:T(8,128)S(1)}, f32[512,128]{1,0:T(8,128)S(1)}, f32[512,128]{1,0:T(8,128)S(1)}, f32[512,128]{1,0:T(8,128)S(1)}, bf16[1024,2048]{1,0:T(8,128)(2,1)S(1)}) custom-call(s32[11]{0:T(128)S(1)} %pad_add_fusion.meta_ref, bf16[1024,2048]{1,0:T(8,128)(2,1)S(1)} %get-tuple-element.117.refs_0_, ...), custom_call_target="tpu_custom_call" | custom-call | flops 2147483648 | bytes 4194304 | tf_op jit(solution)/shard_map/backward_0_second/pallas_call | solution.py:537
  76.8 2.9 %backward_0.1.u_ref = f32[1024,128]{1,0:T(8,128)S(1)} custom-call(s32[11]{0:T(128)S(1)} %pad_add_fusion.meta_ref, bf16[1024,2048]{1,0:T(8,128)(2,1)S(1)} %get-tuple-element.116.first_ref, bf16[1024,2048]{1,0:T(8,128)(2,1)S(1)} %get-tuple-element.118.second_ref, bf16[4096,128]{1,0:T(8,128)(2,1)S(1)} %get-tuple-element.123.refs_2_.refs_4_.keys_ref), custom_call_target="tpu_custom_call" | custom-call | flops 2147483648 | bytes 4194304 | tf_op jit(solution)/shard_map/backward_0/pallas_call | solution.py:537
  81.0 1.7 %collective-permute-done.18 = bf16[512,128]{1,0:T(8,128)(2,1)S(1)} collective-permute-done((bf16[512,128]{1,0:T(8,128)(2,1)S(1)}, bf16[512,128]{1,0:T(8,128)(2,1)S(1)}, u32[]{:S(2)}, u32[]{:S(2)}) %collective-permute-start.18) | collective-permute-done | bytes 131104 | tf_op jit(solution)/shard_map/ppermute | solution.py:19
  (34 shorter events, 14.0 us)
Async XLA Ops:
  2.7 8.6 %collective-permute-start.2 = (bf16[1024,128]{1,0:T(8,128)(2,1)S(1)}, bf16[1024,128]{1,0:T(8,128)(2,1)S(1)}, u32[]{:S(2)}, u32[]{:S(2)}) collective-permute-start(bf16[1024,128]{1,0:T(8,128)(2,1)S(1)} %get-tuple-element.69.refs_2_), channel_id=1, source_target_pairs={{0,4},{4,0},{8,12},{12,8},{16,20},{20,16},{24,28},{28,24},{1,5},{5... | collective-permute-start | bytes 786440 | tf_op jit(solution)/shard_map/ppermute | solution.py:19
  3.2 9.5 %collective-permute-start.3 = (bf16[1024,128]{1,0:T(8,128)(2,1)S(1)}, bf16[1024,128]{1,0:T(8,128)(2,1)S(1)}, u32[]{:S(2)}, u32[]{:S(2)}) collective-permute-start(bf16[1024,128]{1,0:T(8,128)(2,1)S(1)} %get-tuple-element.71), channel_id=1, source_target_pairs={{0,8},{4,12},{8,0},{12,4},{16,24},{20,28},{24,16},{28,20},{1,9},{5... | collective-permute-start | bytes 786440 | tf_op jit(solution)/shard_map/ppermute | solution.py:19
  5.8 8.4 %collective-permute-start.4 = (bf16[1024,128]{1,0:T(8,128)(2,1)S(1)}, bf16[1024,128]{1,0:T(8,128)(2,1)S(1)}, u32[]{:S(2)}, u32[]{:S(2)}) collective-permute-start(bf16[1024,128]{1,0:T(8,128)(2,1)S(1)} %get-tuple-element.72), channel_id=1, source_target_pairs={{0,16},{4,20},{8,24},{12,28},{16,0},{20,4},{24,8},{28,12},{1,17},{... | collective-permute-start | bytes 786440 | tf_op jit(solution)/shard_map/ppermute | solution.py:19
  7.3 10.4 %collective-permute-start = (bf16[1040,128]{1,0:T(8,128)(2,1)S(1)}, bf16[1040,128]{1,0:T(8,128)(2,1)S(1)}, u32[]{:S(2)}, u32[]{:S(2)}) collective-permute-start(bf16[1040,128]{1,0:T(8,128)(2,1)S(1)} %get-tuple-element.92.refs_0_.q_ref), channel_id=1, source_target_pairs={{0,2},{2,3},{3,1},{1,0},{4,6},{6,7},{7,5},{5,4},{8,10},{10,11},{11... | collective-permute-start | bytes 798728 | tf_op jit(solution)/shard_map/ppermute | solution.py:25
  14.1 4.9 %collective-permute-start.5 = (bf16[1024,128]{1,0:T(8,128)(2,1)S(1)}, bf16[1024,128]{1,0:T(8,128)(2,1)S(1)}, u32[]{:S(2)}, u32[]{:S(2)}) collective-permute-start(bf16[1024,128]{1,0:T(8,128)(2,1)S(1)} %collective-permute-done.3.refs_9_), channel_id=1, source_target_pairs={{0,4},{4,0},{8,12},{12,8},{16,20},{20,16},{24,28},{28,24},{1,5},{5... | collective-permute-start | bytes 786440 | tf_op jit(solution)/shard_map/ppermute | solution.py:19
  14.1 4.9 %collective-permute-start.6 = (bf16[1024,128]{1,0:T(8,128)(2,1)S(1)}, bf16[1024,128]{1,0:T(8,128)(2,1)S(1)}, u32[]{:S(2)}, u32[]{:S(2)}) collective-permute-start(bf16[1024,128]{1,0:T(8,128)(2,1)S(1)} %collective-permute-done.4.refs_10_), channel_id=1, source_target_pairs={{0,4},{4,0},{8,12},{12,8},{16,20},{20,16},{24,28},{28,24},{1,5},{5... | collective-permute-start | bytes 786440 | tf_op jit(solution)/shard_map/ppermute | solution.py:19
  14.6 9.1 %collective-permute-start.8 = (bf16[1024,128]{1,0:T(8,128)(2,1)S(1)}, bf16[1024,128]{1,0:T(8,128)(2,1)S(1)}, u32[]{:S(2)}, u32[]{:S(2)}) collective-permute-start(bf16[1024,128]{1,0:T(8,128)(2,1)S(1)} %get-tuple-element.82), channel_id=1, source_target_pairs={{0,24},{4,28},{8,16},{12,20},{16,8},{20,12},{24,0},{28,4},{1,25},{... | collective-permute-start | bytes 786440 | tf_op jit(solution)/shard_map/ppermute | solution.py:19
  16.1 9.2 %collective-permute-start.7 = (bf16[1040,128]{1,0:T(8,128)(2,1)S(1)}, bf16[1040,128]{1,0:T(8,128)(2,1)S(1)}, u32[]{:S(2)}, u32[]{:S(2)}) collective-permute-start(bf16[1040,128]{1,0:T(8,128)(2,1)S(1)} %get-tuple-element.92.refs_0_.q_ref), channel_id=1, source_target_pairs={{0,1},{2,0},{3,2},{1,3},{4,5},{6,4},{7,6},{5,7},{8,9},{10,8},{11,1... | collective-permute-start | bytes 798728 | tf_op jit(solution)/shard_map/ppermute | solution.py:25
  17.7 13.0 %collective-permute-start.1 = (bf16[1040,128]{1,0:T(8,128)(2,1)S(1)}, bf16[1040,128]{1,0:T(8,128)(2,1)S(1)}, u32[]{:S(2)}, u32[]{:S(2)}) collective-permute-start(bf16[1040,128]{1,0:T(8,128)(2,1)S(1)} %collective-permute-done.refs_1_), channel_id=1, source_target_pairs={{0,2},{2,3},{3,1},{1,0},{4,6},{6,7},{7,5},{5,4},{8,10},{10,11},{11... | collective-permute-start | bytes 798728 | tf_op jit(solution)/shard_map/ppermute | solution.py:25
  23.8 1.5 %collective-permute-start.9 = (bf16[1024,128]{1,0:T(8,128)(2,1)S(1)}, bf16[1024,128]{1,0:T(8,128)(2,1)S(1)}, u32[]{:S(2)}, u32[]{:S(2)}) collective-permute-start(bf16[1024,128]{1,0:T(8,128)(2,1)S(1)} %collective-permute-done.8.refs_10_), channel_id=1, source_target_pairs={{0,4},{4,0},{8,12},{12,8},{16,20},{20,16},{24,28},{28,24},{1,5},{5... | collective-permute-start | bytes 786440 | tf_op jit(solution)/shard_map/ppermute | solution.py:19
  34.9 11.8 %collective-permute-start.12 = (f32[1,8,128]{2,1,0:T(8,128)S(1)}, f32[1,8,128]{2,1,0:T(8,128)S(1)}, u32[]{:S(2)}, u32[]{:S(2)}) collective-permute-start(f32[1,8,128]{2,1,0:T(8,128)S(1)} %get-tuple-element.91.refs_3_), channel_id=1, source_target_pairs={{0,3},{1,2},{2,1},{3,0},{4,7},{5,6},{6,5},{7,4},{8,11},{9,10},{10,... | collective-permute-start | bytes 12296 | tf_op jit(solution)/shard_map/ppermute | solution.py:19
  42.8 4.5 %collective-permute-start.11 = (f32[1,8,128]{2,1,0:T(8,128)S(1)}, f32[1,8,128]{2,1,0:T(8,128)S(1)}, u32[]{:S(2)}, u32[]{:S(2)}) collective-permute-start(f32[1,8,128]{2,1,0:T(8,128)S(1)} %get-tuple-element.91.refs_3_), channel_id=1, source_target_pairs={{0,2},{1,3},{2,0},{3,1},{4,6},{5,7},{6,4},{7,5},{8,10},{9,11},{10,... | collective-permute-start | bytes 12296 | tf_op jit(solution)/shard_map/ppermute | solution.py:19
  42.8 4.5 %collective-permute-start.10 = (f32[1,8,128]{2,1,0:T(8,128)S(1)}, f32[1,8,128]{2,1,0:T(8,128)S(1)}, u32[]{:S(2)}, u32[]{:S(2)}) collective-permute-start(f32[1,8,128]{2,1,0:T(8,128)S(1)} %get-tuple-element.91.refs_3_), channel_id=1, source_target_pairs={{0,1},{1,0},{2,3},{3,2},{4,5},{5,4},{6,7},{7,6},{8,9},{9,8},{10,11... | collective-permute-start | bytes 12296 | tf_op jit(solution)/shard_map/ppermute | solution.py:19
  50.7 8.2 %collective-permute-start.13 = (bf16[1024,128]{1,0:T(8,128)(2,1)S(1)}, bf16[1024,128]{1,0:T(8,128)(2,1)S(1)}, u32[]{:S(2)}, u32[]{:S(2)}) collective-permute-start(bf16[1024,128]{1,0:T(8,128)(2,1)S(1)} %get-tuple-element.110), channel_id=1, source_target_pairs={{0,2},{2,3},{3,1},{1,0},{4,6},{6,7},{7,5},{5,4},{8,10},{10,11},{11... | collective-permute-start | bytes 786440 | tf_op jit(solution)/shard_map/ppermute | solution.py:25
  58.9 9.0 %collective-permute-start.14 = (bf16[1024,128]{1,0:T(8,128)(2,1)S(1)}, bf16[1024,128]{1,0:T(8,128)(2,1)S(1)}, u32[]{:S(2)}, u32[]{:S(2)}) collective-permute-start(bf16[1024,128]{1,0:T(8,128)(2,1)S(1)} %add_2.1), channel_id=1, source_target_pairs={{0,2},{2,3},{3,1},{1,0},{4,6},{6,7},{7,5},{5,4},{8,10},{10,11},{11... | collective-permute-start | bytes 786440 | tf_op jit(solution)/shard_map/ppermute | solution.py:25
  69.6 3.5 %collective-permute-start.15 = (bf16[4,512,128]{2,1,0:T(8,128)(2,1)S(1)}, bf16[4,512,128]{2,1,0:T(8,128)(2,1)S(1)}, u32[]{:S(2)}, u32[]{:S(2)}) collective-permute-start(bf16[4,512,128]{2,1,0:T(8,128)(2,1)S(1)} %get-tuple-element.120), channel_id=1, source_target_pairs={{0,4},{4,0},{8,12},{12,8},{16,20},{20,16},{24,28},{28,24},{1,5},{5... | collective-permute-start | bytes 1572872 | tf_op jit(solution)/shard_map/ppermute | solution.py:19
  69.7 9.9 %collective-permute-start.16 = (bf16[1024,128]{1,0:T(8,128)(2,1)S(1)}, bf16[1024,128]{1,0:T(8,128)(2,1)S(1)}, u32[]{:S(2)}, u32[]{:S(2)}) collective-permute-start(bf16[1024,128]{1,0:T(8,128)(2,1)S(1)} %add_3.1), channel_id=1, source_target_pairs={{0,2},{2,3},{3,1},{1,0},{4,6},{6,7},{7,5},{5,4},{8,10},{10,11},{11... | collective-permute-start | bytes 786440 | tf_op jit(solution)/shard_map/ppermute | solution.py:25
  73.2 7.8 %collective-permute-start.17 = (bf16[512,128]{1,0:T(8,128)(2,1)S(1)}, bf16[512,128]{1,0:T(8,128)(2,1)S(1)}, u32[]{:S(2)}, u32[]{:S(2)}) collective-permute-start(bf16[512,128]{1,0:T(8,128)(2,1)S(1)} %get-tuple-element.127), channel_id=1, source_target_pairs={{0,8},{4,12},{8,0},{12,4},{16,24},{20,28},{24,16},{28,20},{1,9},{5... | collective-permute-start | bytes 393224 | tf_op jit(solution)/shard_map/ppermute | solution.py:19
  74.5 8.1 %collective-permute-start.18 = (bf16[512,128]{1,0:T(8,128)(2,1)S(1)}, bf16[512,128]{1,0:T(8,128)(2,1)S(1)}, u32[]{:S(2)}, u32[]{:S(2)}) collective-permute-start(bf16[512,128]{1,0:T(8,128)(2,1)S(1)} %get-tuple-element.128), channel_id=1, source_target_pairs={{0,16},{4,20},{8,24},{12,28},{16,0},{20,4},{24,8},{28,12},{1,17},{... | collective-permute-start | bytes 393224 | tf_op jit(solution)/shard_map/ppermute | solution.py:19
  75.3 7.3 %collective-permute-start.19 = (bf16[512,128]{1,0:T(8,128)(2,1)S(1)}, bf16[512,128]{1,0:T(8,128)(2,1)S(1)}, u32[]{:S(2)}, u32[]{:S(2)}) collective-permute-start(bf16[512,128]{1,0:T(8,128)(2,1)S(1)} %get-tuple-element.129), channel_id=1, source_target_pairs={{0,24},{4,28},{8,16},{12,20},{16,8},{20,12},{24,0},{28,4},{1,25},{... | collective-permute-start | bytes 393224 | tf_op jit(solution)/shard_map/ppermute | solution.py:19

commit v12 on v10

--- a/solution.py
+++ b/solution.py
@@ -685,7 +685,7 @@
     part = backward([(1, True, None)], "backward_1")[0]
     moving = ring_next(part, "head")
     for j in range(2, nh):
-        items = [(j - 1, False, "all"), (j, True, "all" if j == nh - 1 else None)]
+        items = ([(1, False, "all")] if j == 2 else []) + [(j, True, "all")]
         part = backward(items, f"backward_{j}")[0]
         part = pl.pallas_call(
             add_kernel,

time: 79.6 us -> 79.5 us (level)
  transfers between devices with their start and end apart: 20 -> 20, of which waited for: 6 -> 5; matrix products, arithmetic and copies ran while one was open for 1% -> 1% of each run, Pallas kernels for 35% -> 35%
where the time goes in v12:
time: 79.5 us; the launch traced here: 79.4 us
  Pallas kernels  39.4 us (50%)
  starting transfers between devices  28.9 us (36%)
  waiting for transfers between devices  8 us (10%)
  other arithmetic  1.6 us (2%)
  between operations  1.46 us (2%)
    pallas_call x11, Pallas kernels, call(): pl.pallas_call(kernel, out_shape=out_shape, input_output_aliases=aliases,...  35.9 us
    ppermute x14, starting transfers between devices, swap(): return lax.ppermute(value, axis, [(i, i ^ distance) for i in range(size)])  14.7 us
    ppermute x6, starting transfers between devices, ring_next(): lax.ppermute(value, axis, [(ring[i], ring[(i + hop) % size]) for i in ran...  14.2 us
    ppermute x14, waiting for transfers between devices, swap(): return lax.ppermute(value, axis, [(i, i ^ distance) for i in range(size)])  5.91 us
    ppermute x6, waiting for transfers between devices, ring_next(): lax.ppermute(value, axis, [(ring[i], ring[(i + hop) % size]) for i in ran...  2.09 us
    pallas_call x1, Pallas kernels, per_device(): pl.pallas_call(functools.partial(prepare_kernel, cfg), out_shape=[jax.Sha...  2.03 us
  transfers between devices with their start and end apart: 20, of which 5 were waited for; matrix products, arithmetic and copies ran while one was open for 1% of the time, Pallas kernels for 35%

profile of v12, /device:TPU:0, one launch (start us, length us, event | category | flops | bytes accessed | tf_op | source)
XLA Modules:
  0.0 79.4 jit_solution(2839357945525685167)
XLA Ops:
  0.6 2.0 %prepare.1 = (bf16[1040,128]{1,0:T(8,128)(2,1)S(1)}, f32[1,128]{1,0:T(1,128)S(1)}, bf16[1024,128]{1,0:T(8,128)(2,1)S(1)}, bf16[1024,128]{1,0:T(8,128)(2,1)S(1)},...) custom-call(bf16[64,16,128]{2,1,0:T(8,128)(2,1)} %query_ref.1, bf16[16,64]{1,0:T(8,128)(2,1)} %bitcast.25, ...), custom_call_target="tpu_custom_call" | custom-call | flops 131072 | bytes 4194304 | tf_op jit(solution)/shard_map/prepare/pallas_call | solution.py:496
  3.2 2.6 %collective-permute-start.3 = (bf16[1024,128]{1,0:T(8,128)(2,1)S(1)}, bf16[1024,128]{1,0:T(8,128)(2,1)S(1)}, u32[]{:S(2)}, u32[]{:S(2)}) collective-permute-start(bf16[1024,128]{1,0:T(8,128)(2,1)S(1)} %get-tuple-element.71), channel_id=1, source_target_pairs={{0,8},{4,12},{8,0},{12,4},{16,24},{20,28},{24,16},{28,20},{1,9},{5... | collective-permute-start | bytes 786440 | tf_op jit(solution)/shard_map/ppermute | solution.py:19
  5.8 1.5 %collective-permute-start.4 = (bf16[1024,128]{1,0:T(8,128)(2,1)S(1)}, bf16[1024,128]{1,0:T(8,128)(2,1)S(1)}, u32[]{:S(2)}, u32[]{:S(2)}) collective-permute-start(bf16[1024,128]{1,0:T(8,128)(2,1)S(1)} %get-tuple-element.72), channel_id=1, source_target_pairs={{0,16},{4,20},{8,24},{12,28},{16,0},{20,4},{24,8},{28,12},{1,17},{... | collective-permute-start | bytes 786440 | tf_op jit(solution)/shard_map/ppermute | solution.py:19
  7.3 2.6 %collective-permute-start = (bf16[1040,128]{1,0:T(8,128)(2,1)S(1)}, bf16[1040,128]{1,0:T(8,128)(2,1)S(1)}, u32[]{:S(2)}, u32[]{:S(2)}) collective-permute-start(bf16[1040,128]{1,0:T(8,128)(2,1)S(1)} %get-tuple-element.92.refs_0_.q_ref), channel_id=1, source_target_pairs={{0,2},{2,3},{3,1},{1,0},{4,6},{6,7},{7,5},{5,4},{8,10},{10,11},{11... | collective-permute-start | bytes 798728 | tf_op jit(solution)/shard_map/ppermute | solution.py:25
  14.6 1.5 %collective-permute-start.8 = (bf16[1024,128]{1,0:T(8,128)(2,1)S(1)}, bf16[1024,128]{1,0:T(8,128)(2,1)S(1)}, u32[]{:S(2)}, u32[]{:S(2)}) collective-permute-start(bf16[1024,128]{1,0:T(8,128)(2,1)S(1)} %get-tuple-element.82), channel_id=1, source_target_pairs={{0,24},{4,28},{8,16},{12,20},{16,8},{20,12},{24,0},{28,4},{1,25},{... | collective-permute-start | bytes 786440 | tf_op jit(solution)/shard_map/ppermute | solution.py:19
  16.1 1.6 %collective-permute-start.7 = (bf16[1040,128]{1,0:T(8,128)(2,1)S(1)}, bf16[1040,128]{1,0:T(8,128)(2,1)S(1)}, u32[]{:S(2)}, u32[]{:S(2)}) collective-permute-start(bf16[1040,128]{1,0:T(8,128)(2,1)S(1)} %get-tuple-element.92.refs_0_.q_ref), channel_id=1, source_target_pairs={{0,1},{2,0},{3,2},{1,3},{4,5},{6,4},{7,6},{5,7},{8,9},{10,8},{11,1... | collective-permute-start | bytes 798728 | tf_op jit(solution)/shard_map/ppermute | solution.py:25
  17.7 3.7 %forward_early_1.1 = (f32[64,3072]{1,0:T(8,128)S(1)}, bf16[3072,128]{1,0:T(8,128)(2,1)S(1)}, bf16[128,3072]{1,0:T(8,128)(2,1)S(1)}, bf16[64,3072]{1,0:T(8,128)(2...) custom-call(s32[11]{0:T(128)S(1)} %pad_add_fusion.meta_ref, ...), custom_call_target="tpu_custom_call" | custom-call | flops 2147483 | bytes 4194 | tf_op jit(solution)/shard_map/forward_early_1/pallas_call | solution.py:537
  21.4 2.3 %collective-permute-done.8.refs_10_ = bf16[1024,128]{1,0:T(8,128)(2,1)S(1)} collective-permute-done((bf16[1024,128]{1,0:T(8,128)(2,1)S(1)}, bf16[1024,128]{1,0:T(8,128)(2,1)S(1)}, u32[]{:S(2)}, u32[]{:S(2)}) %collective-permute-start.8) | collective-permute-done | bytes 262176 | tf_op jit(solution)/shard_map/ppermute | solution.py:19
  23.8 2.6 %collective-permute-start.1 = (bf16[1040,128]{1,0:T(8,128)(2,1)S(1)}, bf16[1040,128]{1,0:T(8,128)(2,1)S(1)}, u32[]{:S(2)}, u32[]{:S(2)}) collective-permute-start(bf16[1040,128]{1,0:T(8,128)(2,1)S(1)} %collective-permute-done.refs_1_), channel_id=1, source_target_pairs={{0,2},{2,3},{3,1},{1,0},{4,6},{6,7},{7,5},{5,4},{8,10},{10,11},{11... | collective-permute-start | bytes 798728 | tf_op jit(solution)/shard_map/ppermute | solution.py:25
  26.4 4.2 %forward_middle.1 = (f32[64,4096]{1,0:T(8,128)S(1)}, bf16[4096,128]{1,0:T(8,128)(2,1)S(1)}, bf16[128,4096]{1,0:T(8,128)(2,1)S(1)}, bf16[64,4096]{1,0:T(8,128)(2,...) custom-call(s32[11]{0:T(128)S(1)} %pad_add_fusion.meta_ref, ...), custom_call_target="tpu_custom_call" | custom-call | flops 3221225472 | bytes 6291456 | tf_op jit(solution)/shard_map/forward_middle/pallas_call | solution.py:537
  30.6 2.1 %collective-permute-done.1.refs_0_ = bf16[1040,128]{1,0:T(8,128)(2,1)S(1)} collective-permute-done((bf16[1040,128]{1,0:T(8,128)(2,1)S(1)}, bf16[1040,128]{1,0:T(8,128)(2,1)S(1)}, u32[]{:S(2)}, u32[]{:S(2)}) %collective-permute-start.1) | collective-permute-done | bytes 266272 | tf_op jit(solution)/shard_map/ppermute | solution.py:25
  32.7 4.1 %forward_last.1 = (f32[64,4096]{1,0:T(8,128)S(1)}, bf16[1024,4096]{1,0:T(8,128)(2,1)S(1)}, bf16[128,1024]{1,0:T(8,128)(2,1)S(1)}, f32[1,8,128]{2,1,0:T(8,128)S(1)}) custom-call(s32[11]{0:T(128)S(1)} %pad_add_fusion.meta_ref, bf16[1040,128]{1,0:T(8,128)(2,1)S(1)} %collective-permute-done.1.refs_0_, ...), custom_call_target="tpu_custom_call", output_to_operand_aliasing={{0}: (3, {})} | custom-call | flops 2147483648 | bytes 4194304 | tf_op jit(solution)/shard_map/forward_last/pallas_call | solution.py:537
  36.8 3.6 %collective-permute-start.12 = (f32[1,8,128]{2,1,0:T(8,128)S(1)}, f32[1,8,128]{2,1,0:T(8,128)S(1)}, u32[]{:S(2)}, u32[]{:S(2)}) collective-permute-start(f32[1,8,128]{2,1,0:T(8,128)S(1)} %get-tuple-element.91.refs_3_), channel_id=1, source_target_pairs={{0,3},{1,2},{2,1},{3,0},{4,7},{5,6},{6,5},{7,4},{8,11},{9,10},{10,... | collective-permute-start | bytes 12296 | tf_op jit(solution)/shard_map/ppermute | solution.py:19
  41.2 2.9 %own_active.1 = (bf16[1024,2048]{1,0:T(8,128)(2,1)S(1)}, bf16[1024,2048]{1,0:T(8,128)(2,1)S(1)}) custom-call(s32[11]{0:T(128)S(1)} %pad_add_fusion.meta_ref, bf16[1040,128]{1,0:T(8,128)(2,1)S(1)} %get-tuple-element.92.refs_0_.q_ref, bf16[128,4096]{1,0:T(8,128)(2,1)S(1)} %get-tuple-element.88.refs_1_.keys_t_ref), custom_call_target="tpu_custom_call" | custom-call | flops 2147483648 | bytes 4194304 | tf_op jit(solution)/shard_map/own_active/pallas_call | solution.py:537
  44.8 3.6 %backward_1.1 = (bf16[1024,128]{1,0:T(8,128)(2,1)S(1)}, bf16[64,4096]{1,0:T(8,128)(2,1)S(1)}) custom-call(s32[11]{0:T(128)S(1)} %pad_add_fusion.meta_ref, bf16[1024,3072]{1,0:T(8,128)(2,1)S(1)} %get-tuple-element.98.refs_0_, bf16[1024,1024]{1,0:T(8,128)(2,1)S(1)} %get-tuple-element.99.refs_1_, ...), custom_call_target="tpu_custom_call" | custom-call | flops 2147483648 | bytes 4194304 | tf_op jit(solution)/shard_map/backward_1/pallas_call | solution.py:537
  48.4 2.1 %collective-permute-start.13 = (bf16[1024,128]{1,0:T(8,128)(2,1)S(1)}, bf16[1024,128]{1,0:T(8,128)(2,1)S(1)}, u32[]{:S(2)}, u32[]{:S(2)}) collective-permute-start(bf16[1024,128]{1,0:T(8,128)(2,1)S(1)} %get-tuple-element.110), channel_id=1, source_target_pairs={{0,2},{2,3},{3,1},{1,0},{4,6},{6,7},{7,5},{5,4},{8,10},{10,11},{11... | collective-permute-start | bytes 786440 | tf_op jit(solution)/shard_map/ppermute | solution.py:25
  50.5 5.5 %backward_2.1 = (f32[1024,128]{1,0:T(8,128)S(1)}, f32[128,4096]{1,0:T(8,128)S(1)}) custom-call(s32[11]{0:T(128)S(1)} %pad_add_fusion.meta_ref, bf16[1024,3072]{1,0:T(8,128)(2,1)S(1)} %get-tuple-element.98.refs_0_, bf16[1024,1024]{1,0:T(8,128)(2,1)S(1)} %get-tuple-element.99.refs_1_, bf16[1024,4096]{1,0:T(8,128)(2,1)S(1)} %get-tuple-element.105.refs_2_, ...), custom_call_target="tpu_custom_call" | custom-call | flops 6442450944 | bytes 12582912 | tf_op jit(solution)/shard_map/backward_2/pallas_call | solution.py:537
  56.0 2.3 %collective-permute-start.14 = (bf16[1024,128]{1,0:T(8,128)(2,1)S(1)}, bf16[1024,128]{1,0:T(8,128)(2,1)S(1)}, u32[]{:S(2)}, u32[]{:S(2)}) collective-permute-start(bf16[1024,128]{1,0:T(8,128)(2,1)S(1)} %add_2.1), channel_id=1, source_target_pairs={{0,2},{2,3},{3,1},{1,0},{4,6},{6,7},{7,5},{5,4},{8,10},{10,11},{11... | collective-permute-start | bytes 786440 | tf_op jit(solution)/shard_map/ppermute | solution.py:25
  58.3 4.5 %backward_3.1 = (f32[1024,128]{1,0:T(8,128)S(1)}, f32[128,4096]{1,0:T(8,128)S(1)}) custom-call(s32[11]{0:T(128)S(1)} %pad_add_fusion.meta_ref, bf16[1024,4096]{1,0:T(8,128)(2,1)S(1)} %get-tuple-element.103.refs_0_, bf16[128,1024]{1,0:T(8,128)(2,1)S(1)} %get-tuple-element.104.refs_1_, ...), custom_call_target="tpu_custom_call", output_to_operand_aliasing={{1}: (5, {})} | custom-call | flops 4294967296 | bytes 8388608 | tf_op jit(solution)/shard_map/backward_3/pallas_call | solution.py:537
  62.9 1.6 %backward_0_first.1 = (bf16[4,512,128]{2,1,0:T(8,128)(2,1)S(1)}, bf16[1024,2048]{1,0:T(8,128)(2,1)S(1)}) custom-call(s32[11]{0:T(128)S(1)} %pad_add_fusion.meta_ref, bf16[1024,2048]{1,0:T(8,128)(2,1)S(1)} %get-tuple-element.95.refs_0_, bf16[128,1024]{1,0:T(8,128)(2,1)S(1)} %get-tuple-element.96.refs_1_, ...), custom_call_target="tpu_custom_call" | custom-call | flops 2147483648 | bytes 4194304 | tf_op jit(solution)/shard_map/backward_0_first/pallas_call | solution.py:537
  64.6 3.1 %collective-permute-start.16 = (bf16[1024,128]{1,0:T(8,128)(2,1)S(1)}, bf16[1024,128]{1,0:T(8,128)(2,1)S(1)}, u32[]{:S(2)}, u32[]{:S(2)}) collective-permute-start(bf16[1024,128]{1,0:T(8,128)(2,1)S(1)} %add_3.1), channel_id=1, source_target_pairs={{0,2},{2,3},{3,1},{1,0},{4,6},{6,7},{7,5},{5,4},{8,10},{10,11},{11... | collective-permute-start | bytes 786440 | tf_op jit(solution)/shard_map/ppermute | solution.py:25
  67.7 1.7 %backward_0_second.1 = (f32[512,128]{1,0:T(8,128)S(1)}, f32[512,128]{1,0:T(8,128)S(1)}, f32[512,128]{1,0:T(8,128)S(1)}, f32[512,128]{1,0:T(8,128)S(1)}, bf16[1024,2048]{1,0:T(8,128)(2,1)S(1)}) custom-call(s32[11]{0:T(128)S(1)} %pad_add_fusion.meta_ref, bf16[1024,2048]{1,0:T(8,128)(2,1)S(1)} %get-tuple-element.117.refs_0_, ...), custom_call_target="tpu_custom_call" | custom-call | flops 2147483648 | bytes 4194304 | tf_op jit(solution)/shard_map/backward_0_second/pallas_call | solution.py:537
  70.0 1.5 %collective-permute-start.18 = (bf16[512,128]{1,0:T(8,128)(2,1)S(1)}, bf16[512,128]{1,0:T(8,128)(2,1)S(1)}, u32[]{:S(2)}, u32[]{:S(2)}) collective-permute-start(bf16[512,128]{1,0:T(8,128)(2,1)S(1)} %get-tuple-element.128), channel_id=1, source_target_pairs={{0,16},{4,20},{8,24},{12,28},{16,0},{20,4},{24,8},{28,12},{1,17},{... | collective-permute-start | bytes 393224 | tf_op jit(solution)/shard_map/ppermute | solution.py:19
  73.0 2.9 %backward_0.1.u_ref = f32[1024,128]{1,0:T(8,128)S(1)} custom-call(s32[11]{0:T(128)S(1)} %pad_add_fusion.meta_ref, bf16[1024,2048]{1,0:T(8,128)(2,1)S(1)} %get-tuple-element.116.first_ref, bf16[1024,2048]{1,0:T(8,128)(2,1)S(1)} %get-tuple-element.118.second_ref, bf16[4096,128]{1,0:T(8,128)(2,1)S(1)} %get-tuple-element.123.refs_2_.refs_5_.keys_ref), custom_call_target="tpu_custom_call" | custom-call | flops 2147483648 | bytes 4194304 | tf_op jit(solution)/shard_map/backward_0/pallas_call | solution.py:537
  (34 shorter events, 12.1 us)
Async XLA Ops:
  2.7 8.6 %collective-permute-start.2 = (bf16[1024,128]{1,0:T(8,128)(2,1)S(1)}, bf16[1024,128]{1,0:T(8,128)(2,1)S(1)}, u32[]{:S(2)}, u32[]{:S(2)}) collective-permute-start(bf16[1024,128]{1,0:T(8,128)(2,1)S(1)} %get-tuple-element.69.refs_2_), channel_id=1, source_target_pairs={{0,4},{4,0},{8,12},{12,8},{16,20},{20,16},{24,28},{28,24},{1,5},{5... | collective-permute-start | bytes 786440 | tf_op jit(solution)/shard_map/ppermute | solution.py:19
  3.2 9.5 %collective-permute-start.3 = (bf16[1024,128]{1,0:T(8,128)(2,1)S(1)}, bf16[1024,128]{1,0:T(8,128)(2,1)S(1)}, u32[]{:S(2)}, u32[]{:S(2)}) collective-permute-start(bf16[1024,128]{1,0:T(8,128)(2,1)S(1)} %get-tuple-element.71), channel_id=1, source_target_pairs={{0,8},{4,12},{8,0},{12,4},{16,24},{20,28},{24,16},{28,20},{1,9},{5... | collective-permute-start | bytes 786440 | tf_op jit(solution)/shard_map/ppermute | solution.py:19
  5.8 8.4 %collective-permute-start.4 = (bf16[1024,128]{1,0:T(8,128)(2,1)S(1)}, bf16[1024,128]{1,0:T(8,128)(2,1)S(1)}, u32[]{:S(2)}, u32[]{:S(2)}) collective-permute-start(bf16[1024,128]{1,0:T(8,128)(2,1)S(1)} %get-tuple-element.72), channel_id=1, source_target_pairs={{0,16},{4,20},{8,24},{12,28},{16,0},{20,4},{24,8},{28,12},{1,17},{... | collective-permute-start | bytes 786440 | tf_op jit(solution)/shard_map/ppermute | solution.py:19
  7.3 10.4 %collective-permute-start = (bf16[1040,128]{1,0:T(8,128)(2,1)S(1)}, bf16[1040,128]{1,0:T(8,128)(2,1)S(1)}, u32[]{:S(2)}, u32[]{:S(2)}) collective-permute-start(bf16[1040,128]{1,0:T(8,128)(2,1)S(1)} %get-tuple-element.92.refs_0_.q_ref), channel_id=1, source_target_pairs={{0,2},{2,3},{3,1},{1,0},{4,6},{6,7},{7,5},{5,4},{8,10},{10,11},{11... | collective-permute-start | bytes 798728 | tf_op jit(solution)/shard_map/ppermute | solution.py:25
  14.1 3.6 %collective-permute-start.5 = (bf16[1024,128]{1,0:T(8,128)(2,1)S(1)}, bf16[1024,128]{1,0:T(8,128)(2,1)S(1)}, u32[]{:S(2)}, u32[]{:S(2)}) collective-permute-start(bf16[1024,128]{1,0:T(8,128)(2,1)S(1)} %collective-permute-done.3.refs_9_), channel_id=1, source_target_pairs={{0,4},{4,0},{8,12},{12,8},{16,20},{20,16},{24,28},{28,24},{1,5},{5... | collective-permute-start | bytes 786440 | tf_op jit(solution)/shard_map/ppermute | solution.py:19
  14.1 3.6 %collective-permute-start.6 = (bf16[1024,128]{1,0:T(8,128)(2,1)S(1)}, bf16[1024,128]{1,0:T(8,128)(2,1)S(1)}, u32[]{:S(2)}, u32[]{:S(2)}) collective-permute-start(bf16[1024,128]{1,0:T(8,128)(2,1)S(1)} %collective-permute-done.4.refs_10_), channel_id=1, source_target_pairs={{0,4},{4,0},{8,12},{12,8},{16,20},{20,16},{24,28},{28,24},{1,5},{5... | collective-permute-start | bytes 786440 | tf_op jit(solution)/shard_map/ppermute | solution.py:19
  14.6 9.1 %collective-permute-start.8 = (bf16[1024,128]{1,0:T(8,128)(2,1)S(1)}, bf16[1024,128]{1,0:T(8,128)(2,1)S(1)}, u32[]{:S(2)}, u32[]{:S(2)}) collective-permute-start(bf16[1024,128]{1,0:T(8,128)(2,1)S(1)} %get-tuple-element.82), channel_id=1, source_target_pairs={{0,24},{4,28},{8,16},{12,20},{16,8},{20,12},{24,0},{28,4},{1,25},{... | collective-permute-start | bytes 786440 | tf_op jit(solution)/shard_map/ppermute | solution.py:19
  16.1 10.2 %collective-permute-start.7 = (bf16[1040,128]{1,0:T(8,128)(2,1)S(1)}, bf16[1040,128]{1,0:T(8,128)(2,1)S(1)}, u32[]{:S(2)}, u32[]{:S(2)}) collective-permute-start(bf16[1040,128]{1,0:T(8,128)(2,1)S(1)} %get-tuple-element.92.refs_0_.q_ref), channel_id=1, source_target_pairs={{0,1},{2,0},{3,2},{1,3},{4,5},{6,4},{7,6},{5,7},{8,9},{10,8},{11,1... | collective-permute-start | bytes 798728 | tf_op jit(solution)/shard_map/ppermute | solution.py:25
  23.8 2.6 %collective-permute-start.9 = (bf16[1024,128]{1,0:T(8,128)(2,1)S(1)}, bf16[1024,128]{1,0:T(8,128)(2,1)S(1)}, u32[]{:S(2)}, u32[]{:S(2)}) collective-permute-start(bf16[1024,128]{1,0:T(8,128)(2,1)S(1)} %collective-permute-done.8.refs_10_), channel_id=1, source_target_pairs={{0,4},{4,0},{8,12},{12,8},{16,20},{20,16},{24,28},{28,24},{1,5},{5... | collective-permute-start | bytes 786440 | tf_op jit(solution)/shard_map/ppermute | solution.py:19
  23.8 8.9 %collective-permute-start.1 = (bf16[1040,128]{1,0:T(8,128)(2,1)S(1)}, bf16[1040,128]{1,0:T(8,128)(2,1)S(1)}, u32[]{:S(2)}, u32[]{:S(2)}) collective-permute-start(bf16[1040,128]{1,0:T(8,128)(2,1)S(1)} %collective-permute-done.refs_1_), channel_id=1, source_target_pairs={{0,2},{2,3},{3,1},{1,0},{4,6},{6,7},{7,5},{5,4},{8,10},{10,11},{11... | collective-permute-start | bytes 798728 | tf_op jit(solution)/shard_map/ppermute | solution.py:25
  36.8 7.3 %collective-permute-start.12 = (f32[1,8,128]{2,1,0:T(8,128)S(1)}, f32[1,8,128]{2,1,0:T(8,128)S(1)}, u32[]{:S(2)}, u32[]{:S(2)}) collective-permute-start(f32[1,8,128]{2,1,0:T(8,128)S(1)} %get-tuple-element.91.refs_3_), channel_id=1, source_target_pairs={{0,3},{1,2},{2,1},{3,0},{4,7},{5,6},{6,5},{7,4},{8,11},{9,10},{10,... | collective-permute-start | bytes 12296 | tf_op jit(solution)/shard_map/ppermute | solution.py:19
  40.3 4.5 %collective-permute-start.11 = (f32[1,8,128]{2,1,0:T(8,128)S(1)}, f32[1,8,128]{2,1,0:T(8,128)S(1)}, u32[]{:S(2)}, u32[]{:S(2)}) collective-permute-start(f32[1,8,128]{2,1,0:T(8,128)S(1)} %get-tuple-element.91.refs_3_), channel_id=1, source_target_pairs={{0,2},{1,3},{2,0},{3,1},{4,6},{5,7},{6,4},{7,5},{8,10},{9,11},{10,... | collective-permute-start | bytes 12296 | tf_op jit(solution)/shard_map/ppermute | solution.py:19
  40.7 4.2 %collective-permute-start.10 = (f32[1,8,128]{2,1,0:T(8,128)S(1)}, f32[1,8,128]{2,1,0:T(8,128)S(1)}, u32[]{:S(2)}, u32[]{:S(2)}) collective-permute-start(f32[1,8,128]{2,1,0:T(8,128)S(1)} %get-tuple-element.91.refs_3_), channel_id=1, source_target_pairs={{0,1},{1,0},{2,3},{3,2},{4,5},{5,4},{6,7},{7,6},{8,9},{9,8},{10,11... | collective-permute-start | bytes 12296 | tf_op jit(solution)/shard_map/ppermute | solution.py:19
  48.4 7.6 %collective-permute-start.13 = (bf16[1024,128]{1,0:T(8,128)(2,1)S(1)}, bf16[1024,128]{1,0:T(8,128)(2,1)S(1)}, u32[]{:S(2)}, u32[]{:S(2)}) collective-permute-start(bf16[1024,128]{1,0:T(8,128)(2,1)S(1)} %get-tuple-element.110), channel_id=1, source_target_pairs={{0,2},{2,3},{3,1},{1,0},{4,6},{6,7},{7,5},{5,4},{8,10},{10,11},{11... | collective-permute-start | bytes 786440 | tf_op jit(solution)/shard_map/ppermute | solution.py:25
  56.0 6.8 %collective-permute-start.14 = (bf16[1024,128]{1,0:T(8,128)(2,1)S(1)}, bf16[1024,128]{1,0:T(8,128)(2,1)S(1)}, u32[]{:S(2)}, u32[]{:S(2)}) collective-permute-start(bf16[1024,128]{1,0:T(8,128)(2,1)S(1)} %add_2.1), channel_id=1, source_target_pairs={{0,2},{2,3},{3,1},{1,0},{4,6},{6,7},{7,5},{5,4},{8,10},{10,11},{11... | collective-permute-start | bytes 786440 | tf_op jit(solution)/shard_map/ppermute | solution.py:25
  64.5 4.8 %collective-permute-start.15 = (bf16[4,512,128]{2,1,0:T(8,128)(2,1)S(1)}, bf16[4,512,128]{2,1,0:T(8,128)(2,1)S(1)}, u32[]{:S(2)}, u32[]{:S(2)}) collective-permute-start(bf16[4,512,128]{2,1,0:T(8,128)(2,1)S(1)} %get-tuple-element.120), channel_id=1, source_target_pairs={{0,4},{4,0},{8,12},{12,8},{16,20},{20,16},{24,28},{28,24},{1,5},{5... | collective-permute-start | bytes 1572872 | tf_op jit(solution)/shard_map/ppermute | solution.py:19
  64.6 11.3 %collective-permute-start.16 = (bf16[1024,128]{1,0:T(8,128)(2,1)S(1)}, bf16[1024,128]{1,0:T(8,128)(2,1)S(1)}, u32[]{:S(2)}, u32[]{:S(2)}) collective-permute-start(bf16[1024,128]{1,0:T(8,128)(2,1)S(1)} %add_3.1), channel_id=1, source_target_pairs={{0,2},{2,3},{3,1},{1,0},{4,6},{6,7},{7,5},{5,4},{8,10},{10,11},{11... | collective-permute-start | bytes 786440 | tf_op jit(solution)/shard_map/ppermute | solution.py:25
  69.4 7.8 %collective-permute-start.17 = (bf16[512,128]{1,0:T(8,128)(2,1)S(1)}, bf16[512,128]{1,0:T(8,128)(2,1)S(1)}, u32[]{:S(2)}, u32[]{:S(2)}) collective-permute-start(bf16[512,128]{1,0:T(8,128)(2,1)S(1)} %get-tuple-element.127), channel_id=1, source_target_pairs={{0,8},{4,12},{8,0},{12,4},{16,24},{20,28},{24,16},{28,20},{1,9},{5... | collective-permute-start | bytes 393224 | tf_op jit(solution)/shard_map/ppermute | solution.py:19
  70.0 7.2 %collective-permute-start.18 = (bf16[512,128]{1,0:T(8,128)(2,1)S(1)}, bf16[512,128]{1,0:T(8,128)(2,1)S(1)}, u32[]{:S(2)}, u32[]{:S(2)}) collective-permute-start(bf16[512,128]{1,0:T(8,128)(2,1)S(1)} %get-tuple-element.128), channel_id=1, source_target_pairs={{0,16},{4,20},{8,24},{12,28},{16,0},{20,4},{24,8},{28,12},{1,17},{... | collective-permute-start | bytes 393224 | tf_op jit(solution)/shard_map/ppermute | solution.py:19
  71.6 7.0 %collective-permute-start.19 = (bf16[512,128]{1,0:T(8,128)(2,1)S(1)}, bf16[512,128]{1,0:T(8,128)(2,1)S(1)}, u32[]{:S(2)}, u32[]{:S(2)}) collective-permute-start(bf16[512,128]{1,0:T(8,128)(2,1)S(1)} %get-tuple-element.129), channel_id=1, source_target_pairs={{0,24},{4,28},{8,16},{12,20},{16,8},{20,12},{24,0},{28,4},{1,25},{... | collective-permute-start | bytes 393224 | tf_op jit(solution)/shard_map/ppermute | solution.py:19
